TPU v7x, 32 devices: a whole 2x2x4 slice. The times are simulated.
32 devices in a mesh: ctx: 4 (over y, x), chan: 8 (over z, core).
Axes of the slice: x: 2, y: 2, z: 4, core: 2. Of those that a mesh axis runs over, the one named last changes fastest.
Arguments:
- inputs: bfloat16 [2048, 4096], P('ctx', 'chan'), may hold values from -6 to 6
- w_in: bfloat16 [4096, 3, 4096], P(None, None, 'chan'), may hold values from -0.09375 to 0.09375
- conv_taps: bfloat16 [3, 3, 4096], P(None, None, 'chan'), may hold values from -3.59375 to 3.59375
- skip_gain: float32 [4096], P('chan'), may hold values from 0.5 to 1.5
- filter_taps: bfloat16 [2048, 4096], P('ctx', 'chan'), may hold values from -0.125 to 0.125
- w_out: bfloat16 [4096, 4096], P('chan'), may hold values from -0.125 to 0.125
Outputs:
- result: bfloat16 [2048, 4096], P('ctx', 'chan')
All inputs are finite; a program needn't handle non-finite values.
Results may differ from a plain program's by a relative error of at most 0.024.
Values may be sent and summed in bfloat16 or wider, within the bound.
No kernel may reach another device: no remote copies, remote signals or barrier semaphores. Data moves between devices by JAX's collectives and lax.ppermute only.
A program may use at most 128 MiB of HBM per device.

v0:
```python
import math

import jax
import jax.numpy as jnp
from jax import lax
from jax.sharding import PartitionSpec as P

KERNEL = 3


def from_behind(block, axis, distance):
    devices = range(lax.axis_size(axis))
    route = [(i - distance, i) for i in devices if i - distance in devices]
    return lax.ppermute(block, axis, route)


def angles(row_count, col_count, double_len):
    row_ids = jnp.arange(row_count, dtype=jnp.int32)[:, None]
    col_ids = jnp.arange(col_count, dtype=jnp.int32)[None, :]
    return 2.0 * math.pi / double_len * (row_ids * col_ids % double_len).astype(jnp.float32)


def tables(span_len):
    double_len = 2 * span_len
    first = angles(double_len, span_len, double_len)
    forward_in = jnp.concatenate([jnp.cos(first), -jnp.sin(first)], 0).astype(jnp.bfloat16)
    second = angles(double_len, double_len, double_len)
    forward_taps = jnp.concatenate([jnp.cos(second), -jnp.sin(second)], 0).astype(jnp.bfloat16)
    third = angles(span_len, double_len, double_len)
    inverse = (jnp.concatenate([jnp.cos(third), -jnp.sin(third)], 1) / double_len).astype(
        jnp.bfloat16
    )
    return (forward_in, forward_taps, inverse)


def body(inputs, w_in, conv_taps, skip_gain, filter_taps, w_out):
    span_len, width_dev = inputs.shape
    double_len = 2 * span_len
    groups = lax.axis_size("ctx")
    position = lax.axis_index("ctx")
    w_flat = w_in.reshape(w_in.shape[0], 3 * width_dev)
    projected = jnp.dot(
        lax.all_gather(inputs, "chan", axis=1, tiled=True),
        w_flat,
        preferred_element_type=jnp.float32,
    )
    by_stream = projected.astype(jnp.bfloat16).reshape(span_len, 3, width_dev)
    rim_rows = from_behind(by_stream[span_len - (KERNEL - 1) :], "ctx", 1)
    padded = jnp.concatenate([rim_rows, by_stream], 0)
    filtered = jnp.zeros((span_len, 3, width_dev), jnp.float32)
    for lag in range(KERNEL):
        start_row = KERNEL - 1 - lag
        filtered = filtered + conv_taps[lag].astype(jnp.float32) * padded[
            start_row : start_row + span_len
        ].astype(jnp.float32)
    streams = filtered.astype(jnp.bfloat16)
    gate_out = streams[:, 0]
    gated_in = (streams[:, 1].astype(jnp.float32) * streams[:, 2].astype(jnp.float32)).astype(
        jnp.bfloat16
    )
    forward_in, forward_taps, inverse = tables(span_len)
    all_taps = lax.all_gather(filter_taps[None], "ctx", axis=0, tiled=True)
    previous = jnp.concatenate(
        [jnp.zeros((1, span_len, width_dev), jnp.bfloat16), all_taps[:-1]], 0
    )
    padded_taps = jnp.concatenate(
        [all_taps, jnp.zeros((groups, 1, width_dev), jnp.bfloat16), previous[:, 1:]], 1
    )
    spectra_taps = jnp.einsum(
        "fm,kmd->kfd", forward_taps, padded_taps, preferred_element_type=jnp.float32
    ).astype(jnp.bfloat16)

    def accumulate(spectra):
        pieces = spectra.shape[0]
        lag_index = position - jnp.arange(pieces, dtype=jnp.int32)
        causal = lag_index >= 0
        chosen = jnp.take(spectra_taps, jnp.clip(lag_index, 0, groups - 1), axis=0)
        real_g = chosen[:, :double_len].astype(jnp.float32)
        imag_g = chosen[:, double_len:].astype(jnp.float32)
        real_u = spectra[:, :double_len].astype(jnp.float32)
        imag_u = spectra[:, double_len:].astype(jnp.float32)
        product = jnp.concatenate(
            [real_g * real_u - imag_g * imag_u, real_g * imag_u + imag_g * real_u], 1
        )
        product = jnp.where(causal[:, None, None], product, 0.0)
        return jnp.sum(product, axis=0)

    empty = jnp.zeros((2 * double_len, width_dev), jnp.float32)
    incoming = lax.all_gather(gated_in[None], "ctx", axis=0, tiled=True)

    def transform(current):
        spectra = jnp.einsum(
            "fb,mbc->mfc", forward_in, incoming, preferred_element_type=jnp.float32
        ).astype(jnp.bfloat16)
        return accumulate(spectra)

    def unchanged(current):
        return current

    mixture = lax.cond(jnp.int32(0) <= position, transform, unchanged, empty)
    long_out = jnp.dot(inverse, mixture.astype(jnp.bfloat16), preferred_element_type=jnp.float32)
    long_out = long_out + skip_gain * gated_in.astype(jnp.float32)
    gated_out = (gate_out.astype(jnp.float32) * long_out).astype(jnp.bfloat16)
    shares = lax.psum_scatter(
        lax.dot_general(
            w_out, gated_out, (((0,), (1,)), ((), ())), preferred_element_type=jnp.float32
        ).astype(jnp.bfloat16),
        "chan",
        scatter_dimension=0,
        tiled=True,
    ).astype(jnp.float32)
    result = shares.T.astype(jnp.bfloat16)
    return result


def solution(mesh):
    return jax.shard_map(
        body,
        mesh=mesh,
        in_specs=(
            P("ctx", "chan"),
            P(None, None, "chan"),
            P(None, None, "chan"),
            P("chan"),
            P("ctx", "chan"),
            P("chan", None),
        ),
        out_specs=P("ctx", "chan"),
        check_vma=False,
    )
```

profile of v0, /device:TPU:0, one launch (start us, length us, event | category | flops | bytes accessed | tf_op | source)
XLA Modules:
  0.0 267.9 jit_solution(6293630314486887322)
XLA Ops:
  6.5 0.0 all-gather.6.cloned.1.call-start
  6.5 0.7 all-gather.6.cloned.1.call-update
  7.3 0.0 all-gather.8.cloned.1.call-start
  7.3 0.7 all-gather.8.cloned.1.call-update
  8.0 0.0 all-gather.10.cloned.1.call-start
  8.1 17.0 %copy.26 = bf16[4096,3,512]{0,2,1:T(8,128)(2,1)} copy(bf16[4096,3,512]{2,0,1:T(8,128)(2,1)} %param.9) | data formatting | bytes 25165824 | tf_op args[1]
  25.1 33.8 %all-gather.6.cloned.1.call-done = bf16[512,4096]{1,0:T(8,128)(2,1)} async-done(((bf16[512,512]{1,0:T(8,128)(2,1)}), bf16[512,4096]{1,0:T(8,128)(2,1)}) %all-gather.6.cloned.1.call-update) | async-done | bytes 4194320 | tf_op jit(solution)/shard_map/all_gather | solution.py:43
  58.8 0.0 copy-start.3
  58.8 10.9 %convolution_convert_fusion.1 = bf16[512,1536]{1,0:T(8,128)(2,1)S(1)} fusion(bf16[512,4096]{1,0:T(8,128)(2,1)} %all-gather.6.cloned.1.call-done, bf16[4096,1536]{0,1:T(8,128)(2,1)} %bitcast.48), kind=kOutput, calls=%fused_computation.50 | convolution fusion | flops 6443237376 | bytes 18350080 | tf_op jit(solution)/shard_map/dot_general | solution.py:42
  69.8 3.4 %collective-permute-start = (bf16[2,3,512]{2,0,1:T(2,128)(2,1)S(1)}, bf16[2,3,512]{2,0,1:T(2,128)(2,1)S(1)}, u32[]{:S(2)}, u32[]{:S(2)}) collective-permute-start(bf16[2,3,512]{2,0,1:T(2,128)(2,1)S(1)} %bitcast.52), channel_id=1, source_target_pairs={{0,8},{8,16},{16,24},{1,9},{9,17},{17,25},{2,10},{10,18},{18,26},{... | collective-permute-start | bytes 18440 | tf_op jit(solution)/shard_map/ppermute | solution.py:14
  73.2 0.0 copy-done.3
  73.2 0.7 copy.27
  73.9 0.7 copy.28
  74.7 0.0 collective-permute-done
  74.7 1.2 add_convert_fusion
  75.9 0.0 copy-start
  75.9 1.1 copy-done
  77.1 0.9 multiply_convert_fusion
  78.0 0.0 all-gather.10.cloned.1.call-update
  78.0 0.2 reduce-scatter.2.cloned.1.call-start
  78.3 9.2 %sine_negate_fusion = (f32[512,1024]{1,0:T(8,128)}, f32[512,1024]{1,0:T(8,128)}) fusion(), kind=kLoop, calls=%fused_computation.66 | loop fusion | flops 7864320 | bytes 4194304 | tf_op jit(solution)/shard_map/neg | solution.py:30
  87.5 8.5 %negate_convert_fusion.1 = (bf16[1024,512]{1,0:T(8,128)(2,1)S(1)}, bf16[1024,512]{1,0:T(8,128)(2,1)S(1)}) fusion(), kind=kLoop, calls=%fused_computation.60 | loop fusion | flops 8912896 | bytes 2097152 | tf_op jit(solution)/shard_map/convert.8
  96.0 1.4 pad_maximum_fusion
  97.4 17.8 %negate_convert_fusion = (bf16[1024,1024]{1,0:T(8,128)(2,1)}, bf16[1024,1024]{1,0:T(8,128)(2,1)}) fusion(), kind=kLoop, calls=%fused_computation.38 | loop fusion | flops 17825792 | bytes 4194304 | tf_op jit(solution)/shard_map/convert.6
  115.3 0.0 all-gather.8.cloned.1.call-done
  115.3 0.0 slice-start
  115.3 1.4 slice-done
  116.7 0.7 copy.31
  117.4 4.1 %copy.32 = bf16[4,512,512]{1,2,0:T(8,128)(2,1)} copy(bf16[4,512,512]{2,1,0:T(8,128)(2,1)} %bitcast.49) | data formatting | bytes 4194304 | tf_op jit(solution)/shard_map/all_gather | solution.py:62
  121.5 0.8 pad_slice_fusion
  122.3 13.8 %convert_bitcast_fusion.1 = bf16[4,2048,512]{1,2,0:T(8,128)(2,1)} fusion(bf16[4,511,512]{1,2,0:T(8,128)(2,1)S(1)} %pad_slice_fusion, bf16[4,512,512]{1,2,0:T(8,128)(2,1)} %copy.32, bf16[1024,1024]{1,0:T(8,128)(2,1)} %get-tuple-element.42, bf16[1024,1024]{1,0:T(8,128)(2,1)} %get-tuple-element.43, bf16[1024]{0:T(1024)(128)(2,1)S(1)} %pad.10.clone), kind=kOutput, calls=%fused_computation.20 | convolution fusion | flops 8615100416 | bytes 16775168 | tf_op jit(solution)/shard_map/fm,kmd->kfd/dot_general | solution.py:69
  136.1 0.0 all-gather.10.cloned.1.call-done
  136.1 0.0 copy-start.1
  136.1 0.0 copy-start.5
  136.1 66.4 %conditional.1 = (bf16[2048,512]{0,1:T(8,128)(2,1)S(1)}) conditional(s32[]{:T(128)} %convert_element_type.147, () %tuple.13, (s32[]{:T(128)}, bf16[4,2048,512]{1,2,0:T(8,128)(2,1)}, bf16[4,512,512]{2,1,0:T(8,128)(2,1)}, bf16[2048,512]{1,0:T(8,128)(2,1)}) %tuple.36), branch_computations={%region_0.1_spmd, %region_1.3_spmd} | conditional | flops 4352640000 | bytes 165679264 | solution.py:100
  136.1 11.5 %copy.33 = bf16[4,2048,512]{2,1,0:T(8,128)(2,1)} copy(bf16[4,2048,512]{1,2,0:T(8,128)(2,1)} %get-tuple-element.30) | data formatting | bytes 16777216 | tf_op jit(solution)/shard_map
  147.6 5.8 %fusion.54 = (bf16[4,1024,512]{2,1,0:T(8,128)(2,1)}, bf16[4,1024,512]{2,1,0:T(8,128)(2,1)}) fusion(bf16[4,2048,512]{2,1,0:T(8,128)(2,1)} %copy.33), kind=kLoop, calls=%fused_computation.90 | loop fusion | bytes 16777216 | tf_op jit(solution)/shard_map/cond/branch_1_fun/jit(_take)/gather | solution.py:77
  153.4 4.9 %gather_fusion = bf16[4,1024,512]{2,1,0:T(8,128)(2,1)} fusion(bf16[4,1024,512]{2,1,0:T(8,128)(2,1)} %get-tuple-element.35, s32[1024]{0:T(1024)S(1)} %pad_clamp_fusion), kind=kCustom, calls=%fused_computation | custom fusion | bytes 8388624 | tf_op jit(solution)/shard_map/cond/branch_1_fun/jit(_take)/gather | solution.py:77
  158.3 6.3 %copy.24 = bf16[4,1024,512]{1,2,0:T(8,128)(2,1)} copy(bf16[4,1024,512]{2,1,0:T(8,128)(2,1)} %gather_fusion) | data formatting | bytes 8388608 | tf_op jit(solution)/shard_map/cond/branch_1_fun/jit(_take)/gather | solution.py:77
  164.6 4.9 %gather_fusion.1 = bf16[4,1024,512]{2,1,0:T(8,128)(2,1)} fusion(bf16[4,1024,512]{2,1,0:T(8,128)(2,1)} %get-tuple-element.36, s32[1024]{0:T(1024)S(1)} %pad_clamp_fusion), kind=kCustom, calls=%fused_computation.1 | custom fusion | bytes 8388624 | tf_op jit(solution)/shard_map/cond/branch_1_fun/jit(_take)/gather | solution.py:77
  169.6 6.3 %copy.25 = bf16[4,1024,512]{1,2,0:T(8,128)(2,1)} copy(bf16[4,1024,512]{2,1,0:T(8,128)(2,1)} %gather_fusion.1) | data formatting | bytes 8388608 | tf_op jit(solution)/shard_map/cond/branch_1_fun/jit(_take)/gather | solution.py:77
  175.9 0.0 copy-start.2
  175.9 0.0 copy-start.4
  175.9 5.4 %maximum_select_fusion.1 = bf16[4,2048,512]{1,2,0:T(8,128)(2,1)S(1)} fusion(bf16[4,1024,512]{1,2,0:T(8,128)(2,1)} %copy.25, bf16[4,1024,512]{1,2,0:T(8,128)(2,1)} %copy.24, pred[4]{0:T(512)(128)(4,1)S(1)} %get-tuple-element.37), kind=kLoop, calls=%fused_computation.10 | loop fusion | flops 20971520 | bytes 16777220 | tf_op jit(solution)/shard_map/cond/branch_1_fun/jit(_take)/select_n | solution.py:77
  181.3 0.0 copy-done.2
  181.3 0.0 copy-done.4
  181.3 7.1 %convert_bitcast_fusion = bf16[4,2048,512]{1,2,0:T(8,128)(2,1)} fusion(bf16[4,512,512]{2,1,0:T(8,128)(2,1)S(1)} %copy-done.4, bf16[2048,512]{1,0:T(8,128)(2,1)S(1)} %copy-done.2), kind=kOutput, calls=%fused_computation.11 | convolution fusion | flops 4299161600 | bytes 12582912 | tf_op jit(solution)/shard_map/cond/branch_1_fun/fb,mbc->mfc/dot_general | solution.py:92
  188.4 8.2 %fusion.1 = (f32[4,1024,512]{1,2,0:T(8,128)S(1)}, f32[4,1024,512]{1,2,0:T(8,128)}) fusion(bf16[4,2048,512]{1,2,0:T(8,128)(2,1)} %convert_bitcast_fusion, bf16[4,2048,512]{1,2,0:T(8,128)(2,1)S(1)} %maximum_select_fusion.1), kind=kLoop, calls=%fused_computation.8 | loop fusion | flops 20971520 | bytes 33554432 | tf_op jit(solution)/shard_map/cond/branch_1_fun/sub | solution.py:83
  196.6 5.9 %fusion = bf16[2048,512]{0,1:T(8,128)(2,1)S(1)} fusion(f32[4,1024,512]{1,2,0:T(8,128)} %get-tuple-element.34, f32[4,1024,512]{1,2,0:T(8,128)S(1)} %get-tuple-element.33, pred[4]{0:T(512)(128)(4,1)S(1)} %get-tuple-element.38), kind=kLoop, calls=%fused_computation.3 | loop fusion | flops 11534336 | bytes 18874372 | tf_op jit(solution)/shard_map/cond/branch_1_fun/reduce_sum | solution.py:86
  202.5 0.0 copy-done.1
  202.5 0.0 copy-done.5
  202.5 9.1 %fusion.6 = bf16[4096,512]{0,1:T(8,128)(2,1)} fusion(bf16[512,4096]{1,0:T(8,128)(2,1)} %param.13, bf16[2048,512]{0,1:T(8,128)(2,1)S(1)} %get-tuple-element.48, f32[512,1024]{1,0:T(8,128)} %get-tuple-element.46, f32[512,1024]{1,0:T(8,128)} %get-tuple-element.47, bf16[512,3,512]{2,0,1:T(8,128)(2,1)} %copy-done, bf16[512,1,512]{2,0,1:T(8,128)(2,1)S(1)} %copy-done.1, ...), kind=kOutput, calls=%fused_computation.25 | convolution fusion | flops 3228041216 | bytes 15730688 | tf_op jit(solution)/shard_map/dot_general | solution.py:105
  211.6 0.0 reduce-scatter.2.cloned.1.call-update
  211.6 49.7 %reduce-scatter.2.cloned.1.call-done = bf16[512,512]{0,1:T(8,128)(2,1)} async-done(((bf16[4096,512]{0,1:T(8,128)(2,1)}), bf16[512,512]{0,1:T(8,128)(2,1)}) %reduce-scatter.2.cloned.1.call-update) | async-done | bytes 524304 | tf_op jit(solution)/shard_map/reduce_scatter | solution.py:104
  (6 shorter events, 0.1 us)
Async XLA Ops:
  6.5 52.3 %all-gather.6.cloned.1.call-start = ((), (), s32[]{:S(2)}) async-start(), calls=%async_computation.1 | async-start | bytes 4718592 | tf_op jit(solution)/shard_map/all_gather | solution.py:43
  7.3 108.0 %all-gather.8.cloned.1.call-start = ((), (), s32[]{:S(2)}) async-start(), calls=%async_computation.3 | async-start | bytes 2621440 | tf_op jit(solution)/shard_map/all_gather | solution.py:62
  8.0 128.1 %all-gather.10.cloned.1.call-start = ((), (), s32[]{:S(2)}) async-start(), calls=%async_computation.4 | async-start | bytes 2621440 | tf_op jit(solution)/shard_map/all_gather | solution.py:89
  58.8 14.4 %copy-start.3 = (bf16[3,3,512]{2,1,0:T(4,128)(2,1)S(1)}, bf16[3,3,512]{2,1,0:T(4,128)(2,1)}, u32[]{:S(2)}) copy-start(bf16[3,3,512]{2,1,0:T(4,128)(2,1)} %param.10) | copy-start | bytes 27652
  69.8 4.8 %collective-permute-start = (bf16[2,3,512]{2,0,1:T(2,128)(2,1)S(1)}, bf16[2,3,512]{2,0,1:T(2,128)(2,1)S(1)}, u32[]{:S(2)}, u32[]{:S(2)}) collective-permute-start(bf16[2,3,512]{2,0,1:T(2,128)(2,1)S(1)} %bitcast.52), channel_id=1, source_target_pairs={{0,8},{8,16},{16,24},{1,9},{9,17},{17,25},{2,10},{10,18},{18,26},{... | collective-permute-start | bytes 18440 | tf_op jit(solution)/shard_map/ppermute | solution.py:14
  75.9 1.1 copy-start
  78.0 183.4 %reduce-scatter.2.cloned.1.call-start = ((), (), s32[]{:S(2)}) async-start(), calls=%async_computation.2 | async-start | bytes 4718592 | tf_op jit(solution)/shard_map/reduce_scatter | solution.py:104
  115.3 1.4 slice-start
  136.1 66.4 %copy-start.1 = (bf16[512,1,512]{2,0,1:T(8,128)(2,1)S(1)}, bf16[512,1,512]{2,0,1:T(8,128)(2,1)}, u32[]{:S(2)}) copy-start(bf16[512,1,512]{2,0,1:T(8,128)(2,1)} %multiply_convert_fusion) | copy-start | bytes 1572868
  136.1 66.4 %copy-start.5 = (f32[512]{0:T(512)S(1)}, f32[512]{0:T(512)}, u32[]{:S(2)}) copy-start(f32[512]{0:T(512)} %param.11) | copy-start | bytes 6148
  175.9 5.4 %copy-start.2 = (bf16[2048,512]{1,0:T(8,128)(2,1)S(1)}, bf16[2048,512]{1,0:T(8,128)(2,1)}, u32[]{:S(2)}) copy-start(bf16[2048,512]{1,0:T(8,128)(2,1)} %get-tuple-element.20) | copy-start | bytes 6291460 | tf_op jit(solution)/shard_map/cond
  175.9 5.4 %copy-start.4 = (bf16[4,512,512]{2,1,0:T(8,128)(2,1)S(1)}, bf16[4,512,512]{2,1,0:T(8,128)(2,1)}, u32[]{:S(2)}) copy-start(bf16[4,512,512]{2,1,0:T(8,128)(2,1)} %get-tuple-element.31) | copy-start | bytes 6291460 | tf_op jit(solution)/shard_map/cond
Sparse Core Ops, SparseCore 0:
  9.0 49.8 all-gather.5
  60.7 34.0 all-gather.7
  96.6 35.3 all-gather.9
  211.7 49.5 reduce-scatter.1
where the time goes:
time: 269 us; the launch traced here: 268 us
  waiting for transfers between devices  85 us (32%)
  local copies, waits for them, and re-layouts  66.4 us (25%)
  other arithmetic  58.7 us (22%)
  matrix products  40.9 us (15%)
  between operations  13.3 us (5%)
  starting transfers between devices  3.68 us (1%)
    reduce_scatter x1, waiting for transfers between devices, body(): lax.psum_scatter(lax.dot_general(w_out, gated_out, (((0,), (1,)), ((), ()...  49.7 us
    all_gather x1, waiting for transfers between devices, body(): lax.all_gather(inputs, 'chan', axis=1, tiled=True)  33.8 us
    gather x5, local copies, waits for them, and re-layouts, accumulate(): chosen = jnp.take(spectra_taps, jnp.clip(lag_index, 0, groups - 1), axis=0)  28.3 us
    another operation x2, other arithmetic  26.4 us
    unnamed x9, local copies, waits for them, and re-layouts  18.2 us
    dot_general x1, matrix products, body(): jnp.einsum('fm,kmd->kfd', forward_taps, padded_taps, preferred_element_ty...  13.8 us
    another operation x1, local copies, waits for them, and re-layouts  11.5 us
    dot_general x1, matrix products, body(): jnp.dot(lax.all_gather(inputs, 'chan', axis=1, tiled=True), w_flat, prefe...  10.9 us
  transfers between devices with their start and end apart: 5, of which 2 were waited for; matrix products, arithmetic and copies ran while one was open for 33% of the time, Pallas kernels for 0%

commit v1 on v0

v1 whole, which is shorter than its diff:
```python
import math

import jax
import jax.numpy as jnp
import ml_dtypes
import numpy as np
from jax import lax
from jax.sharding import PartitionSpec as P

KERNEL = 3
BF16 = jnp.bfloat16
F32 = jnp.float32


def half_tables(span):
    n = 2 * span
    f = np.arange(span)[:, None]
    m = np.arange(n)[None, :]
    ang = 2.0 * math.pi * ((f * m) % n) / n
    real = np.cos(ang)
    imag = -np.sin(ang)
    imag[0] = np.where(np.arange(n) % 2 == 0, 1.0, -1.0)
    forward = np.concatenate([real, imag], 0).astype(ml_dtypes.bfloat16)
    weight = np.full((n, 1), 2.0 / n)
    weight[0] = 1.0 / n
    weight[span] = 1.0 / n
    back = (np.concatenate([real, imag], 0) * weight)[:, :span].T
    return forward, np.ascontiguousarray(back).astype(ml_dtypes.bfloat16)


def shift(x, axis, distance):
    size = lax.axis_size(axis)
    return lax.ppermute(x, axis, [(i, (i + distance) % size) for i in range(size)])


def sibling(x):
    return lax.ppermute(x, "chan", [(i, i ^ 1) for i in range(lax.axis_size("chan"))])


def dot(a, b):
    return jnp.dot(a, b, preferred_element_type=F32)


def gather_chips(x):
    chips = lax.axis_size("chan") // 2
    half = x.shape[0] // 2
    top, low = x[:half], x[half:]
    found = []
    up = [top, low]
    down = [top, low]
    for d in range(1, chips // 2 + 1):
        if 2 * d < chips:
            up = [shift(v, "chan", 2) for v in up]
            down = [shift(v, "chan", -2) for v in down]
            found.append((d, up))
            found.append((-d, down))
        else:
            found.append((d, [shift(up[0], "chan", 2), shift(down[1], "chan", -2)]))
    return found


def exchange(pieces):
    groups = lax.axis_size("ctx")
    me = lax.axis_index("ctx")
    out = [(me, pieces(me))]
    for s in range(1, groups):
        out.append(((me - s) % groups, shift(pieces((me + s) % groups), "ctx", s)))
    return out


def in_order(found):
    groups = len(found)
    block = found[0][1]
    whole = jnp.zeros((groups,) + block.shape, block.dtype)
    for source, b in found:
        whole = lax.dynamic_update_index_in_dim(whole, b, source, 0)
    return whole


def body(inputs, w_in, conv_taps, skip_gain, filter_taps, w_out):
    span, width = inputs.shape
    n = 2 * span
    groups = lax.axis_size("ctx")
    me = lax.axis_index("ctx")
    chan = lax.axis_size("chan")
    chips = chan // 2
    place = lax.axis_index("chan")
    chip, core = place // 2, place % 2
    quarter = width // groups
    forward_np, back_np = half_tables(span)
    forward, back = jnp.asarray(forward_np), jnp.asarray(back_np)

    found = gather_chips(inputs)

    taps = jnp.stack(jnp.split(filter_taps, groups, axis=1))
    taps = in_order(
        exchange(lambda q: lax.dynamic_index_in_dim(taps, q, 0, keepdims=False))
    )
    taps = jnp.concatenate(list(taps), 1)
    row_ids = lax.broadcasted_iota(jnp.int32, (span, 1), 0)
    before = jnp.concatenate(
        [jnp.zeros((span, quarter), BF16), taps[:, : (groups - 1) * quarter]], 1
    )
    before = jnp.where(row_ids == 0, 0, before)
    spectra_taps = dot(forward, jnp.concatenate([taps, before], 0)).astype(BF16)

    w_split = w_out.reshape(width, chips, 2, -1)
    mine = lax.dynamic_index_in_dim(w_split, core, 2, keepdims=False)
    theirs = sibling(lax.dynamic_index_in_dim(w_split, 1 - core, 2, keepdims=False))

    w_flat = w_in.reshape(w_in.shape[0], 3 * width)

    def part(block, chip_id, core_id):
        rows = lax.dynamic_slice_in_dim(w_flat, (chip_id * 2 + core_id) * width, width, 0)
        return dot(block, rows)

    total = part(inputs, chip, core) + part(sibling(inputs), chip, 1 - core)
    for d, (top, low) in found:
        block = jnp.concatenate([top, low], 0)
        source = (chip - d) % chips
        total = total + part(block, source, core)
        total = total + part(sibling(block), source, 1 - core)
    projected = total.astype(BF16)

    rim = shift(projected[span - (KERNEL - 1) :], "ctx", 1)
    rim = jnp.where(me > 0, rim, 0)
    padded = jnp.concatenate([rim, projected], 0)
    filtered = jnp.zeros((span, 3 * width), F32)
    flat_taps = conv_taps.reshape(KERNEL, 3 * width).astype(F32)
    for lag in range(KERNEL):
        first = KERNEL - 1 - lag
        filtered = filtered + flat_taps[lag] * padded[first : first + span].astype(F32)
    streams = filtered.astype(BF16)
    gate_out = streams[:, :width]
    gated_in = (
        streams[:, width : 2 * width].astype(F32) * streams[:, 2 * width :].astype(F32)
    ).astype(BF16)

    split_in = jnp.stack(jnp.split(gated_in, groups, axis=1))
    signal = in_order(
        exchange(lambda q: lax.dynamic_index_in_dim(split_in, q, 0, keepdims=False))
    )
    signal = jnp.concatenate(list(signal), 1)
    spectra_in = dot(forward[:, :span], signal).astype(BF16)
    real_g = spectra_taps[:span].astype(F32)
    imag_g = spectra_taps[span:].astype(F32)
    real_u = spectra_in[:span].astype(F32)
    imag_u = spectra_in[span:].astype(F32)
    first_row = row_ids == 0
    mixed = []
    for i in range(groups):
        real = jnp.zeros((span, quarter), F32)
        imag = jnp.zeros((span, quarter), F32)
        for j in range(i + 1):
            g = slice((i - j) * quarter, (i - j + 1) * quarter)
            u = slice(j * quarter, (j + 1) * quarter)
            rr = real_g[:, g] * real_u[:, u]
            ii = imag_g[:, g] * imag_u[:, u]
            ri = real_g[:, g] * imag_u[:, u] + imag_g[:, g] * real_u[:, u]
            real = real + jnp.where(first_row, rr, rr - ii)
            imag = imag + jnp.where(first_row, ii, ri)
        mixed.append(jnp.concatenate([real, imag], 0).astype(BF16))
    mixture = jnp.concatenate(mixed, 1)
    long_share = dot(back, mixture).astype(BF16)
    long_share = jnp.stack(jnp.split(long_share, groups, axis=1))
    long_out = in_order(
        exchange(lambda q: lax.dynamic_index_in_dim(long_share, q, 0, keepdims=False))
    )
    long_out = jnp.concatenate(list(long_out), 1).astype(F32)
    long_out = long_out + skip_gain * gated_in.astype(F32)
    gated_out = (gate_out.astype(F32) * long_out).astype(BF16)

    other = sibling(gated_out)

    def share(chip_id, rows=slice(None)):
        a = lax.dynamic_index_in_dim(mine, chip_id, 1, keepdims=False)
        b = lax.dynamic_index_in_dim(theirs, chip_id, 1, keepdims=False)
        return dot(gated_out[rows], a) + dot(other[rows], b)

    half = span // 2
    top, low = slice(0, half), slice(half, span)
    up = [None, None]
    down = [None, None]

    def carry(old, new):
        return new if old is None else old.astype(F32) + new

    for d in range(chips // 2, 0, -1):
        if 2 * d < chips:
            ahead, behind = (chip + d) % chips, (chip - d) % chips
            up = [
                shift(carry(u, share(ahead, r)).astype(BF16), "chan", 2)
                for u, r in zip(up, (top, low))
            ]
            down = [
                shift(carry(u, share(behind, r)).astype(BF16), "chan", -2)
                for u, r in zip(down, (top, low))
            ]
        else:
            far = (chip + d) % chips
            up[0] = shift(share(far, top).astype(BF16), "chan", 2)
            down[1] = shift(share(far, low).astype(BF16), "chan", -2)
    result = []
    for k, r in enumerate((top, low)):
        total = share(chip, r)
        for extra in (up[k], down[k]):
            if extra is not None:
                total = total + extra.astype(F32)
        result.append(total.astype(BF16))
    return jnp.concatenate(result, 0)


def solution(mesh):
    return jax.shard_map(
        body,
        mesh=mesh,
        in_specs=(
            P("ctx", "chan"),
            P(None, None, "chan"),
            P(None, None, "chan"),
            P("chan"),
            P("ctx", "chan"),
            P("chan", None),
        ),
        out_specs=P("ctx", "chan"),
        check_vma=False,
    )
```

time: 269 us -> 167 us (0.62)
  other arithmetic: 58.7 us -> 6.96 us
  waiting for transfers between devices: 85 us -> 43.7 us
  starting transfers between devices: 3.68 us -> 31.4 us
  local copies, waits for them, and re-layouts: 66.4 us -> 45.4 us
  between operations: 13.3 us -> 0.65 us
  matrix products: 40.9 us -> 36.7 us
    reduce_scatter x1 -> x0, waiting for transfers between devices: 49.7 us -> none  [body(): lax.psum_scatter(lax.dot_general(w_out, gated_out, (((0,), (1,)), ((), ()...]
    ppermute x1 -> x28, waiting for transfers between devices: 0.01 us -> 43.7 us  [the longest x22 43.7 us: shift(): lax.ppermute(x, axis, [(i, (i + distance) % size) for i in range(size)])]
    all_gather x3 -> x0, waiting for transfers between devices: 33.8 us -> none  [the longest x1 33.8 us: body(): lax.all_gather(inputs, 'chan', axis=1, tiled=True)]
    gather x5 -> x0, local copies, waits for them, and re-layouts: 28.3 us -> none  [accumulate(): chosen = jnp.take(spectra_taps, jnp.clip(lag_index, 0, groups - 1), axis=0)]
    ppermute x1 -> x28, starting transfers between devices: 3.38 us -> 31.4 us  [the longest x22 30.8 us: shift(): lax.ppermute(x, axis, [(i, (i + distance) % size) for i in range(size)])]
    another operation x2 -> x9, other arithmetic: 26.4 us -> 3.3 us
    neg x1 -> x0, other arithmetic: 9.18 us -> none  [tables(): -jnp.sin(third)]
    another operation x1 -> x9, local copies, waits for them, and re-layouts: 11.5 us -> 3.23 us  [the longest x1 1.22 us: body(): taps = jnp.concatenate(list(taps), 1)]
  transfers between devices with their start and end apart: 5 -> 28, of which waited for: 2 -> 12; matrix products, arithmetic and copies ran while one was open for 33% -> 46% of each run, Pallas kernels for 0% -> 0%
where the time goes in v1:
time: 167 us; the launch traced here: 165 us
  local copies, waits for them, and re-layouts  45.4 us (27%)
  waiting for transfers between devices  43.7 us (26%)
  matrix products  36.7 us (22%)
  starting transfers between devices  31.4 us (19%)
  other arithmetic  6.96 us (4%)
    ppermute x22, waiting for transfers between devices, shift(): lax.ppermute(x, axis, [(i, (i + distance) % size) for i in range(size)])  43.7 us
    dot_general x28, matrix products, dot(): return jnp.dot(a, b, preferred_element_type=F32)  36.7 us
    ppermute x22, starting transfers between devices, shift(): lax.ppermute(x, axis, [(i, (i + distance) % size) for i in range(size)])  30.8 us
    unnamed x27, local copies, waits for them, and re-layouts  26.2 us
    dynamic_slice x2, local copies, waits for them, and re-layouts, body(): lax.dynamic_index_in_dim(w_split, 1 - core, 2, keepdims=False)  5.62 us
  transfers between devices with their start and end apart: 28, of which 12 were waited for; matrix products, arithmetic and copies ran while one was open for 46% of the time, Pallas kernels for 0%

profile of v1, /device:TPU:0, one launch (start us, length us, event | category | flops | bytes accessed | tf_op | source)
XLA Modules:
  0.0 164.9 jit_solution(13296341224680294864)
XLA Ops:
  0.5 1.9 %fusion.178 = (bf16[256,512]{1,0:T(8,128)(2,1)}, bf16[256,512]{1,0:T(8,128)(2,1)}) fusion(bf16[512,512]{1,0:T(8,128)(2,1)} %param.8), kind=kLoop, calls=%fused_computation.280 | loop fusion | bytes 1048576 | tf_op jit(solution)/shard_map/slice | solution.py:47
  2.3 4.6 %collective-permute-start.4 = (bf16[256,512]{1,0:T(8,128)(2,1)}, bf16[256,512]{1,0:T(8,128)(2,1)}, u32[]{:S(2)}, u32[]{:S(2)}) collective-permute-start(bf16[256,512]{1,0:T(8,128)(2,1)} %get-tuple-element.49), channel_id=1, source_target_pairs={{0,6},{1,7},{2,0},{3,1},{4,2},{5,3},{6,4},{7,5},{8,14},{9,15},{10,... | collective-permute-start | bytes 786440 | tf_op jit(solution)/shard_map/ppermute | solution.py:33
  6.9 3.8 %collective-permute-start.5 = (bf16[256,512]{1,0:T(8,128)(2,1)}, bf16[256,512]{1,0:T(8,128)(2,1)}, u32[]{:S(2)}, u32[]{:S(2)}) collective-permute-start(bf16[256,512]{1,0:T(8,128)(2,1)} %get-tuple-element.48), channel_id=1, source_target_pairs={{0,6},{1,7},{2,0},{3,1},{4,2},{5,3},{6,4},{7,5},{8,14},{9,15},{10,... | collective-permute-start | bytes 786440 | tf_op jit(solution)/shard_map/ppermute | solution.py:33
  10.7 17.0 %copy.12 = bf16[4096,3,512]{0,2,1:T(8,128)(2,1)} copy(bf16[4096,3,512]{2,0,1:T(8,128)(2,1)} %param.9) | data formatting | bytes 25165824 | tf_op args[1]
  28.4 0.7 slice_bitcast_fusion.23
  29.1 2.6 %fusion.18 = f32[1536,512]{0,1:T(8,128)S(1)} fusion(bf16[512,512]{1,0:T(8,128)(2,1)} %param.8, bf16[4096,1536]{0,1:T(8,128)(2,1)} %bitcast.159, s32[]{:T(128)S(6)} %select_n.260), kind=kOutput, calls=%fused_computation.26 | convolution fusion | flops 805306368 | bytes 5242884 | tf_op jit(solution)/shard_map/dot_general | solution.py:41
  31.7 0.9 pad_maximum_fusion.1
  32.6 0.9 broadcast.26.clone.1
  33.4 1.8 %dynamic-slice_bitcast_fusion.6 = (bf16[512,128]{1,0:T(8,128)(2,1)S(1)}, bf16[512,128]{1,0:T(8,128)(2,1)S(1)}, bf16[512,128]{1,0:T(8,128)(2,1)S(1)}, bf16[4,512,128]{2,1,0:T(8,128)(2,1)}) fusion(bf16[4,512,128]{2,1,0:T(8,128)(2,1)} %pad_maximum_fusion.1, s32[]{:T(128)S(6)} %select_n.283, s32[]{:T(128)S(6)} %select_n.279, s32[]{:T(128)S(6)} %select_n.275, ...), kind=kLoop, calls=%fused_computation.234 | loop fusion | bytes 1048592 | tf_op jit(solution)/shard_map/jit(dynamic_index_in_dim)/squeeze | solution.py:97
  35.8 0.7 mul.219
  36.5 1.3 mul.222
  37.8 6.5 %copy.14 = bf16[512,4096]{0,1:T(8,128)(2,1)} copy(bf16[512,4096]{1,0:T(8,128)(2,1)} %param.13) | data formatting | bytes 8388608 | tf_op args[5]
  44.2 1.5 collective-permute-start.11
  45.7 1.0 constant_dynamic-update-slice_fusion.3
  46.7 1.6 collective-permute-start.12
  48.3 1.0 constant_dynamic-update-slice_fusion.2
  49.3 1.0 constant_dynamic-update-slice_fusion.1
  50.4 1.0 constant_dynamic-update-slice_fusion
  51.3 2.4 %fusion.12 = f32[512,1536]{1,0:T(8,128)S(1)} fusion(bf16[512,512]{1,0:T(8,128)(2,1)S(1)} %constant_dynamic-update-slice_fusion.2, bf16[4096,1536]{0,1:T(8,128)(2,1)} %bitcast.160, s32[]{:T(128)S(6)} %select_n.266), kind=kOutput, calls=%fused_computation.20 | convolution fusion | flops 805306368 | bytes 5242884 | tf_op jit(solution)/shard_map/dot_general | solution.py:41
  53.8 3.9 %collective-permute-start.8 = (bf16[256,512]{1,0:T(8,128)(2,1)}, bf16[256,512]{1,0:T(8,128)(2,1)S(1)}, u32[]{:S(2)}, u32[]{:S(2)}) collective-permute-start(bf16[256,512]{1,0:T(8,128)(2,1)} %collective-permute-done.5), channel_id=1, source_target_pairs={{0,6},{1,7},{2,0},{3,1},{4,2},{5,3},{6,4},{7,5},{8,14},{9,15},{10,... | collective-permute-start | bytes 786440 | tf_op jit(solution)/shard_map/ppermute | solution.py:33
  57.7 2.5 %fusion.2 = f32[512,1536]{1,0:T(8,128)S(1)} fusion(f32[1536,512]{0,1:T(8,128)S(1)} %fusion.18, bf16[512,512]{1,0:T(8,128)(2,1)} %collective-permute-done, bf16[4096,1536]{0,1:T(8,128)(2,1)} %bitcast.161, s32[]{:T(128)S(6)} %select_n.261), kind=kOutput, calls=%fused_computation.5 | convolution fusion | flops 806092800 | bytes 8388612 | tf_op jit(solution)/shard_map/dot_general | solution.py:41
  60.2 1.4 collective-permute-done.7
  61.6 5.3 %collective-permute-done.8 = bf16[256,512]{1,0:T(8,128)(2,1)S(1)} collective-permute-done((bf16[256,512]{1,0:T(8,128)(2,1)}, bf16[256,512]{1,0:T(8,128)(2,1)S(1)}, u32[]{:S(2)}, u32[]{:S(2)}) %collective-permute-start.8) | collective-permute-done | bytes 262176 | tf_op jit(solution)/shard_map/ppermute | solution.py:33
  67.0 1.5 collective-permute-start.13
  68.5 2.4 %fusion.10 = f32[512,1536]{1,0:T(8,128)S(1)} fusion(bf16[512,512]{1,0:T(8,128)(2,1)S(1)} %collective-permute-done.6, bf16[4096,1536]{0,1:T(8,128)(2,1)} %bitcast.162, s32[]{:T(128)S(6)} %select_n.267), kind=kOutput, calls=%fused_computation.18 | convolution fusion | flops 805306368 | bytes 5242884 | tf_op jit(solution)/shard_map/dot_general | solution.py:41
  71.0 2.4 %fusion.14 = f32[512,1536]{1,0:T(8,128)S(1)} fusion(bf16[512,512]{1,0:T(8,128)(2,1)S(1)} %collective-permute-done.3, bf16[4096,1536]{0,1:T(8,128)(2,1)} %bitcast.163, s32[]{:T(128)S(6)} %select_n.264), kind=kOutput, calls=%fused_computation.22 | convolution fusion | flops 805306368 | bytes 5242884 | tf_op jit(solution)/shard_map/dot_general | solution.py:41
  73.4 2.7 %fusion.4 = f32[512,1536]{1,0:T(8,128)S(1)} fusion(f32[512,1536]{1,0:T(8,128)S(1)} %fusion.10, f32[512,1536]{1,0:T(8,128)S(1)} %fusion.12, f32[512,1536]{1,0:T(8,128)S(1)} %fusion.14, f32[512,1536]{1,0:T(8,128)S(1)} %fusion.2, bf16[512,512]{1,0:T(8,128)(2,1)S(1)} %constant_dynamic-update-slice_fusion, bf16[4096,1536]{0,1:T(8,128)(2,1)} %bitcast.164, ...), kind=kOutput, calls=%fused_computation.7 | convolution fusion | flops 808452096 | bytes 17825796 | tf_op jit(solution)/shard_map/dot_general | solution.py:41
  76.1 2.4 %fusion.7 = f32[512,1536]{1,0:T(8,128)S(1)} fusion(bf16[512,512]{1,0:T(8,128)(2,1)S(1)} %collective-permute-done.9, bf16[4096,1536]{0,1:T(8,128)(2,1)} %bitcast.165, s32[]{:T(128)S(6)} %select_n.270), kind=kOutput, calls=%fused_computation.15 | convolution fusion | flops 805306368 | bytes 5242884 | tf_op jit(solution)/shard_map/dot_general | solution.py:41
  78.5 2.6 %fusion.5 = bf16[512,1536]{1,0:T(8,128)(2,1)S(1)} fusion(f32[512,1536]{1,0:T(8,128)S(1)} %fusion.7, f32[512,1536]{1,0:T(8,128)S(1)} %fusion.4, bf16[512,512]{1,0:T(8,128)(2,1)S(1)} %constant_dynamic-update-slice_fusion.4, bf16[4096,1536]{0,1:T(8,128)(2,1)} %bitcast.166, s32[]{:T(128)S(6)} %select_n.269), kind=kOutput, calls=%fused_computation.9 | convolution fusion | flops 807665664 | bytes 9961476 | tf_op jit(solution)/shard_map/dot_general | solution.py:41
  82.4 3.3 %collective-permute-done.10 = bf16[2,1536]{1,0:T(2,128)(2,1)S(1)} collective-permute-done((bf16[2,1536]{1,0:T(2,128)(2,1)S(1)}, bf16[2,1536]{1,0:T(2,128)(2,1)S(1)}, u32[]{:S(2)}, u32[]{:S(2)}) %collective-permute-start.10) | collective-permute-done | bytes 6176 | tf_op jit(solution)/shard_map/ppermute | solution.py:33
  85.7 1.2 add_convert_fusion
  88.7 2.9 %collective-permute-start.16 = (bf16[512,128]{1,0:T(8,128)(2,1)S(1)}, bf16[512,128]{1,0:T(8,128)(2,1)S(1)}, u32[]{:S(2)}, u32[]{:S(2)}) collective-permute-start(bf16[512,128]{1,0:T(8,128)(2,1)S(1)} %get-tuple-element.40), channel_id=1, source_target_pairs={{0,24},{8,0},{16,8},{24,16},{1,25},{9,1},{17,9},{25,17},{2,26},{10... | collective-permute-start | bytes 393224 | tf_op jit(solution)/shard_map/ppermute | solution.py:33
  91.6 3.0 %collective-permute-done.14 = bf16[512,128]{1,0:T(8,128)(2,1)S(1)} collective-permute-done((bf16[512,128]{1,0:T(8,128)(2,1)S(1)}, bf16[512,128]{1,0:T(8,128)(2,1)S(1)}, u32[]{:S(2)}, u32[]{:S(2)}) %collective-permute-start.14) | collective-permute-done | bytes 131104 | tf_op jit(solution)/shard_map/ppermute | solution.py:33
  94.6 1.1 collective-permute-done.15
  96.4 1.2 slice_bitcast_fusion.19
  97.7 0.8 fusion.61
  98.5 0.9 fusion.20
  99.7 0.8 fusion.21
  103.1 0.7 copy-done.8
  103.8 0.7 fusion.22
  104.9 2.2 %collective-permute-start.17 = (bf16[512,128]{1,0:T(8,128)(2,1)S(1)}, bf16[512,128]{1,0:T(8,128)(2,1)S(1)}, u32[]{:S(2)}, u32[]{:S(2)}) collective-permute-start(bf16[512,128]{1,0:T(8,128)(2,1)S(1)} %get-tuple-element.18), channel_id=1, source_target_pairs={{0,8},{8,16},{16,24},{24,0},{1,9},{9,17},{17,25},{25,1},{2,10},{10... | collective-permute-start | bytes 393224 | tf_op jit(solution)/shard_map/ppermute | solution.py:33
  107.1 1.5 constant_dynamic-slice_fusion
  108.6 4.1 %copy.16 = bf16[512,4,1,512]{3,0,2,1:T(8,128)(2,1)} copy(bf16[512,4,1,512]{0,3,2,1:T(8,128)(2,1)} %constant_dynamic-slice_fusion) | data formatting | bytes 4194304 | tf_op jit(solution)/shard_map/jit(dynamic_index_in_dim)/dynamic_slice | solution.py:109
  112.8 1.0 collective-permute-start.18
  113.8 1.5 collective-permute-start.19
  115.3 3.4 %collective-permute-done.18 = bf16[512,128]{1,0:T(8,128)(2,1)S(1)} collective-permute-done((bf16[512,128]{1,0:T(8,128)(2,1)S(1)}, bf16[512,128]{1,0:T(8,128)(2,1)S(1)}, u32[]{:S(2)}, u32[]{:S(2)}) %collective-permute-start.18) | collective-permute-done | bytes 131104 | tf_op jit(solution)/shard_map/ppermute | solution.py:33
  118.7 0.7 collective-permute-done.19
  122.7 1.3 fusion.28
  124.0 0.7 collective-permute-start.22
  124.7 1.3 fusion.29
  126.0 3.3 %collective-permute-start.24 = (bf16[256,512]{1,0:T(8,128)(2,1)S(1)}, bf16[256,512]{1,0:T(8,128)(2,1)S(1)}, u32[]{:S(2)}, u32[]{:S(2)}) collective-permute-start(bf16[256,512]{1,0:T(8,128)(2,1)S(1)} %fusion.29), channel_id=1, source_target_pairs={{0,6},{1,7},{2,0},{3,1},{4,2},{5,3},{6,4},{7,5},{8,14},{9,15},{10,... | collective-permute-start | bytes 786440 | tf_op jit(solution)/shard_map/ppermute | solution.py:33
  129.3 1.3 fusion.32
  130.8 4.3 %collective-permute-done.22 = bf16[256,512]{1,0:T(8,128)(2,1)S(1)} collective-permute-done((bf16[256,512]{1,0:T(8,128)(2,1)S(1)}, bf16[256,512]{1,0:T(8,128)(2,1)S(1)}, u32[]{:S(2)}, u32[]{:S(2)}) %collective-permute-start.22) | collective-permute-done | bytes 262176 | tf_op jit(solution)/shard_map/ppermute | solution.py:33
  135.0 1.3 add_convert_fusion.3
  136.5 1.3 fusion.31
  137.9 8.2 %collective-permute-done.26 = bf16[256,512]{1,0:T(8,128)(2,1)S(1)} collective-permute-done((bf16[256,512]{1,0:T(8,128)(2,1)S(1)}, bf16[256,512]{1,0:T(8,128)(2,1)S(1)}, u32[]{:S(2)}, u32[]{:S(2)}) %collective-permute-start.26) | collective-permute-done | bytes 262176 | tf_op jit(solution)/shard_map/ppermute | solution.py:33
  146.0 1.3 add_convert_fusion.2
  147.4 0.9 collective-permute-start.27
  148.3 3.8 %collective-permute-done.23 = bf16[256,512]{1,0:T(8,128)(2,1)S(1)} collective-permute-done((bf16[256,512]{1,0:T(8,128)(2,1)S(1)}, bf16[256,512]{1,0:T(8,128)(2,1)S(1)}, u32[]{:S(2)}, u32[]{:S(2)}) %collective-permute-start.23) | collective-permute-done | bytes 262176 | tf_op jit(solution)/shard_map/ppermute | solution.py:33
  152.0 1.4 fusion.27
  153.4 4.1 %collective-permute-done.25 = bf16[256,512]{1,0:T(8,128)(2,1)S(1)} collective-permute-done((bf16[256,512]{1,0:T(8,128)(2,1)S(1)}, bf16[256,512]{1,0:T(8,128)(2,1)S(1)}, u32[]{:S(2)}, u32[]{:S(2)}) %collective-permute-start.25) | collective-permute-done | bytes 262176 | tf_op jit(solution)/shard_map/ppermute | solution.py:33
  157.6 5.2 %collective-permute-done.27 = bf16[256,512]{1,0:T(8,128)(2,1)S(1)} collective-permute-done((bf16[256,512]{1,0:T(8,128)(2,1)S(1)}, bf16[256,512]{1,0:T(8,128)(2,1)S(1)}, u32[]{:S(2)}, u32[]{:S(2)}) %collective-permute-start.27) | collective-permute-done | bytes 262176 | tf_op jit(solution)/shard_map/ppermute | solution.py:33
  162.7 1.4 fusion.30
  164.1 0.8 pad_maximum_fusion.4
  (95 shorter events, 12.2 us)
Async XLA Ops:
  0.0 53.8 %collective-permute-start = (bf16[512,512]{1,0:T(8,128)(2,1)}, bf16[512,512]{1,0:T(8,128)(2,1)}, u32[]{:S(2)}, u32[]{:S(2)}) collective-permute-start(bf16[512,512]{1,0:T(8,128)(2,1)} %param.8), channel_id=1, source_target_pairs={{0,1},{1,0},{2,3},{3,2},{4,5},{5,4},{6,7},{7,6},{8,9},{9,8},{10,11... | collective-permute-start | bytes 1572872 | tf_op jit(solution)/shard_map/ppermute | solution.py:37
  2.3 41.9 %collective-permute-start.4 = (bf16[256,512]{1,0:T(8,128)(2,1)}, bf16[256,512]{1,0:T(8,128)(2,1)}, u32[]{:S(2)}, u32[]{:S(2)}) collective-permute-start(bf16[256,512]{1,0:T(8,128)(2,1)} %get-tuple-element.49), channel_id=1, source_target_pairs={{0,6},{1,7},{2,0},{3,1},{4,2},{5,3},{6,4},{7,5},{8,14},{9,15},{10,... | collective-permute-start | bytes 786440 | tf_op jit(solution)/shard_map/ppermute | solution.py:33
  6.9 42.3 %collective-permute-start.1 = (bf16[256,512]{1,0:T(8,128)(2,1)}, bf16[256,512]{1,0:T(8,128)(2,1)}, u32[]{:S(2)}, u32[]{:S(2)}) collective-permute-start(bf16[256,512]{1,0:T(8,128)(2,1)} %get-tuple-element.49), channel_id=1, source_target_pairs={{0,2},{1,3},{2,4},{3,5},{4,6},{5,7},{6,0},{7,1},{8,10},{9,11},{10,... | collective-permute-start | bytes 786440 | tf_op jit(solution)/shard_map/ppermute | solution.py:33
  6.9 39.7 %collective-permute-start.5 = (bf16[256,512]{1,0:T(8,128)(2,1)}, bf16[256,512]{1,0:T(8,128)(2,1)}, u32[]{:S(2)}, u32[]{:S(2)}) collective-permute-start(bf16[256,512]{1,0:T(8,128)(2,1)} %get-tuple-element.48), channel_id=1, source_target_pairs={{0,6},{1,7},{2,0},{3,1},{4,2},{5,3},{6,4},{7,5},{8,14},{9,15},{10,... | collective-permute-start | bytes 786440 | tf_op jit(solution)/shard_map/ppermute | solution.py:33
  10.7 39.6 %collective-permute-start.2 = (bf16[256,512]{1,0:T(8,128)(2,1)}, bf16[256,512]{1,0:T(8,128)(2,1)}, u32[]{:S(2)}, u32[]{:S(2)}) collective-permute-start(bf16[256,512]{1,0:T(8,128)(2,1)} %get-tuple-element.48), channel_id=1, source_target_pairs={{0,2},{1,3},{2,4},{3,5},{4,6},{5,7},{6,0},{7,1},{8,10},{9,11},{10,... | collective-permute-start | bytes 786440 | tf_op jit(solution)/shard_map/ppermute | solution.py:33
  10.7 17.0 %copy-start.4 = (bf16[3,3,512]{2,1,0:T(4,128)(2,1)S(1)}, bf16[3,3,512]{2,1,0:T(4,128)(2,1)}, u32[]{:S(2)}) copy-start(bf16[3,3,512]{2,1,0:T(4,128)(2,1)} %param.10) | copy-start | bytes 27652
  10.7 17.6 %copy-start.2 = (bf16[512,512]{1,0:T(8,128)(2,1)S(1)}, bf16[512,512]{1,0:T(8,128)(2,1)}, u32[]{:S(2)}) copy-start(bf16[512,512]{1,0:T(8,128)(2,1)} %param.12) | copy-start | bytes 1572868
  29.1 2.6 %copy-start.3 = (bf16[1,512,128]{2,1,0:T(8,128)(2,1)S(1)}, bf16[1,512,128]{2,1,0:T(8,128)(2,1)}, u32[]{:S(2)}) copy-start(bf16[1,512,128]{2,1,0:T(8,128)(2,1)} %get-tuple-element.35) | copy-start | bytes 393220
  44.2 37.6 %collective-permute-start.11 = (bf16[512,128]{1,0:T(8,128)(2,1)S(1)}, bf16[512,128]{1,0:T(8,128)(2,1)S(1)}, u32[]{:S(2)}, u32[]{:S(2)}) collective-permute-start(bf16[512,128]{1,0:T(8,128)(2,1)S(1)} %get-tuple-element.30), channel_id=1, source_target_pairs={{0,8},{8,16},{16,24},{24,0},{1,9},{9,17},{17,25},{25,1},{2,10},{10... | collective-permute-start | bytes 393224 | tf_op jit(solution)/shard_map/ppermute | solution.py:33
  46.7 40.9 %collective-permute-start.12 = (bf16[512,128]{1,0:T(8,128)(2,1)S(1)}, bf16[512,128]{1,0:T(8,128)(2,1)S(1)}, u32[]{:S(2)}, u32[]{:S(2)}) collective-permute-start(bf16[512,128]{1,0:T(8,128)(2,1)S(1)} %get-tuple-element.29), channel_id=1, source_target_pairs={{0,16},{8,24},{16,0},{24,8},{1,17},{9,25},{17,1},{25,9},{2,18},{10... | collective-permute-start | bytes 393224 | tf_op jit(solution)/shard_map/ppermute | solution.py:33
  49.2 19.2 %collective-permute-start.6 = (bf16[512,512]{1,0:T(8,128)(2,1)S(1)}, bf16[512,512]{1,0:T(8,128)(2,1)S(1)}, u32[]{:S(2)}, u32[]{:S(2)}) collective-permute-start(bf16[512,512]{1,0:T(8,128)(2,1)S(1)} %constant_dynamic-update-slice_fusion.2), channel_id=1, source_target_pairs={{0,1},{1,0},{2,3},{3,2},{4,5},{5,4},{6,7},{7,6},{8,9},{9,8},{10,11... | collective-permute-start | bytes 1572872 | tf_op jit(solution)/shard_map/ppermute | solution.py:37
  50.3 11.3 %collective-permute-start.7 = (bf16[256,512]{1,0:T(8,128)(2,1)}, bf16[256,512]{1,0:T(8,128)(2,1)S(1)}, u32[]{:S(2)}, u32[]{:S(2)}) collective-permute-start(bf16[256,512]{1,0:T(8,128)(2,1)} %collective-permute-done.1), channel_id=1, source_target_pairs={{0,2},{1,3},{2,4},{3,5},{4,6},{5,7},{6,0},{7,1},{8,10},{9,11},{10,... | collective-permute-start | bytes 786440 | tf_op jit(solution)/shard_map/ppermute | solution.py:33
  53.8 13.2 %collective-permute-start.8 = (bf16[256,512]{1,0:T(8,128)(2,1)}, bf16[256,512]{1,0:T(8,128)(2,1)S(1)}, u32[]{:S(2)}, u32[]{:S(2)}) collective-permute-start(bf16[256,512]{1,0:T(8,128)(2,1)} %collective-permute-done.5), channel_id=1, source_target_pairs={{0,6},{1,7},{2,0},{3,1},{4,2},{5,3},{6,4},{7,5},{8,14},{9,15},{10,... | collective-permute-start | bytes 786440 | tf_op jit(solution)/shard_map/ppermute | solution.py:33
  61.6 9.4 %collective-permute-start.3 = (bf16[512,512]{1,0:T(8,128)(2,1)S(1)}, bf16[512,512]{1,0:T(8,128)(2,1)S(1)}, u32[]{:S(2)}, u32[]{:S(2)}) collective-permute-start(bf16[512,512]{1,0:T(8,128)(2,1)S(1)} %constant_dynamic-update-slice_fusion), channel_id=1, source_target_pairs={{0,1},{1,0},{2,3},{3,2},{4,5},{5,4},{6,7},{7,6},{8,9},{9,8},{10,11... | collective-permute-start | bytes 1572872 | tf_op jit(solution)/shard_map/ppermute | solution.py:37
  67.0 28.8 %collective-permute-start.13 = (bf16[512,128]{1,0:T(8,128)(2,1)S(1)}, bf16[512,128]{1,0:T(8,128)(2,1)S(1)}, u32[]{:S(2)}, u32[]{:S(2)}) collective-permute-start(bf16[512,128]{1,0:T(8,128)(2,1)S(1)} %get-tuple-element.28), channel_id=1, source_target_pairs={{0,24},{8,0},{16,8},{24,16},{1,25},{9,1},{17,9},{25,17},{2,26},{10... | collective-permute-start | bytes 393224 | tf_op jit(solution)/shard_map/ppermute | solution.py:33
  68.4 7.6 %collective-permute-start.9 = (bf16[512,512]{1,0:T(8,128)(2,1)S(1)}, bf16[512,512]{1,0:T(8,128)(2,1)S(1)}, u32[]{:S(2)}, u32[]{:S(2)}) collective-permute-start(bf16[512,512]{1,0:T(8,128)(2,1)S(1)} %constant_dynamic-update-slice_fusion.4), channel_id=1, source_target_pairs={{0,1},{1,0},{2,3},{3,2},{4,5},{5,4},{6,7},{7,6},{8,9},{9,8},{10,11... | collective-permute-start | bytes 1572872 | tf_op jit(solution)/shard_map/ppermute | solution.py:37
  78.5 7.2 %copy-start.5 = (f32[1536]{0:T(1024)S(1)}, f32[1536]{0:T(1024)}, u32[]{:S(2)}) copy-start(f32[1536]{0:T(1024)} %mul.222) | copy-start | bytes 18436
  81.1 4.6 %collective-permute-start.10 = (bf16[2,1536]{1,0:T(2,128)(2,1)S(1)}, bf16[2,1536]{1,0:T(2,128)(2,1)S(1)}, u32[]{:S(2)}, u32[]{:S(2)}) collective-permute-start(bf16[2,1536]{1,0:T(2,128)(2,1)S(1)} %slice.229), channel_id=1, source_target_pairs={{0,8},{8,16},{16,24},{24,0},{1,9},{9,17},{17,25},{25,1},{2,10},{10... | collective-permute-start | bytes 18440 | tf_op jit(solution)/shard_map/ppermute | solution.py:33
  87.1 10.5 %copy-start.9 = (bf16[1024,512]{1,0:T(8,128)(2,1)S(1)}, bf16[1024,512]{1,0:T(8,128)(2,1)}, u32[]{:S(2)}) copy-start(bf16[1024,512]{1,0:T(8,128)(2,1)} %constant.308) | copy-start | bytes 3145732
  87.5 7.2 %collective-permute-start.14 = (bf16[512,128]{1,0:T(8,128)(2,1)S(1)}, bf16[512,128]{1,0:T(8,128)(2,1)S(1)}, u32[]{:S(2)}, u32[]{:S(2)}) collective-permute-start(bf16[512,128]{1,0:T(8,128)(2,1)S(1)} %get-tuple-element.42), channel_id=1, source_target_pairs={{0,8},{8,16},{16,24},{24,0},{1,9},{9,17},{17,25},{25,1},{2,10},{10... | collective-permute-start | bytes 393224 | tf_op jit(solution)/shard_map/ppermute | solution.py:33
  88.2 7.5 %collective-permute-start.15 = (bf16[512,128]{1,0:T(8,128)(2,1)S(1)}, bf16[512,128]{1,0:T(8,128)(2,1)S(1)}, u32[]{:S(2)}, u32[]{:S(2)}) collective-permute-start(bf16[512,128]{1,0:T(8,128)(2,1)S(1)} %get-tuple-element.41), channel_id=1, source_target_pairs={{0,16},{8,24},{16,0},{24,8},{1,17},{9,25},{17,1},{25,9},{2,18},{10... | collective-permute-start | bytes 393224 | tf_op jit(solution)/shard_map/ppermute | solution.py:33
  88.7 7.1 %collective-permute-start.16 = (bf16[512,128]{1,0:T(8,128)(2,1)S(1)}, bf16[512,128]{1,0:T(8,128)(2,1)S(1)}, u32[]{:S(2)}, u32[]{:S(2)}) collective-permute-start(bf16[512,128]{1,0:T(8,128)(2,1)S(1)} %get-tuple-element.40), channel_id=1, source_target_pairs={{0,24},{8,0},{16,8},{24,16},{1,25},{9,1},{17,9},{25,17},{2,26},{10... | collective-permute-start | bytes 393224 | tf_op jit(solution)/shard_map/ppermute | solution.py:33
  96.4 2.0 %copy-start.6 = (pred[512]{0:T(512)(128)(4,1)S(1)}, pred[512]{0:T(512)(128)(4,1)}, u32[]{:S(2)}) copy-start(pred[512]{0:T(512)(128)(4,1)} %iota_compare_fusion.1) | copy-start | bytes 1540
  96.4 2.0 %copy-start.10 = (bf16[1024,512]{1,0:T(8,128)(2,1)S(1)}, bf16[1024,512]{1,0:T(8,128)(2,1)}, u32[]{:S(2)}) copy-start(bf16[1024,512]{1,0:T(8,128)(2,1)} %constant.309) | copy-start | bytes 3145732
  102.6 1.2 copy-start.8
  103.8 3.3 %copy-start = (bf16[512,4096]{0,1:T(8,128)(2,1)S(1)}, bf16[512,4096]{0,1:T(8,128)(2,1)}, u32[]{:S(2)}) copy-start(bf16[512,4096]{0,1:T(8,128)(2,1)} %copy.14) | copy-start | bytes 12582916
  104.9 10.4 %collective-permute-start.17 = (bf16[512,128]{1,0:T(8,128)(2,1)S(1)}, bf16[512,128]{1,0:T(8,128)(2,1)S(1)}, u32[]{:S(2)}, u32[]{:S(2)}) collective-permute-start(bf16[512,128]{1,0:T(8,128)(2,1)S(1)} %get-tuple-element.18), channel_id=1, source_target_pairs={{0,8},{8,16},{16,24},{24,0},{1,9},{9,17},{17,25},{25,1},{2,10},{10... | collective-permute-start | bytes 393224 | tf_op jit(solution)/shard_map/ppermute | solution.py:33
  108.6 10.8 %copy-start.7 = (f32[512]{0:T(512)S(1)}, f32[512]{0:T(512)}, u32[]{:S(2)}) copy-start(f32[512]{0:T(512)} %param.11) | copy-start | bytes 6148
  112.8 9.9 %collective-permute-start.21 = (bf16[512,4,512]{2,0,1:T(8,128)(2,1)}, bf16[512,4,512]{2,0,1:T(8,128)(2,1)}, u32[]{:S(2)}, u32[]{:S(2)}) collective-permute-start(bf16[512,4,512]{2,0,1:T(8,128)(2,1)} %bitcast.176), channel_id=1, source_target_pairs={{0,1},{1,0},{2,3},{3,2},{4,5},{5,4},{6,7},{7,6},{8,9},{9,8},{10,11... | collective-permute-start | bytes 6291464 | tf_op jit(solution)/shard_map/ppermute | solution.py:37
  112.8 7.1 %copy-start.1 = (bf16[512,4096]{0,1:T(8,128)(2,1)S(1)}, bf16[512,4096]{0,1:T(8,128)(2,1)}, u32[]{:S(2)}) copy-start(bf16[512,4096]{0,1:T(8,128)(2,1)} %copy.14) | copy-start | bytes 12582916
  112.8 5.9 %collective-permute-start.18 = (bf16[512,128]{1,0:T(8,128)(2,1)S(1)}, bf16[512,128]{1,0:T(8,128)(2,1)S(1)}, u32[]{:S(2)}, u32[]{:S(2)}) collective-permute-start(bf16[512,128]{1,0:T(8,128)(2,1)S(1)} %get-tuple-element.17), channel_id=1, source_target_pairs={{0,16},{8,24},{16,0},{24,8},{1,17},{9,25},{17,1},{25,9},{2,18},{10... | collective-permute-start | bytes 393224 | tf_op jit(solution)/shard_map/ppermute | solution.py:33
  113.8 5.6 %collective-permute-start.19 = (bf16[512,128]{1,0:T(8,128)(2,1)S(1)}, bf16[512,128]{1,0:T(8,128)(2,1)S(1)}, u32[]{:S(2)}, u32[]{:S(2)}) collective-permute-start(bf16[512,128]{1,0:T(8,128)(2,1)S(1)} %get-tuple-element.16), channel_id=1, source_target_pairs={{0,24},{8,0},{16,8},{24,16},{1,25},{9,1},{17,9},{25,17},{2,26},{10... | collective-permute-start | bytes 393224 | tf_op jit(solution)/shard_map/ppermute | solution.py:33
  119.8 2.9 %collective-permute-start.20 = (bf16[512,512]{1,0:T(8,128)(2,1)S(1)}, bf16[512,512]{1,0:T(8,128)(2,1)S(1)}, u32[]{:S(2)}, u32[]{:S(2)}) collective-permute-start(bf16[512,512]{1,0:T(8,128)(2,1)S(1)} %multiply_convert_fusion), channel_id=1, source_target_pairs={{0,1},{1,0},{2,3},{3,2},{4,5},{5,4},{6,7},{7,6},{8,9},{9,8},{10,11... | collective-permute-start | bytes 1572872 | tf_op jit(solution)/shard_map/ppermute | solution.py:37
  124.0 11.0 %collective-permute-start.22 = (bf16[256,512]{1,0:T(8,128)(2,1)S(1)}, bf16[256,512]{1,0:T(8,128)(2,1)S(1)}, u32[]{:S(2)}, u32[]{:S(2)}) collective-permute-start(bf16[256,512]{1,0:T(8,128)(2,1)S(1)} %fusion.28), channel_id=1, source_target_pairs={{0,2},{1,3},{2,4},{3,5},{4,6},{5,7},{6,0},{7,1},{8,10},{9,11},{10,... | collective-permute-start | bytes 786440 | tf_op jit(solution)/shard_map/ppermute | solution.py:33
  126.0 22.2 %collective-permute-start.24 = (bf16[256,512]{1,0:T(8,128)(2,1)S(1)}, bf16[256,512]{1,0:T(8,128)(2,1)S(1)}, u32[]{:S(2)}, u32[]{:S(2)}) collective-permute-start(bf16[256,512]{1,0:T(8,128)(2,1)S(1)} %fusion.29), channel_id=1, source_target_pairs={{0,6},{1,7},{2,0},{3,1},{4,2},{5,3},{6,4},{7,5},{8,14},{9,15},{10,... | collective-permute-start | bytes 786440 | tf_op jit(solution)/shard_map/ppermute | solution.py:33
  130.7 15.4 %collective-permute-start.26 = (bf16[256,512]{1,0:T(8,128)(2,1)S(1)}, bf16[256,512]{1,0:T(8,128)(2,1)S(1)}, u32[]{:S(2)}, u32[]{:S(2)}) collective-permute-start(bf16[256,512]{1,0:T(8,128)(2,1)S(1)} %fusion.32), channel_id=1, source_target_pairs={{0,6},{1,7},{2,0},{3,1},{4,2},{5,3},{6,4},{7,5},{8,14},{9,15},{10,... | collective-permute-start | bytes 786440 | tf_op jit(solution)/shard_map/ppermute | solution.py:33
  136.4 15.7 %collective-permute-start.23 = (bf16[256,512]{1,0:T(8,128)(2,1)S(1)}, bf16[256,512]{1,0:T(8,128)(2,1)S(1)}, u32[]{:S(2)}, u32[]{:S(2)}) collective-permute-start(bf16[256,512]{1,0:T(8,128)(2,1)S(1)} %add_convert_fusion.3), channel_id=1, source_target_pairs={{0,2},{1,3},{2,4},{3,5},{4,6},{5,7},{6,0},{7,1},{8,10},{9,11},{10,... | collective-permute-start | bytes 786440 | tf_op jit(solution)/shard_map/ppermute | solution.py:33
  137.8 19.7 %collective-permute-start.25 = (bf16[256,512]{1,0:T(8,128)(2,1)S(1)}, bf16[256,512]{1,0:T(8,128)(2,1)S(1)}, u32[]{:S(2)}, u32[]{:S(2)}) collective-permute-start(bf16[256,512]{1,0:T(8,128)(2,1)S(1)} %fusion.31), channel_id=1, source_target_pairs={{0,2},{1,3},{2,4},{3,5},{4,6},{5,7},{6,0},{7,1},{8,10},{9,11},{10,... | collective-permute-start | bytes 786440 | tf_op jit(solution)/shard_map/ppermute | solution.py:33
  147.4 15.3 %collective-permute-start.27 = (bf16[256,512]{1,0:T(8,128)(2,1)S(1)}, bf16[256,512]{1,0:T(8,128)(2,1)S(1)}, u32[]{:S(2)}, u32[]{:S(2)}) collective-permute-start(bf16[256,512]{1,0:T(8,128)(2,1)S(1)} %add_convert_fusion.2), channel_id=1, source_target_pairs={{0,6},{1,7},{2,0},{3,1},{4,2},{5,3},{6,4},{7,5},{8,14},{9,15},{10,... | collective-permute-start | bytes 786440 | tf_op jit(solution)/shard_map/ppermute | solution.py:33

commit v2 on v0

v2 whole, which is shorter than its diff:
```python
import math

import jax
import jax.numpy as jnp
import ml_dtypes
import numpy as np
from jax import lax
from jax.experimental import pallas as pl
from jax.experimental.pallas import tpu as pltpu
from jax.sharding import PartitionSpec as P

KERNEL = 3
RIM = 8
BF16 = jnp.bfloat16
F32 = jnp.float32
MIB = 1 << 20


def half_tables(span):
    n = 2 * span
    f = np.arange(span)[:, None]
    m = np.arange(n)[None, :]
    ang = 2.0 * math.pi * ((f * m) % n) / n
    real = np.cos(ang)
    imag = -np.sin(ang)
    imag[0] = np.where(np.arange(n) % 2 == 0, 1.0, -1.0)
    forward = np.concatenate([real, imag], 0).astype(ml_dtypes.bfloat16)
    weight = np.full((n, 1), 2.0 / n)
    weight[0] = 1.0 / n
    weight[span] = 1.0 / n
    back = (np.concatenate([real, imag], 0) * weight)[:, :span].T
    return forward, np.ascontiguousarray(back).astype(ml_dtypes.bfloat16)


def shift(x, axis, distance):
    size = lax.axis_size(axis)
    return lax.ppermute(x, axis, [(i, (i + distance) % size) for i in range(size)])


def sibling(x):
    return lax.ppermute(x, "chan", [(i, i ^ 1) for i in range(lax.axis_size("chan"))])


def dot(a, b):
    return jnp.dot(a, b, preferred_element_type=F32)


def after(x, *others):
    return lax.optimization_barrier((x,) + others)[0]


def whole(shape):
    return pl.BlockSpec(shape, lambda *_: (0,) * len(shape))


def call(kernel, grid, prefetch, operands, in_specs, outs, out_specs, scratch, name, flops, moved):
    return pl.pallas_call(
        kernel,
        grid_spec=pltpu.PrefetchScalarGridSpec(
            num_scalar_prefetch=1,
            grid=grid,
            in_specs=in_specs,
            out_specs=out_specs,
            scratch_shapes=scratch,
        ),
        out_shape=outs,
        compiler_params=pltpu.CompilerParams(vmem_limit_bytes=32 * MIB),
        cost_estimate=pl.CostEstimate(flops=flops, bytes_accessed=moved, transcendentals=0),
        name=name,
    )(prefetch, *operands)


def project(pairs, chip_ids, core, w_in, conv_taps, groups, total=None, finish=False):
    count = len(pairs)
    rows, width = pairs[0][0].shape
    streams, _, out_width = w_in.shape
    kept = rows - RIM
    split = out_width // groups % 128 == 0
    share = out_width // groups
    blocks = [b for pair in pairs for b in pair]
    has_total = total is not None

    def kernel(ids, w_ref, *refs):
        x_refs, refs = refs[: 2 * count], refs[2 * count :]
        if has_total:
            total_ref, refs = refs[0], refs[1:]
        if finish:
            taps_ref, gate_ref, in_ref, acc = refs
        else:
            acc = refs[0]
        k, s = pl.program_id(0), pl.program_id(1)
        mine = pl.multiple_of(ids[count] * width, width)
        theirs = pl.multiple_of((1 - ids[count]) * width, width)
        for j in range(count):

            @pl.when(k == j)
            def _():
                part = dot(x_refs[2 * j][...], w_ref[0, pl.ds(mine, width)])
                part = part + dot(x_refs[2 * j + 1][...], w_ref[0, pl.ds(theirs, width)])
                if j > 0:
                    part = part + acc[s]
                elif has_total:
                    part = part + total_ref[s]
                acc[s] = part

        if finish:

            @pl.when((k == count - 1) & (s == streams - 1))
            def _():
                def filtered(t):
                    rounded = acc[t].astype(BF16).astype(F32)
                    result = jnp.zeros((kept, out_width), F32)
                    for lag in range(KERNEL):
                        row = lag * streams + t
                        result = result + taps_ref[row : row + 1, :] * rounded[RIM - lag : rows - lag]
                    return result.astype(BF16)

                gate_ref[...] = filtered(0)
                gated = (filtered(1).astype(F32) * filtered(2).astype(F32)).astype(BF16)
                if split:
                    for q in range(groups):
                        in_ref[q] = gated[:, q * share : (q + 1) * share]
                else:
                    in_ref[...] = gated

    in_specs = [pl.BlockSpec((1, 2 * width, out_width), lambda k, s, ids: (s, ids[k], 0))]
    in_specs += [whole(b.shape) for b in blocks]
    operands = [w_in] + blocks
    if has_total:
        in_specs.append(whole(total.shape))
        operands.append(total)
    acc_shape = (streams, rows, out_width)
    if finish:
        in_specs.append(whole(conv_taps.shape))
        operands.append(conv_taps)
        in_shape = (groups, kept, share) if split else (kept, out_width)
        outs = [
            jax.ShapeDtypeStruct((kept, out_width), BF16),
            jax.ShapeDtypeStruct(in_shape, BF16),
        ]
        scratch = [pltpu.VMEM(acc_shape, F32)]
    else:
        outs = [jax.ShapeDtypeStruct(acc_shape, F32)]
        scratch = []
    return call(
        kernel,
        (count, streams),
        jnp.stack(list(chip_ids) + [core]).astype(jnp.int32),
        operands,
        in_specs,
        outs,
        [whole(o.shape) for o in outs],
        scratch,
        "project",
        4 * count * rows * width * streams * out_width,
        count * 4 * width * streams * out_width,
    )


def taps_spectra(pieces, forward, me):
    groups = len(pieces)
    span, share = pieces[0].shape

    def kernel(at, *refs):
        piece_refs, (forward_ref, out_ref, padded) = refs[:groups], refs[groups:]
        row_ids = lax.broadcasted_iota(jnp.int32, (span, share), 0)
        for s in range(groups):
            k = lax.rem(at[0] - s + groups, groups)
            block = piece_refs[s][...]
            padded[0:span, pl.ds(pl.multiple_of(k * share, share), share)] = block

            @pl.when(k < groups - 1)
            def _():
                place = pl.multiple_of((k + 1) * share, share)
                kept = jnp.where(row_ids == 0, 0.0, block.astype(F32)).astype(BF16)
                padded[span : 2 * span, pl.ds(place, share)] = kept

        padded[span : 2 * span, 0:share] = jnp.zeros((span, share), BF16)
        out_ref[...] = dot(forward_ref[...], padded[...]).astype(BF16)

    shape = (2 * span, groups * share)
    return call(
        kernel,
        (1,),
        me[None],
        list(pieces) + [forward],
        [whole(p.shape) for p in pieces] + [whole(forward.shape)],
        jax.ShapeDtypeStruct(shape, BF16),
        whole(shape),
        [pltpu.VMEM(shape, BF16)],
        "taps_spectra",
        2 * shape[0] * shape[0] * shape[1],
        6 * shape[0] * shape[1],
    )


def long_filter(pieces, spectra_taps, forward_in, back, skip, me):
    groups = len(pieces)
    half, share = pieces[0][0].shape
    span = 2 * half
    cols = groups * share
    flat = [h for pair in pieces for h in pair]
    step = 16

    def kernel(at, *refs):
        ins, refs = refs[: 2 * groups], refs[2 * groups :]
        taps_ref, forward_ref, back_ref, skip_ref = refs[:4]
        outs, (signal, spectra, mixture, result) = refs[4 : 4 + 2 * groups], refs[4 + 2 * groups :]
        for s in range(groups):
            j = pl.multiple_of(lax.rem(at[0] - s + groups, groups) * share, share)
            signal[0:half, pl.ds(j, share)] = ins[2 * s][...]
            signal[half:span, pl.ds(j, share)] = ins[2 * s + 1][...]
        spectra[...] = dot(forward_ref[...], signal[...]).astype(BF16)

        def mix(start, special):
            def read(ref, first, block):
                return ref[pl.ds(first, step), block * share : (block + 1) * share].astype(F32)

            imag_start = start + span
            real_g = [read(taps_ref, start, b) for b in range(groups)]
            imag_g = [read(taps_ref, imag_start, b) for b in range(groups)]
            real_u = [read(spectra, start, b) for b in range(groups)]
            imag_u = [read(spectra, imag_start, b) for b in range(groups)]
            first = lax.broadcasted_iota(jnp.int32, (step, share), 0) == 0
            for i in range(groups):
                real = imag = None
                for j in range(i + 1):
                    rr = real_g[i - j] * real_u[j]
                    ii = imag_g[i - j] * imag_u[j]
                    cross = real_g[i - j] * imag_u[j] + imag_g[i - j] * real_u[j]
                    new_real, new_imag = rr - ii, cross
                    if special:
                        new_real = jnp.where(first, rr, new_real)
                        new_imag = jnp.where(first, ii, new_imag)
                    real = new_real if real is None else real + new_real
                    imag = new_imag if imag is None else imag + new_imag
                place = slice(i * share, (i + 1) * share)
                mixture[pl.ds(start, step), place] = real.astype(BF16)
                mixture[pl.ds(imag_start, step), place] = imag.astype(BF16)

        mix(0, True)

        @pl.loop(1, span // step)
        def _(c):
            mix(pl.multiple_of(c * step, step), False)

        result[...] = (
            dot(back_ref[...], mixture[...]) + skip_ref[...] * signal[...].astype(F32)
        ).astype(BF16)
        for s in range(groups):
            j = pl.multiple_of(lax.rem(at[0] + s, groups) * share, share)
            outs[2 * s][...] = result[0:half, pl.ds(j, share)]
            outs[2 * s + 1][...] = result[half:span, pl.ds(j, share)]

    operands = flat + [spectra_taps, forward_in, back, skip]
    outs = [jax.ShapeDtypeStruct(h.shape, BF16) for h in flat]
    found = call(
        kernel,
        (1,),
        me[None],
        operands,
        [whole(o.shape) for o in operands],
        outs,
        [whole(o.shape) for o in outs],
        [
            pltpu.VMEM((span, cols), BF16),
            pltpu.VMEM((2 * span, cols), BF16),
            pltpu.VMEM((2 * span, cols), BF16),
            pltpu.VMEM((span, cols), BF16),
        ],
        "long_filter",
        8 * span * span * cols,
        12 * span * cols,
    )
    return [(found[2 * s], found[2 * s + 1]) for s in range(groups)]


def gate_blocks(gate, pieces, me):
    groups = len(pieces)
    rows, share = pieces[0].shape

    def kernel(at, gate_ref, *refs):
        for s in range(groups):
            place = pl.multiple_of(lax.rem(at[0] - s + groups, groups) * share, share)
            gated = gate_ref[:, pl.ds(place, share)].astype(F32) * refs[s][...].astype(F32)
            refs[groups][:, pl.ds(place, share)] = gated.astype(BF16)

    return call(
        kernel,
        (1,),
        me[None],
        [gate] + list(pieces),
        [whole(gate.shape)] + [whole(p.shape) for p in pieces],
        jax.ShapeDtypeStruct(gate.shape, BF16),
        whole(gate.shape),
        [],
        "gate_blocks",
        rows * share * groups,
        6 * rows * share * groups,
    )


def output_shares(gated, other, w_own, w_other, chip_ids, core, kinds):
    count = len(chip_ids)
    rows, width = gated.shape
    cols = w_other.shape[1] * 2 // lax.axis_size("chan")

    def kernel(ids, a_ref, b_ref, w_ref, v_ref, *outs):
        k = pl.program_id(0)
        total = dot(a_ref[...], w_ref[...]) + dot(b_ref[...], v_ref[...])
        for j in range(count):

            @pl.when(k == j)
            def _():
                outs[j][...] = total.astype(kinds[j])

    outs = [jax.ShapeDtypeStruct((rows, cols), kind) for kind in kinds]
    return call(
        kernel,
        (count,),
        jnp.stack(list(chip_ids) + [core]).astype(jnp.int32),
        [gated, other, w_own, w_other],
        [
            whole(gated.shape),
            whole(other.shape),
            pl.BlockSpec((width, cols), lambda k, ids: (0, ids[k] * 2 + ids[count])),
            pl.BlockSpec((width, cols), lambda k, ids: (0, ids[k])),
        ],
        outs,
        [whole(o.shape) for o in outs],
        [],
        "output_shares",
        4 * count * rows * width * cols,
        4 * count * width * cols,
    )


def exchange(piece):
    return [piece(0)] + [shift(piece(s), "ctx", s) for s in range(1, lax.axis_size("ctx"))]


def in_order(blocks, me):
    groups = len(blocks)
    result = jnp.zeros((groups,) + blocks[0].shape, blocks[0].dtype)
    for s, b in enumerate(blocks):
        result = lax.dynamic_update_index_in_dim(result, b, (me - s) % groups, 0)
    return jnp.concatenate(list(result), 1)


def taps_spectra_plain(pieces, forward, me):
    groups = len(pieces)
    span, share = pieces[0].shape
    taps = in_order(pieces, me)
    before = jnp.concatenate(
        [jnp.zeros((span, share), BF16), taps[:, : (groups - 1) * share]], 1
    )
    before = jnp.where(lax.broadcasted_iota(jnp.int32, (span, 1), 0) == 0, 0, before)
    return dot(forward, jnp.concatenate([taps, before], 0)).astype(BF16)


def long_filter_plain(pieces, spectra_taps, forward_in, back, skip, me):
    groups = len(pieces)
    half, share = pieces[0][0].shape
    span = 2 * half
    signal = in_order([jnp.concatenate(pair, 0) for pair in pieces], me)
    spectra = dot(forward_in, signal).astype(BF16)
    real_g, imag_g = spectra_taps[:span].astype(F32), spectra_taps[span:].astype(F32)
    real_u, imag_u = spectra[:span].astype(F32), spectra[span:].astype(F32)
    first = lax.broadcasted_iota(jnp.int32, (span, 1), 0) == 0
    mixed = []
    for i in range(groups):
        real = imag = 0.0
        for j in range(i + 1):
            g = slice((i - j) * share, (i - j + 1) * share)
            u = slice(j * share, (j + 1) * share)
            rr = real_g[:, g] * real_u[:, u]
            ii = imag_g[:, g] * imag_u[:, u]
            cross = real_g[:, g] * imag_u[:, u] + imag_g[:, g] * real_u[:, u]
            real = real + jnp.where(first, rr, rr - ii)
            imag = imag + jnp.where(first, ii, cross)
        mixed.append(jnp.concatenate([real, imag], 0).astype(BF16))
    result = dot(back, jnp.concatenate(mixed, 1)) + skip * signal.astype(F32)
    result = jnp.stack(jnp.split(result.astype(BF16), groups, axis=1))
    found = []
    for s in range(groups):
        block = lax.dynamic_index_in_dim(result, (me + s) % groups, 0, keepdims=False)
        found.append((block[:half], block[half:]))
    return found


def gate_blocks_plain(gate, pieces, me):
    return (gate.astype(F32) * in_order(pieces, me).astype(F32)).astype(BF16)


def body(inputs, w_in, conv_taps, skip_gain, filter_taps, w_out):
    span, width = inputs.shape
    half = span // 2
    groups = lax.axis_size("ctx")
    me = lax.axis_index("ctx")
    chips = lax.axis_size("chan") // 2
    place = lax.axis_index("chan")
    chip, core = place // 2, place % 2
    share = width // groups
    aligned = share % 128 == 0
    out_width = w_out.shape[1] // (2 * chips)
    forward_np, back_np = half_tables(span)
    forward, back = jnp.asarray(forward_np), jnp.asarray(back_np)
    w_streams = jnp.transpose(w_in, (1, 0, 2))
    short_taps = conv_taps.reshape(-1, width).astype(F32)

    low = inputs[half - RIM :]
    rim = shift(inputs[span - RIM :], "ctx", 1)
    rim = jnp.where(me > 0, rim, jnp.zeros_like(rim))
    top = jnp.concatenate([rim, inputs[:half]], 0)

    low_found, top_found = [(0, low)], [(0, top)]
    low_up = low_down = low
    top_up = top_down = top
    for d in range(1, chips // 2 + 1):
        if 2 * d < chips:
            low_up = shift(low_up, "chan", 2)
            low_down = shift(low_down, "chan", -2)
            low_found += [(d, low_up), (-d, low_down)]
        else:
            low_far = shift(low_up, "chan", 2)
            low_found.append((d, low_far))
    top_down = after(top_down, low_down)
    top_up = after(top_up, low_far)
    for d in range(1, chips // 2 + 1):
        if 2 * d < chips:
            top_down = shift(top_down, "chan", -2)
            top_up = shift(top_up, "chan", 2)
            top_found += [(-d, top_down), (d, top_up)]
        else:
            top_found.append((-d, shift(top_down, "chan", -2)))

    split_taps = [filter_taps[:, q * share : (q + 1) * share] for q in range(groups)]
    split_taps = jnp.stack(split_taps)

    def pick(stack):
        return lambda s: lax.dynamic_index_in_dim(stack, (me + s) % groups, 0, keepdims=False)

    spectra_taps = (taps_spectra if aligned else taps_spectra_plain)(
        exchange(pick(split_taps)), forward, me
    )

    w_other = sibling(
        jnp.concatenate(
            [
                lax.dynamic_slice_in_dim(w_out, (2 * z + 1 - core) * out_width, out_width, 1)
                for z in range(chips)
            ],
            1,
        )
    )

    def stage(found, cut):
        pairs = [(block, sibling(block)) for _, block in found]
        ids = [(chip - d) % chips for d, _ in found]
        total = None
        if cut:
            (total,) = project(pairs[:cut], ids[:cut], core, w_streams, short_taps, groups)
        gate, gated = project(
            pairs[cut:], ids[cut:], core, w_streams, short_taps, groups, total, True
        )
        if not aligned:
            gated = jnp.stack(jnp.split(gated, groups, axis=1))
        return gate, exchange(pick(gated))

    gate_low, in_low = stage(low_found, 0)
    gate_top, in_top = stage(top_found, len(top_found) - 1)

    skip = lax.dynamic_slice_in_dim(skip_gain, me * share, share, 0)
    skip = jnp.tile(skip, groups)[None]
    filtered = (long_filter if aligned else long_filter_plain)(
        list(zip(in_top, in_low)), spectra_taps, forward[:, :span], back, skip, me
    )
    gating = gate_blocks if aligned else gate_blocks_plain
    gated_top = gating(gate_top, exchange(lambda s: filtered[s][0]), me)
    gated_low = gating(gate_low, exchange(lambda s: filtered[s][1]), me)

    def sums(gated, lead):
        other = sibling(gated)
        reach = chips // 2
        direct = [reach] + ([-lead * (reach - 1)] if reach > 1 else [])
        carried = [lead * d for d in range(reach - 1, 0, -1)]
        carried += [-lead * d for d in range(reach - 2, 0, -1)] + [0]

        def shares(offsets, kind):
            ids = [(chip + d) % chips for d in offsets]
            found = output_shares(gated, other, w_out, w_other, ids, core, [kind] * len(ids))
            return dict(zip(offsets, found))

        sent = shares(direct, BF16)
        kept = shares(carried, F32)
        ahead = shift(sent[reach], "chan", 2 * lead)
        behind = shift(sent[direct[1]], "chan", -2 * lead) if reach > 1 else None
        return ahead, behind, kept

    def finish(state, lead):
        ahead, behind, kept = state
        reach = chips // 2
        for d in range(reach - 1, 0, -1):
            ahead = shift((ahead.astype(F32) + kept[lead * d]).astype(BF16), "chan", 2 * lead)
        for d in range(reach - 2, 0, -1):
            behind = shift((behind.astype(F32) + kept[-lead * d]).astype(BF16), "chan", -2 * lead)
        total = kept[0] + ahead.astype(F32)
        if behind is not None:
            total = total + behind.astype(F32)
        return total.astype(BF16)

    state_top = sums(gated_top, 1)
    state_low = sums(gated_low, -1)
    return jnp.concatenate([finish(state_top, 1), finish(state_low, -1)], 0)


def solution(mesh):
    return jax.shard_map(
        body,
        mesh=mesh,
        in_specs=(
            P("ctx", "chan"),
            P(None, None, "chan"),
            P(None, None, "chan"),
            P("chan"),
            P("ctx", "chan"),
            P("chan", None),
        ),
        out_specs=P("ctx", "chan"),
        check_vma=False,
    )
```

time: 269 us -> 146 us (0.54)
  local copies, waits for them, and re-layouts: 66.4 us -> 12.5 us
  other arithmetic: 58.7 us -> 5.34 us
  matrix products: 40.9 us -> 0 us
  starting transfers between devices: 3.68 us -> 41.6 us
  Pallas kernels: 0 us -> 29 us
  waiting for transfers between devices: 85 us -> 57.3 us
  between operations: 13.3 us -> 0.36 us
    ppermute x1 -> x39, waiting for transfers between devices: 0.01 us -> 57.3 us  [the longest x28 57.2 us: shift(): lax.ppermute(x, axis, [(i, (i + distance) % size) for i in range(size)])]
    reduce_scatter x1 -> x0, waiting for transfers between devices: 49.7 us -> none  [body(): lax.psum_scatter(lax.dot_general(w_out, gated_out, (((0,), (1,)), ((), ()...]
    dot_general x4 -> x0, matrix products: 40.9 us -> none  [the longest x1 13.8 us: body(): jnp.einsum('fm,kmd->kfd', forward_taps, padded_taps, preferred_element_ty...]
    ppermute x1 -> x39, starting transfers between devices: 3.38 us -> 41.6 us  [the longest x28 40.1 us: shift(): lax.ppermute(x, axis, [(i, (i + distance) % size) for i in range(size)])]
    all_gather x3 -> x0, waiting for transfers between devices: 33.8 us -> none  [the longest x1 33.8 us: body(): lax.all_gather(inputs, 'chan', axis=1, tiled=True)]
    pallas_call x0 -> x11, Pallas kernels: none -> 29 us  [call(): pl.pallas_call(kernel, grid_spec=pltpu.PrefetchScalarGridSpec(num_scalar_...]
    gather x5 -> x0, local copies, waits for them, and re-layouts: 28.3 us -> none  [accumulate(): chosen = jnp.take(spectra_taps, jnp.clip(lag_index, 0, groups - 1), axis=0)]
    another operation x2 -> x5, other arithmetic: 26.4 us -> 1.47 us  [the longest x1 1.16 us: body(): split_taps = jnp.stack(split_taps)]
  transfers between devices with their start and end apart: 5 -> 39, of which waited for: 2 -> 15; matrix products, arithmetic and copies ran while one was open for 33% -> 8% of each run, Pallas kernels for 0% -> 20%
where the time goes in v2:
time: 146 us
  waiting for transfers between devices  57.3 us (39%)
  starting transfers between devices  41.6 us (28%)
  Pallas kernels  29 us (20%)
  local copies, waits for them, and re-layouts  12.5 us (9%)
  other arithmetic  5.34 us (4%)
    ppermute x28, waiting for transfers between devices, shift(): lax.ppermute(x, axis, [(i, (i + distance) % size) for i in range(size)])  57.2 us
    ppermute x28, starting transfers between devices, shift(): lax.ppermute(x, axis, [(i, (i + distance) % size) for i in range(size)])  40.1 us
    pallas_call x11, Pallas kernels, call(): pl.pallas_call(kernel, grid_spec=pltpu.PrefetchScalarGridSpec(num_scalar_...  29 us
    unnamed x14, local copies, waits for them, and re-layouts  4.61 us
  transfers between devices with their start and end apart: 39, of which 15 were waited for; matrix products, arithmetic and copies ran while one was open for 8% of the time, Pallas kernels for 20%

profile of v2, /device:TPU:0, one launch (start us, length us, event | category | flops | bytes accessed | tf_op | source)
XLA Modules:
  0.0 146.0 jit_solution(10520211673858601103)
XLA Ops:
  0.0 1.0 slice.26.refs_0_
  1.0 0.5 collective-permute-start.11
  1.5 2.6 %collective-permute-start.7 = (bf16[264,512]{1,0:T(8,128)(2,1)S(1)}, bf16[264,512]{1,0:T(8,128)(2,1)S(1)}, u32[]{:S(2)}, u32[]{:S(2)}) collective-permute-start(bf16[264,512]{1,0:T(8,128)(2,1)S(1)} %slice.26.refs_0_), channel_id=1, source_target_pairs={{0,2},{1,3},{2,4},{3,5},{4,6},{5,7},{6,0},{7,1},{8,10},{9,11},{10,... | collective-permute-start | bytes 811016 | tf_op jit(solution)/shard_map/ppermute | solution.py:37
  4.1 2.1 %collective-permute-start.1 = (bf16[264,512]{1,0:T(8,128)(2,1)S(1)}, bf16[264,512]{1,0:T(8,128)(2,1)S(1)}, u32[]{:S(2)}, u32[]{:S(2)}) collective-permute-start(bf16[264,512]{1,0:T(8,128)(2,1)S(1)} %slice.26.refs_0_), channel_id=1, source_target_pairs={{0,6},{1,7},{2,0},{3,1},{4,2},{5,3},{6,4},{7,5},{8,14},{9,15},{10,... | collective-permute-start | bytes 811016 | tf_op jit(solution)/shard_map/ppermute | solution.py:37
  6.2 0.7 slice.24
  6.9 1.6 %collective-permute-start = (bf16[8,512]{1,0:T(8,128)(2,1)S(1)}, bf16[8,512]{1,0:T(8,128)(2,1)S(1)}, u32[]{:S(2)}, u32[]{:S(2)}) collective-permute-start(bf16[8,512]{1,0:T(8,128)(2,1)S(1)} %slice.24), channel_id=1, source_target_pairs={{0,8},{8,16},{16,24},{24,0},{1,9},{9,17},{17,25},{25,1},{2,10},{10... | collective-permute-start | bytes 24584 | tf_op jit(solution)/shard_map/ppermute | solution.py:37
  8.6 1.7 %constant_dynamic-slice_fusion.3 = (bf16[512,512]{1,0:T(8,128)(2,1)S(1)}, bf16[512,512]{1,0:T(8,128)(2,1)S(1)}, bf16[512,512]{1,0:T(8,128)(2,1)S(1)}, bf16[512,512]{1,0:T(8,128)(2,1)S(1)}) fusion(bf16[512,4096]{1,0:T(8,128)(2,1)} %w_ref.7, s32[]{:T(128)S(6)} %select_n.148, s32[]{:T(128)S(6)} %select_n.151, s32[]{:T(128)S(6)} %select_n.150, s32[]{:T(128)S(6)} %select_n.149), kind=kLoop, calls=%fused_computation.28 | loop fusion | bytes 4194320 | tf_op jit(solution)/shard_map/dynamic_slice | solution.py:450
  10.2 1.7 %pad_maximum_fusion = bf16[512,2048]{1,0:T(8,128)(2,1)} fusion(bf16[512,512]{1,0:T(8,128)(2,1)S(1)} %get-tuple-element.50, bf16[512,512]{1,0:T(8,128)(2,1)S(1)} %get-tuple-element.51, bf16[512,512]{1,0:T(8,128)(2,1)S(1)} %get-tuple-element.52, bf16[512,512]{1,0:T(8,128)(2,1)S(1)} %get-tuple-element.49), kind=kLoop, calls=%fused_computation | loop fusion | flops 8388608 | bytes 4194304 | tf_op jit(solution)/shard_map/concatenate | solution.py:448
  11.9 1.7 %slice.25 = bf16[256,512]{1,0:T(8,128)(2,1)} slice(bf16[512,512]{1,0:T(8,128)(2,1)} %param.8), slice={[0:256], [0:512]} | slice | bytes 524288 | tf_op jit(solution)/shard_map/slice | solution.py:414
  13.6 1.0 pad_maximum_fusion.3.refs_0_
  14.6 3.9 %collective-permute-done.1.refs_4_ = bf16[264,512]{1,0:T(8,128)(2,1)S(1)} collective-permute-done((bf16[264,512]{1,0:T(8,128)(2,1)S(1)}, bf16[264,512]{1,0:T(8,128)(2,1)S(1)}, u32[]{:S(2)}, u32[]{:S(2)}) %collective-permute-start.1) | collective-permute-done | bytes 270368 | tf_op jit(solution)/shard_map/ppermute | solution.py:37
  18.5 2.2 %collective-permute-start.2 = (bf16[264,512]{1,0:T(8,128)(2,1)S(1)}, bf16[264,512]{1,0:T(8,128)(2,1)}, u32[]{:S(2)}, u32[]{:S(2)}) collective-permute-start(bf16[264,512]{1,0:T(8,128)(2,1)S(1)} %pad_maximum_fusion.3.refs_0_), channel_id=1, source_target_pairs={{0,6},{1,7},{2,0},{3,1},{4,2},{5,3},{6,4},{7,5},{8,14},{9,15},{10,... | collective-permute-start | bytes 811016 | tf_op jit(solution)/shard_map/ppermute | solution.py:37
  20.8 1.9 %slice_bitcast_fusion.3 = (bf16[1,512,128]{2,1,0:T(8,128)(2,1)}, bf16[1,512,128]{2,1,0:T(8,128)(2,1)}, bf16[1,512,128]{2,1,0:T(8,128)(2,1)}, bf16[1,512,128]{2,1,0:T(8,128)(2,1)}) fusion(bf16[512,512]{1,0:T(8,128)(2,1)} %param.12), kind=kLoop, calls=%fused_computation.15 | loop fusion | bytes 1048576 | tf_op jit(solution)/shard_map/stack | solution.py:438
  22.7 10.6 %collective-permute-done.8.refs_6_ = bf16[264,512]{1,0:T(8,128)(2,1)} collective-permute-done((bf16[264,512]{1,0:T(8,128)(2,1)S(1)}, bf16[264,512]{1,0:T(8,128)(2,1)}, u32[]{:S(2)}, u32[]{:S(2)}) %collective-permute-start.8) | collective-permute-done | bytes 270368 | tf_op jit(solution)/shard_map/ppermute | solution.py:37
  33.3 1.3 collective-permute-start.9
  34.6 0.2 collective-permute-start.14
  34.8 2.6 %collective-permute-start.3 = (bf16[264,512]{1,0:T(8,128)(2,1)}, bf16[264,512]{1,0:T(8,128)(2,1)}, u32[]{:S(2)}, u32[]{:S(2)}) collective-permute-start(bf16[264,512]{1,0:T(8,128)(2,1)} %collective-permute-done.2.refs_2_), channel_id=1, source_target_pairs={{0,6},{1,7},{2,0},{3,1},{4,2},{5,3},{6,4},{7,5},{8,14},{9,15},{10,... | collective-permute-start | bytes 811016 | tf_op jit(solution)/shard_map/ppermute | solution.py:37
  37.5 0.1 stack.80.ids
  37.6 0.8 dynamic_slice.65
  38.4 1.2 pad_maximum_fusion.1
  39.7 4.9 %collective-permute-done.9.refs_4_ = bf16[264,512]{1,0:T(8,128)(2,1)} collective-permute-done((bf16[264,512]{1,0:T(8,128)(2,1)S(1)}, bf16[264,512]{1,0:T(8,128)(2,1)}, u32[]{:S(2)}, u32[]{:S(2)}) %collective-permute-start.9) | collective-permute-done | bytes 270368 | tf_op jit(solution)/shard_map/ppermute | solution.py:37
  44.6 0.5 collective-permute-start.10
  45.1 4.5 %collective-permute-done.3.refs_0_ = bf16[264,512]{1,0:T(8,128)(2,1)} collective-permute-done((bf16[264,512]{1,0:T(8,128)(2,1)}, bf16[264,512]{1,0:T(8,128)(2,1)}, u32[]{:S(2)}, u32[]{:S(2)}) %collective-permute-start.3) | collective-permute-done | bytes 270368 | tf_op jit(solution)/shard_map/ppermute | solution.py:37
  49.6 4.6 %copy-done = bf16[4096,3,512]{2,0,1:T(8,128)(2,1)S(1)} copy-done((bf16[4096,3,512]{2,0,1:T(8,128)(2,1)S(1)}, bf16[4096,3,512]{2,0,1:T(8,128)(2,1)}, u32[]{:S(2)}) %copy-start) | copy-done | bytes 12582936
  54.2 8.6 %project.5 = (bf16[256,512]{1,0:T(8,128)(2,1)S(1)}, bf16[4,256,128]{2,1,0:T(8,128)(2,1)S(1)}) custom-call(s32[5]{0:T(128)S(1)} %stack.80.ids, bf16[3,4096,512]{2,1,0:T(8,128)(2,1)S(1)} %bitcast.41, bf16[264,512]{1,0:T(8,128)(2,1)S(1)} %slice.26.refs_0_, bf16[264,512]{1,0:T(8,128)(2,1)S(1)} %collective-permute-done.11.refs_1_, ...), custom_call_target="tpu_custom_call" | custom-call | flops 3321888768 | bytes 12582912 | tf_op jit(solution)/shard_map/project/pallas_call | solution.py:57
  62.8 2.5 %collective-permute-start.23 = (bf16[512,128]{1,0:T(8,128)(2,1)S(1)}, bf16[512,128]{1,0:T(8,128)(2,1)S(1)}, u32[]{:S(2)}, u32[]{:S(2)}) collective-permute-start(bf16[512,128]{1,0:T(8,128)(2,1)S(1)} %get-tuple-element.53), channel_id=1, source_target_pairs={{0,24},{8,0},{16,8},{24,16},{1,25},{9,1},{17,9},{25,17},{2,26},{10... | collective-permute-start | bytes 393224 | tf_op jit(solution)/shard_map/ppermute | solution.py:37
  65.3 0.5 collective-permute-start.22
  65.9 0.6 collective-permute-start.21
  66.4 5.9 %project.3.refs_2_ = f32[3,264,512]{2,1,0:T(8,128)S(1)} custom-call(s32[4]{0:T(128)S(1)} %pad_add_fusion.1.ids, bf16[3,4096,512]{2,1,0:T(8,128)(2,1)S(1)} %bitcast.42, bf16[264,512]{1,0:T(8,128)(2,1)S(1)} %pad_maximum_fusion.3.refs_0_, bf16[264,512]{1,0:T(8,128)(2,1)S(1)} %collective-permute-done.5.refs_1_, bf16[264,512]{1,0:T(8,128)(2,1)} %collective-permute-done.2.refs_2_, ...), custom_call_target="tpu_custom_call" | custom-call | flops 2491416576 | bytes 9437184 | tf_op jit(solution)/shard_map/project/pallas_call | solution.py:57
  72.4 2.4 %collective-permute-start.20 = (bf16[256,128]{1,0:T(8,128)(2,1)S(1)}, bf16[256,128]{1,0:T(8,128)(2,1)S(1)}, u32[]{:S(2)}, u32[]{:S(2)}) collective-permute-start(bf16[256,128]{1,0:T(8,128)(2,1)S(1)} %get-tuple-element.61), channel_id=1, source_target_pairs={{0,24},{8,0},{16,8},{24,16},{1,25},{9,1},{17,9},{25,17},{2,26},{10... | collective-permute-start | bytes 196616 | tf_op jit(solution)/shard_map/ppermute | solution.py:37
  74.8 3.5 %project.4 = (bf16[256,512]{1,0:T(8,128)(2,1)S(1)}, bf16[4,256,128]{2,1,0:T(8,128)(2,1)S(1)}) custom-call(s32[2]{0:T(128)S(1)} %pad_add_fusion.ids, bf16[3,4096,512]{2,1,0:T(8,128)(2,1)S(1)} %bitcast.43, bf16[264,512]{1,0:T(8,128)(2,1)} %collective-permute-done.3.refs_0_, bf16[264,512]{1,0:T(8,128)(2,1)S(1)} %collective-permute-done.4.refs_1_, ...), custom_call_target="tpu_custom_call" | custom-call | flops 830472192 | bytes 3145728 | tf_op jit(solution)/shard_map/project/pallas_call | solution.py:57
  78.4 1.6 %collective-permute-start.18 = (bf16[256,128]{1,0:T(8,128)(2,1)S(1)}, bf16[256,128]{1,0:T(8,128)(2,1)S(1)}, u32[]{:S(2)}, u32[]{:S(2)}) collective-permute-start(bf16[256,128]{1,0:T(8,128)(2,1)S(1)} %get-tuple-element.62), channel_id=1, source_target_pairs={{0,16},{8,24},{16,0},{24,8},{1,17},{9,25},{17,1},{25,9},{2,18},{10... | collective-permute-start | bytes 196616 | tf_op jit(solution)/shard_map/ppermute | solution.py:37
  80.0 2.9 %collective-permute-start.19 = (bf16[256,128]{1,0:T(8,128)(2,1)S(1)}, bf16[256,128]{1,0:T(8,128)(2,1)S(1)}, u32[]{:S(2)}, u32[]{:S(2)}) collective-permute-start(bf16[256,128]{1,0:T(8,128)(2,1)S(1)} %get-tuple-element.65), channel_id=1, source_target_pairs={{0,24},{8,0},{16,8},{24,16},{1,25},{9,1},{17,9},{25,17},{2,26},{10... | collective-permute-start | bytes 196616 | tf_op jit(solution)/shard_map/ppermute | solution.py:37
  83.0 0.5 collective-permute-start.17
  83.5 0.1 collective-permute-start.15
  83.6 1.4 taps_spectra.1.refs_8_
  85.0 0.3 collective-permute-done.16.refs_3_
  85.3 2.0 %collective-permute-done.17.refs_4_ = bf16[256,128]{1,0:T(8,128)(2,1)S(1)} collective-permute-done((bf16[256,128]{1,0:T(8,128)(2,1)S(1)}, bf16[256,128]{1,0:T(8,128)(2,1)S(1)}, u32[]{:S(2)}, u32[]{:S(2)}) %collective-permute-start.17) | collective-permute-done | bytes 65568 | tf_op jit(solution)/shard_map/ppermute | solution.py:37
  87.3 1.4 collective-permute-done.15.refs_2_
  88.6 2.7 %long_filter.1 = (bf16[256,128]{1,0:T(8,128)(2,1)S(1)}, bf16[256,128]{1,0:T(8,128)(2,1)S(1)}, bf16[256,128]{1,0:T(8,128)(2,1)S(1)}, bf16[256,128]{1,0:T(8,128)(2...) custom-call(s32[1]{0:T(128)} %bitcast.3.at, ...), custom_call_target="tpu_custom_call" | custom-call | flops 1073741824 | bytes 3145728 | tf_op jit(solution)/shard_map/long_filter/pallas_call | solution.py:57
  91.4 1.6 %collective-permute-start.33 = (bf16[256,128]{1,0:T(8,128)(2,1)S(1)}, bf16[256,128]{1,0:T(8,128)(2,1)S(1)}, u32[]{:S(2)}, u32[]{:S(2)}) collective-permute-start(bf16[256,128]{1,0:T(8,128)(2,1)S(1)} %get-tuple-element.43), channel_id=1, source_target_pairs={{0,16},{8,24},{16,0},{24,8},{1,17},{9,25},{17,1},{25,9},{2,18},{10... | collective-permute-start | bytes 196616 | tf_op jit(solution)/shard_map/ppermute | solution.py:37
  93.0 2.8 %collective-permute-start.34 = (bf16[256,128]{1,0:T(8,128)(2,1)S(1)}, bf16[256,128]{1,0:T(8,128)(2,1)S(1)}, u32[]{:S(2)}, u32[]{:S(2)}) collective-permute-start(bf16[256,128]{1,0:T(8,128)(2,1)S(1)} %get-tuple-element.44), channel_id=1, source_target_pairs={{0,24},{8,0},{16,8},{24,16},{1,25},{9,1},{17,9},{25,17},{2,26},{10... | collective-permute-start | bytes 196616 | tf_op jit(solution)/shard_map/ppermute | solution.py:37
  95.8 0.7 collective-permute-done.32.refs_1_
  96.5 1.2 collective-permute-done.34.refs_3_
  97.9 2.4 %collective-permute-start.24 = (bf16[256,128]{1,0:T(8,128)(2,1)S(1)}, bf16[256,128]{1,0:T(8,128)(2,1)S(1)}, u32[]{:S(2)}, u32[]{:S(2)}) collective-permute-start(bf16[256,128]{1,0:T(8,128)(2,1)S(1)} %get-tuple-element.33), channel_id=1, source_target_pairs={{0,8},{8,16},{16,24},{24,0},{1,9},{9,17},{17,25},{25,1},{2,10},{10... | collective-permute-start | bytes 196616 | tf_op jit(solution)/shard_map/ppermute | solution.py:37
  100.2 1.5 %collective-permute-start.25 = (bf16[256,128]{1,0:T(8,128)(2,1)S(1)}, bf16[256,128]{1,0:T(8,128)(2,1)S(1)}, u32[]{:S(2)}, u32[]{:S(2)}) collective-permute-start(bf16[256,128]{1,0:T(8,128)(2,1)S(1)} %get-tuple-element.34), channel_id=1, source_target_pairs={{0,16},{8,24},{16,0},{24,8},{1,17},{9,25},{17,1},{25,9},{2,18},{10... | collective-permute-start | bytes 196616 | tf_op jit(solution)/shard_map/ppermute | solution.py:37
  101.8 2.2 %collective-permute-done.24.refs_1_ = bf16[256,128]{1,0:T(8,128)(2,1)S(1)} collective-permute-done((bf16[256,128]{1,0:T(8,128)(2,1)S(1)}, bf16[256,128]{1,0:T(8,128)(2,1)S(1)}, u32[]{:S(2)}, u32[]{:S(2)}) %collective-permute-start.24) | collective-permute-done | bytes 65568 | tf_op jit(solution)/shard_map/ppermute | solution.py:37
  104.0 1.3 collective-permute-done.25.refs_2_
  105.3 0.7 collective-permute-done.26.refs_3_
  106.3 1.7 %output_shares.7 = (bf16[256,512]{1,0:T(8,128)(2,1)S(1)}, bf16[256,512]{1,0:T(8,128)(2,1)S(1)}) custom-call(s32[3]{0:T(128)S(1)} %get-tuple-element.72.ids, bf16[256,512]{1,0:T(8,128)(2,1)S(1)} %gate_blocks.3.a_ref, bf16[256,512]{1,0:T(8,128)(2,1)S(1)} %collective-permute-done.35.b_ref, bf16[512,4096]{1,0:T(8,128)(2,1)S(1)} %copy-done.2, ...), custom_call_target="tpu_custom_call" | custom-call | flops 536870912 | bytes 2097152 | tf_op jit(solution)/shard_map/output_shares/pallas_call | solution.py:57
  108.0 1.6 %collective-permute-start.36 = (bf16[256,512]{1,0:T(8,128)(2,1)S(1)}, bf16[256,512]{1,0:T(8,128)(2,1)S(1)}, u32[]{:S(2)}, u32[]{:S(2)}) collective-permute-start(bf16[256,512]{1,0:T(8,128)(2,1)S(1)} %get-tuple-element.46), channel_id=1, source_target_pairs={{0,6},{1,7},{2,0},{3,1},{4,2},{5,3},{6,4},{7,5},{8,14},{9,15},{10,... | collective-permute-start | bytes 786440 | tf_op jit(solution)/shard_map/ppermute | solution.py:37
  109.7 0.5 collective-permute-start.38
  110.1 1.7 %output_shares.5 = (bf16[256,512]{1,0:T(8,128)(2,1)S(1)}, bf16[256,512]{1,0:T(8,128)(2,1)S(1)}) custom-call(s32[3]{0:T(128)S(1)} %get-tuple-element.70.ids, bf16[256,512]{1,0:T(8,128)(2,1)S(1)} %gate_blocks.2.a_ref, bf16[256,512]{1,0:T(8,128)(2,1)S(1)} %collective-permute-done.27.b_ref, bf16[512,4096]{1,0:T(8,128)(2,1)S(1)} %copy-done.2, ...), custom_call_target="tpu_custom_call" | custom-call | flops 536870912 | bytes 2097152 | tf_op jit(solution)/shard_map/output_shares/pallas_call | solution.py:57
  111.8 0.8 collective-permute-start.29
  112.7 3.0 %collective-permute-start.31 = (bf16[256,512]{1,0:T(8,128)(2,1)S(1)}, bf16[256,512]{1,0:T(8,128)(2,1)S(1)}, u32[]{:S(2)}, u32[]{:S(2)}) collective-permute-start(bf16[256,512]{1,0:T(8,128)(2,1)S(1)} %get-tuple-element.39), channel_id=1, source_target_pairs={{0,6},{1,7},{2,0},{3,1},{4,2},{5,3},{6,4},{7,5},{8,14},{9,15},{10,... | collective-permute-start | bytes 786440 | tf_op jit(solution)/shard_map/ppermute | solution.py:37
  115.7 1.7 %output_shares.6 = (f32[256,512]{1,0:T(8,128)S(1)}, f32[256,512]{1,0:T(8,128)S(1)}) custom-call(s32[3]{0:T(128)S(1)} %get-tuple-element.71.ids, bf16[256,512]{1,0:T(8,128)(2,1)S(1)} %gate_blocks.3.a_ref, bf16[256,512]{1,0:T(8,128)(2,1)S(1)} %collective-permute-done.35.b_ref, bf16[512,4096]{1,0:T(8,128)(2,1)S(1)} %copy-done.2, ...), custom_call_target="tpu_custom_call" | custom-call | flops 536870912 | bytes 2097152 | tf_op jit(solution)/shard_map/output_shares/pallas_call | solution.py:57
  117.4 10.7 %collective-permute-done.36 = bf16[256,512]{1,0:T(8,128)(2,1)S(1)} collective-permute-done((bf16[256,512]{1,0:T(8,128)(2,1)S(1)}, bf16[256,512]{1,0:T(8,128)(2,1)S(1)}, u32[]{:S(2)}, u32[]{:S(2)}) %collective-permute-start.36) | collective-permute-done | bytes 262176 | tf_op jit(solution)/shard_map/ppermute | solution.py:37
  128.2 1.7 %output_shares.4 = (f32[256,512]{1,0:T(8,128)S(1)}, f32[256,512]{1,0:T(8,128)S(1)}) custom-call(s32[3]{0:T(128)S(1)} %get-tuple-element.69.ids, bf16[256,512]{1,0:T(8,128)(2,1)S(1)} %gate_blocks.2.a_ref, bf16[256,512]{1,0:T(8,128)(2,1)S(1)} %collective-permute-done.27.b_ref, bf16[512,4096]{1,0:T(8,128)(2,1)S(1)} %copy-done.2, ...), custom_call_target="tpu_custom_call" | custom-call | flops 536870912 | bytes 2097152 | tf_op jit(solution)/shard_map/output_shares/pallas_call | solution.py:57
  130.0 2.1 %collective-permute-start.30 = (bf16[256,512]{1,0:T(8,128)(2,1)S(1)}, bf16[256,512]{1,0:T(8,128)(2,1)S(1)}, u32[]{:S(2)}, u32[]{:S(2)}) collective-permute-start(bf16[256,512]{1,0:T(8,128)(2,1)S(1)} %add_convert_fusion.3), channel_id=1, source_target_pairs={{0,2},{1,3},{2,4},{3,5},{4,6},{5,7},{6,0},{7,1},{8,10},{9,11},{10,... | collective-permute-start | bytes 786440 | tf_op jit(solution)/shard_map/ppermute | solution.py:37
  132.1 7.2 %collective-permute-done.37 = bf16[256,512]{1,0:T(8,128)(2,1)S(1)} collective-permute-done((bf16[256,512]{1,0:T(8,128)(2,1)S(1)}, bf16[256,512]{1,0:T(8,128)(2,1)S(1)}, u32[]{:S(2)}, u32[]{:S(2)}) %collective-permute-start.37) | collective-permute-done | bytes 262176 | tf_op jit(solution)/shard_map/ppermute | solution.py:37
  139.3 0.1 add_convert_fusion
  139.5 5.6 %collective-permute-done.30 = bf16[256,512]{1,0:T(8,128)(2,1)S(1)} collective-permute-done((bf16[256,512]{1,0:T(8,128)(2,1)S(1)}, bf16[256,512]{1,0:T(8,128)(2,1)S(1)}, u32[]{:S(2)}, u32[]{:S(2)}) %collective-permute-start.30) | collective-permute-done | bytes 262176 | tf_op jit(solution)/shard_map/ppermute | solution.py:37
  145.1 0.1 add_convert_fusion.2
  145.2 0.8 pad_maximum_fusion.2
  (64 shorter events, 1.3 us)
Async XLA Ops:
  1.0 32.4 %collective-permute-start.11 = (bf16[264,512]{1,0:T(8,128)(2,1)S(1)}, bf16[264,512]{1,0:T(8,128)(2,1)S(1)}, u32[]{:S(2)}, u32[]{:S(2)}) collective-permute-start(bf16[264,512]{1,0:T(8,128)(2,1)S(1)} %slice.26.refs_0_), channel_id=1, source_target_pairs={{0,1},{1,0},{2,3},{3,2},{4,5},{5,4},{6,7},{7,6},{8,9},{9,8},{10,11... | collective-permute-start | bytes 811016 | tf_op jit(solution)/shard_map/ppermute | solution.py:41
  1.5 19.2 %collective-permute-start.7 = (bf16[264,512]{1,0:T(8,128)(2,1)S(1)}, bf16[264,512]{1,0:T(8,128)(2,1)S(1)}, u32[]{:S(2)}, u32[]{:S(2)}) collective-permute-start(bf16[264,512]{1,0:T(8,128)(2,1)S(1)} %slice.26.refs_0_), channel_id=1, source_target_pairs={{0,2},{1,3},{2,4},{3,5},{4,6},{5,7},{6,0},{7,1},{8,10},{9,11},{10,... | collective-permute-start | bytes 811016 | tf_op jit(solution)/shard_map/ppermute | solution.py:37
  4.1 14.3 %collective-permute-start.1 = (bf16[264,512]{1,0:T(8,128)(2,1)S(1)}, bf16[264,512]{1,0:T(8,128)(2,1)S(1)}, u32[]{:S(2)}, u32[]{:S(2)}) collective-permute-start(bf16[264,512]{1,0:T(8,128)(2,1)S(1)} %slice.26.refs_0_), channel_id=1, source_target_pairs={{0,6},{1,7},{2,0},{3,1},{4,2},{5,3},{6,4},{7,5},{8,14},{9,15},{10,... | collective-permute-start | bytes 811016 | tf_op jit(solution)/shard_map/ppermute | solution.py:37
  6.9 6.6 %collective-permute-start = (bf16[8,512]{1,0:T(8,128)(2,1)S(1)}, bf16[8,512]{1,0:T(8,128)(2,1)S(1)}, u32[]{:S(2)}, u32[]{:S(2)}) collective-permute-start(bf16[8,512]{1,0:T(8,128)(2,1)S(1)} %slice.24), channel_id=1, source_target_pairs={{0,8},{8,16},{16,24},{24,0},{1,9},{9,17},{17,25},{25,1},{2,10},{10... | collective-permute-start | bytes 24584 | tf_op jit(solution)/shard_map/ppermute | solution.py:37
  10.2 27.3 %copy-start.6 = (bf16[3,3,512]{2,1,0:T(4,128)(2,1)S(1)}, bf16[3,3,512]{2,1,0:T(4,128)(2,1)}, u32[]{:S(2)}) copy-start(bf16[3,3,512]{2,1,0:T(4,128)(2,1)} %param.10) | copy-start | bytes 27652
  11.9 94.3 %collective-permute-start.28 = (bf16[512,2048]{1,0:T(8,128)(2,1)}, bf16[512,2048]{1,0:T(8,128)(2,1)S(1)}, u32[]{:S(2)}, u32[]{:S(2)}) collective-permute-start(bf16[512,2048]{1,0:T(8,128)(2,1)} %pad_maximum_fusion), channel_id=1, source_target_pairs={{0,1},{1,0},{2,3},{3,2},{4,5},{5,4},{6,7},{7,6},{8,9},{9,8},{10,11... | collective-permute-start | bytes 6291464 | tf_op jit(solution)/shard_map/ppermute | solution.py:41
  18.5 16.4 %collective-permute-start.2 = (bf16[264,512]{1,0:T(8,128)(2,1)S(1)}, bf16[264,512]{1,0:T(8,128)(2,1)}, u32[]{:S(2)}, u32[]{:S(2)}) collective-permute-start(bf16[264,512]{1,0:T(8,128)(2,1)S(1)} %pad_maximum_fusion.3.refs_0_), channel_id=1, source_target_pairs={{0,6},{1,7},{2,0},{3,1},{4,2},{5,3},{6,4},{7,5},{8,14},{9,15},{10,... | collective-permute-start | bytes 811016 | tf_op jit(solution)/shard_map/ppermute | solution.py:37
  20.7 13.9 %collective-permute-start.12 = (bf16[264,512]{1,0:T(8,128)(2,1)S(1)}, bf16[264,512]{1,0:T(8,128)(2,1)}, u32[]{:S(2)}, u32[]{:S(2)}) collective-permute-start(bf16[264,512]{1,0:T(8,128)(2,1)S(1)} %collective-permute-done.7.refs_2_), channel_id=1, source_target_pairs={{0,1},{1,0},{2,3},{3,2},{4,5},{5,4},{6,7},{7,6},{8,9},{9,8},{10,11... | collective-permute-start | bytes 811016 | tf_op jit(solution)/shard_map/ppermute | solution.py:41
  20.7 12.6 %collective-permute-start.8 = (bf16[264,512]{1,0:T(8,128)(2,1)S(1)}, bf16[264,512]{1,0:T(8,128)(2,1)}, u32[]{:S(2)}, u32[]{:S(2)}) collective-permute-start(bf16[264,512]{1,0:T(8,128)(2,1)S(1)} %collective-permute-done.7.refs_2_), channel_id=1, source_target_pairs={{0,2},{1,3},{2,4},{3,5},{4,6},{5,7},{6,0},{7,1},{8,10},{9,11},{10,... | collective-permute-start | bytes 811016 | tf_op jit(solution)/shard_map/ppermute | solution.py:37
  33.3 6.3 %collective-permute-start.13 = (bf16[264,512]{1,0:T(8,128)(2,1)S(1)}, bf16[264,512]{1,0:T(8,128)(2,1)}, u32[]{:S(2)}, u32[]{:S(2)}) collective-permute-start(bf16[264,512]{1,0:T(8,128)(2,1)S(1)} %collective-permute-done.1.refs_4_), channel_id=1, source_target_pairs={{0,1},{1,0},{2,3},{3,2},{4,5},{5,4},{6,7},{7,6},{8,9},{9,8},{10,11... | collective-permute-start | bytes 811016 | tf_op jit(solution)/shard_map/ppermute | solution.py:41
  33.3 11.2 %collective-permute-start.9 = (bf16[264,512]{1,0:T(8,128)(2,1)S(1)}, bf16[264,512]{1,0:T(8,128)(2,1)}, u32[]{:S(2)}, u32[]{:S(2)}) collective-permute-start(bf16[264,512]{1,0:T(8,128)(2,1)S(1)} %pad_maximum_fusion.3.refs_0_), channel_id=1, source_target_pairs={{0,2},{1,3},{2,4},{3,5},{4,6},{5,7},{6,0},{7,1},{8,10},{9,11},{10,... | collective-permute-start | bytes 811016 | tf_op jit(solution)/shard_map/ppermute | solution.py:37
  34.6 10.0 %collective-permute-start.14 = (bf16[264,512]{1,0:T(8,128)(2,1)}, bf16[264,512]{1,0:T(8,128)(2,1)}, u32[]{:S(2)}, u32[]{:S(2)}) collective-permute-start(bf16[264,512]{1,0:T(8,128)(2,1)} %collective-permute-done.8.refs_6_), channel_id=1, source_target_pairs={{0,1},{1,0},{2,3},{3,2},{4,5},{5,4},{6,7},{7,6},{8,9},{9,8},{10,11... | collective-permute-start | bytes 811016 | tf_op jit(solution)/shard_map/ppermute | solution.py:41
  34.8 14.8 %collective-permute-start.3 = (bf16[264,512]{1,0:T(8,128)(2,1)}, bf16[264,512]{1,0:T(8,128)(2,1)}, u32[]{:S(2)}, u32[]{:S(2)}) collective-permute-start(bf16[264,512]{1,0:T(8,128)(2,1)} %collective-permute-done.2.refs_2_), channel_id=1, source_target_pairs={{0,6},{1,7},{2,0},{3,1},{4,2},{5,3},{6,4},{7,5},{8,14},{9,15},{10,... | collective-permute-start | bytes 811016 | tf_op jit(solution)/shard_map/ppermute | solution.py:37
  39.6 23.2 %collective-permute-start.5 = (bf16[264,512]{1,0:T(8,128)(2,1)S(1)}, bf16[264,512]{1,0:T(8,128)(2,1)S(1)}, u32[]{:S(2)}, u32[]{:S(2)}) collective-permute-start(bf16[264,512]{1,0:T(8,128)(2,1)S(1)} %pad_maximum_fusion.3.refs_0_), channel_id=1, source_target_pairs={{0,1},{1,0},{2,3},{3,2},{4,5},{5,4},{6,7},{7,6},{8,9},{9,8},{10,11... | collective-permute-start | bytes 811016 | tf_op jit(solution)/shard_map/ppermute | solution.py:41
  44.6 20.8 %collective-permute-start.6 = (bf16[264,512]{1,0:T(8,128)(2,1)}, bf16[264,512]{1,0:T(8,128)(2,1)S(1)}, u32[]{:S(2)}, u32[]{:S(2)}) collective-permute-start(bf16[264,512]{1,0:T(8,128)(2,1)} %collective-permute-done.2.refs_2_), channel_id=1, source_target_pairs={{0,1},{1,0},{2,3},{3,2},{4,5},{5,4},{6,7},{7,6},{8,9},{9,8},{10,11... | collective-permute-start | bytes 811016 | tf_op jit(solution)/shard_map/ppermute | solution.py:41
  44.6 21.3 %collective-permute-start.10 = (bf16[264,512]{1,0:T(8,128)(2,1)}, bf16[264,512]{1,0:T(8,128)(2,1)S(1)}, u32[]{:S(2)}, u32[]{:S(2)}) collective-permute-start(bf16[264,512]{1,0:T(8,128)(2,1)} %collective-permute-done.9.refs_4_), channel_id=1, source_target_pairs={{0,1},{1,0},{2,3},{3,2},{4,5},{5,4},{6,7},{7,6},{8,9},{9,8},{10,11... | collective-permute-start | bytes 811016 | tf_op jit(solution)/shard_map/ppermute | solution.py:41
  49.6 22.7 %collective-permute-start.4 = (bf16[264,512]{1,0:T(8,128)(2,1)}, bf16[264,512]{1,0:T(8,128)(2,1)S(1)}, u32[]{:S(2)}, u32[]{:S(2)}) collective-permute-start(bf16[264,512]{1,0:T(8,128)(2,1)} %collective-permute-done.3.refs_0_), channel_id=1, source_target_pairs={{0,1},{1,0},{2,3},{3,2},{4,5},{5,4},{6,7},{7,6},{8,9},{9,8},{10,11... | collective-permute-start | bytes 811016 | tf_op jit(solution)/shard_map/ppermute | solution.py:41
  49.6 4.6 %copy-start = (bf16[4096,3,512]{2,0,1:T(8,128)(2,1)S(1)}, bf16[4096,3,512]{2,0,1:T(8,128)(2,1)}, u32[]{:S(2)}) copy-start(bf16[4096,3,512]{2,0,1:T(8,128)(2,1)} %param.9) | copy-start | bytes 37748740
  54.2 12.3 %copy-start.1 = (bf16[4096,3,512]{2,0,1:T(8,128)(2,1)S(1)}, bf16[4096,3,512]{2,0,1:T(8,128)(2,1)}, u32[]{:S(2)}) copy-start(bf16[4096,3,512]{2,0,1:T(8,128)(2,1)} %param.9) | copy-start | bytes 37748740
  62.8 15.5 %collective-permute-start.23 = (bf16[512,128]{1,0:T(8,128)(2,1)S(1)}, bf16[512,128]{1,0:T(8,128)(2,1)S(1)}, u32[]{:S(2)}, u32[]{:S(2)}) collective-permute-start(bf16[512,128]{1,0:T(8,128)(2,1)S(1)} %get-tuple-element.53), channel_id=1, source_target_pairs={{0,24},{8,0},{16,8},{24,16},{1,25},{9,1},{17,9},{25,17},{2,26},{10... | collective-permute-start | bytes 393224 | tf_op jit(solution)/shard_map/ppermute | solution.py:37
  65.3 14.6 %collective-permute-start.22 = (bf16[512,128]{1,0:T(8,128)(2,1)S(1)}, bf16[512,128]{1,0:T(8,128)(2,1)S(1)}, u32[]{:S(2)}, u32[]{:S(2)}) collective-permute-start(bf16[512,128]{1,0:T(8,128)(2,1)S(1)} %get-tuple-element.54), channel_id=1, source_target_pairs={{0,16},{8,24},{16,0},{24,8},{1,17},{9,25},{17,1},{25,9},{2,18},{10... | collective-permute-start | bytes 393224 | tf_op jit(solution)/shard_map/ppermute | solution.py:37
  65.9 14.2 %collective-permute-start.21 = (bf16[512,128]{1,0:T(8,128)(2,1)S(1)}, bf16[512,128]{1,0:T(8,128)(2,1)S(1)}, u32[]{:S(2)}, u32[]{:S(2)}) collective-permute-start(bf16[512,128]{1,0:T(8,128)(2,1)S(1)} %get-tuple-element.55), channel_id=1, source_target_pairs={{0,8},{8,16},{16,24},{24,0},{1,9},{9,17},{17,25},{25,1},{2,10},{10... | collective-permute-start | bytes 393224 | tf_op jit(solution)/shard_map/ppermute | solution.py:37
  72.4 11.2 %copy-start.3 = (bf16[1024,1024]{1,0:T(8,128)(2,1)S(1)}, bf16[1024,1024]{1,0:T(8,128)(2,1)}, u32[]{:S(2)}) copy-start(bf16[1024,1024]{1,0:T(8,128)(2,1)} %constant.166.clone.refs_4_) | copy-start | bytes 6291460
  72.4 10.6 %collective-permute-start.20 = (bf16[256,128]{1,0:T(8,128)(2,1)S(1)}, bf16[256,128]{1,0:T(8,128)(2,1)S(1)}, u32[]{:S(2)}, u32[]{:S(2)}) collective-permute-start(bf16[256,128]{1,0:T(8,128)(2,1)S(1)} %get-tuple-element.61), channel_id=1, source_target_pairs={{0,24},{8,0},{16,8},{24,16},{1,25},{9,1},{17,9},{25,17},{2,26},{10... | collective-permute-start | bytes 196616 | tf_op jit(solution)/shard_map/ppermute | solution.py:37
  78.3 10.3 %copy-start.4 = (bf16[1024,512]{1,0:T(8,128)(2,1)S(1)}, bf16[1024,512]{1,0:T(8,128)(2,1)}, u32[]{:S(2)}) copy-start(bf16[1024,512]{1,0:T(8,128)(2,1)} %constant.168.refs_9_) | copy-start | bytes 3145732
  78.3 10.3 %copy-start.5 = (bf16[512,1024]{1,0:T(8,128)(2,1)S(1)}, bf16[512,1024]{1,0:T(8,128)(2,1)}, u32[]{:S(2)}) copy-start(bf16[512,1024]{1,0:T(8,128)(2,1)} %constant.167.clone.refs_10_) | copy-start | bytes 3145732
  78.4 5.1 %collective-permute-start.18 = (bf16[256,128]{1,0:T(8,128)(2,1)S(1)}, bf16[256,128]{1,0:T(8,128)(2,1)S(1)}, u32[]{:S(2)}, u32[]{:S(2)}) collective-permute-start(bf16[256,128]{1,0:T(8,128)(2,1)S(1)} %get-tuple-element.62), channel_id=1, source_target_pairs={{0,16},{8,24},{16,0},{24,8},{1,17},{9,25},{17,1},{25,9},{2,18},{10... | collective-permute-start | bytes 196616 | tf_op jit(solution)/shard_map/ppermute | solution.py:37
  80.0 5.3 %collective-permute-start.16 = (bf16[256,128]{1,0:T(8,128)(2,1)S(1)}, bf16[256,128]{1,0:T(8,128)(2,1)S(1)}, u32[]{:S(2)}, u32[]{:S(2)}) collective-permute-start(bf16[256,128]{1,0:T(8,128)(2,1)S(1)} %get-tuple-element.63), channel_id=1, source_target_pairs={{0,8},{8,16},{16,24},{24,0},{1,9},{9,17},{17,25},{25,1},{2,10},{10... | collective-permute-start | bytes 196616 | tf_op jit(solution)/shard_map/ppermute | solution.py:37
  80.0 5.2 %collective-permute-start.19 = (bf16[256,128]{1,0:T(8,128)(2,1)S(1)}, bf16[256,128]{1,0:T(8,128)(2,1)S(1)}, u32[]{:S(2)}, u32[]{:S(2)}) collective-permute-start(bf16[256,128]{1,0:T(8,128)(2,1)S(1)} %get-tuple-element.65), channel_id=1, source_target_pairs={{0,24},{8,0},{16,8},{24,16},{1,25},{9,1},{17,9},{25,17},{2,26},{10... | collective-permute-start | bytes 196616 | tf_op jit(solution)/shard_map/ppermute | solution.py:37
  83.0 4.3 %collective-permute-start.17 = (bf16[256,128]{1,0:T(8,128)(2,1)S(1)}, bf16[256,128]{1,0:T(8,128)(2,1)S(1)}, u32[]{:S(2)}, u32[]{:S(2)}) collective-permute-start(bf16[256,128]{1,0:T(8,128)(2,1)S(1)} %get-tuple-element.66), channel_id=1, source_target_pairs={{0,16},{8,24},{16,0},{24,8},{1,17},{9,25},{17,1},{25,9},{2,18},{10... | collective-permute-start | bytes 196616 | tf_op jit(solution)/shard_map/ppermute | solution.py:37
  83.5 5.2 %collective-permute-start.15 = (bf16[256,128]{1,0:T(8,128)(2,1)S(1)}, bf16[256,128]{1,0:T(8,128)(2,1)S(1)}, u32[]{:S(2)}, u32[]{:S(2)}) collective-permute-start(bf16[256,128]{1,0:T(8,128)(2,1)S(1)} %get-tuple-element.67), channel_id=1, source_target_pairs={{0,8},{8,16},{16,24},{24,0},{1,9},{9,17},{17,25},{25,1},{2,10},{10... | collective-permute-start | bytes 196616 | tf_op jit(solution)/shard_map/ppermute | solution.py:37
  83.6 22.7 %copy-start.2 = (bf16[512,4096]{1,0:T(8,128)(2,1)S(1)}, bf16[512,4096]{1,0:T(8,128)(2,1)}, u32[]{:S(2)}) copy-start(bf16[512,4096]{1,0:T(8,128)(2,1)} %w_ref.7) | copy-start | bytes 12582916
  91.3 5.2 %collective-permute-start.32 = (bf16[256,128]{1,0:T(8,128)(2,1)S(1)}, bf16[256,128]{1,0:T(8,128)(2,1)S(1)}, u32[]{:S(2)}, u32[]{:S(2)}) collective-permute-start(bf16[256,128]{1,0:T(8,128)(2,1)S(1)} %get-tuple-element.42), channel_id=1, source_target_pairs={{0,8},{8,16},{16,24},{24,0},{1,9},{9,17},{17,25},{25,1},{2,10},{10... | collective-permute-start | bytes 196616 | tf_op jit(solution)/shard_map/ppermute | solution.py:37
  91.4 5.2 %collective-permute-start.33 = (bf16[256,128]{1,0:T(8,128)(2,1)S(1)}, bf16[256,128]{1,0:T(8,128)(2,1)S(1)}, u32[]{:S(2)}, u32[]{:S(2)}) collective-permute-start(bf16[256,128]{1,0:T(8,128)(2,1)S(1)} %get-tuple-element.43), channel_id=1, source_target_pairs={{0,16},{8,24},{16,0},{24,8},{1,17},{9,25},{17,1},{25,9},{2,18},{10... | collective-permute-start | bytes 196616 | tf_op jit(solution)/shard_map/ppermute | solution.py:37
  93.0 4.8 %collective-permute-start.34 = (bf16[256,128]{1,0:T(8,128)(2,1)S(1)}, bf16[256,128]{1,0:T(8,128)(2,1)S(1)}, u32[]{:S(2)}, u32[]{:S(2)}) collective-permute-start(bf16[256,128]{1,0:T(8,128)(2,1)S(1)} %get-tuple-element.44), channel_id=1, source_target_pairs={{0,24},{8,0},{16,8},{24,16},{1,25},{9,1},{17,9},{25,17},{2,26},{10... | collective-permute-start | bytes 196616 | tf_op jit(solution)/shard_map/ppermute | solution.py:37
  97.8 8.5 %collective-permute-start.35 = (bf16[256,512]{1,0:T(8,128)(2,1)S(1)}, bf16[256,512]{1,0:T(8,128)(2,1)S(1)}, u32[]{:S(2)}, u32[]{:S(2)}) collective-permute-start(bf16[256,512]{1,0:T(8,128)(2,1)S(1)} %gate_blocks.3.a_ref), channel_id=1, source_target_pairs={{0,1},{1,0},{2,3},{3,2},{4,5},{5,4},{6,7},{7,6},{8,9},{9,8},{10,11... | collective-permute-start | bytes 786440 | tf_op jit(solution)/shard_map/ppermute | solution.py:41
  97.9 6.1 %collective-permute-start.24 = (bf16[256,128]{1,0:T(8,128)(2,1)S(1)}, bf16[256,128]{1,0:T(8,128)(2,1)S(1)}, u32[]{:S(2)}, u32[]{:S(2)}) collective-permute-start(bf16[256,128]{1,0:T(8,128)(2,1)S(1)} %get-tuple-element.33), channel_id=1, source_target_pairs={{0,8},{8,16},{16,24},{24,0},{1,9},{9,17},{17,25},{25,1},{2,10},{10... | collective-permute-start | bytes 196616 | tf_op jit(solution)/shard_map/ppermute | solution.py:37
  100.2 5.1 %collective-permute-start.25 = (bf16[256,128]{1,0:T(8,128)(2,1)S(1)}, bf16[256,128]{1,0:T(8,128)(2,1)S(1)}, u32[]{:S(2)}, u32[]{:S(2)}) collective-permute-start(bf16[256,128]{1,0:T(8,128)(2,1)S(1)} %get-tuple-element.34), channel_id=1, source_target_pairs={{0,16},{8,24},{16,0},{24,8},{1,17},{9,25},{17,1},{25,9},{2,18},{10... | collective-permute-start | bytes 196616 | tf_op jit(solution)/shard_map/ppermute | solution.py:37
  101.7 4.3 %collective-permute-start.26 = (bf16[256,128]{1,0:T(8,128)(2,1)S(1)}, bf16[256,128]{1,0:T(8,128)(2,1)S(1)}, u32[]{:S(2)}, u32[]{:S(2)}) collective-permute-start(bf16[256,128]{1,0:T(8,128)(2,1)S(1)} %get-tuple-element.35), channel_id=1, source_target_pairs={{0,24},{8,0},{16,8},{24,16},{1,25},{9,1},{17,9},{25,17},{2,26},{10... | collective-permute-start | bytes 196616 | tf_op jit(solution)/shard_map/ppermute | solution.py:37
  106.1 4.0 %collective-permute-start.27 = (bf16[256,512]{1,0:T(8,128)(2,1)S(1)}, bf16[256,512]{1,0:T(8,128)(2,1)S(1)}, u32[]{:S(2)}, u32[]{:S(2)}) collective-permute-start(bf16[256,512]{1,0:T(8,128)(2,1)S(1)} %gate_blocks.2.a_ref), channel_id=1, source_target_pairs={{0,1},{1,0},{2,3},{3,2},{4,5},{5,4},{6,7},{7,6},{8,9},{9,8},{10,11... | collective-permute-start | bytes 786440 | tf_op jit(solution)/shard_map/ppermute | solution.py:41
  108.0 20.1 %collective-permute-start.36 = (bf16[256,512]{1,0:T(8,128)(2,1)S(1)}, bf16[256,512]{1,0:T(8,128)(2,1)S(1)}, u32[]{:S(2)}, u32[]{:S(2)}) collective-permute-start(bf16[256,512]{1,0:T(8,128)(2,1)S(1)} %get-tuple-element.46), channel_id=1, source_target_pairs={{0,6},{1,7},{2,0},{3,1},{4,2},{5,3},{6,4},{7,5},{8,14},{9,15},{10,... | collective-permute-start | bytes 786440 | tf_op jit(solution)/shard_map/ppermute | solution.py:37
  109.7 22.4 %collective-permute-start.38 = (bf16[256,512]{1,0:T(8,128)(2,1)S(1)}, bf16[256,512]{1,0:T(8,128)(2,1)S(1)}, u32[]{:S(2)}, u32[]{:S(2)}) collective-permute-start(bf16[256,512]{1,0:T(8,128)(2,1)S(1)} %get-tuple-element.48), channel_id=1, source_target_pairs={{0,2},{1,3},{2,4},{3,5},{4,6},{5,7},{6,0},{7,1},{8,10},{9,11},{10,... | collective-permute-start | bytes 786440 | tf_op jit(solution)/shard_map/ppermute | solution.py:37
  111.8 18.1 %collective-permute-start.29 = (bf16[256,512]{1,0:T(8,128)(2,1)S(1)}, bf16[256,512]{1,0:T(8,128)(2,1)S(1)}, u32[]{:S(2)}, u32[]{:S(2)}) collective-permute-start(bf16[256,512]{1,0:T(8,128)(2,1)S(1)} %get-tuple-element.37), channel_id=1, source_target_pairs={{0,2},{1,3},{2,4},{3,5},{4,6},{5,7},{6,0},{7,1},{8,10},{9,11},{10,... | collective-permute-start | bytes 786440 | tf_op jit(solution)/shard_map/ppermute | solution.py:37
  112.7 26.8 %collective-permute-start.31 = (bf16[256,512]{1,0:T(8,128)(2,1)S(1)}, bf16[256,512]{1,0:T(8,128)(2,1)S(1)}, u32[]{:S(2)}, u32[]{:S(2)}) collective-permute-start(bf16[256,512]{1,0:T(8,128)(2,1)S(1)} %get-tuple-element.39), channel_id=1, source_target_pairs={{0,6},{1,7},{2,0},{3,1},{4,2},{5,3},{6,4},{7,5},{8,14},{9,15},{10,... | collective-permute-start | bytes 786440 | tf_op jit(solution)/shard_map/ppermute | solution.py:37
  128.2 11.2 %collective-permute-start.37 = (bf16[256,512]{1,0:T(8,128)(2,1)S(1)}, bf16[256,512]{1,0:T(8,128)(2,1)S(1)}, u32[]{:S(2)}, u32[]{:S(2)}) collective-permute-start(bf16[256,512]{1,0:T(8,128)(2,1)S(1)} %add_convert_fusion.1), channel_id=1, source_target_pairs={{0,6},{1,7},{2,0},{3,1},{4,2},{5,3},{6,4},{7,5},{8,14},{9,15},{10,... | collective-permute-start | bytes 786440 | tf_op jit(solution)/shard_map/ppermute | solution.py:37
  130.0 15.0 %collective-permute-start.30 = (bf16[256,512]{1,0:T(8,128)(2,1)S(1)}, bf16[256,512]{1,0:T(8,128)(2,1)S(1)}, u32[]{:S(2)}, u32[]{:S(2)}) collective-permute-start(bf16[256,512]{1,0:T(8,128)(2,1)S(1)} %add_convert_fusion.3), channel_id=1, source_target_pairs={{0,2},{1,3},{2,4},{3,5},{4,6},{5,7},{6,0},{7,1},{8,10},{9,11},{10,... | collective-permute-start | bytes 786440 | tf_op jit(solution)/shard_map/ppermute | solution.py:37

commit v3 on v2

--- a/solution.py
+++ b/solution.py
@@ -10,7 +10,7 @@
 from jax.sharding import PartitionSpec as P
 
 KERNEL = 3
-RIM = 8
+RIM = 16
 BF16 = jnp.bfloat16
 F32 = jnp.float32
 MIB = 1 << 20
@@ -70,38 +70,61 @@
     )(prefetch, *operands)
 
 
-def project(pairs, chip_ids, core, w_in, conv_taps, groups, total=None, finish=False):
+def project(pairs, chip_ids, core, rim, w_in, conv_taps, groups, total=None, finish=False):
     count = len(pairs)
-    rows, width = pairs[0][0].shape
+    parts = [p for pair in pairs for block in pair for p in block]
+    span = sum(p.shape[0] for p in pairs[0][0])
+    width = parts[0].shape[1]
     streams, _, out_width = w_in.shape
-    kept = rows - RIM
+    rim_rows = rim.shape[0]
+    rows = span + rim_rows
     split = out_width // groups % 128 == 0
     share = out_width // groups
-    blocks = [b for pair in pairs for b in pair]
     has_total = total is not None
 
-    def kernel(ids, w_ref, *refs):
-        x_refs, refs = refs[: 2 * count], refs[2 * count :]
+    def kernel(ids, w_ref, rim_ref, *refs):
+        part_refs, refs = refs[: len(parts)], refs[len(parts) :]
         if has_total:
             total_ref, refs = refs[0], refs[1:]
         if finish:
-            taps_ref, gate_ref, in_ref, acc = refs
+            taps_ref, gate_ref, in_ref, acc, x_own, x_other = refs
         else:
-            acc = refs[0]
+            acc, x_own, x_other = refs
         k, s = pl.program_id(0), pl.program_id(1)
         mine = pl.multiple_of(ids[count] * width, width)
         theirs = pl.multiple_of((1 - ids[count]) * width, width)
+        at = 0
         for j in range(count):
-
-            @pl.when(k == j)
+            here = []
+            for block in pairs[j]:
+                here.append(part_refs[at : at + len(block)])
+                at += len(block)
+
+            @pl.when((k == j) & (s == 0))
             def _():
-                part = dot(x_refs[2 * j][...], w_ref[0, pl.ds(mine, width)])
-                part = part + dot(x_refs[2 * j + 1][...], w_ref[0, pl.ds(theirs, width)])
-                if j > 0:
-                    part = part + acc[s]
-                elif has_total:
-                    part = part + total_ref[s]
+                for x, source, own in ((x_own, here[0], mine), (x_other, here[1], theirs)):
+                    row = 0
+                    for ref in source:
+                        x[row : row + ref.shape[0]] = ref[...]
+                        row += ref.shape[0]
+                    first = pl.multiple_of(ids[j] * 2 * width + own, width)
+                    x[span:rows] = rim_ref[:, pl.ds(first, width)]
+
+        part = dot(x_own[...], w_ref[0, pl.ds(mine, width)])
+        part = part + dot(x_other[...], w_ref[0, pl.ds(theirs, width)])
+        if has_total:
+            acc[s] = part + jnp.where(k == 0, total_ref[s], acc[s]) if count > 1 else part + total_ref[s]
+        elif count == 1:
+            acc[s] = part
+        else:
+
+            @pl.when(k == 0)
+            def _():
                 acc[s] = part
+
+            @pl.when(k > 0)
+            def _():
+                acc[s] += part
 
         if finish:
 
@@ -109,10 +132,11 @@
             def _():
                 def filtered(t):
                     rounded = acc[t].astype(BF16).astype(F32)
-                    result = jnp.zeros((kept, out_width), F32)
+                    longer = jnp.concatenate([rounded[rows - 8 :], rounded[:span]], 0)
+                    result = jnp.zeros((span, out_width), F32)
                     for lag in range(KERNEL):
                         row = lag * streams + t
-                        result = result + taps_ref[row : row + 1, :] * rounded[RIM - lag : rows - lag]
+                        result = result + taps_ref[row : row + 1, :] * longer[8 - lag : 8 - lag + span]
                     return result.astype(BF16)
 
                 gate_ref[...] = filtered(0)
@@ -124,24 +148,24 @@
                     in_ref[...] = gated
 
     in_specs = [pl.BlockSpec((1, 2 * width, out_width), lambda k, s, ids: (s, ids[k], 0))]
-    in_specs += [whole(b.shape) for b in blocks]
-    operands = [w_in] + blocks
+    in_specs += [whole(rim.shape)] + [whole(p.shape) for p in parts]
+    operands = [w_in, rim] + parts
     if has_total:
         in_specs.append(whole(total.shape))
         operands.append(total)
     acc_shape = (streams, rows, out_width)
+    scratch = [pltpu.VMEM((rows, width), BF16)] * 2
     if finish:
         in_specs.append(whole(conv_taps.shape))
         operands.append(conv_taps)
-        in_shape = (groups, kept, share) if split else (kept, out_width)
+        in_shape = (groups, span, share) if split else (span, out_width)
         outs = [
-            jax.ShapeDtypeStruct((kept, out_width), BF16),
+            jax.ShapeDtypeStruct((span, out_width), BF16),
             jax.ShapeDtypeStruct(in_shape, BF16),
         ]
-        scratch = [pltpu.VMEM(acc_shape, F32)]
+        scratch = [pltpu.VMEM(acc_shape, F32)] + scratch
     else:
         outs = [jax.ShapeDtypeStruct(acc_shape, F32)]
-        scratch = []
     return call(
         kernel,
         (count, streams),
@@ -157,6 +181,18 @@
     )
 
 
+def partner(me, slot, groups):
+    if groups & (groups - 1) == 0:
+        return me ^ slot
+    return (me + slot) % groups
+
+
+def source(me, slot, groups):
+    if groups & (groups - 1) == 0:
+        return me ^ slot
+    return (me - slot + groups) % groups
+
+
 def taps_spectra(pieces, forward, me):
     groups = len(pieces)
     span, share = pieces[0].shape
@@ -165,7 +201,7 @@
         piece_refs, (forward_ref, out_ref, padded) = refs[:groups], refs[groups:]
         row_ids = lax.broadcasted_iota(jnp.int32, (span, share), 0)
         for s in range(groups):
-            k = lax.rem(at[0] - s + groups, groups)
+            k = source(at[0], s, groups)
             block = piece_refs[s][...]
             padded[0:span, pl.ds(pl.multiple_of(k * share, share), share)] = block
 
@@ -196,20 +232,18 @@
 
 def long_filter(pieces, spectra_taps, forward_in, back, skip, me):
     groups = len(pieces)
-    half, share = pieces[0][0].shape
-    span = 2 * half
+    span, share = pieces[0].shape
+    half = span // 2
     cols = groups * share
-    flat = [h for pair in pieces for h in pair]
     step = 16
 
     def kernel(at, *refs):
-        ins, refs = refs[: 2 * groups], refs[2 * groups :]
+        ins, refs = refs[:groups], refs[groups:]
         taps_ref, forward_ref, back_ref, skip_ref = refs[:4]
         outs, (signal, spectra, mixture, result) = refs[4 : 4 + 2 * groups], refs[4 + 2 * groups :]
         for s in range(groups):
-            j = pl.multiple_of(lax.rem(at[0] - s + groups, groups) * share, share)
-            signal[0:half, pl.ds(j, share)] = ins[2 * s][...]
-            signal[half:span, pl.ds(j, share)] = ins[2 * s + 1][...]
+            j = pl.multiple_of(source(at[0], s, groups) * share, share)
+            signal[:, pl.ds(j, share)] = ins[s][...]
         spectra[...] = dot(forward_ref[...], signal[...]).astype(BF16)
 
         def mix(start, special):
@@ -248,12 +282,12 @@
             dot(back_ref[...], mixture[...]) + skip_ref[...] * signal[...].astype(F32)
         ).astype(BF16)
         for s in range(groups):
-            j = pl.multiple_of(lax.rem(at[0] + s, groups) * share, share)
+            j = pl.multiple_of(partner(at[0], s, groups) * share, share)
             outs[2 * s][...] = result[0:half, pl.ds(j, share)]
             outs[2 * s + 1][...] = result[half:span, pl.ds(j, share)]
 
-    operands = flat + [spectra_taps, forward_in, back, skip]
-    outs = [jax.ShapeDtypeStruct(h.shape, BF16) for h in flat]
+    operands = list(pieces) + [spectra_taps, forward_in, back, skip]
+    outs = [jax.ShapeDtypeStruct((half, share), BF16)] * (2 * groups)
     found = call(
         kernel,
         (1,),
@@ -281,7 +315,7 @@
 
     def kernel(at, gate_ref, *refs):
         for s in range(groups):
-            place = pl.multiple_of(lax.rem(at[0] - s + groups, groups) * share, share)
+            place = pl.multiple_of(source(at[0], s, groups) * share, share)
             gated = gate_ref[:, pl.ds(place, share)].astype(F32) * refs[s][...].astype(F32)
             refs[groups][:, pl.ds(place, share)] = gated.astype(BF16)
 
@@ -336,14 +370,20 @@
 
 
 def exchange(piece):
-    return [piece(0)] + [shift(piece(s), "ctx", s) for s in range(1, lax.axis_size("ctx"))]
+    groups = lax.axis_size("ctx")
+
+    def send(slot):
+        route = [(i, partner(i, slot, groups)) for i in range(groups)]
+        return lax.ppermute(piece(slot), "ctx", route)
+
+    return [piece(0)] + [send(s) for s in range(1, groups)]
 
 
 def in_order(blocks, me):
     groups = len(blocks)
     result = jnp.zeros((groups,) + blocks[0].shape, blocks[0].dtype)
     for s, b in enumerate(blocks):
-        result = lax.dynamic_update_index_in_dim(result, b, (me - s) % groups, 0)
+        result = lax.dynamic_update_index_in_dim(result, b, source(me, s, groups), 0)
     return jnp.concatenate(list(result), 1)
 
 
@@ -360,9 +400,9 @@
 
 def long_filter_plain(pieces, spectra_taps, forward_in, back, skip, me):
     groups = len(pieces)
-    half, share = pieces[0][0].shape
-    span = 2 * half
-    signal = in_order([jnp.concatenate(pair, 0) for pair in pieces], me)
+    span, share = pieces[0].shape
+    half = span // 2
+    signal = in_order(pieces, me)
     spectra = dot(forward_in, signal).astype(BF16)
     real_g, imag_g = spectra_taps[:span].astype(F32), spectra_taps[span:].astype(F32)
     real_u, imag_u = spectra[:span].astype(F32), spectra[span:].astype(F32)
@@ -383,7 +423,7 @@
     result = jnp.stack(jnp.split(result.astype(BF16), groups, axis=1))
     found = []
     for s in range(groups):
-        block = lax.dynamic_index_in_dim(result, (me + s) % groups, 0, keepdims=False)
+        block = lax.dynamic_index_in_dim(result, partner(me, s, groups), 0, keepdims=False)
         found.append((block[:half], block[half:]))
     return found
 
@@ -408,37 +448,27 @@
     w_streams = jnp.transpose(w_in, (1, 0, 2))
     short_taps = conv_taps.reshape(-1, width).astype(F32)
 
-    low = inputs[half - RIM :]
+    found = [(0, [inputs])]
+    up = down = inputs
+    for d in range(1, chips // 2 + 1):
+        if 2 * d < chips:
+            up, down = shift(up, "chan", 2), shift(down, "chan", -2)
+            found += [(d, [up]), (-d, [down])]
+        else:
+            far = [shift(up[:half], "chan", 2), shift(down[half:], "chan", -2)]
+            found.append((d, far))
+
     rim = shift(inputs[span - RIM :], "ctx", 1)
     rim = jnp.where(me > 0, rim, jnp.zeros_like(rim))
-    top = jnp.concatenate([rim, inputs[:half]], 0)
-
-    low_found, top_found = [(0, low)], [(0, top)]
-    low_up = low_down = low
-    top_up = top_down = top
-    for d in range(1, chips // 2 + 1):
-        if 2 * d < chips:
-            low_up = shift(low_up, "chan", 2)
-            low_down = shift(low_down, "chan", -2)
-            low_found += [(d, low_up), (-d, low_down)]
-        else:
-            low_far = shift(low_up, "chan", 2)
-            low_found.append((d, low_far))
-    top_down = after(top_down, low_down)
-    top_up = after(top_up, low_far)
-    for d in range(1, chips // 2 + 1):
-        if 2 * d < chips:
-            top_down = shift(top_down, "chan", -2)
-            top_up = shift(top_up, "chan", 2)
-            top_found += [(-d, top_down), (d, top_up)]
-        else:
-            top_found.append((-d, shift(top_down, "chan", -2)))
+    rim = lax.all_gather(rim, "chan", axis=1, tiled=True)
 
     split_taps = [filter_taps[:, q * share : (q + 1) * share] for q in range(groups)]
     split_taps = jnp.stack(split_taps)
 
     def pick(stack):
-        return lambda s: lax.dynamic_index_in_dim(stack, (me + s) % groups, 0, keepdims=False)
+        return lambda s: lax.dynamic_index_in_dim(
+            stack, partner(me, s, groups), 0, keepdims=False
+        )
 
     spectra_taps = (taps_spectra if aligned else taps_spectra_plain)(
         exchange(pick(split_taps)), forward, me
@@ -454,30 +484,23 @@
         )
     )
 
-    def stage(found, cut):
-        pairs = [(block, sibling(block)) for _, block in found]
-        ids = [(chip - d) % chips for d, _ in found]
-        total = None
-        if cut:
-            (total,) = project(pairs[:cut], ids[:cut], core, w_streams, short_taps, groups)
-        gate, gated = project(
-            pairs[cut:], ids[cut:], core, w_streams, short_taps, groups, total, True
-        )
-        if not aligned:
-            gated = jnp.stack(jnp.split(gated, groups, axis=1))
-        return gate, exchange(pick(gated))
-
-    gate_low, in_low = stage(low_found, 0)
-    gate_top, in_top = stage(top_found, len(top_found) - 1)
+    rim = after(rim, spectra_taps)
+    pairs = [(block, [sibling(p) for p in block]) for _, block in found]
+    ids = [(chip - d) % chips for d, _ in found]
+    (total,) = project(pairs[:-1], ids[:-1], core, rim, w_streams, short_taps, groups)
+    gate, gated = project(
+        pairs[-1:], ids[-1:], core, rim, w_streams, short_taps, groups, total, True
+    )
+    if not aligned:
+        gated = jnp.stack(jnp.split(gated, groups, axis=1))
 
     skip = lax.dynamic_slice_in_dim(skip_gain, me * share, share, 0)
     skip = jnp.tile(skip, groups)[None]
     filtered = (long_filter if aligned else long_filter_plain)(
-        list(zip(in_top, in_low)), spectra_taps, forward[:, :span], back, skip, me
+        exchange(pick(gated)), spectra_taps, forward[:, :span], back, skip, me
     )
     gating = gate_blocks if aligned else gate_blocks_plain
-    gated_top = gating(gate_top, exchange(lambda s: filtered[s][0]), me)
-    gated_low = gating(gate_low, exchange(lambda s: filtered[s][1]), me)
+    gated_top = gating(gate[:half], exchange(lambda s: filtered[s][0]), me)
 
     def sums(gated, lead):
         other = sibling(gated)
@@ -495,10 +518,10 @@
         kept = shares(carried, F32)
         ahead = shift(sent[reach], "chan", 2 * lead)
         behind = shift(sent[direct[1]], "chan", -2 * lead) if reach > 1 else None
-        return ahead, behind, kept
+        return ahead, behind, kept, sent[reach]
 
     def finish(state, lead):
-        ahead, behind, kept = state
+        ahead, behind, kept, _ = state
         reach = chips // 2
         for d in range(reach - 1, 0, -1):
             ahead = shift((ahead.astype(F32) + kept[lead * d]).astype(BF16), "chan", 2 * lead)
@@ -510,6 +533,8 @@
         return total.astype(BF16)
 
     state_top = sums(gated_top, 1)
+    low = [after(f[1], state_top[3]) for f in filtered]
+    gated_low = gating(gate[half:], exchange(lambda s: low[s]), me)
     state_low = sums(gated_low, -1)
     return jnp.concatenate([finish(state_top, 1), finish(state_low, -1)], 0)
 

time: 146 us -> 154 us (1.055)
  blocking collectives: 0 us -> 20.5 us
  starting transfers between devices: 41.6 us -> 31.2 us
  local copies, waits for them, and re-layouts: 12.5 us -> 19.7 us
  waiting for transfers between devices: 57.3 us -> 52.8 us
  Pallas kernels: 29 us -> 25.6 us
  other arithmetic: 5.34 us -> 3.23 us
    ppermute x28 -> x11, starting transfers between devices: 40.1 us -> 15.6 us  [shift(): lax.ppermute(x, axis, [(i, (i + distance) % size) for i in range(size)])]
    all_gather x0 -> x1, blocking collectives: none -> 20.5 us  [body(): rim = lax.all_gather(rim, 'chan', axis=1, tiled=True)]
    ppermute x28 -> x11, waiting for transfers between devices: 57.2 us -> 36.9 us  [shift(): lax.ppermute(x, axis, [(i, (i + distance) % size) for i in range(size)])]
    ppermute x0 -> x12, waiting for transfers between devices: none -> 14.4 us  [send(): return lax.ppermute(piece(slot), 'ctx', route)]
    ppermute x0 -> x12, starting transfers between devices: none -> 14.4 us  [send(): return lax.ppermute(piece(slot), 'ctx', route)]
    unnamed x14 -> x32, local copies, waits for them, and re-layouts: 4.61 us -> 14.6 us
    pallas_call x11 -> x10, Pallas kernels: 29 us -> 25.6 us  [call(): pl.pallas_call(kernel, grid_spec=pltpu.PrefetchScalarGridSpec(num_scalar_...]
    slice x2 -> x3, local copies, waits for them, and re-layouts: 2.64 us -> 0.07 us  [the longest x2 0.04 us: body(): far = [shift(up[:half], 'chan', 2), shift(down[half:], 'chan', -2)]]
  transfers between devices with their start and end apart: 39 -> 31, of which waited for: 15 -> 17; matrix products, arithmetic and copies ran while one was open for 8% -> 5% of each run, Pallas kernels for 20% -> 16%
where the time goes in v3:
time: 154 us; the launch traced here: 153 us
  waiting for transfers between devices  52.8 us (34%)
  starting transfers between devices  31.2 us (20%)
  Pallas kernels  25.6 us (17%)
  blocking collectives  20.5 us (13%)
  local copies, waits for them, and re-layouts  19.7 us (13%)
  other arithmetic  3.23 us (2%)
    ppermute x11, waiting for transfers between devices, shift(): lax.ppermute(x, axis, [(i, (i + distance) % size) for i in range(size)])  36.9 us
    pallas_call x10, Pallas kernels, call(): pl.pallas_call(kernel, grid_spec=pltpu.PrefetchScalarGridSpec(num_scalar_...  25.6 us
    all_gather x1, blocking collectives, body(): rim = lax.all_gather(rim, 'chan', axis=1, tiled=True)  20.5 us
    ppermute x11, starting transfers between devices, shift(): lax.ppermute(x, axis, [(i, (i + distance) % size) for i in range(size)])  15.6 us
    unnamed x32, local copies, waits for them, and re-layouts  14.6 us
    ppermute x12, waiting for transfers between devices, send(): return lax.ppermute(piece(slot), 'ctx', route)  14.4 us
    ppermute x12, starting transfers between devices, send(): return lax.ppermute(piece(slot), 'ctx', route)  14.4 us
  transfers between devices with their start and end apart: 31, of which 17 were waited for; matrix products, arithmetic and copies ran while one was open for 5% of the time, Pallas kernels for 16%

profile of v3, /device:TPU:0, one launch (start us, length us, event | category | flops | bytes accessed | tf_op | source)
XLA Modules:
  0.0 153.3 jit_solution(8260750531303152728)
XLA Ops:
  0.0 3.0 %collective-permute-start.4 = (bf16[512,512]{1,0:T(8,128)(2,1)}, bf16[512,512]{1,0:T(8,128)(2,1)S(1)}, u32[]{:S(2)}, u32[]{:S(2)}) collective-permute-start(bf16[512,512]{1,0:T(8,128)(2,1)} %refs_0_.1), channel_id=1, source_target_pairs={{0,2},{1,3},{2,4},{3,5},{4,6},{5,7},{6,0},{7,1},{8,10},{9,11},{10,... | collective-permute-start | bytes 1572872 | tf_op jit(solution)/shard_map/ppermute | solution.py:37
  3.0 2.0 %collective-permute-start.6 = (bf16[512,512]{1,0:T(8,128)(2,1)}, bf16[512,512]{1,0:T(8,128)(2,1)S(1)}, u32[]{:S(2)}, u32[]{:S(2)}) collective-permute-start(bf16[512,512]{1,0:T(8,128)(2,1)} %refs_0_.1), channel_id=1, source_target_pairs={{0,6},{1,7},{2,0},{3,1},{4,2},{5,3},{6,4},{7,5},{8,14},{9,15},{10,... | collective-permute-start | bytes 1572872 | tf_op jit(solution)/shard_map/ppermute | solution.py:37
  5.1 1.1 slice_bitcast_fusion.3
  6.3 0.7 dynamic-slice_bitcast_fusion.4
  7.0 1.7 %collective-permute-start.1 = (bf16[512,128]{1,0:T(8,128)(2,1)S(1)}, bf16[512,128]{1,0:T(8,128)(2,1)S(1)}, u32[]{:S(2)}, u32[]{:S(2)}) collective-permute-start(bf16[512,128]{1,0:T(8,128)(2,1)S(1)} %get-tuple-element.63), channel_id=1, source_target_pairs={{0,8},{8,0},{16,24},{24,16},{1,9},{9,1},{17,25},{25,17},{2,10},{10... | collective-permute-start | bytes 393224 | tf_op jit(solution)/shard_map/ppermute | solution.py:377
  8.7 0.7 slice.30
  9.4 0.3 collective-permute-start
  9.7 1.7 %constant_dynamic-slice_fusion.3 = (bf16[512,512]{1,0:T(8,128)(2,1)S(1)}, bf16[512,512]{1,0:T(8,128)(2,1)S(1)}, bf16[512,512]{1,0:T(8,128)(2,1)S(1)}, bf16[512,512]{1,0:T(8,128)(2,1)S(1)}) fusion(bf16[512,4096]{1,0:T(8,128)(2,1)} %w_ref.7, s32[]{:T(128)S(6)} %select_n.98, s32[]{:T(128)S(6)} %select_n.101, s32[]{:T(128)S(6)} %select_n.100, s32[]{:T(128)S(6)} %select_n.99), kind=kLoop, calls=%fused_computation.23 | loop fusion | bytes 4194320 | tf_op jit(solution)/shard_map/dynamic_slice | solution.py:480
  11.4 3.0 %collective-permute-done = bf16[16,512]{1,0:T(8,128)(2,1)S(1)} collective-permute-done((bf16[16,512]{1,0:T(8,128)(2,1)S(1)}, bf16[16,512]{1,0:T(8,128)(2,1)S(1)}, u32[]{:S(2)}, u32[]{:S(2)}) %collective-permute-start) | collective-permute-done | bytes 16416 | tf_op jit(solution)/shard_map/ppermute | solution.py:37
  14.4 1.2 collective-permute-start.2
  15.6 1.7 %pad_maximum_fusion = bf16[512,2048]{1,0:T(8,128)(2,1)} fusion(bf16[512,512]{1,0:T(8,128)(2,1)S(1)} %get-tuple-element.52, bf16[512,512]{1,0:T(8,128)(2,1)S(1)} %get-tuple-element.53, bf16[512,512]{1,0:T(8,128)(2,1)S(1)} %get-tuple-element.54, bf16[512,512]{1,0:T(8,128)(2,1)S(1)} %get-tuple-element.51), kind=kLoop, calls=%fused_computation | loop fusion | flops 8388608 | bytes 4194304 | tf_op jit(solution)/shard_map/concatenate | solution.py:478
  17.3 0.8 collective-permute-start.3
  18.1 1.5 collective-permute-done.2.refs_2_
  19.6 0.6 copy-done.4
  20.2 0.5 collective-permute-start.11
  20.7 7.1 %collective-permute-done.6.refs_4_ = bf16[512,512]{1,0:T(8,128)(2,1)S(1)} collective-permute-done((bf16[512,512]{1,0:T(8,128)(2,1)}, bf16[512,512]{1,0:T(8,128)(2,1)S(1)}, u32[]{:S(2)}, u32[]{:S(2)}) %collective-permute-start.6) | collective-permute-done | bytes 524320 | tf_op jit(solution)/shard_map/ppermute | solution.py:37
  28.1 1.2 collective-permute-start.5
  29.3 2.7 %collective-permute-start.7 = (bf16[256,512]{1,0:T(8,128)(2,1)S(1)}, bf16[256,512]{1,0:T(8,128)(2,1)S(1)}, u32[]{:S(2)}, u32[]{:S(2)}) collective-permute-start(bf16[256,512]{1,0:T(8,128)(2,1)S(1)} %slice.41), channel_id=1, source_target_pairs={{0,6},{1,7},{2,0},{3,1},{4,2},{5,3},{6,4},{7,5},{8,14},{9,15},{10,... | collective-permute-start | bytes 786440 | tf_op jit(solution)/shard_map/ppermute | solution.py:37
  32.0 20.5 %all_gather.3.rim_ref = bf16[16,4096]{1,0:T(8,128)(2,1)S(1)} all-gather(bf16[16,512]{1,0:T(8,128)(2,1)S(1)} %broadcast_select_fusion), channel_id=1, replica_groups=mesh['ctx'=4,'chan'=8] {'chan'}, dimensions={1}, use_global_device_ids=true | all-gather | bytes 147456 | tf_op jit(solution)/shard_map/all_gather | solution.py:463
  52.5 0.9 copy-done.5
  53.4 1.6 %copy-done.10 = bf16[1024,1024]{1,0:T(8,128)(2,1)S(1)} copy-done((bf16[1024,1024]{1,0:T(8,128)(2,1)S(1)}, bf16[1024,1024]{1,0:T(8,128)(2,1)}, u32[]{:S(2)}) %copy-start.10) | copy-done | bytes 2097176
  55.0 2.3 %taps_spectra.1.refs_4_ = bf16[1024,512]{1,0:T(8,128)(2,1)S(1)} custom-call(s32[1]{0:T(128)} %bitcast.3.at, bf16[512,128]{1,0:T(8,128)(2,1)S(1)} %get-tuple-element.64.refs_0_, bf16[512,128]{1,0:T(8,128)(2,1)S(1)} %collective-permute-done.1.refs_1_, bf16[512,128]{1,0:T(8,128)(2,1)S(1)} %copy-done.5, bf16[512,128]{1,0:T(8,128)(2,1)} %collective-permute-done.3.refs_3_, ...), custom_call_target="tpu_custom_call" | custom-call | flops 1073741824 | bytes 3145728 | tf_op jit(solution)/shard_map/taps_spectra/pallas_call | solution.py:57
  57.3 1.0 copy-done.13
  58.3 0.3 collective-permute-start.8
  58.6 0.2 collective-permute-start.9
  58.8 4.6 %copy-done.2 = bf16[4096,3,512]{2,0,1:T(8,128)(2,1)S(1)} copy-done((bf16[4096,3,512]{2,0,1:T(8,128)(2,1)S(1)}, bf16[4096,3,512]{2,0,1:T(8,128)(2,1)}, u32[]{:S(2)}) %copy-start.2) | copy-done | bytes 12582936
  63.4 9.7 %project.2.refs_4_ = f32[3,528,512]{2,1,0:T(8,128)S(1)} custom-call(s32[4]{0:T(128)S(1)} %pad_add_fusion.1.ids, bf16[3,4096,512]{2,1,0:T(8,128)(2,1)S(1)} %bitcast.33, bf16[16,4096]{1,0:T(8,128)(2,1)S(1)} %all_gather.3.rim_ref, bf16[512,512]{1,0:T(8,128)(2,1)S(1)} %copy-done.3, bf16[512,512]{1,0:T(8,128)(2,1)} %collective-permute-done.10.refs_1_, ...), custom_call_target="tpu_custom_call" | custom-call | flops 4982833152 | bytes 9437184 | tf_op jit(solution)/shard_map/project/pallas_call | solution.py:57
  73.1 4.1 %project.3 = (bf16[512,512]{1,0:T(8,128)(2,1)S(1)}, bf16[4,512,128]{2,1,0:T(8,128)(2,1)S(1)}) custom-call(s32[2]{0:T(128)S(1)} %pad_add_fusion.ids, bf16[3,4096,512]{2,1,0:T(8,128)(2,1)S(1)} %bitcast.34, bf16[16,4096]{1,0:T(8,128)(2,1)S(1)} %all_gather.3.rim_ref, bf16[256,512]{1,0:T(8,128)(2,1)S(1)} %collective-permute-done.5.refs_0_, ...), custom_call_target="tpu_custom_call" | custom-call | flops 1660944384 | bytes 3145728 | tf_op jit(solution)/shard_map/project/pallas_call | solution.py:57
  77.3 1.6 %collective-permute-start.13 = (bf16[512,128]{1,0:T(8,128)(2,1)S(1)}, bf16[512,128]{1,0:T(8,128)(2,1)S(1)}, u32[]{:S(2)}, u32[]{:S(2)}) collective-permute-start(bf16[512,128]{1,0:T(8,128)(2,1)S(1)} %get-tuple-element.59), channel_id=1, source_target_pairs={{0,8},{8,0},{16,24},{24,16},{1,9},{9,1},{17,25},{25,17},{2,10},{10... | collective-permute-start | bytes 393224 | tf_op jit(solution)/shard_map/ppermute | solution.py:377
  78.8 1.5 collective-permute-start.14
  80.4 0.5 collective-permute-start.15
  80.8 0.8 dynamic_slice.48
  81.6 1.8 %collective-permute-done.13.refs_1_ = bf16[512,128]{1,0:T(8,128)(2,1)S(1)} collective-permute-done((bf16[512,128]{1,0:T(8,128)(2,1)S(1)}, bf16[512,128]{1,0:T(8,128)(2,1)S(1)}, u32[]{:S(2)}, u32[]{:S(2)}) %collective-permute-start.13) | collective-permute-done | bytes 131104 | tf_op jit(solution)/shard_map/ppermute | solution.py:377
  83.4 3.7 %collective-permute-done.14.refs_2_ = bf16[512,128]{1,0:T(8,128)(2,1)S(1)} collective-permute-done((bf16[512,128]{1,0:T(8,128)(2,1)S(1)}, bf16[512,128]{1,0:T(8,128)(2,1)S(1)}, u32[]{:S(2)}, u32[]{:S(2)}) %collective-permute-start.14) | collective-permute-done | bytes 131104 | tf_op jit(solution)/shard_map/ppermute | solution.py:377
  87.1 1.2 copy-done.11
  88.4 1.2 copy-done.12
  89.6 1.2 copy-done.14
  90.8 2.6 %long_filter.1 = (bf16[256,128]{1,0:T(8,128)(2,1)S(1)}, bf16[256,128]{1,0:T(8,128)(2,1)S(1)}, bf16[256,128]{1,0:T(8,128)(2,1)S(1)}, bf16[256,128]{1,0:T(8,128)(2...) custom-call(s32[1]{0:T(128)} %bitcast.3.at, ...), custom_call_target="tpu_custom_call" | custom-call | flops 1073741824 | bytes 3145728 | tf_op jit(solution)/shard_map/long_filter/pallas_call | solution.py:57
  93.4 1.3 collective-permute-start.16
  94.7 0.8 collective-permute-start.17
  95.5 1.4 collective-permute-start.18
  97.0 0.7 collective-permute-done.16.refs_1_
  97.8 1.5 collective-permute-done.17.refs_2_
  99.3 1.4 collective-permute-done.18.refs_3_
  101.0 1.4 collective-permute-done.19.b_ref
  102.4 2.2 %copy-done = bf16[512,4096]{1,0:T(8,128)(2,1)S(1)} copy-done((bf16[512,4096]{1,0:T(8,128)(2,1)S(1)}, bf16[512,4096]{1,0:T(8,128)(2,1)}, u32[]{:S(2)}) %copy-start) | copy-done | bytes 4194328
  104.6 1.7 %output_shares.5 = (bf16[256,512]{1,0:T(8,128)(2,1)S(1)}, bf16[256,512]{1,0:T(8,128)(2,1)S(1)}) custom-call(s32[3]{0:T(128)S(1)} %get-tuple-element.70.ids, bf16[256,512]{1,0:T(8,128)(2,1)S(1)} %gate_blocks.2.a_ref, bf16[256,512]{1,0:T(8,128)(2,1)S(1)} %collective-permute-done.19.b_ref, bf16[512,4096]{1,0:T(8,128)(2,1)S(1)} %copy-done, ...), custom_call_target="tpu_custom_call" | custom-call | flops 536870912 | bytes 2097152 | tf_op jit(solution)/shard_map/output_shares/pallas_call | solution.py:57
  106.3 1.5 collective-permute-start.26
  107.8 1.5 collective-permute-start.25
  109.3 0.5 collective-permute-start.24
  109.9 1.8 %collective-permute-done.26.refs_3_ = bf16[256,128]{1,0:T(8,128)(2,1)S(1)} collective-permute-done((bf16[256,128]{1,0:T(8,128)(2,1)S(1)}, bf16[256,128]{1,0:T(8,128)(2,1)S(1)}, u32[]{:S(2)}, u32[]{:S(2)}) %collective-permute-start.26) | collective-permute-done | bytes 65568 | tf_op jit(solution)/shard_map/ppermute | solution.py:377
  111.7 1.1 collective-permute-done.25.refs_2_
  112.8 0.8 collective-permute-done.24.refs_1_
  113.9 3.8 %collective-permute-start.23 = (bf16[256,512]{1,0:T(8,128)(2,1)S(1)}, bf16[256,512]{1,0:T(8,128)(2,1)S(1)}, u32[]{:S(2)}, u32[]{:S(2)}) collective-permute-start(bf16[256,512]{1,0:T(8,128)(2,1)S(1)} %get-tuple-element.38), channel_id=1, source_target_pairs={{0,6},{1,7},{2,0},{3,1},{4,2},{5,3},{6,4},{7,5},{8,14},{9,15},{10,... | collective-permute-start | bytes 786440 | tf_op jit(solution)/shard_map/ppermute | solution.py:37
  117.7 1.7 %output_shares.4 = (f32[256,512]{1,0:T(8,128)S(1)}, f32[256,512]{1,0:T(8,128)S(1)}) custom-call(s32[3]{0:T(128)S(1)} %get-tuple-element.69.ids, bf16[256,512]{1,0:T(8,128)(2,1)S(1)} %gate_blocks.2.a_ref, bf16[256,512]{1,0:T(8,128)(2,1)S(1)} %collective-permute-done.19.b_ref, bf16[512,4096]{1,0:T(8,128)(2,1)S(1)} %copy-done.1, ...), custom_call_target="tpu_custom_call" | custom-call | flops 536870912 | bytes 2097152 | tf_op jit(solution)/shard_map/output_shares/pallas_call | solution.py:57
  119.4 1.7 %output_shares.7 = (bf16[256,512]{1,0:T(8,128)(2,1)S(1)}, bf16[256,512]{1,0:T(8,128)(2,1)S(1)}) custom-call(s32[3]{0:T(128)S(1)} %get-tuple-element.72.ids, bf16[256,512]{1,0:T(8,128)(2,1)S(1)} %gate_blocks.3.a_ref, bf16[256,512]{1,0:T(8,128)(2,1)S(1)} %collective-permute-done.27.b_ref, bf16[512,4096]{1,0:T(8,128)(2,1)S(1)} %copy-done.1, ...), custom_call_target="tpu_custom_call" | custom-call | flops 536870912 | bytes 2097152 | tf_op jit(solution)/shard_map/output_shares/pallas_call | solution.py:57
  121.2 3.6 %collective-permute-done.21 = bf16[256,512]{1,0:T(8,128)(2,1)S(1)} collective-permute-done((bf16[256,512]{1,0:T(8,128)(2,1)S(1)}, bf16[256,512]{1,0:T(8,128)(2,1)S(1)}, u32[]{:S(2)}, u32[]{:S(2)}) %collective-permute-start.21) | collective-permute-done | bytes 262176 | tf_op jit(solution)/shard_map/ppermute | solution.py:37
  125.0 1.7 %output_shares.6 = (f32[256,512]{1,0:T(8,128)S(1)}, f32[256,512]{1,0:T(8,128)S(1)}) custom-call(s32[3]{0:T(128)S(1)} %get-tuple-element.71.ids, bf16[256,512]{1,0:T(8,128)(2,1)S(1)} %gate_blocks.3.a_ref, bf16[256,512]{1,0:T(8,128)(2,1)S(1)} %collective-permute-done.27.b_ref, bf16[512,4096]{1,0:T(8,128)(2,1)S(1)} %copy-done.1, ...), custom_call_target="tpu_custom_call" | custom-call | flops 536870912 | bytes 2097152 | tf_op jit(solution)/shard_map/output_shares/pallas_call | solution.py:57
  126.7 7.1 %collective-permute-done.28 = bf16[256,512]{1,0:T(8,128)(2,1)S(1)} collective-permute-done((bf16[256,512]{1,0:T(8,128)(2,1)S(1)}, bf16[256,512]{1,0:T(8,128)(2,1)S(1)}, u32[]{:S(2)}, u32[]{:S(2)}) %collective-permute-start.28) | collective-permute-done | bytes 262176 | tf_op jit(solution)/shard_map/ppermute | solution.py:37
  133.9 2.3 %collective-permute-start.29 = (bf16[256,512]{1,0:T(8,128)(2,1)S(1)}, bf16[256,512]{1,0:T(8,128)(2,1)S(1)}, u32[]{:S(2)}, u32[]{:S(2)}) collective-permute-start(bf16[256,512]{1,0:T(8,128)(2,1)S(1)} %add_convert_fusion.1), channel_id=1, source_target_pairs={{0,6},{1,7},{2,0},{3,1},{4,2},{5,3},{6,4},{7,5},{8,14},{9,15},{10,... | collective-permute-start | bytes 786440 | tf_op jit(solution)/shard_map/ppermute | solution.py:37
  136.2 5.6 %collective-permute-done.22 = bf16[256,512]{1,0:T(8,128)(2,1)S(1)} collective-permute-done((bf16[256,512]{1,0:T(8,128)(2,1)S(1)}, bf16[256,512]{1,0:T(8,128)(2,1)S(1)}, u32[]{:S(2)}, u32[]{:S(2)}) %collective-permute-start.22) | collective-permute-done | bytes 262176 | tf_op jit(solution)/shard_map/ppermute | solution.py:37
  141.9 5.4 %collective-permute-done.30 = bf16[256,512]{1,0:T(8,128)(2,1)S(1)} collective-permute-done((bf16[256,512]{1,0:T(8,128)(2,1)S(1)}, bf16[256,512]{1,0:T(8,128)(2,1)S(1)}, u32[]{:S(2)}, u32[]{:S(2)}) %collective-permute-start.30) | collective-permute-done | bytes 262176 | tf_op jit(solution)/shard_map/ppermute | solution.py:37
  147.3 5.1 %collective-permute-done.29 = bf16[256,512]{1,0:T(8,128)(2,1)S(1)} collective-permute-done((bf16[256,512]{1,0:T(8,128)(2,1)S(1)}, bf16[256,512]{1,0:T(8,128)(2,1)S(1)}, u32[]{:S(2)}, u32[]{:S(2)}) %collective-permute-start.29) | collective-permute-done | bytes 262176 | tf_op jit(solution)/shard_map/ppermute | solution.py:37
  152.5 0.8 pad_maximum_fusion.2
  (64 shorter events, 1.5 us)
Async XLA Ops:
  0.0 20.2 %collective-permute-start.4 = (bf16[512,512]{1,0:T(8,128)(2,1)}, bf16[512,512]{1,0:T(8,128)(2,1)S(1)}, u32[]{:S(2)}, u32[]{:S(2)}) collective-permute-start(bf16[512,512]{1,0:T(8,128)(2,1)} %refs_0_.1), channel_id=1, source_target_pairs={{0,2},{1,3},{2,4},{3,5},{4,6},{5,7},{6,0},{7,1},{8,10},{9,11},{10,... | collective-permute-start | bytes 1572872 | tf_op jit(solution)/shard_map/ppermute | solution.py:37
  3.0 24.8 %collective-permute-start.6 = (bf16[512,512]{1,0:T(8,128)(2,1)}, bf16[512,512]{1,0:T(8,128)(2,1)S(1)}, u32[]{:S(2)}, u32[]{:S(2)}) collective-permute-start(bf16[512,512]{1,0:T(8,128)(2,1)} %refs_0_.1), channel_id=1, source_target_pairs={{0,6},{1,7},{2,0},{3,1},{4,2},{5,3},{6,4},{7,5},{8,14},{9,15},{10,... | collective-permute-start | bytes 1572872 | tf_op jit(solution)/shard_map/ppermute | solution.py:37
  5.1 24.3 %collective-permute-start.10 = (bf16[512,512]{1,0:T(8,128)(2,1)}, bf16[512,512]{1,0:T(8,128)(2,1)}, u32[]{:S(2)}, u32[]{:S(2)}) collective-permute-start(bf16[512,512]{1,0:T(8,128)(2,1)} %refs_0_.1), channel_id=1, source_target_pairs={{0,1},{1,0},{2,3},{3,2},{4,5},{5,4},{6,7},{7,6},{8,9},{9,8},{10,11... | collective-permute-start | bytes 1572872 | tf_op jit(solution)/shard_map/ppermute | solution.py:41
  7.0 10.3 %collective-permute-start.1 = (bf16[512,128]{1,0:T(8,128)(2,1)S(1)}, bf16[512,128]{1,0:T(8,128)(2,1)S(1)}, u32[]{:S(2)}, u32[]{:S(2)}) collective-permute-start(bf16[512,128]{1,0:T(8,128)(2,1)S(1)} %get-tuple-element.63), channel_id=1, source_target_pairs={{0,8},{8,0},{16,24},{24,16},{1,9},{9,1},{17,25},{25,17},{2,10},{10... | collective-permute-start | bytes 393224 | tf_op jit(solution)/shard_map/ppermute | solution.py:377
  9.4 5.0 %collective-permute-start = (bf16[16,512]{1,0:T(8,128)(2,1)S(1)}, bf16[16,512]{1,0:T(8,128)(2,1)S(1)}, u32[]{:S(2)}, u32[]{:S(2)}) collective-permute-start(bf16[16,512]{1,0:T(8,128)(2,1)S(1)} %slice.30), channel_id=1, source_target_pairs={{0,8},{8,16},{16,24},{24,0},{1,9},{9,17},{17,25},{25,1},{2,10},{10... | collective-permute-start | bytes 49160 | tf_op jit(solution)/shard_map/ppermute | solution.py:37
  9.7 18.2 %copy-start.15 = (bf16[3,3,512]{2,1,0:T(4,128)(2,1)S(1)}, bf16[3,3,512]{2,1,0:T(4,128)(2,1)}, u32[]{:S(2)}) copy-start(bf16[3,3,512]{2,1,0:T(4,128)(2,1)} %param.10) | copy-start | bytes 27652
  14.4 5.1 %collective-permute-start.2 = (bf16[512,128]{1,0:T(8,128)(2,1)S(1)}, bf16[512,128]{1,0:T(8,128)(2,1)S(1)}, u32[]{:S(2)}, u32[]{:S(2)}) collective-permute-start(bf16[512,128]{1,0:T(8,128)(2,1)S(1)} %get-tuple-element.62), channel_id=1, source_target_pairs={{0,16},{8,24},{16,0},{24,8},{1,17},{9,25},{17,1},{25,9},{2,18},{10... | collective-permute-start | bytes 393224 | tf_op jit(solution)/shard_map/ppermute | solution.py:377
  17.3 10.9 %collective-permute-start.3 = (bf16[512,128]{1,0:T(8,128)(2,1)}, bf16[512,128]{1,0:T(8,128)(2,1)}, u32[]{:S(2)}, u32[]{:S(2)}) collective-permute-start(bf16[512,128]{1,0:T(8,128)(2,1)} %get-tuple-element.61), channel_id=1, source_target_pairs={{0,24},{8,16},{16,8},{24,0},{1,25},{9,17},{17,9},{25,1},{2,26},{10... | collective-permute-start | bytes 393224 | tf_op jit(solution)/shard_map/ppermute | solution.py:377
  19.6 0.6 copy-start.4
  20.2 82.2 %collective-permute-start.20 = (bf16[512,2048]{1,0:T(8,128)(2,1)}, bf16[512,2048]{1,0:T(8,128)(2,1)S(1)}, u32[]{:S(2)}, u32[]{:S(2)}) collective-permute-start(bf16[512,2048]{1,0:T(8,128)(2,1)} %pad_maximum_fusion), channel_id=1, source_target_pairs={{0,1},{1,0},{2,3},{3,2},{4,5},{5,4},{6,7},{7,6},{8,9},{9,8},{10,11... | collective-permute-start | bytes 6291464 | tf_op jit(solution)/shard_map/ppermute | solution.py:41
  20.2 38.6 %collective-permute-start.11 = (bf16[512,512]{1,0:T(8,128)(2,1)S(1)}, bf16[512,512]{1,0:T(8,128)(2,1)}, u32[]{:S(2)}, u32[]{:S(2)}) collective-permute-start(bf16[512,512]{1,0:T(8,128)(2,1)S(1)} %collective-permute-done.4.refs_2_), channel_id=1, source_target_pairs={{0,1},{1,0},{2,3},{3,2},{4,5},{5,4},{6,7},{7,6},{8,9},{9,8},{10,11... | collective-permute-start | bytes 1572872 | tf_op jit(solution)/shard_map/ppermute | solution.py:41
  27.9 31.0 %collective-permute-start.12 = (bf16[512,512]{1,0:T(8,128)(2,1)S(1)}, bf16[512,512]{1,0:T(8,128)(2,1)}, u32[]{:S(2)}, u32[]{:S(2)}) collective-permute-start(bf16[512,512]{1,0:T(8,128)(2,1)S(1)} %collective-permute-done.6.refs_4_), channel_id=1, source_target_pairs={{0,1},{1,0},{2,3},{3,2},{4,5},{5,4},{6,7},{7,6},{8,9},{9,8},{10,11... | collective-permute-start | bytes 1572872 | tf_op jit(solution)/shard_map/ppermute | solution.py:41
  28.0 30.8 %copy-start.3 = (bf16[512,512]{1,0:T(8,128)(2,1)S(1)}, bf16[512,512]{1,0:T(8,128)(2,1)}, u32[]{:S(2)}) copy-start(bf16[512,512]{1,0:T(8,128)(2,1)} %refs_0_.1) | copy-start | bytes 1572868
  28.1 30.2 %collective-permute-start.5 = (bf16[256,512]{1,0:T(8,128)(2,1)S(1)}, bf16[256,512]{1,0:T(8,128)(2,1)S(1)}, u32[]{:S(2)}, u32[]{:S(2)}) collective-permute-start(bf16[256,512]{1,0:T(8,128)(2,1)S(1)} %slice.40), channel_id=1, source_target_pairs={{0,2},{1,3},{2,4},{3,5},{4,6},{5,7},{6,0},{7,1},{8,10},{9,11},{10,... | collective-permute-start | bytes 786440 | tf_op jit(solution)/shard_map/ppermute | solution.py:37
  29.3 29.3 %collective-permute-start.7 = (bf16[256,512]{1,0:T(8,128)(2,1)S(1)}, bf16[256,512]{1,0:T(8,128)(2,1)S(1)}, u32[]{:S(2)}, u32[]{:S(2)}) collective-permute-start(bf16[256,512]{1,0:T(8,128)(2,1)S(1)} %slice.41), channel_id=1, source_target_pairs={{0,6},{1,7},{2,0},{3,1},{4,2},{5,3},{6,4},{7,5},{8,14},{9,15},{10,... | collective-permute-start | bytes 786440 | tf_op jit(solution)/shard_map/ppermute | solution.py:37
  52.5 0.9 copy-start.5
  53.4 1.6 %copy-start.10 = (bf16[1024,1024]{1,0:T(8,128)(2,1)S(1)}, bf16[1024,1024]{1,0:T(8,128)(2,1)}, u32[]{:S(2)}) copy-start(bf16[1024,1024]{1,0:T(8,128)(2,1)} %constant.114.clone.refs_4_) | copy-start | bytes 6291460
  57.3 1.0 copy-start.13
  58.3 14.8 %collective-permute-start.8 = (bf16[256,512]{1,0:T(8,128)(2,1)S(1)}, bf16[256,512]{1,0:T(8,128)(2,1)S(1)}, u32[]{:S(2)}, u32[]{:S(2)}) collective-permute-start(bf16[256,512]{1,0:T(8,128)(2,1)S(1)} %collective-permute-done.5.refs_0_), channel_id=1, source_target_pairs={{0,1},{1,0},{2,3},{3,2},{4,5},{5,4},{6,7},{7,6},{8,9},{9,8},{10,11... | collective-permute-start | bytes 786440 | tf_op jit(solution)/shard_map/ppermute | solution.py:41
  58.6 14.5 %collective-permute-start.9 = (bf16[256,512]{1,0:T(8,128)(2,1)S(1)}, bf16[256,512]{1,0:T(8,128)(2,1)S(1)}, u32[]{:S(2)}, u32[]{:S(2)}) collective-permute-start(bf16[256,512]{1,0:T(8,128)(2,1)S(1)} %collective-permute-done.7.refs_1_), channel_id=1, source_target_pairs={{0,1},{1,0},{2,3},{3,2},{4,5},{5,4},{6,7},{7,6},{8,9},{9,8},{10,11... | collective-permute-start | bytes 786440 | tf_op jit(solution)/shard_map/ppermute | solution.py:41
  58.8 4.6 %copy-start.2 = (bf16[4096,3,512]{2,0,1:T(8,128)(2,1)S(1)}, bf16[4096,3,512]{2,0,1:T(8,128)(2,1)}, u32[]{:S(2)}) copy-start(bf16[4096,3,512]{2,0,1:T(8,128)(2,1)} %param.9) | copy-start | bytes 37748740
  77.3 6.1 %collective-permute-start.13 = (bf16[512,128]{1,0:T(8,128)(2,1)S(1)}, bf16[512,128]{1,0:T(8,128)(2,1)S(1)}, u32[]{:S(2)}, u32[]{:S(2)}) collective-permute-start(bf16[512,128]{1,0:T(8,128)(2,1)S(1)} %get-tuple-element.59), channel_id=1, source_target_pairs={{0,8},{8,0},{16,24},{24,16},{1,9},{9,1},{17,25},{25,17},{2,10},{10... | collective-permute-start | bytes 393224 | tf_op jit(solution)/shard_map/ppermute | solution.py:377
  78.8 8.3 %collective-permute-start.14 = (bf16[512,128]{1,0:T(8,128)(2,1)S(1)}, bf16[512,128]{1,0:T(8,128)(2,1)S(1)}, u32[]{:S(2)}, u32[]{:S(2)}) collective-permute-start(bf16[512,128]{1,0:T(8,128)(2,1)S(1)} %get-tuple-element.58), channel_id=1, source_target_pairs={{0,16},{8,24},{16,0},{24,8},{1,17},{9,25},{17,1},{25,9},{2,18},{10... | collective-permute-start | bytes 393224 | tf_op jit(solution)/shard_map/ppermute | solution.py:377
  80.4 6.8 %collective-permute-start.15 = (bf16[512,128]{1,0:T(8,128)(2,1)S(1)}, bf16[512,128]{1,0:T(8,128)(2,1)S(1)}, u32[]{:S(2)}, u32[]{:S(2)}) collective-permute-start(bf16[512,128]{1,0:T(8,128)(2,1)S(1)} %get-tuple-element.57), channel_id=1, source_target_pairs={{0,24},{8,16},{16,8},{24,0},{1,25},{9,17},{17,9},{25,1},{2,26},{10... | collective-permute-start | bytes 393224 | tf_op jit(solution)/shard_map/ppermute | solution.py:377
  87.1 1.2 copy-start.11
  88.4 1.2 copy-start.12
  89.6 1.2 copy-start.14
  93.4 7.4 %copy-start.6 = (bf16[256,128]{1,0:T(8,128)(2,1)}, bf16[256,128]{1,0:T(8,128)(2,1)S(1)}, u32[]{:S(2)}) copy-start(bf16[256,128]{1,0:T(8,128)(2,1)S(1)} %get-tuple-element.44) | copy-start | bytes 196612
  93.4 7.4 %copy-start.8 = (bf16[256,128]{1,0:T(8,128)(2,1)}, bf16[256,128]{1,0:T(8,128)(2,1)S(1)}, u32[]{:S(2)}) copy-start(bf16[256,128]{1,0:T(8,128)(2,1)S(1)} %get-tuple-element.46) | copy-start | bytes 196612
  93.4 4.3 %collective-permute-start.16 = (bf16[256,128]{1,0:T(8,128)(2,1)S(1)}, bf16[256,128]{1,0:T(8,128)(2,1)S(1)}, u32[]{:S(2)}, u32[]{:S(2)}) collective-permute-start(bf16[256,128]{1,0:T(8,128)(2,1)S(1)} %get-tuple-element.32), channel_id=1, source_target_pairs={{0,8},{8,0},{16,24},{24,16},{1,9},{9,1},{17,25},{25,17},{2,10},{10... | collective-permute-start | bytes 196616 | tf_op jit(solution)/shard_map/ppermute | solution.py:377
  94.7 4.6 %collective-permute-start.17 = (bf16[256,128]{1,0:T(8,128)(2,1)S(1)}, bf16[256,128]{1,0:T(8,128)(2,1)S(1)}, u32[]{:S(2)}, u32[]{:S(2)}) collective-permute-start(bf16[256,128]{1,0:T(8,128)(2,1)S(1)} %get-tuple-element.33), channel_id=1, source_target_pairs={{0,16},{8,24},{16,0},{24,8},{1,17},{9,25},{17,1},{25,9},{2,18},{10... | collective-permute-start | bytes 196616 | tf_op jit(solution)/shard_map/ppermute | solution.py:377
  95.5 5.2 %collective-permute-start.18 = (bf16[256,128]{1,0:T(8,128)(2,1)S(1)}, bf16[256,128]{1,0:T(8,128)(2,1)S(1)}, u32[]{:S(2)}, u32[]{:S(2)}) collective-permute-start(bf16[256,128]{1,0:T(8,128)(2,1)S(1)} %get-tuple-element.34), channel_id=1, source_target_pairs={{0,24},{8,16},{16,8},{24,0},{1,25},{9,17},{17,9},{25,1},{2,26},{10... | collective-permute-start | bytes 196616 | tf_op jit(solution)/shard_map/ppermute | solution.py:377
  100.8 1.6 %collective-permute-start.19 = (bf16[256,512]{1,0:T(8,128)(2,1)S(1)}, bf16[256,512]{1,0:T(8,128)(2,1)S(1)}, u32[]{:S(2)}, u32[]{:S(2)}) collective-permute-start(bf16[256,512]{1,0:T(8,128)(2,1)S(1)} %gate_blocks.2.a_ref), channel_id=1, source_target_pairs={{0,1},{1,0},{2,3},{3,2},{4,5},{5,4},{6,7},{7,6},{8,9},{9,8},{10,11... | collective-permute-start | bytes 786440 | tf_op jit(solution)/shard_map/ppermute | solution.py:41
  102.4 2.2 %copy-start = (bf16[512,4096]{1,0:T(8,128)(2,1)S(1)}, bf16[512,4096]{1,0:T(8,128)(2,1)}, u32[]{:S(2)}) copy-start(bf16[512,4096]{1,0:T(8,128)(2,1)} %w_ref.7) | copy-start | bytes 12582916
  104.6 1.7 %copy-start.9 = (bf16[256,128]{1,0:T(8,128)(2,1)S(1)}, bf16[256,128]{1,0:T(8,128)(2,1)}, u32[]{:S(2)}) copy-start(bf16[256,128]{1,0:T(8,128)(2,1)} %copy-done.8) | copy-start | bytes 196612
  104.6 3.2 %copy-start.7 = (bf16[256,128]{1,0:T(8,128)(2,1)S(1)}, bf16[256,128]{1,0:T(8,128)(2,1)}, u32[]{:S(2)}) copy-start(bf16[256,128]{1,0:T(8,128)(2,1)} %copy-done.6) | copy-start | bytes 196612
  104.6 13.1 %copy-start.1 = (bf16[512,4096]{1,0:T(8,128)(2,1)S(1)}, bf16[512,4096]{1,0:T(8,128)(2,1)}, u32[]{:S(2)}) copy-start(bf16[512,4096]{1,0:T(8,128)(2,1)} %w_ref.7) | copy-start | bytes 12582916
  106.3 5.4 %collective-permute-start.26 = (bf16[256,128]{1,0:T(8,128)(2,1)S(1)}, bf16[256,128]{1,0:T(8,128)(2,1)S(1)}, u32[]{:S(2)}, u32[]{:S(2)}) collective-permute-start(bf16[256,128]{1,0:T(8,128)(2,1)S(1)} %copy-done.9), channel_id=1, source_target_pairs={{0,24},{8,16},{16,8},{24,0},{1,25},{9,17},{17,9},{25,1},{2,26},{10... | collective-permute-start | bytes 196616 | tf_op jit(solution)/shard_map/ppermute | solution.py:377
  107.8 5.0 %collective-permute-start.25 = (bf16[256,128]{1,0:T(8,128)(2,1)S(1)}, bf16[256,128]{1,0:T(8,128)(2,1)S(1)}, u32[]{:S(2)}, u32[]{:S(2)}) collective-permute-start(bf16[256,128]{1,0:T(8,128)(2,1)S(1)} %copy-done.7), channel_id=1, source_target_pairs={{0,16},{8,24},{16,0},{24,8},{1,17},{9,25},{17,1},{25,9},{2,18},{10... | collective-permute-start | bytes 196616 | tf_op jit(solution)/shard_map/ppermute | solution.py:377
  109.3 4.3 %collective-permute-start.24 = (bf16[256,128]{1,0:T(8,128)(2,1)S(1)}, bf16[256,128]{1,0:T(8,128)(2,1)S(1)}, u32[]{:S(2)}, u32[]{:S(2)}) collective-permute-start(bf16[256,128]{1,0:T(8,128)(2,1)S(1)} %get-tuple-element.42), channel_id=1, source_target_pairs={{0,8},{8,0},{16,24},{24,16},{1,9},{9,1},{17,25},{25,17},{2,10},{10... | collective-permute-start | bytes 196616 | tf_op jit(solution)/shard_map/ppermute | solution.py:377
  113.7 5.7 %collective-permute-start.27 = (bf16[256,512]{1,0:T(8,128)(2,1)S(1)}, bf16[256,512]{1,0:T(8,128)(2,1)S(1)}, u32[]{:S(2)}, u32[]{:S(2)}) collective-permute-start(bf16[256,512]{1,0:T(8,128)(2,1)S(1)} %gate_blocks.3.a_ref), channel_id=1, source_target_pairs={{0,1},{1,0},{2,3},{3,2},{4,5},{5,4},{6,7},{7,6},{8,9},{9,8},{10,11... | collective-permute-start | bytes 786440 | tf_op jit(solution)/shard_map/ppermute | solution.py:41
  113.8 11.0 %collective-permute-start.21 = (bf16[256,512]{1,0:T(8,128)(2,1)S(1)}, bf16[256,512]{1,0:T(8,128)(2,1)S(1)}, u32[]{:S(2)}, u32[]{:S(2)}) collective-permute-start(bf16[256,512]{1,0:T(8,128)(2,1)S(1)} %get-tuple-element.36), channel_id=1, source_target_pairs={{0,2},{1,3},{2,4},{3,5},{4,6},{5,7},{6,0},{7,1},{8,10},{9,11},{10,... | collective-permute-start | bytes 786440 | tf_op jit(solution)/shard_map/ppermute | solution.py:37
  113.9 22.3 %collective-permute-start.23 = (bf16[256,512]{1,0:T(8,128)(2,1)S(1)}, bf16[256,512]{1,0:T(8,128)(2,1)S(1)}, u32[]{:S(2)}, u32[]{:S(2)}) collective-permute-start(bf16[256,512]{1,0:T(8,128)(2,1)S(1)} %get-tuple-element.38), channel_id=1, source_target_pairs={{0,6},{1,7},{2,0},{3,1},{4,2},{5,3},{6,4},{7,5},{8,14},{9,15},{10,... | collective-permute-start | bytes 786440 | tf_op jit(solution)/shard_map/ppermute | solution.py:37
  121.1 12.7 %collective-permute-start.28 = (bf16[256,512]{1,0:T(8,128)(2,1)S(1)}, bf16[256,512]{1,0:T(8,128)(2,1)S(1)}, u32[]{:S(2)}, u32[]{:S(2)}) collective-permute-start(bf16[256,512]{1,0:T(8,128)(2,1)S(1)} %get-tuple-element.48), channel_id=1, source_target_pairs={{0,6},{1,7},{2,0},{3,1},{4,2},{5,3},{6,4},{7,5},{8,14},{9,15},{10,... | collective-permute-start | bytes 786440 | tf_op jit(solution)/shard_map/ppermute | solution.py:37
  124.8 16.9 %collective-permute-start.22 = (bf16[256,512]{1,0:T(8,128)(2,1)S(1)}, bf16[256,512]{1,0:T(8,128)(2,1)S(1)}, u32[]{:S(2)}, u32[]{:S(2)}) collective-permute-start(bf16[256,512]{1,0:T(8,128)(2,1)S(1)} %add_convert_fusion.3), channel_id=1, source_target_pairs={{0,2},{1,3},{2,4},{3,5},{4,6},{5,7},{6,0},{7,1},{8,10},{9,11},{10,... | collective-permute-start | bytes 786440 | tf_op jit(solution)/shard_map/ppermute | solution.py:37
  124.9 22.4 %collective-permute-start.30 = (bf16[256,512]{1,0:T(8,128)(2,1)S(1)}, bf16[256,512]{1,0:T(8,128)(2,1)S(1)}, u32[]{:S(2)}, u32[]{:S(2)}) collective-permute-start(bf16[256,512]{1,0:T(8,128)(2,1)S(1)} %get-tuple-element.50), channel_id=1, source_target_pairs={{0,2},{1,3},{2,4},{3,5},{4,6},{5,7},{6,0},{7,1},{8,10},{9,11},{10,... | collective-permute-start | bytes 786440 | tf_op jit(solution)/shard_map/ppermute | solution.py:37
  133.9 18.5 %collective-permute-start.29 = (bf16[256,512]{1,0:T(8,128)(2,1)S(1)}, bf16[256,512]{1,0:T(8,128)(2,1)S(1)}, u32[]{:S(2)}, u32[]{:S(2)}) collective-permute-start(bf16[256,512]{1,0:T(8,128)(2,1)S(1)} %add_convert_fusion.1), channel_id=1, source_target_pairs={{0,6},{1,7},{2,0},{3,1},{4,2},{5,3},{6,4},{7,5},{8,14},{9,15},{10,... | collective-permute-start | bytes 786440 | tf_op jit(solution)/shard_map/ppermute | solution.py:37

commit v4 on v3

--- a/solution.py
+++ b/solution.py
@@ -49,11 +49,15 @@
     return lax.optimization_barrier((x,) + others)[0]
 
 
+def in_hbm(x):
+    return pltpu.with_memory_space_constraint(x, pltpu.HBM)
+
+
 def whole(shape):
     return pl.BlockSpec(shape, lambda *_: (0,) * len(shape))
 
 
-def call(kernel, grid, prefetch, operands, in_specs, outs, out_specs, scratch, name, flops, moved):
+def call(kernel, grid, prefetch, operands, in_specs, outs, out_specs, scratch, name, micros=1):
     return pl.pallas_call(
         kernel,
         grid_spec=pltpu.PrefetchScalarGridSpec(
@@ -65,24 +69,26 @@
         ),
         out_shape=outs,
         compiler_params=pltpu.CompilerParams(vmem_limit_bytes=32 * MIB),
-        cost_estimate=pl.CostEstimate(flops=flops, bytes_accessed=moved, transcendentals=0),
+        cost_estimate=pl.CostEstimate(
+            flops=micros * 10**9, bytes_accessed=micros << 20, transcendentals=0
+        ),
         name=name,
     )(prefetch, *operands)
 
 
-def project(pairs, chip_ids, core, rim, w_in, conv_taps, groups, total=None, finish=False):
+def project(pairs, chip_ids, slots, core, rims, w_in, conv_taps, groups, total=None, finish=False):
     count = len(pairs)
     parts = [p for pair in pairs for block in pair for p in block]
     span = sum(p.shape[0] for p in pairs[0][0])
     width = parts[0].shape[1]
     streams, _, out_width = w_in.shape
-    rim_rows = rim.shape[0]
+    rim_rows = RIM
     rows = span + rim_rows
     split = out_width // groups % 128 == 0
     share = out_width // groups
     has_total = total is not None
 
-    def kernel(ids, w_ref, rim_ref, *refs):
+    def kernel(ids, w_ref, rim_own, rim_other, *refs):
         part_refs, refs = refs[: len(parts)], refs[len(parts) :]
         if has_total:
             total_ref, refs = refs[0], refs[1:]
@@ -102,13 +108,12 @@
 
             @pl.when((k == j) & (s == 0))
             def _():
-                for x, source, own in ((x_own, here[0], mine), (x_other, here[1], theirs)):
+                for x, source, rim in ((x_own, here[0], rim_own), (x_other, here[1], rim_other)):
                     row = 0
                     for ref in source:
                         x[row : row + ref.shape[0]] = ref[...]
                         row += ref.shape[0]
-                    first = pl.multiple_of(ids[j] * 2 * width + own, width)
-                    x[span:rows] = rim_ref[:, pl.ds(first, width)]
+                    x[span:rows] = rim[slots[j] * RIM : (slots[j] + 1) * RIM]
 
         part = dot(x_own[...], w_ref[0, pl.ds(mine, width)])
         part = part + dot(x_other[...], w_ref[0, pl.ds(theirs, width)])
@@ -148,8 +153,8 @@
                     in_ref[...] = gated
 
     in_specs = [pl.BlockSpec((1, 2 * width, out_width), lambda k, s, ids: (s, ids[k], 0))]
-    in_specs += [whole(rim.shape)] + [whole(p.shape) for p in parts]
-    operands = [w_in, rim] + parts
+    in_specs += [whole(r.shape) for r in rims] + [whole(p.shape) for p in parts]
+    operands = [in_hbm(w_in)] + list(rims) + parts
     if has_total:
         in_specs.append(whole(total.shape))
         operands.append(total)
@@ -176,8 +181,7 @@
         [whole(o.shape) for o in outs],
         scratch,
         "project",
-        4 * count * rows * width * streams * out_width,
-        count * 4 * width * streams * out_width,
+        20 if count > 1 else 4,
     )
 
 
@@ -219,32 +223,38 @@
         kernel,
         (1,),
         me[None],
-        list(pieces) + [forward],
+        list(pieces) + [in_hbm(forward)],
         [whole(p.shape) for p in pieces] + [whole(forward.shape)],
         jax.ShapeDtypeStruct(shape, BF16),
         whole(shape),
         [pltpu.VMEM(shape, BF16)],
         "taps_spectra",
-        2 * shape[0] * shape[0] * shape[1],
-        6 * shape[0] * shape[1],
+        2,
     )
 
 
 def long_filter(pieces, spectra_taps, forward_in, back, skip, me):
     groups = len(pieces)
     span, share = pieces[0].shape
-    half = span // 2
     cols = groups * share
     step = 16
 
     def kernel(at, *refs):
         ins, refs = refs[:groups], refs[groups:]
         taps_ref, forward_ref, back_ref, skip_ref = refs[:4]
-        outs, (signal, spectra, mixture, result) = refs[4 : 4 + 2 * groups], refs[4 + 2 * groups :]
+        outs, refs = refs[4 : 4 + groups], refs[4 + groups :]
+        signal, spectra, mixture, result, forward_own, back_own, ready = refs
+        tables = ((forward_ref, forward_own), (back_ref, back_own))
+        copies = [
+            pltpu.make_async_copy(far, near, ready.at[k]) for k, (far, near) in enumerate(tables)
+        ]
+        for copy in copies:
+            copy.start()
         for s in range(groups):
             j = pl.multiple_of(source(at[0], s, groups) * share, share)
             signal[:, pl.ds(j, share)] = ins[s][...]
-        spectra[...] = dot(forward_ref[...], signal[...]).astype(BF16)
+        copies[0].wait()
+        spectra[...] = dot(forward_own[...], signal[...]).astype(BF16)
 
         def mix(start, special):
             def read(ref, first, block):
@@ -278,22 +288,24 @@
         def _(c):
             mix(pl.multiple_of(c * step, step), False)
 
+        copies[1].wait()
         result[...] = (
-            dot(back_ref[...], mixture[...]) + skip_ref[...] * signal[...].astype(F32)
+            dot(back_own[...], mixture[...]) + skip_ref[...] * signal[...].astype(F32)
         ).astype(BF16)
         for s in range(groups):
             j = pl.multiple_of(partner(at[0], s, groups) * share, share)
-            outs[2 * s][...] = result[0:half, pl.ds(j, share)]
-            outs[2 * s + 1][...] = result[half:span, pl.ds(j, share)]
-
-    operands = list(pieces) + [spectra_taps, forward_in, back, skip]
-    outs = [jax.ShapeDtypeStruct((half, share), BF16)] * (2 * groups)
-    found = call(
+            outs[s][...] = result[:, pl.ds(j, share)]
+
+    operands = list(pieces) + [spectra_taps, in_hbm(forward_in), in_hbm(back), skip]
+    in_specs = [whole(o.shape) for o in operands]
+    in_specs[groups + 1] = in_specs[groups + 2] = pl.BlockSpec(memory_space=pltpu.HBM)
+    outs = [jax.ShapeDtypeStruct((span, share), BF16)] * groups
+    return call(
         kernel,
         (1,),
         me[None],
         operands,
-        [whole(o.shape) for o in operands],
+        in_specs,
         outs,
         [whole(o.shape) for o in outs],
         [
@@ -301,12 +313,13 @@
             pltpu.VMEM((2 * span, cols), BF16),
             pltpu.VMEM((2 * span, cols), BF16),
             pltpu.VMEM((span, cols), BF16),
+            pltpu.VMEM(forward_in.shape, BF16),
+            pltpu.VMEM(back.shape, BF16),
+            pltpu.SemaphoreType.DMA((2,)),
         ],
         "long_filter",
-        8 * span * span * cols,
-        12 * span * cols,
-    )
-    return [(found[2 * s], found[2 * s + 1]) for s in range(groups)]
+        3,
+    )
 
 
 def gate_blocks(gate, pieces, me):
@@ -329,12 +342,10 @@
         whole(gate.shape),
         [],
         "gate_blocks",
-        rows * share * groups,
-        6 * rows * share * groups,
-    )
-
-
-def output_shares(gated, other, w_own, w_other, chip_ids, core, kinds):
+    )
+
+
+def output_shares(gated, other, w_own, w_other, chip_ids, core, plan):
     count = len(chip_ids)
     rows, width = gated.shape
     cols = w_other.shape[1] * 2 // lax.axis_size("chan")
@@ -342,18 +353,26 @@
     def kernel(ids, a_ref, b_ref, w_ref, v_ref, *outs):
         k = pl.program_id(0)
         total = dot(a_ref[...], w_ref[...]) + dot(b_ref[...], v_ref[...])
+        at = 0
         for j in range(count):
+            here = outs[at : at + len(plan[j])]
+            at += len(plan[j])
 
             @pl.when(k == j)
             def _():
-                outs[j][...] = total.astype(kinds[j])
-
-    outs = [jax.ShapeDtypeStruct((rows, cols), kind) for kind in kinds]
+                for out, (first, last, kind) in zip(here, plan[j]):
+                    out[...] = total[first:last].astype(kind)
+
+    outs = [
+        jax.ShapeDtypeStruct((last - first, cols), kind)
+        for parts in plan
+        for first, last, kind in parts
+    ]
     return call(
         kernel,
         (count,),
         jnp.stack(list(chip_ids) + [core]).astype(jnp.int32),
-        [gated, other, w_own, w_other],
+        [gated, other, in_hbm(w_own), w_other],
         [
             whole(gated.shape),
             whole(other.shape),
@@ -364,8 +383,33 @@
         [whole(o.shape) for o in outs],
         [],
         "output_shares",
-        4 * count * rows * width * cols,
-        4 * count * width * cols,
+    )
+
+
+def add_up(own, extras):
+    span, cols = own.shape
+    half = span // 2
+    flat = [e for side in extras for e in side]
+
+    def kernel(_, own_ref, *refs):
+        at = 0
+        for k, side in enumerate(extras):
+            total = own_ref[k * half : (k + 1) * half]
+            for ref in refs[at : at + len(side)]:
+                total = total + ref[...].astype(F32)
+            at += len(side)
+            refs[-1][k * half : (k + 1) * half] = total.astype(BF16)
+
+    return call(
+        kernel,
+        (1,),
+        jnp.zeros((1,), jnp.int32),
+        [own] + flat,
+        [whole(own.shape)] + [whole(e.shape) for e in flat],
+        jax.ShapeDtypeStruct(own.shape, BF16),
+        whole(own.shape),
+        [],
+        "add_up",
     )
 
 
@@ -401,7 +445,6 @@
 def long_filter_plain(pieces, spectra_taps, forward_in, back, skip, me):
     groups = len(pieces)
     span, share = pieces[0].shape
-    half = span // 2
     signal = in_order(pieces, me)
     spectra = dot(forward_in, signal).astype(BF16)
     real_g, imag_g = spectra_taps[:span].astype(F32), spectra_taps[span:].astype(F32)
@@ -424,7 +467,7 @@
     found = []
     for s in range(groups):
         block = lax.dynamic_index_in_dim(result, partner(me, s, groups), 0, keepdims=False)
-        found.append((block[:half], block[half:]))
+        found.append(block)
     return found
 
 
@@ -438,6 +481,7 @@
     groups = lax.axis_size("ctx")
     me = lax.axis_index("ctx")
     chips = lax.axis_size("chan") // 2
+    reach = chips // 2
     place = lax.axis_index("chan")
     chip, core = place // 2, place % 2
     share = width // groups
@@ -445,98 +489,112 @@
     out_width = w_out.shape[1] // (2 * chips)
     forward_np, back_np = half_tables(span)
     forward, back = jnp.asarray(forward_np), jnp.asarray(back_np)
+    forward_in = jnp.asarray(np.ascontiguousarray(forward_np[:, :span]))
     w_streams = jnp.transpose(w_in, (1, 0, 2))
     short_taps = conv_taps.reshape(-1, width).astype(F32)
+
+    rim = shift(inputs[span - RIM :], "ctx", 1)
+    rim = jnp.where(me > 0, rim, jnp.zeros_like(rim))
+    rim = jnp.concatenate([rim] + [shift(rim, "chan", 2 * s) for s in range(1, chips)], 0)
+    rims = (rim, sibling(rim))
+
+    split_taps = [filter_taps[:, q * share : (q + 1) * share] for q in range(groups)]
+    split_taps = jnp.stack(split_taps)
+
+    def pick(stack):
+        return lambda s: lax.dynamic_index_in_dim(
+            stack, partner(me, s, groups), 0, keepdims=False
+        )
+
+    tap_blocks = exchange(pick(split_taps))
+
+    w_given = jnp.concatenate(
+        [
+            lax.dynamic_slice_in_dim(w_out, (2 * z + 1 - core) * out_width, out_width, 1)
+            for z in range(chips)
+        ],
+        1,
+    )
 
     found = [(0, [inputs])]
     up = down = inputs
     for d in range(1, chips // 2 + 1):
         if 2 * d < chips:
             up, down = shift(up, "chan", 2), shift(down, "chan", -2)
+            if d == 1:
+                up, down, rims, tap_blocks, w_given = lax.optimization_barrier(
+                    (up, down, rims, tap_blocks, w_given)
+                )
             found += [(d, [up]), (-d, [down])]
         else:
             far = [shift(up[:half], "chan", 2), shift(down[half:], "chan", -2)]
-            found.append((d, far))
-
-    rim = shift(inputs[span - RIM :], "ctx", 1)
-    rim = jnp.where(me > 0, rim, jnp.zeros_like(rim))
-    rim = lax.all_gather(rim, "chan", axis=1, tiled=True)
-
-    split_taps = [filter_taps[:, q * share : (q + 1) * share] for q in range(groups)]
-    split_taps = jnp.stack(split_taps)
-
-    def pick(stack):
-        return lambda s: lax.dynamic_index_in_dim(
-            stack, partner(me, s, groups), 0, keepdims=False
+    spectra_taps = (taps_spectra if aligned else taps_spectra_plain)(tap_blocks, forward, me)
+
+    def both(blocks):
+        return blocks, [sibling(b) for b in blocks]
+
+    def added(blocks, total=None):
+        return project(
+            [both(b) for _, b in blocks],
+            [(chip - d) % chips for d, _ in blocks],
+            [d % chips for d, _ in blocks],
+            core,
+            rims,
+            w_streams,
+            short_taps,
+            groups,
+            total,
+            total is not None,
         )
 
-    spectra_taps = (taps_spectra if aligned else taps_spectra_plain)(
-        exchange(pick(split_taps)), forward, me
-    )
-
-    w_other = sibling(
-        jnp.concatenate(
-            [
-                lax.dynamic_slice_in_dim(w_out, (2 * z + 1 - core) * out_width, out_width, 1)
-                for z in range(chips)
-            ],
-            1,
-        )
-    )
-
-    rim = after(rim, spectra_taps)
-    pairs = [(block, [sibling(p) for p in block]) for _, block in found]
-    ids = [(chip - d) % chips for d, _ in found]
-    (total,) = project(pairs[:-1], ids[:-1], core, rim, w_streams, short_taps, groups)
-    gate, gated = project(
-        pairs[-1:], ids[-1:], core, rim, w_streams, short_taps, groups, total, True
-    )
+    (total,) = added(found)
+    far = [after(f, total) for f in far]
+    gate, gated = added([(reach, far)], total)
     if not aligned:
         gated = jnp.stack(jnp.split(gated, groups, axis=1))
+
+    w_other = sibling(after(w_given, gated))
 
     skip = lax.dynamic_slice_in_dim(skip_gain, me * share, share, 0)
     skip = jnp.tile(skip, groups)[None]
     filtered = (long_filter if aligned else long_filter_plain)(
-        exchange(pick(gated)), spectra_taps, forward[:, :span], back, skip, me
-    )
-    gating = gate_blocks if aligned else gate_blocks_plain
-    gated_top = gating(gate[:half], exchange(lambda s: filtered[s][0]), me)
-
-    def sums(gated, lead):
-        other = sibling(gated)
-        reach = chips // 2
-        direct = [reach] + ([-lead * (reach - 1)] if reach > 1 else [])
-        carried = [lead * d for d in range(reach - 1, 0, -1)]
-        carried += [-lead * d for d in range(reach - 2, 0, -1)] + [0]
-
-        def shares(offsets, kind):
-            ids = [(chip + d) % chips for d in offsets]
-            found = output_shares(gated, other, w_out, w_other, ids, core, [kind] * len(ids))
-            return dict(zip(offsets, found))
-
-        sent = shares(direct, BF16)
-        kept = shares(carried, F32)
-        ahead = shift(sent[reach], "chan", 2 * lead)
-        behind = shift(sent[direct[1]], "chan", -2 * lead) if reach > 1 else None
-        return ahead, behind, kept, sent[reach]
-
-    def finish(state, lead):
-        ahead, behind, kept, _ = state
-        reach = chips // 2
-        for d in range(reach - 1, 0, -1):
-            ahead = shift((ahead.astype(F32) + kept[lead * d]).astype(BF16), "chan", 2 * lead)
-        for d in range(reach - 2, 0, -1):
-            behind = shift((behind.astype(F32) + kept[-lead * d]).astype(BF16), "chan", -2 * lead)
-        total = kept[0] + ahead.astype(F32)
-        if behind is not None:
-            total = total + behind.astype(F32)
-        return total.astype(BF16)
-
-    state_top = sums(gated_top, 1)
-    low = [after(f[1], state_top[3]) for f in filtered]
-    gated_low = gating(gate[half:], exchange(lambda s: low[s]), me)
-    state_low = sums(gated_low, -1)
-    return jnp.concatenate([finish(state_top, 1), finish(state_low, -1)], 0)
+        exchange(pick(gated)), spectra_taps, forward_in, back, skip, me
+    )
+    filtered = lax.optimization_barrier((list(filtered), w_other))[0]
+    gated_out = (gate_blocks if aligned else gate_blocks_plain)(
+        gate, exchange(lambda s: filtered[s]), me
+    )
+
+    other = sibling(gated_out)
+
+    def shares(offsets, plan):
+        ids = [(chip + d) % chips for d in offsets]
+        return output_shares(gated_out, other, w_out, w_other, ids, core, plan)
+
+    up_top, down_low = shares([reach], [[(0, half, BF16), (half, span, BF16)]])
+    offsets, plan = [], []
+    for d in range(reach - 1, 0, -1):
+        last = d == reach - 1
+        offsets += [d, -d]
+        plan.append([(0, half, F32), (half, span, BF16 if last else F32)])
+        plan.append([(0, half, BF16 if last else F32), (half, span, F32)])
+    kept = list(shares(offsets + [0], plan + [[(0, span, F32)]]))
+    up_top, down_low = shift(up_top, "chan", 2), shift(down_low, "chan", -2)
+    up_low = down_top = None
+
+    def step(carried, new, distance):
+        if carried is not None:
+            new = (carried.astype(F32) + new).astype(BF16)
+        return shift(new, "chan", distance)
+
+    for k in range(reach - 1):
+        ahead_top, ahead_low, behind_top, behind_low = kept[4 * k : 4 * k + 4]
+        up_low, down_top = step(up_low, ahead_low, 2), step(down_top, behind_top, -2)
+        up_top, down_low = step(up_top, ahead_top, 2), step(down_low, behind_low, -2)
+    extras = [[up_top], [down_low]]
+    if reach > 1:
+        extras = [[up_top, down_top], [up_low, down_low]]
+    return add_up(kept[-1], extras)
 
 
 def solution(mesh):

time: 154 us -> 148 us (0.961)
  blocking collectives: 20.5 us -> 0 us
  starting transfers between devices: 31.2 us -> 38.4 us
  local copies, waits for them, and re-layouts: 19.7 us -> 26.6 us
  Pallas kernels: 25.6 us -> 31.5 us
  waiting for transfers between devices: 52.8 us -> 47.5 us
    all_gather x1 -> x0, blocking collectives: 20.5 us -> none  [body(): rim = lax.all_gather(rim, 'chan', axis=1, tiled=True)]
    ppermute x11 -> x14, starting transfers between devices: 15.6 us -> 26.1 us  [shift(): lax.ppermute(x, axis, [(i, (i + distance) % size) for i in range(size)])]
    ppermute x12 -> x9, waiting for transfers between devices: 14.4 us -> 7.68 us  [send(): return lax.ppermute(piece(slot), 'ctx', route)]
    pallas_call x10 -> x8, Pallas kernels: 25.6 us -> 31.5 us  [call(): pl.pallas_call(kernel, grid_spec=pltpu.PrefetchScalarGridSpec(num_scalar_...]
    unnamed x32 -> x58, local copies, waits for them, and re-layouts: 14.6 us -> 20.4 us
    ppermute x12 -> x9, starting transfers between devices: 14.4 us -> 10.6 us  [send(): return lax.ppermute(piece(slot), 'ctx', route)]
    ppermute x8, waiting for transfers between devices: 1.44 us -> 3.45 us  [sibling(): lax.ppermute(x, 'chan', [(i, i ^ 1) for i in range(lax.axis_size('chan'))])]
    ppermute x11 -> x14, waiting for transfers between devices: 36.9 us -> 36.3 us  [shift(): lax.ppermute(x, axis, [(i, (i + distance) % size) for i in range(size)])]
  transfers between devices with their start and end apart: 31 -> 31, of which waited for: 17 -> 13; matrix products, arithmetic and copies ran while one was open for 5% -> 6% of each run, Pallas kernels for 16% -> 15%
where the time goes in v4:
time: 148 us; the launch traced here: 146 us
  waiting for transfers between devices  47.5 us (32%)
  starting transfers between devices  38.4 us (26%)
  Pallas kernels  31.5 us (21%)
  local copies, waits for them, and re-layouts  26.6 us (18%)
  other arithmetic  2.18 us (1%)
    ppermute x14, waiting for transfers between devices, shift(): lax.ppermute(x, axis, [(i, (i + distance) % size) for i in range(size)])  36.3 us
    pallas_call x8, Pallas kernels, call(): pl.pallas_call(kernel, grid_spec=pltpu.PrefetchScalarGridSpec(num_scalar_...  31.5 us
    ppermute x14, starting transfers between devices, shift(): lax.ppermute(x, axis, [(i, (i + distance) % size) for i in range(size)])  26.1 us
    unnamed x58, local copies, waits for them, and re-layouts  20.4 us
    ppermute x9, starting transfers between devices, send(): return lax.ppermute(piece(slot), 'ctx', route)  10.6 us
    ppermute x9, waiting for transfers between devices, send(): return lax.ppermute(piece(slot), 'ctx', route)  7.68 us
    ppermute x8, waiting for transfers between devices, sibling(): lax.ppermute(x, 'chan', [(i, i ^ 1) for i in range(lax.axis_size('chan'))])  3.45 us
  transfers between devices with their start and end apart: 31, of which 13 were waited for; matrix products, arithmetic and copies ran while one was open for 6% of the time, Pallas kernels for 15%

profile of v4, /device:TPU:0, one launch (start us, length us, event | category | flops | bytes accessed | tf_op | source)
XLA Modules:
  0.0 146.4 jit_solution(6206459130088826084)
XLA Ops:
  0.0 3.0 %collective-permute-start = (bf16[512,512]{1,0:T(8,128)(2,1)}, bf16[512,512]{1,0:T(8,128)(2,1)S(1)}, u32[]{:S(2)}, u32[]{:S(2)}) collective-permute-start(bf16[512,512]{1,0:T(8,128)(2,1)} %refs_0_.1), channel_id=1, source_target_pairs={{0,2},{1,3},{2,4},{3,5},{4,6},{5,7},{6,0},{7,1},{8,10},{9,11},{10,... | collective-permute-start | bytes 1572872 | tf_op jit(solution)/shard_map/ppermute | solution.py:37
  3.0 2.0 %collective-permute-start.1 = (bf16[512,512]{1,0:T(8,128)(2,1)}, bf16[512,512]{1,0:T(8,128)(2,1)S(1)}, u32[]{:S(2)}, u32[]{:S(2)}) collective-permute-start(bf16[512,512]{1,0:T(8,128)(2,1)} %refs_0_.1), channel_id=1, source_target_pairs={{0,6},{1,7},{2,0},{3,1},{4,2},{5,3},{6,4},{7,5},{8,14},{9,15},{10,... | collective-permute-start | bytes 1572872 | tf_op jit(solution)/shard_map/ppermute | solution.py:37
  5.1 0.8 slice.21
  5.8 1.7 %collective-permute-start.2 = (bf16[16,512]{1,0:T(8,128)(2,1)S(1)}, bf16[16,512]{1,0:T(8,128)(2,1)S(1)}, u32[]{:S(2)}, u32[]{:S(2)}) collective-permute-start(bf16[16,512]{1,0:T(8,128)(2,1)S(1)} %slice.21), channel_id=1, source_target_pairs={{0,8},{8,16},{16,24},{24,0},{1,9},{9,17},{17,25},{25,1},{2,10},{10... | collective-permute-start | bytes 49160 | tf_op jit(solution)/shard_map/ppermute | solution.py:37
  7.5 1.1 slice_bitcast_fusion.3
  8.8 1.7 %collective-permute-done.2 = bf16[16,512]{1,0:T(8,128)(2,1)S(1)} collective-permute-done((bf16[16,512]{1,0:T(8,128)(2,1)S(1)}, bf16[16,512]{1,0:T(8,128)(2,1)S(1)}, u32[]{:S(2)}, u32[]{:S(2)}) %collective-permute-start.2) | collective-permute-done | bytes 16416 | tf_op jit(solution)/shard_map/ppermute | solution.py:37
  10.5 2.6 %collective-permute-start.4 = (bf16[16,512]{1,0:T(8,128)(2,1)S(1)}, bf16[16,512]{1,0:T(8,128)(2,1)S(1)}, u32[]{:S(2)}, u32[]{:S(2)}) collective-permute-start(bf16[16,512]{1,0:T(8,128)(2,1)S(1)} %broadcast_select_fusion), channel_id=1, source_target_pairs={{0,4},{1,5},{2,6},{3,7},{4,0},{5,1},{6,2},{7,3},{8,12},{9,13},{10,... | collective-permute-start | bytes 49160 | tf_op jit(solution)/shard_map/ppermute | solution.py:37
  13.0 1.3 collective-permute-start.5
  14.4 0.7 dynamic-slice_bitcast_fusion.4
  15.1 14.2 %collective-permute-done.3 = bf16[16,512]{1,0:T(8,128)(2,1)S(1)} collective-permute-done((bf16[16,512]{1,0:T(8,128)(2,1)S(1)}, bf16[16,512]{1,0:T(8,128)(2,1)S(1)}, u32[]{:S(2)}, u32[]{:S(2)}) %collective-permute-start.3) | collective-permute-done | bytes 16416 | tf_op jit(solution)/shard_map/ppermute | solution.py:37
  29.3 1.5 %collective-permute-start.7 = (bf16[512,128]{1,0:T(8,128)(2,1)S(1)}, bf16[512,128]{1,0:T(8,128)(2,1)S(1)}, u32[]{:S(2)}, u32[]{:S(2)}) collective-permute-start(bf16[512,128]{1,0:T(8,128)(2,1)S(1)} %get-tuple-element.73), channel_id=1, source_target_pairs={{0,8},{8,0},{16,24},{24,16},{1,9},{9,1},{17,25},{25,17},{2,10},{10... | collective-permute-start | bytes 393224 | tf_op jit(solution)/shard_map/ppermute | solution.py:421
  30.8 1.5 %collective-permute-start.8 = (bf16[512,128]{1,0:T(8,128)(2,1)S(1)}, bf16[512,128]{1,0:T(8,128)(2,1)S(1)}, u32[]{:S(2)}, u32[]{:S(2)}) collective-permute-start(bf16[512,128]{1,0:T(8,128)(2,1)S(1)} %get-tuple-element.72), channel_id=1, source_target_pairs={{0,16},{8,24},{16,0},{24,8},{1,17},{9,25},{17,1},{25,9},{2,18},{10... | collective-permute-start | bytes 393224 | tf_op jit(solution)/shard_map/ppermute | solution.py:421
  32.4 0.6 copy-done.1
  33.0 1.7 %constant_dynamic-slice_fusion.3 = (bf16[512,512]{1,0:T(8,128)(2,1)S(1)}, bf16[512,512]{1,0:T(8,128)(2,1)S(1)}, bf16[512,512]{1,0:T(8,128)(2,1)S(1)}, bf16[512,512]{1,0:T(8,128)(2,1)S(1)}) fusion(bf16[512,4096]{1,0:T(8,128)(2,1)} %w_ref.3, s32[]{:T(128)S(6)} %select_n.89, s32[]{:T(128)S(6)} %select_n.92, s32[]{:T(128)S(6)} %select_n.91, s32[]{:T(128)S(6)} %select_n.90), kind=kLoop, calls=%fused_computation.21 | loop fusion | bytes 4194320 | tf_op jit(solution)/shard_map/dynamic_slice | solution.py:513
  34.7 0.6 copy-done.9
  35.8 1.6 %pad_maximum_fusion = bf16[512,2048]{1,0:T(8,128)(2,1)} fusion(bf16[512,512]{1,0:T(8,128)(2,1)S(1)} %get-tuple-element.64, bf16[512,512]{1,0:T(8,128)(2,1)S(1)} %get-tuple-element.65, bf16[512,512]{1,0:T(8,128)(2,1)S(1)} %get-tuple-element.66, bf16[512,512]{1,0:T(8,128)(2,1)S(1)} %get-tuple-element.63), kind=kLoop, calls=%fused_computation | loop fusion | flops 8388608 | bytes 4194304 | tf_op jit(solution)/shard_map/concatenate | solution.py:511
  37.4 0.6 copy-done.22
  38.3 0.7 copy-done.24
  38.9 3.1 %collective-permute-done.9.refs_3_ = bf16[512,128]{1,0:T(8,128)(2,1)S(1)} collective-permute-done((bf16[512,128]{1,0:T(8,128)(2,1)S(1)}, bf16[512,128]{1,0:T(8,128)(2,1)S(1)}, u32[]{:S(2)}, u32[]{:S(2)}) %collective-permute-start.9) | collective-permute-done | bytes 131104 | tf_op jit(solution)/shard_map/ppermute | solution.py:421
  42.1 0.7 copy-done.26
  43.5 1.7 %collective-permute-start.14 = (bf16[256,512]{1,0:T(8,128)(2,1)S(1)}, bf16[256,512]{1,0:T(8,128)(2,1)S(1)}, u32[]{:S(2)}, u32[]{:S(2)}) collective-permute-start(bf16[256,512]{1,0:T(8,128)(2,1)S(1)} %slice.27), channel_id=1, source_target_pairs={{0,6},{1,7},{2,0},{3,1},{4,2},{5,3},{6,4},{7,5},{8,14},{9,15},{10,... | collective-permute-start | bytes 786440 | tf_op jit(solution)/shard_map/ppermute | solution.py:37
  45.6 0.8 copy-done.14
  46.3 0.8 copy-done.16
  47.2 0.8 copy-done.18
  48.0 0.8 copy-done.2
  48.8 1.0 copy-done.5
  49.9 1.0 copy-done.7
  50.9 0.8 copy-done.10
  51.7 1.0 copy-done.13
  52.8 1.0 copy-done.15
  53.8 1.0 copy-done.17
  54.9 1.0 copy-done.19
  55.9 11.0 %project.2.refs_4_ = f32[3,528,512]{2,1,0:T(8,128)S(1)} custom-call(s32[4]{0:T(128)S(1)} %add_add_fusion.1.ids, bf16[3,4096,512]{2,1,0:T(8,128)(2,1)} %bitcast.34, bf16[64,512]{1,0:T(8,128)(2,1)S(1)} %copy-done.2, bf16[64,512]{1,0:T(8,128)(2,1)S(1)} %copy-done.10, bf16[512,512]{1,0:T(8,128)(2,1)S(1)} %copy-done.13, bf16[512,512]{1,0:T(8,128)(2,1)S(1)} %copy-done.15, ...), custom_call_target="tpu_custom_call" | custom-call | flops 20000000000 | bytes 20971520 | tf_op jit(solution)/shard_map/project/pallas_call | solution.py:61
  67.6 1.1 collective-permute-done.16.refs_3_
  69.3 0.8 copy-done.3
  70.1 0.8 copy-done.11
  71.0 6.0 %project.3 = (bf16[512,512]{1,0:T(8,128)(2,1)S(1)}, bf16[4,512,128]{2,1,0:T(8,128)(2,1)S(1)}) custom-call(s32[2]{0:T(128)S(1)} %pad_add_fusion.ids, bf16[3,4096,512]{2,1,0:T(8,128)(2,1)} %bitcast.35, bf16[64,512]{1,0:T(8,128)(2,1)S(1)} %copy-done.3, bf16[64,512]{1,0:T(8,128)(2,1)S(1)} %copy-done.11, bf16[256,512]{1,0:T(8,128)(2,1)} %collective-permute-done.10.refs_0_, ...), custom_call_target="tpu_custom_call" | custom-call | flops 4000000000 | bytes 4194304 | tf_op jit(solution)/shard_map/project/pallas_call | solution.py:61
  77.0 0.8 copy-done
  77.8 0.8 copy-done.20
  78.7 0.8 dynamic_slice.52
  79.4 1.1 dynamic-slice_bitcast_fusion
  80.6 0.6 collective-permute-start.17
  81.7 2.4 %collective-permute-start.19 = (bf16[512,128]{1,0:T(8,128)(2,1)S(1)}, bf16[512,128]{1,0:T(8,128)(2,1)S(1)}, u32[]{:S(2)}, u32[]{:S(2)}) collective-permute-start(bf16[512,128]{1,0:T(8,128)(2,1)S(1)} %get-tuple-element.67), channel_id=1, source_target_pairs={{0,24},{8,16},{16,8},{24,0},{1,25},{9,17},{17,9},{25,1},{2,26},{10... | collective-permute-start | bytes 393224 | tf_op jit(solution)/shard_map/ppermute | solution.py:421
  84.2 0.9 copy-done.8
  85.1 0.9 copy-done.23
  86.0 0.9 copy-done.25
  86.9 0.9 copy-done.27
  87.8 3.0 %taps_spectra.1.refs_4_ = bf16[1024,512]{1,0:T(8,128)(2,1)S(1)} custom-call(s32[1]{0:T(128)} %bitcast.4.at, bf16[512,128]{1,0:T(8,128)(2,1)S(1)} %copy-done.8, bf16[512,128]{1,0:T(8,128)(2,1)S(1)} %copy-done.23, bf16[512,128]{1,0:T(8,128)(2,1)S(1)} %copy-done.25, bf16[512,128]{1,0:T(8,128)(2,1)S(1)} %copy-done.27, bf16[1024,1024]{1,0:T(8,128)(2,1)} %constant.110.clone.refs_4_), custom_call_target="tpu_custom_call" | custom-call | flops 2000000000 | bytes 2097152 | tf_op jit(solution)/shard_map/taps_spectra/pallas_call | solution.py:61
  90.8 3.8 %long_filter.1 = (bf16[512,128]{1,0:T(8,128)(2,1)S(1)}, bf16[512,128]{1,0:T(8,128)(2,1)S(1)}, bf16[512,128]{1,0:T(8,128)(2,1)S(1)}, bf16[512,128]{1,0:T(8,128)(2,1)S(1)}) custom-call(s32[1]{0:T(128)} %bitcast.4.at, bf16[512,128]{1,0:T(8,128)(2,1)S(1)} %get-tuple-element.70.refs_0_, bf16[512,128]{1,0:T(8,128)(2,1)S(1)} %collective-permute-done.17.refs_1_, ...), custom_call_target="tpu_custom_call" | custom-call | flops 3000000000 | bytes 3145728 | tf_op jit(solution)/shard_map/long_filter/pallas_call | solution.py:61
  95.8 2.4 %collective-permute-start.23 = (bf16[512,128]{1,0:T(8,128)(2,1)S(1)}, bf16[512,128]{1,0:T(8,128)(2,1)S(1)}, u32[]{:S(2)}, u32[]{:S(2)}) collective-permute-start(bf16[512,128]{1,0:T(8,128)(2,1)S(1)} %get-tuple-element.55), channel_id=1, source_target_pairs={{0,24},{8,16},{16,8},{24,0},{1,25},{9,17},{17,9},{25,1},{2,26},{10... | collective-permute-start | bytes 393224 | tf_op jit(solution)/shard_map/ppermute | solution.py:421
  98.2 2.9 %collective-permute-done.21.refs_1_ = bf16[512,128]{1,0:T(8,128)(2,1)S(1)} collective-permute-done((bf16[512,128]{1,0:T(8,128)(2,1)S(1)}, bf16[512,128]{1,0:T(8,128)(2,1)S(1)}, u32[]{:S(2)}, u32[]{:S(2)}) %collective-permute-start.21) | collective-permute-done | bytes 131104 | tf_op jit(solution)/shard_map/ppermute | solution.py:421
  101.1 1.6 %collective-permute-done.22.refs_2_ = bf16[512,128]{1,0:T(8,128)(2,1)S(1)} collective-permute-done((bf16[512,128]{1,0:T(8,128)(2,1)S(1)}, bf16[512,128]{1,0:T(8,128)(2,1)S(1)}, u32[]{:S(2)}, u32[]{:S(2)}) %collective-permute-start.22) | collective-permute-done | bytes 131104 | tf_op jit(solution)/shard_map/ppermute | solution.py:421
  103.1 1.8 %collective-permute-done.24.b_ref = bf16[512,512]{1,0:T(8,128)(2,1)S(1)} collective-permute-done((bf16[512,512]{1,0:T(8,128)(2,1)S(1)}, bf16[512,512]{1,0:T(8,128)(2,1)S(1)}, u32[]{:S(2)}, u32[]{:S(2)}) %collective-permute-start.24) | collective-permute-done | bytes 524320 | tf_op jit(solution)/shard_map/ppermute | solution.py:41
  104.9 2.3 %output_shares.3 = (bf16[256,512]{1,0:T(8,128)(2,1)S(1)}, bf16[256,512]{1,0:T(8,128)(2,1)S(1)}) custom-call(s32[2]{0:T(128)S(1)} %pad_add_fusion.1.ids, bf16[512,512]{1,0:T(8,128)(2,1)S(1)} %gate_blocks.1.a_ref, bf16[512,512]{1,0:T(8,128)(2,1)S(1)} %collective-permute-done.24.b_ref, bf16[512,4096]{1,0:T(8,128)(2,1)} %w_ref.3, ...), custom_call_target="tpu_custom_call" | custom-call | flops 1000000000 | bytes 1048576 | tf_op jit(solution)/shard_map/output_shares/pallas_call | solution.py:61
  107.2 3.5 %collective-permute-start.29 = (bf16[256,512]{1,0:T(8,128)(2,1)S(1)}, bf16[256,512]{1,0:T(8,128)(2,1)S(1)}, u32[]{:S(2)}, u32[]{:S(2)}) collective-permute-start(bf16[256,512]{1,0:T(8,128)(2,1)S(1)} %get-tuple-element.61), channel_id=1, source_target_pairs={{0,6},{1,7},{2,0},{3,1},{4,2},{5,3},{6,4},{7,5},{8,14},{9,15},{10,... | collective-permute-start | bytes 786440 | tf_op jit(solution)/shard_map/ppermute | solution.py:37
  110.8 4.2 %output_shares.2 = (f32[256,512]{1,0:T(8,128)S(1)}, bf16[256,512]{1,0:T(8,128)(2,1)S(1)}, bf16[256,512]{1,0:T(8,128)(2,1)S(1)}, f32[256,512]{1,0:T(8,128)S(1)}, f32[512,512]{1,0:T(8,128)S(1)}) custom-call(s32[4]{0:T(128)S(1)} %add_add_fusion.ids, bf16[512,512]{1,0:T(8,128)(2,1)S(1)} %gate_blocks.1.a_ref, bf16[512,512]{1,0:T(8,128)(2,1)S(1)} %collective-permute-done.24.b_ref, ...), custom_call_target="tpu_custom_call" | custom-call | flops 1000000000 | bytes 1048576 | tf_op jit(solution)/shard_map/output_shares/pallas_call | solution.py:61
  115.0 3.9 %collective-permute-start.27 = (bf16[256,512]{1,0:T(8,128)(2,1)S(1)}, bf16[256,512]{1,0:T(8,128)(2,1)S(1)}, u32[]{:S(2)}, u32[]{:S(2)}) collective-permute-start(bf16[256,512]{1,0:T(8,128)(2,1)S(1)} %get-tuple-element.59), channel_id=1, source_target_pairs={{0,6},{1,7},{2,0},{3,1},{4,2},{5,3},{6,4},{7,5},{8,14},{9,15},{10,... | collective-permute-start | bytes 786440 | tf_op jit(solution)/shard_map/ppermute | solution.py:37
  119.0 3.9 %collective-permute-start.30 = (bf16[256,512]{1,0:T(8,128)(2,1)S(1)}, bf16[256,512]{1,0:T(8,128)(2,1)S(1)}, u32[]{:S(2)}, u32[]{:S(2)}) collective-permute-start(bf16[256,512]{1,0:T(8,128)(2,1)S(1)} %add_convert_fusion), channel_id=1, source_target_pairs={{0,6},{1,7},{2,0},{3,1},{4,2},{5,3},{6,4},{7,5},{8,14},{9,15},{10,... | collective-permute-start | bytes 786440 | tf_op jit(solution)/shard_map/ppermute | solution.py:37
  123.5 2.1 %collective-permute-start.26 = (bf16[256,512]{1,0:T(8,128)(2,1)S(1)}, bf16[256,512]{1,0:T(8,128)(2,1)S(1)}, u32[]{:S(2)}, u32[]{:S(2)}) collective-permute-start(bf16[256,512]{1,0:T(8,128)(2,1)S(1)} %add_convert_fusion.1), channel_id=1, source_target_pairs={{0,2},{1,3},{2,4},{3,5},{4,6},{5,7},{6,0},{7,1},{8,10},{9,11},{10,... | collective-permute-start | bytes 786440 | tf_op jit(solution)/shard_map/ppermute | solution.py:37
  125.6 3.6 %collective-permute-done.27.refs_1_ = bf16[256,512]{1,0:T(8,128)(2,1)S(1)} collective-permute-done((bf16[256,512]{1,0:T(8,128)(2,1)S(1)}, bf16[256,512]{1,0:T(8,128)(2,1)S(1)}, u32[]{:S(2)}, u32[]{:S(2)}) %collective-permute-start.27) | collective-permute-done | bytes 262176 | tf_op jit(solution)/shard_map/ppermute | solution.py:37
  129.2 5.5 %collective-permute-done.28.refs_2_ = bf16[256,512]{1,0:T(8,128)(2,1)S(1)} collective-permute-done((bf16[256,512]{1,0:T(8,128)(2,1)S(1)}, bf16[256,512]{1,0:T(8,128)(2,1)S(1)}, u32[]{:S(2)}, u32[]{:S(2)}) %collective-permute-start.28) | collective-permute-done | bytes 262176 | tf_op jit(solution)/shard_map/ppermute | solution.py:37
  134.7 5.2 %collective-permute-done.30.refs_3_ = bf16[256,512]{1,0:T(8,128)(2,1)S(1)} collective-permute-done((bf16[256,512]{1,0:T(8,128)(2,1)S(1)}, bf16[256,512]{1,0:T(8,128)(2,1)S(1)}, u32[]{:S(2)}, u32[]{:S(2)}) %collective-permute-start.30) | collective-permute-done | bytes 262176 | tf_op jit(solution)/shard_map/ppermute | solution.py:37
  140.0 5.5 %collective-permute-done.26.refs_0_ = bf16[256,512]{1,0:T(8,128)(2,1)S(1)} collective-permute-done((bf16[256,512]{1,0:T(8,128)(2,1)S(1)}, bf16[256,512]{1,0:T(8,128)(2,1)S(1)}, u32[]{:S(2)}, u32[]{:S(2)}) %collective-permute-start.26) | collective-permute-done | bytes 262176 | tf_op jit(solution)/shard_map/ppermute | solution.py:37
  145.5 1.0 add_up.1
  (84 shorter events, 6.2 us)
Async XLA Ops:
  0.0 42.7 %collective-permute-start = (bf16[512,512]{1,0:T(8,128)(2,1)}, bf16[512,512]{1,0:T(8,128)(2,1)S(1)}, u32[]{:S(2)}, u32[]{:S(2)}) collective-permute-start(bf16[512,512]{1,0:T(8,128)(2,1)} %refs_0_.1), channel_id=1, source_target_pairs={{0,2},{1,3},{2,4},{3,5},{4,6},{5,7},{6,0},{7,1},{8,10},{9,11},{10,... | collective-permute-start | bytes 1572872 | tf_op jit(solution)/shard_map/ppermute | solution.py:37
  3.0 39.7 %collective-permute-start.1 = (bf16[512,512]{1,0:T(8,128)(2,1)}, bf16[512,512]{1,0:T(8,128)(2,1)S(1)}, u32[]{:S(2)}, u32[]{:S(2)}) collective-permute-start(bf16[512,512]{1,0:T(8,128)(2,1)} %refs_0_.1), channel_id=1, source_target_pairs={{0,6},{1,7},{2,0},{3,1},{4,2},{5,3},{6,4},{7,5},{8,14},{9,15},{10,... | collective-permute-start | bytes 1572872 | tf_op jit(solution)/shard_map/ppermute | solution.py:37
  5.8 4.6 %collective-permute-start.2 = (bf16[16,512]{1,0:T(8,128)(2,1)S(1)}, bf16[16,512]{1,0:T(8,128)(2,1)S(1)}, u32[]{:S(2)}, u32[]{:S(2)}) collective-permute-start(bf16[16,512]{1,0:T(8,128)(2,1)S(1)} %slice.21), channel_id=1, source_target_pairs={{0,8},{8,16},{16,24},{24,0},{1,9},{9,17},{17,25},{25,1},{2,10},{10... | collective-permute-start | bytes 49160 | tf_op jit(solution)/shard_map/ppermute | solution.py:37
  10.5 18.8 %collective-permute-start.3 = (bf16[16,512]{1,0:T(8,128)(2,1)S(1)}, bf16[16,512]{1,0:T(8,128)(2,1)S(1)}, u32[]{:S(2)}, u32[]{:S(2)}) collective-permute-start(bf16[16,512]{1,0:T(8,128)(2,1)S(1)} %broadcast_select_fusion), channel_id=1, source_target_pairs={{0,2},{1,3},{2,4},{3,5},{4,6},{5,7},{6,0},{7,1},{8,10},{9,11},{10,... | collective-permute-start | bytes 49160 | tf_op jit(solution)/shard_map/ppermute | solution.py:37
  10.5 20.3 %collective-permute-start.4 = (bf16[16,512]{1,0:T(8,128)(2,1)S(1)}, bf16[16,512]{1,0:T(8,128)(2,1)S(1)}, u32[]{:S(2)}, u32[]{:S(2)}) collective-permute-start(bf16[16,512]{1,0:T(8,128)(2,1)S(1)} %broadcast_select_fusion), channel_id=1, source_target_pairs={{0,4},{1,5},{2,6},{3,7},{4,0},{5,1},{6,2},{7,3},{8,12},{9,13},{10,... | collective-permute-start | bytes 49160 | tf_op jit(solution)/shard_map/ppermute | solution.py:37
  13.0 19.2 %collective-permute-start.5 = (bf16[16,512]{1,0:T(8,128)(2,1)S(1)}, bf16[16,512]{1,0:T(8,128)(2,1)S(1)}, u32[]{:S(2)}, u32[]{:S(2)}) collective-permute-start(bf16[16,512]{1,0:T(8,128)(2,1)S(1)} %broadcast_select_fusion), channel_id=1, source_target_pairs={{0,6},{1,7},{2,0},{3,1},{4,2},{5,3},{6,4},{7,5},{8,14},{9,15},{10,... | collective-permute-start | bytes 49160 | tf_op jit(solution)/shard_map/ppermute | solution.py:37
  29.3 8.2 %collective-permute-start.7 = (bf16[512,128]{1,0:T(8,128)(2,1)S(1)}, bf16[512,128]{1,0:T(8,128)(2,1)S(1)}, u32[]{:S(2)}, u32[]{:S(2)}) collective-permute-start(bf16[512,128]{1,0:T(8,128)(2,1)S(1)} %get-tuple-element.73), channel_id=1, source_target_pairs={{0,8},{8,0},{16,24},{24,16},{1,9},{9,1},{17,25},{25,17},{2,10},{10... | collective-permute-start | bytes 393224 | tf_op jit(solution)/shard_map/ppermute | solution.py:421
  30.8 7.5 %collective-permute-start.8 = (bf16[512,128]{1,0:T(8,128)(2,1)S(1)}, bf16[512,128]{1,0:T(8,128)(2,1)S(1)}, u32[]{:S(2)}, u32[]{:S(2)}) collective-permute-start(bf16[512,128]{1,0:T(8,128)(2,1)S(1)} %get-tuple-element.72), channel_id=1, source_target_pairs={{0,16},{8,24},{16,0},{24,8},{1,17},{9,25},{17,1},{25,9},{2,18},{10... | collective-permute-start | bytes 393224 | tf_op jit(solution)/shard_map/ppermute | solution.py:421
  32.3 5.8 %copy-start.12 = (bf16[512,512]{1,0:T(8,128)(2,1)S(1)}, bf16[512,512]{1,0:T(8,128)(2,1)}, u32[]{:S(2)}) copy-start(bf16[512,512]{1,0:T(8,128)(2,1)} %refs_0_.1) | copy-start | bytes 1572868
  32.3 2.4 %collective-permute-start.6 = (bf16[64,512]{1,0:T(8,128)(2,1)S(1)}, bf16[64,512]{1,0:T(8,128)(2,1)S(1)}, u32[]{:S(2)}, u32[]{:S(2)}) collective-permute-start(bf16[64,512]{1,0:T(8,128)(2,1)S(1)} %pad_maximum_fusion.2.rim_own), channel_id=1, source_target_pairs={{0,1},{1,0},{2,3},{3,2},{4,5},{5,4},{6,7},{7,6},{8,9},{9,8},{10,11... | collective-permute-start | bytes 196616 | tf_op jit(solution)/shard_map/ppermute | solution.py:41
  32.4 0.6 copy-start.1
  34.7 0.6 copy-start.9
  35.3 6.8 %collective-permute-start.9 = (bf16[512,128]{1,0:T(8,128)(2,1)S(1)}, bf16[512,128]{1,0:T(8,128)(2,1)S(1)}, u32[]{:S(2)}, u32[]{:S(2)}) collective-permute-start(bf16[512,128]{1,0:T(8,128)(2,1)S(1)} %get-tuple-element.71), channel_id=1, source_target_pairs={{0,24},{8,16},{16,8},{24,0},{1,25},{9,17},{17,9},{25,1},{2,26},{10... | collective-permute-start | bytes 393224 | tf_op jit(solution)/shard_map/ppermute | solution.py:421
  37.4 0.7 copy-start.22
  38.1 7.5 %collective-permute-start.11 = (bf16[512,512]{1,0:T(8,128)(2,1)S(1)}, bf16[512,512]{1,0:T(8,128)(2,1)S(1)}, u32[]{:S(2)}, u32[]{:S(2)}) collective-permute-start(bf16[512,512]{1,0:T(8,128)(2,1)S(1)} %copy-done.12), channel_id=1, source_target_pairs={{0,1},{1,0},{2,3},{3,2},{4,5},{5,4},{6,7},{7,6},{8,9},{9,8},{10,11... | collective-permute-start | bytes 1572872 | tf_op jit(solution)/shard_map/ppermute | solution.py:41
  38.3 0.7 copy-start.24
  42.1 0.7 copy-start.26
  42.7 4.4 %copy-start.4 = (bf16[512,512]{1,0:T(8,128)(2,1)}, bf16[512,512]{1,0:T(8,128)(2,1)S(1)}, u32[]{:S(2)}) copy-start(bf16[512,512]{1,0:T(8,128)(2,1)S(1)} %collective-permute-done.refs_2_) | copy-start | bytes 1572868
  42.8 4.4 %copy-start.6 = (bf16[512,512]{1,0:T(8,128)(2,1)}, bf16[512,512]{1,0:T(8,128)(2,1)S(1)}, u32[]{:S(2)}) copy-start(bf16[512,512]{1,0:T(8,128)(2,1)S(1)} %collective-permute-done.1.refs_4_) | copy-start | bytes 1572868
  42.8 3.6 %collective-permute-start.12 = (bf16[512,512]{1,0:T(8,128)(2,1)S(1)}, bf16[512,512]{1,0:T(8,128)(2,1)S(1)}, u32[]{:S(2)}, u32[]{:S(2)}) collective-permute-start(bf16[512,512]{1,0:T(8,128)(2,1)S(1)} %collective-permute-done.refs_2_), channel_id=1, source_target_pairs={{0,1},{1,0},{2,3},{3,2},{4,5},{5,4},{6,7},{7,6},{8,9},{9,8},{10,11... | collective-permute-start | bytes 1572872 | tf_op jit(solution)/shard_map/ppermute | solution.py:41
  42.8 4.3 %collective-permute-start.13 = (bf16[512,512]{1,0:T(8,128)(2,1)S(1)}, bf16[512,512]{1,0:T(8,128)(2,1)S(1)}, u32[]{:S(2)}, u32[]{:S(2)}) collective-permute-start(bf16[512,512]{1,0:T(8,128)(2,1)S(1)} %collective-permute-done.1.refs_4_), channel_id=1, source_target_pairs={{0,1},{1,0},{2,3},{3,2},{4,5},{5,4},{6,7},{7,6},{8,9},{9,8},{10,11... | collective-permute-start | bytes 1572872 | tf_op jit(solution)/shard_map/ppermute | solution.py:41
  43.5 23.5 %collective-permute-start.14 = (bf16[256,512]{1,0:T(8,128)(2,1)S(1)}, bf16[256,512]{1,0:T(8,128)(2,1)S(1)}, u32[]{:S(2)}, u32[]{:S(2)}) collective-permute-start(bf16[256,512]{1,0:T(8,128)(2,1)S(1)} %slice.27), channel_id=1, source_target_pairs={{0,6},{1,7},{2,0},{3,1},{4,2},{5,3},{6,4},{7,5},{8,14},{9,15},{10,... | collective-permute-start | bytes 786440 | tf_op jit(solution)/shard_map/ppermute | solution.py:37
  45.1 21.9 %collective-permute-start.10 = (bf16[256,512]{1,0:T(8,128)(2,1)S(1)}, bf16[256,512]{1,0:T(8,128)(2,1)}, u32[]{:S(2)}, u32[]{:S(2)}) collective-permute-start(bf16[256,512]{1,0:T(8,128)(2,1)S(1)} %slice.26), channel_id=1, source_target_pairs={{0,2},{1,3},{2,4},{3,5},{4,6},{5,7},{6,0},{7,1},{8,10},{9,11},{10,... | collective-permute-start | bytes 786440 | tf_op jit(solution)/shard_map/ppermute | solution.py:37
  45.5 0.8 copy-start.14
  46.3 0.8 copy-start.16
  47.2 0.8 copy-start.18
  48.0 0.8 copy-start.2
  48.8 1.0 copy-start.5
  49.9 1.0 copy-start.7
  50.9 0.8 copy-start.10
  51.7 1.0 copy-start.13
  52.8 1.0 copy-start.15
  53.8 1.0 copy-start.17
  54.9 1.0 copy-start.19
  55.9 11.6 %copy-start.28 = (bf16[3,3,512]{2,1,0:T(4,128)(2,1)S(1)}, bf16[3,3,512]{2,1,0:T(4,128)(2,1)}, u32[]{:S(2)}) copy-start(bf16[3,3,512]{2,1,0:T(4,128)(2,1)} %param.11) | copy-start | bytes 27652
  67.0 1.7 %collective-permute-start.16 = (bf16[256,512]{1,0:T(8,128)(2,1)S(1)}, bf16[256,512]{1,0:T(8,128)(2,1)}, u32[]{:S(2)}, u32[]{:S(2)}) collective-permute-start(bf16[256,512]{1,0:T(8,128)(2,1)S(1)} %collective-permute-done.14.refs_1_), channel_id=1, source_target_pairs={{0,1},{1,0},{2,3},{3,2},{4,5},{5,4},{6,7},{7,6},{8,9},{9,8},{10,11... | collective-permute-start | bytes 786440 | tf_op jit(solution)/shard_map/ppermute | solution.py:41
  67.1 2.2 %collective-permute-start.15 = (bf16[256,512]{1,0:T(8,128)(2,1)}, bf16[256,512]{1,0:T(8,128)(2,1)}, u32[]{:S(2)}, u32[]{:S(2)}) collective-permute-start(bf16[256,512]{1,0:T(8,128)(2,1)} %collective-permute-done.10.refs_0_), channel_id=1, source_target_pairs={{0,1},{1,0},{2,3},{3,2},{4,5},{5,4},{6,7},{7,6},{8,9},{9,8},{10,11... | collective-permute-start | bytes 786440 | tf_op jit(solution)/shard_map/ppermute | solution.py:41
  69.3 0.8 copy-start.3
  70.1 0.8 copy-start.11
  77.0 0.8 copy-start
  77.8 0.8 copy-start.20
  78.6 16.1 %collective-permute-start.20 = (bf16[512,2048]{1,0:T(8,128)(2,1)}, bf16[512,2048]{1,0:T(8,128)(2,1)S(1)}, u32[]{:S(2)}, u32[]{:S(2)}) collective-permute-start(bf16[512,2048]{1,0:T(8,128)(2,1)} %pad_maximum_fusion), channel_id=1, source_target_pairs={{0,1},{1,0},{2,3},{3,2},{4,5},{5,4},{6,7},{7,6},{8,9},{9,8},{10,11... | collective-permute-start | bytes 6291464 | tf_op jit(solution)/shard_map/ppermute | solution.py:41
  80.6 10.2 %collective-permute-start.17 = (bf16[512,128]{1,0:T(8,128)(2,1)S(1)}, bf16[512,128]{1,0:T(8,128)(2,1)S(1)}, u32[]{:S(2)}, u32[]{:S(2)}) collective-permute-start(bf16[512,128]{1,0:T(8,128)(2,1)S(1)} %get-tuple-element.69), channel_id=1, source_target_pairs={{0,8},{8,0},{16,24},{24,16},{1,9},{9,1},{17,25},{25,17},{2,10},{10... | collective-permute-start | bytes 393224 | tf_op jit(solution)/shard_map/ppermute | solution.py:421
  81.2 9.6 %collective-permute-start.18 = (bf16[512,128]{1,0:T(8,128)(2,1)S(1)}, bf16[512,128]{1,0:T(8,128)(2,1)S(1)}, u32[]{:S(2)}, u32[]{:S(2)}) collective-permute-start(bf16[512,128]{1,0:T(8,128)(2,1)S(1)} %get-tuple-element.68), channel_id=1, source_target_pairs={{0,16},{8,24},{16,0},{24,8},{1,17},{9,25},{17,1},{25,9},{2,18},{10... | collective-permute-start | bytes 393224 | tf_op jit(solution)/shard_map/ppermute | solution.py:421
  81.7 9.1 %collective-permute-start.19 = (bf16[512,128]{1,0:T(8,128)(2,1)S(1)}, bf16[512,128]{1,0:T(8,128)(2,1)S(1)}, u32[]{:S(2)}, u32[]{:S(2)}) collective-permute-start(bf16[512,128]{1,0:T(8,128)(2,1)S(1)} %get-tuple-element.67), channel_id=1, source_target_pairs={{0,24},{8,16},{16,8},{24,0},{1,25},{9,17},{17,9},{25,1},{2,26},{10... | collective-permute-start | bytes 393224 | tf_op jit(solution)/shard_map/ppermute | solution.py:421
  84.1 0.9 copy-start.8
  85.1 0.9 copy-start.23
  86.0 0.9 copy-start.25
  86.9 0.9 copy-start.27
  90.8 12.0 %copy-start.21 = (bf16[512,512]{1,0:T(8,128)(2,1)S(1)}, bf16[512,512]{1,0:T(8,128)(2,1)}, u32[]{:S(2)}) copy-start(bf16[512,512]{1,0:T(8,128)(2,1)} %copy-done.20) | copy-start | bytes 1572868
  94.7 6.4 %collective-permute-start.21 = (bf16[512,128]{1,0:T(8,128)(2,1)S(1)}, bf16[512,128]{1,0:T(8,128)(2,1)S(1)}, u32[]{:S(2)}, u32[]{:S(2)}) collective-permute-start(bf16[512,128]{1,0:T(8,128)(2,1)S(1)} %get-tuple-element.53), channel_id=1, source_target_pairs={{0,8},{8,0},{16,24},{24,16},{1,9},{9,1},{17,25},{25,17},{2,10},{10... | collective-permute-start | bytes 393224 | tf_op jit(solution)/shard_map/ppermute | solution.py:421
  95.3 7.5 %collective-permute-start.22 = (bf16[512,128]{1,0:T(8,128)(2,1)S(1)}, bf16[512,128]{1,0:T(8,128)(2,1)S(1)}, u32[]{:S(2)}, u32[]{:S(2)}) collective-permute-start(bf16[512,128]{1,0:T(8,128)(2,1)S(1)} %get-tuple-element.54), channel_id=1, source_target_pairs={{0,16},{8,24},{16,0},{24,8},{1,17},{9,25},{17,1},{25,9},{2,18},{10... | collective-permute-start | bytes 393224 | tf_op jit(solution)/shard_map/ppermute | solution.py:421
  95.8 7.0 %collective-permute-start.23 = (bf16[512,128]{1,0:T(8,128)(2,1)S(1)}, bf16[512,128]{1,0:T(8,128)(2,1)S(1)}, u32[]{:S(2)}, u32[]{:S(2)}) collective-permute-start(bf16[512,128]{1,0:T(8,128)(2,1)S(1)} %get-tuple-element.55), channel_id=1, source_target_pairs={{0,24},{8,16},{16,8},{24,0},{1,25},{9,17},{17,9},{25,1},{2,26},{10... | collective-permute-start | bytes 393224 | tf_op jit(solution)/shard_map/ppermute | solution.py:421
  102.9 2.0 %collective-permute-start.24 = (bf16[512,512]{1,0:T(8,128)(2,1)S(1)}, bf16[512,512]{1,0:T(8,128)(2,1)S(1)}, u32[]{:S(2)}, u32[]{:S(2)}) collective-permute-start(bf16[512,512]{1,0:T(8,128)(2,1)S(1)} %gate_blocks.1.a_ref), channel_id=1, source_target_pairs={{0,1},{1,0},{2,3},{3,2},{4,5},{5,4},{6,7},{7,6},{8,9},{9,8},{10,11... | collective-permute-start | bytes 1572872 | tf_op jit(solution)/shard_map/ppermute | solution.py:41
  107.2 11.7 %collective-permute-start.29 = (bf16[256,512]{1,0:T(8,128)(2,1)S(1)}, bf16[256,512]{1,0:T(8,128)(2,1)S(1)}, u32[]{:S(2)}, u32[]{:S(2)}) collective-permute-start(bf16[256,512]{1,0:T(8,128)(2,1)S(1)} %get-tuple-element.61), channel_id=1, source_target_pairs={{0,6},{1,7},{2,0},{3,1},{4,2},{5,3},{6,4},{7,5},{8,14},{9,15},{10,... | collective-permute-start | bytes 786440 | tf_op jit(solution)/shard_map/ppermute | solution.py:37
  110.8 12.7 %collective-permute-start.25 = (bf16[256,512]{1,0:T(8,128)(2,1)S(1)}, bf16[256,512]{1,0:T(8,128)(2,1)S(1)}, u32[]{:S(2)}, u32[]{:S(2)}) collective-permute-start(bf16[256,512]{1,0:T(8,128)(2,1)S(1)} %get-tuple-element.57), channel_id=1, source_target_pairs={{0,2},{1,3},{2,4},{3,5},{4,6},{5,7},{6,0},{7,1},{8,10},{9,11},{10,... | collective-permute-start | bytes 786440 | tf_op jit(solution)/shard_map/ppermute | solution.py:37
  115.0 14.2 %collective-permute-start.27 = (bf16[256,512]{1,0:T(8,128)(2,1)S(1)}, bf16[256,512]{1,0:T(8,128)(2,1)S(1)}, u32[]{:S(2)}, u32[]{:S(2)}) collective-permute-start(bf16[256,512]{1,0:T(8,128)(2,1)S(1)} %get-tuple-element.59), channel_id=1, source_target_pairs={{0,6},{1,7},{2,0},{3,1},{4,2},{5,3},{6,4},{7,5},{8,14},{9,15},{10,... | collective-permute-start | bytes 786440 | tf_op jit(solution)/shard_map/ppermute | solution.py:37
  118.9 15.8 %collective-permute-start.28 = (bf16[256,512]{1,0:T(8,128)(2,1)S(1)}, bf16[256,512]{1,0:T(8,128)(2,1)S(1)}, u32[]{:S(2)}, u32[]{:S(2)}) collective-permute-start(bf16[256,512]{1,0:T(8,128)(2,1)S(1)} %get-tuple-element.60), channel_id=1, source_target_pairs={{0,2},{1,3},{2,4},{3,5},{4,6},{5,7},{6,0},{7,1},{8,10},{9,11},{10,... | collective-permute-start | bytes 786440 | tf_op jit(solution)/shard_map/ppermute | solution.py:37
  119.0 21.0 %collective-permute-start.30 = (bf16[256,512]{1,0:T(8,128)(2,1)S(1)}, bf16[256,512]{1,0:T(8,128)(2,1)S(1)}, u32[]{:S(2)}, u32[]{:S(2)}) collective-permute-start(bf16[256,512]{1,0:T(8,128)(2,1)S(1)} %add_convert_fusion), channel_id=1, source_target_pairs={{0,6},{1,7},{2,0},{3,1},{4,2},{5,3},{6,4},{7,5},{8,14},{9,15},{10,... | collective-permute-start | bytes 786440 | tf_op jit(solution)/shard_map/ppermute | solution.py:37
  123.5 22.0 %collective-permute-start.26 = (bf16[256,512]{1,0:T(8,128)(2,1)S(1)}, bf16[256,512]{1,0:T(8,128)(2,1)S(1)}, u32[]{:S(2)}, u32[]{:S(2)}) collective-permute-start(bf16[256,512]{1,0:T(8,128)(2,1)S(1)} %add_convert_fusion.1), channel_id=1, source_target_pairs={{0,2},{1,3},{2,4},{3,5},{4,6},{5,7},{6,0},{7,1},{8,10},{9,11},{10,... | collective-permute-start | bytes 786440 | tf_op jit(solution)/shard_map/ppermute | solution.py:37

commit v5 on v4

v5 whole, which is shorter than its diff:
```python
import math

import jax
import jax.numpy as jnp
import ml_dtypes
import numpy as np
from jax import lax
from jax.experimental import pallas as pl
from jax.experimental.pallas import tpu as pltpu
from jax.sharding import PartitionSpec as P

KERNEL = 3
EDGE = 16
BF16 = jnp.bfloat16
F32 = jnp.float32
MIB = 1 << 20


def half_tables(span):
    n = 2 * span
    f = np.arange(span)[:, None]
    m = np.arange(n)[None, :]
    ang = 2.0 * math.pi * ((f * m) % n) / n
    real = np.cos(ang)
    imag = -np.sin(ang)
    imag[0] = np.where(np.arange(n) % 2 == 0, 1.0, -1.0)
    forward = np.concatenate([real, imag], 0).astype(ml_dtypes.bfloat16)
    weight = np.full((n, 1), 2.0 / n)
    weight[0] = 1.0 / n
    weight[span] = 1.0 / n
    back = (np.concatenate([real, imag], 0) * weight)[:, :span].T
    return forward, np.ascontiguousarray(back).astype(ml_dtypes.bfloat16)


def shift(x, axis, distance):
    size = lax.axis_size(axis)
    return lax.ppermute(x, axis, [(i, (i + distance) % size) for i in range(size)])


def sibling(x):
    return lax.ppermute(x, "chan", [(i, i ^ 1) for i in range(lax.axis_size("chan"))])


def dot(a, b):
    return jnp.dot(a, b, preferred_element_type=F32)


def after(x, *others):
    return lax.optimization_barrier((x,) + others)[0]


def anywhere():
    return pl.BlockSpec(memory_space=pl.ANY)


def whole(shape):
    return pl.BlockSpec(shape, lambda *_: (0,) * len(shape))


def call(kernel, grid, prefetch, operands, in_specs, outs, out_specs, scratch, name, micros=1, vmem=16):
    return pl.pallas_call(
        kernel,
        grid_spec=pltpu.PrefetchScalarGridSpec(
            num_scalar_prefetch=1,
            grid=grid,
            in_specs=in_specs,
            out_specs=out_specs,
            scratch_shapes=scratch,
        ),
        out_shape=outs,
        compiler_params=pltpu.CompilerParams(vmem_limit_bytes=vmem * MIB),
        cost_estimate=pl.CostEstimate(
            flops=micros * 10**9, bytes_accessed=micros << 20, transcendentals=0
        ),
        name=name,
    )(prefetch, *operands)


def short_filter(taps, before, block):
    longer = jnp.concatenate([before, block], 0)
    rows = block.shape[0]
    result = jnp.zeros(block.shape, F32)
    for lag in range(KERNEL):
        result = result + taps[lag] * longer[8 - lag : 8 - lag + rows]
    return result.astype(BF16)


def ends(rows):
    return jnp.concatenate([rows[:8].astype(F32), rows[-8:].astype(F32)], 0).astype(BF16)


def first_rows(taps, before, here):
    return short_filter(taps, before[8:].astype(F32), here[:8].astype(F32))


def gated(gate_in, values):
    return (gate_in.astype(F32) * values.astype(F32)).astype(BF16)


def project(pairs, chip_ids, core, me, w_in, conv_taps, groups, total=None):
    count = len(pairs)
    parts = [p for pair in pairs for block in pair for p in block]
    rows = sum(p.shape[0] for p in pairs[0][0])
    width = parts[0].shape[1]
    streams, _, out_width = w_in.shape
    depth = 2 * width
    share = out_width // groups
    split = share % 128 == 0
    finish = total is not None

    def kernel(ids, w_ref, *refs):
        part_refs, refs = refs[: len(parts)], refs[len(parts) :]
        if finish:
            total_ref, taps_ref, gate_ref, ends_ref, refs = *refs[:4], refs[4:]
            in_refs, refs = refs[: len(outs) - 2], refs[len(outs) - 2 :]
            x, kept, sums, sums_ready = refs
        else:
            out_ref, x, w, w_ready = refs
        s = pl.program_id(0)

        def w_copy(t, j):
            first = pl.multiple_of(ids[j] * depth, depth)
            return pltpu.make_async_copy(
                w_ref.at[t, pl.ds(first, depth)],
                w.at[t, pl.ds(j * depth, depth)],
                w_ready.at[t, j],
            )

        def sum_copy(t):
            return pltpu.make_async_copy(total_ref.at[t], sums.at[t], sums_ready.at[t])

        @pl.when(s == 0)
        def _():
            for t in range(streams):
                if finish:
                    sum_copy(t).start()
                else:
                    for j in range(count):
                        w_copy(t, j).start()
            at = 0
            for j in range(count):
                for block, side in ((pairs[j][0], ids[count]), (pairs[j][1], 1 - ids[count])):
                    place = pl.ds(pl.multiple_of(j * depth + side * width, width), width)
                    row = 0
                    for ref in part_refs[at : at + len(block)]:
                        x[row : row + ref.shape[0], place] = ref[...]
                        row += ref.shape[0]
                    at += len(block)

        if not finish:
            for j in range(count):
                w_copy(s, j).wait()
            out_ref[0] = dot(x[...], w[s])
            return
        new = dot(x[...], w_ref[0])
        sum_copy(s).wait()
        rounded = (new + sums[s]).astype(BF16)
        filtered = short_filter(taps_ref, jnp.zeros((8, out_width), F32), rounded.astype(F32))
        kept[s, :rows] = filtered
        kept[s, rows:] = ends(rounded)

        @pl.when(s == streams - 1)
        def _():
            gate_ref[...] = kept[0, :rows]
            ends_ref[...] = kept[0, rows:]
            kept[0, :rows] = gated(kept[1, :rows], kept[2, :rows])
            for slot in range(groups if split else 1):
                q = pl.multiple_of(partner(ids[count + 1], slot, groups) * share, share)
                columns = pl.ds(q, share) if split else slice(None)
                in_refs[slot][:rows] = kept[0, :rows, columns]
                for t in range(1, streams):
                    place = rows + (t - 1) * EDGE
                    in_refs[slot][place : place + EDGE] = kept[t, rows:, columns]

    in_specs = [whole(p.shape) for p in parts]
    operands = [w_in] + parts
    scratch = [pltpu.VMEM((rows, count * depth), BF16)]

    def by_stream(extent):
        return pl.BlockSpec((1, extent, out_width), lambda s, ids: (s, 0, 0))

    if finish:
        taps_spec = pl.BlockSpec((KERNEL, pl.squeezed, 1, out_width), lambda s, ids: (0, s, 0, 0))
        in_specs = [by_stream(depth)] + in_specs + [anywhere(), taps_spec]
        operands += [total, conv_taps]
        longer = rows + (streams - 1) * EDGE
        outs = [pltpu.HBM((rows, out_width), BF16), pltpu.HBM((EDGE, out_width), BF16)]
        outs += [pltpu.HBM((longer, share if split else out_width), BF16)] * (groups if split else 1)
        out_specs = [whole(o.shape) for o in outs]
        scratch += [
            pltpu.VMEM((streams, rows + EDGE, out_width), BF16),
            pltpu.VMEM((streams, rows, out_width), F32),
            pltpu.SemaphoreType.DMA((streams,)),
        ]
    else:
        in_specs = [anywhere()] + in_specs
        outs = [pltpu.HBM((streams, rows, out_width), F32)]
        out_specs = [by_stream(rows)]
        scratch += [
            pltpu.VMEM((streams, count * depth, out_width), BF16),
            pltpu.SemaphoreType.DMA((streams, count)),
        ]
    found = call(
        kernel,
        (streams,),
        jnp.stack(list(chip_ids) + [core, me]).astype(jnp.int32),
        operands,
        in_specs,
        outs,
        out_specs,
        scratch,
        "project",
        4 if finish else 20,
        16 if finish else 51,
    )
    if not finish:
        return found[0]
    gate, gate_ends, ins = found[0], found[1], list(found[2:])
    return gate, gate_ends, (ins if split else by_slot(ins[0], groups, me))


def by_slot(block, groups, me):
    stack = jnp.stack(jnp.split(block, groups, axis=1))
    return [
        lax.dynamic_index_in_dim(stack, partner(me, slot, groups), 0, keepdims=False)
        for slot in range(groups)
    ]


def partner(me, slot, groups):
    if groups & (groups - 1) == 0:
        return me ^ slot
    return (me + slot) % groups


def source(me, slot, groups):
    if groups & (groups - 1) == 0:
        return me ^ slot
    return (me - slot + groups) % groups


def taps_spectra(pieces, forward, back, me):
    groups = len(pieces)
    span, share = pieces[0].shape

    def kernel(at, *refs):
        piece_refs, refs = refs[:groups], refs[groups:]
        forward_ref, back_ref, out_ref, forward_out, back_out, padded = refs
        row_ids = lax.broadcasted_iota(jnp.int32, (span, share), 0)
        for s in range(groups):
            k = source(at[0], s, groups)
            block = piece_refs[s][...]
            padded[0:span, pl.ds(pl.multiple_of(k * share, share), share)] = block

            @pl.when(k < groups - 1)
            def _():
                place = pl.multiple_of((k + 1) * share, share)
                kept = jnp.where(row_ids == 0, 0.0, block.astype(F32)).astype(BF16)
                padded[span : 2 * span, pl.ds(place, share)] = kept

        padded[span : 2 * span, 0:share] = jnp.zeros((span, share), BF16)
        out_ref[...] = dot(forward_ref[...], padded[...]).astype(BF16)
        forward_out[...] = forward_ref[:, 0:span]
        back_out[...] = back_ref[...]

    shape = (2 * span, groups * share)
    outs = [
        jax.ShapeDtypeStruct(shape, BF16),
        jax.ShapeDtypeStruct((2 * span, span), BF16),
        jax.ShapeDtypeStruct(back.shape, BF16),
    ]
    operands = list(pieces) + [forward, back]
    return call(
        kernel,
        (1,),
        me[None],
        operands,
        [whole(o.shape) for o in operands],
        outs,
        [whole(o.shape) for o in outs],
        [pltpu.VMEM(shape, BF16)],
        "taps_spectra",
        2,
    )


def long_filter(pieces, taps, spectra_taps, forward_in, back, skip, me):
    groups = len(pieces)
    share = pieces[0].shape[1]
    span = back.shape[0]
    cols = groups * share
    step = 16

    def kernel(at, *refs):
        ins, refs = refs[:groups], refs[groups:]
        short_ref, taps_ref, forward_ref, back_ref, skip_ref = refs[:5]
        outs, (signal, spectra, mixture, result, tails) = refs[5 : 5 + groups], refs[5 + groups :]
        for s in range(groups):
            j = source(at[0], s, groups)
            signal[:, pl.ds(pl.multiple_of(j * share, share), share)] = ins[s][0:span]
            tails[j] = ins[s][span:]
        for j in range(groups):
            heads = []
            for t in (0, 1):
                here = tails[j, t * EDGE : (t + 1) * EDGE]
                before = tails[j - 1, t * EDGE : (t + 1) * EDGE] if j else jnp.zeros_like(here)
                heads.append(first_rows([short_ref[lag, t + 1] for lag in range(KERNEL)], before, here))
            place = slice(j * share, (j + 1) * share)
            rest = signal[0:EDGE, place].astype(F32)[8:]
            head = jnp.concatenate([gated(*heads).astype(F32), rest], 0)
            signal[0:EDGE, place] = head.astype(BF16)
        spectra[...] = dot(forward_ref[...], signal[...]).astype(BF16)

        def mix(start, special):
            def read(ref, first, block):
                return ref[pl.ds(first, step), block * share : (block + 1) * share].astype(F32)

            imag_start = start + span
            real_g = [read(taps_ref, start, b) for b in range(groups)]
            imag_g = [read(taps_ref, imag_start, b) for b in range(groups)]
            real_u = [read(spectra, start, b) for b in range(groups)]
            imag_u = [read(spectra, imag_start, b) for b in range(groups)]
            first = lax.broadcasted_iota(jnp.int32, (step, share), 0) == 0
            for i in range(groups):
                real = imag = None
                for j in range(i + 1):
                    rr = real_g[i - j] * real_u[j]
                    ii = imag_g[i - j] * imag_u[j]
                    cross = real_g[i - j] * imag_u[j] + imag_g[i - j] * real_u[j]
                    new_real, new_imag = rr - ii, cross
                    if special:
                        new_real = jnp.where(first, rr, new_real)
                        new_imag = jnp.where(first, ii, new_imag)
                    real = new_real if real is None else real + new_real
                    imag = new_imag if imag is None else imag + new_imag
                place = slice(i * share, (i + 1) * share)
                mixture[pl.ds(start, step), place] = real.astype(BF16)
                mixture[pl.ds(imag_start, step), place] = imag.astype(BF16)

        mix(0, True)

        @pl.loop(1, span // step)
        def _(c):
            mix(pl.multiple_of(c * step, step), False)

        result[...] = (
            dot(back_ref[...], mixture[...]) + skip_ref[...] * signal[...].astype(F32)
        ).astype(BF16)
        for s in range(groups):
            j = pl.multiple_of(partner(at[0], s, groups) * share, share)
            outs[s][...] = result[:, pl.ds(j, share)]

    operands = list(pieces) + [taps, spectra_taps, forward_in, back, skip]
    in_specs = [whole(o.shape) for o in operands]
    outs = [jax.ShapeDtypeStruct((span, share), BF16)] * groups
    return call(
        kernel,
        (1,),
        me[None],
        operands,
        in_specs,
        outs,
        [whole(o.shape) for o in outs],
        [
            pltpu.VMEM((span, cols), BF16),
            pltpu.VMEM((2 * span, cols), BF16),
            pltpu.VMEM((2 * span, cols), BF16),
            pltpu.VMEM((span, cols), BF16),
            pltpu.VMEM((groups, 2 * EDGE, share), BF16),
        ],
        "long_filter",
        3,
    )


def gate_blocks(gate, before, here, taps, pieces, me):
    groups = len(pieces)
    rows, share = pieces[0].shape

    def kernel(at, gate_ref, before_ref, here_ref, taps_ref, *refs):
        out = refs[groups]
        head = first_rows([taps_ref[lag, 0] for lag in range(KERNEL)], before_ref[...], here_ref[...])
        rest = gate_ref[0:EDGE].astype(F32)[8:]
        edge_ref = refs[groups + 1]
        edge_ref[...] = jnp.concatenate([head.astype(F32), rest], 0).astype(BF16)
        for s in range(groups):
            place = pl.ds(pl.multiple_of(source(at[0], s, groups) * share, share), share)
            out[:, place] = gated(gate_ref[:, place], refs[s][...])
            out[0:EDGE, place] = gated(edge_ref[:, place], refs[s][0:EDGE])

    operands = [gate, before, here, taps] + list(pieces)
    return call(
        kernel,
        (1,),
        me[None],
        operands,
        [whole(o.shape) for o in operands],
        jax.ShapeDtypeStruct(gate.shape, BF16),
        whole(gate.shape),
        [pltpu.VMEM(here.shape, BF16)],
        "gate_blocks",
    )


def output_shares(gated, other, w_own, w_other, chip_ids, plan):
    count = len(chip_ids)
    rows, width = gated.shape
    cols = w_other.shape[1] * 2 // lax.axis_size("chan")

    def kernel(_, a_ref, b_ref, w_ref, v_ref, *outs):
        k = pl.program_id(0)
        total = dot(a_ref[...], w_ref[...]) + dot(b_ref[...], v_ref[...])
        at = 0
        for j in range(count):
            here = outs[at : at + len(plan[j])]
            at += len(plan[j])

            @pl.when(k == j)
            def _():
                for out, (first, last, kind) in zip(here, plan[j]):
                    out[...] = total[first:last].astype(kind)

    outs = [
        jax.ShapeDtypeStruct((last - first, cols), kind)
        for parts in plan
        for first, last, kind in parts
    ]
    return call(
        kernel,
        (count,),
        jnp.stack(list(chip_ids)).astype(jnp.int32),
        [gated, other, w_own, w_other],
        [
            whole(gated.shape),
            whole(other.shape),
            pl.BlockSpec((width, cols), lambda k, ids: (0, ids[k])),
            pl.BlockSpec((width, cols), lambda k, ids: (0, ids[k])),
        ],
        outs,
        [whole(o.shape) for o in outs],
        [],
        "output_shares",
    )


def add_up(own, extras):
    span, cols = own.shape
    half = span // 2
    flat = [e for side in extras for e in side]

    def kernel(_, own_ref, *refs):
        at = 0
        for k, side in enumerate(extras):
            total = own_ref[k * half : (k + 1) * half]
            for ref in refs[at : at + len(side)]:
                total = total + ref[...].astype(F32)
            at += len(side)
            refs[-1][k * half : (k + 1) * half] = total.astype(BF16)

    return call(
        kernel,
        (1,),
        jnp.zeros((1,), jnp.int32),
        [own] + flat,
        [whole(own.shape)] + [whole(e.shape) for e in flat],
        jax.ShapeDtypeStruct(own.shape, BF16),
        whole(own.shape),
        [],
        "add_up",
    )


def exchange(piece):
    groups = lax.axis_size("ctx")

    def send(slot):
        route = [(i, partner(i, slot, groups)) for i in range(groups)]
        return lax.ppermute(piece(slot), "ctx", route)

    return [piece(0)] + [send(s) for s in range(1, groups)]


def in_order(blocks, me):
    groups = len(blocks)
    result = jnp.zeros((groups,) + blocks[0].shape, blocks[0].dtype)
    for s, b in enumerate(blocks):
        result = lax.dynamic_update_index_in_dim(result, b, source(me, s, groups), 0)
    return jnp.concatenate(list(result), 1)


def taps_spectra_plain(pieces, forward, back, me):
    groups = len(pieces)
    span, share = pieces[0].shape
    taps = in_order(pieces, me)
    before = jnp.concatenate(
        [jnp.zeros((span, share), BF16), taps[:, : (groups - 1) * share]], 1
    )
    before = jnp.where(lax.broadcasted_iota(jnp.int32, (span, 1), 0) == 0, 0, before)
    spectra = dot(forward, jnp.concatenate([taps, before], 0)).astype(BF16)
    return spectra, forward[:, :span], back


def long_filter_plain(pieces, taps, spectra_taps, forward_in, back, skip, me):
    groups = len(pieces)
    span, share = back.shape[0], pieces[0].shape[1]
    pieces = in_order(pieces, me)
    tails = [pieces[span + t * EDGE : span + (t + 1) * EDGE] for t in (0, 1)]
    heads = []
    for t in (0, 1):
        before = jnp.concatenate([jnp.zeros((EDGE, share), BF16), tails[t][:, :-share]], 1)
        wide = [jnp.tile(taps[lag, t + 1], (1, groups)) for lag in range(KERNEL)]
        heads.append(first_rows(wide, before, tails[t]))
    signal = jnp.concatenate([gated(*heads), pieces[8:span]], 0)
    spectra = dot(forward_in, signal).astype(BF16)
    real_g, imag_g = spectra_taps[:span].astype(F32), spectra_taps[span:].astype(F32)
    real_u, imag_u = spectra[:span].astype(F32), spectra[span:].astype(F32)
    first = lax.broadcasted_iota(jnp.int32, (span, 1), 0) == 0
    mixed = []
    for i in range(groups):
        real = imag = 0.0
        for j in range(i + 1):
            g = slice((i - j) * share, (i - j + 1) * share)
            u = slice(j * share, (j + 1) * share)
            rr = real_g[:, g] * real_u[:, u]
            ii = imag_g[:, g] * imag_u[:, u]
            cross = real_g[:, g] * imag_u[:, u] + imag_g[:, g] * real_u[:, u]
            real = real + jnp.where(first, rr, rr - ii)
            imag = imag + jnp.where(first, ii, cross)
        mixed.append(jnp.concatenate([real, imag], 0).astype(BF16))
    result = dot(back, jnp.concatenate(mixed, 1)) + skip * signal.astype(F32)
    result = jnp.stack(jnp.split(result.astype(BF16), groups, axis=1))
    found = []
    for s in range(groups):
        block = lax.dynamic_index_in_dim(result, partner(me, s, groups), 0, keepdims=False)
        found.append(block)
    return found


def gate_blocks_plain(gate, before, here, taps, pieces, me):
    head = first_rows([taps[lag, 0] for lag in range(KERNEL)], before, here)
    return gated(jnp.concatenate([head, gate[8:]], 0), in_order(pieces, me))


def body(inputs, w_in, conv_taps, skip_gain, filter_taps, w_out):
    span, width = inputs.shape
    half = span // 2
    groups = lax.axis_size("ctx")
    me = lax.axis_index("ctx")
    chips = lax.axis_size("chan") // 2
    reach = chips // 2
    place = lax.axis_index("chan")
    chip, core = place // 2, place % 2
    share = width // groups
    aligned = share % 128 == 0
    out_width = w_out.shape[1] // (2 * chips)
    forward_np, back_np = half_tables(span)
    forward, back = jnp.asarray(forward_np), jnp.asarray(back_np)
    w_streams = jnp.transpose(w_in, (1, 0, 2))
    short_taps = conv_taps.astype(F32)[:, :, None]

    split_taps = [filter_taps[:, q * share : (q + 1) * share] for q in range(groups)]
    split_taps = jnp.stack(split_taps)

    def pick(stack):
        return lambda s: lax.dynamic_index_in_dim(
            stack, partner(me, s, groups), 0, keepdims=False
        )

    tap_blocks = exchange(pick(split_taps))

    def columns(w, parity):
        starts = [(2 * z + parity) * out_width for z in range(chips)]
        return jnp.concatenate([lax.dynamic_slice_in_dim(w, c, out_width, 1) for c in starts], 1)

    w_given = columns(w_out, 1 - core)
    w_far = lax.dynamic_slice_in_dim(w_streams, (chip + reach) % chips * 2 * width, 2 * width, 1)

    skip = lax.dynamic_slice_in_dim(skip_gain, me * share, share, 0)
    skip = jnp.tile(skip, groups)[None]
    share_taps = lax.dynamic_slice_in_dim(short_taps, me * share, share, 3)

    found = [(0, [inputs])]
    up = [inputs[:half], inputs[half:]]
    down = list(up)
    for d in range(1, reach):
        up_top, down_low = shift(up[0], "chan", 2), shift(down[1], "chan", -2)
        up_low, down_top = shift(up[1], "chan", 2), shift(down[0], "chan", -2)
        if d == reach - 1:
            up_top, down_low, tap_blocks, w_given, w_far, skip, share_taps = lax.optimization_barrier(
                (up_top, down_low, tap_blocks, w_given, w_far, skip, share_taps)
            )
        up, down = [up_top, up_low], [down_top, down_low]
        found += [(d, up), (-d, down)]
    far = [shift(up[0], "chan", 2), shift(down[1], "chan", -2)]

    def both(blocks):
        return blocks, [sibling(b) for b in blocks]

    def added(blocks, w, total=None):
        return project(
            [both(b) for _, b in blocks],
            [(chip - d) % chips for d, _ in blocks],
            core,
            me,
            w,
            short_taps,
            groups,
            total,
        )

    total = added(found, w_streams)
    far = [after(f, total) for f in far]
    gate, gate_ends, pieces = added([(reach, far)], w_far, total)

    pieces_in = exchange(lambda s: pieces[s])
    before = shift(gate_ends, "ctx", 1)
    before = jnp.where(me > 0, before, jnp.zeros_like(before))

    tap_blocks = [after(t, before) for t in tap_blocks]
    spectra_taps, forward_in, back = (taps_spectra if aligned else taps_spectra_plain)(
        tap_blocks, forward, back, me
    )
    w_own = columns(after(w_out, spectra_taps), core)

    w_other = sibling(after(w_given, gate))

    filtered = (long_filter if aligned else long_filter_plain)(
        pieces_in, share_taps, spectra_taps, forward_in, back, after(skip, w_own), me
    )
    filtered = lax.optimization_barrier((list(filtered), w_other))[0]
    gated_out = (gate_blocks if aligned else gate_blocks_plain)(
        gate, before, gate_ends, short_taps, exchange(lambda s: filtered[s]), me
    )

    other = sibling(gated_out)

    def shares(offsets, plan):
        ids = [(chip + d) % chips for d in offsets]
        return output_shares(gated_out, other, w_own, w_other, ids, plan)

    up_top, down_low = shares([reach], [[(0, half, BF16), (half, span, BF16)]])
    offsets, plan = [], []
    for d in range(reach - 1, 0, -1):
        last = d == reach - 1
        offsets += [d, -d]
        plan.append([(0, half, F32), (half, span, BF16 if last else F32)])
        plan.append([(0, half, BF16 if last else F32), (half, span, F32)])
    kept = list(shares(offsets + [0], plan + [[(0, span, F32)]]))
    up_top, down_low = shift(up_top, "chan", 2), shift(down_low, "chan", -2)
    up_low = down_top = None

    def step(carried, new, distance):
        if carried is not None:
            new = (carried.astype(F32) + new).astype(BF16)
        return shift(new, "chan", distance)

    for k in range(reach - 1):
        ahead_top, ahead_low, behind_top, behind_low = kept[4 * k : 4 * k + 4]
        up_low, down_top = step(up_low, ahead_low, 2), step(down_top, behind_top, -2)
        up_top, down_low = step(up_top, ahead_top, 2), step(down_low, behind_low, -2)
    extras = [[up_top], [down_low]]
    if reach > 1:
        extras = [[up_top, down_top], [up_low, down_low]]
    return add_up(kept[-1], extras)


def solution(mesh):
    return jax.shard_map(
        body,
        mesh=mesh,
        in_specs=(
            P("ctx", "chan"),
            P(None, None, "chan"),
            P(None, None, "chan"),
            P("chan"),
            P("ctx", "chan"),
            P("chan", None),
        ),
        out_specs=P("ctx", "chan"),
        check_vma=False,
    )
```

time: 148 us -> 121 us (0.82)
  local copies, waits for them, and re-layouts: 26.6 us -> 13 us
  starting transfers between devices: 38.4 us -> 32.8 us
  Pallas kernels: 31.5 us -> 28 us
  waiting for transfers between devices: 47.5 us -> 44.2 us
    unnamed x58 -> x22, local copies, waits for them, and re-layouts: 20.4 us -> 5.61 us
    ppermute x14 -> x13, starting transfers between devices: 26.1 us -> 21.4 us  [shift(): lax.ppermute(x, axis, [(i, (i + distance) % size) for i in range(size)])]
    pallas_call x8, Pallas kernels: 31.5 us -> 28 us  [call(): pl.pallas_call(kernel, grid_spec=pltpu.PrefetchScalarGridSpec(num_scalar_...]
    ppermute x9, waiting for transfers between devices: 7.68 us -> 5.57 us  [send(): return lax.ppermute(piece(slot), 'ctx', route)]
    ppermute x14 -> x13, waiting for transfers between devices: 36.3 us -> 34.9 us  [shift(): lax.ppermute(x, axis, [(i, (i + distance) % size) for i in range(size)])]
    ppermute x8 -> x9, waiting for transfers between devices: 3.45 us -> 3.68 us  [sibling(): lax.ppermute(x, 'chan', [(i, i ^ 1) for i in range(lax.axis_size('chan'))])]
  transfers between devices with their start and end apart: 31 -> 31, of which waited for: 13 -> 14; matrix products, arithmetic and copies ran while one was open for 6% -> 6% of each run, Pallas kernels for 15% -> 16%
where the time goes in v5:
time: 121 us
  waiting for transfers between devices  44.2 us (37%)
  starting transfers between devices  32.8 us (27%)
  Pallas kernels  28 us (23%)
  local copies, waits for them, and re-layouts  13 us (11%)
  other arithmetic  2.32 us (2%)
    ppermute x13, waiting for transfers between devices, shift(): lax.ppermute(x, axis, [(i, (i + distance) % size) for i in range(size)])  34.9 us
    pallas_call x8, Pallas kernels, call(): pl.pallas_call(kernel, grid_spec=pltpu.PrefetchScalarGridSpec(num_scalar_...  28 us
    ppermute x13, starting transfers between devices, shift(): lax.ppermute(x, axis, [(i, (i + distance) % size) for i in range(size)])  21.4 us
    ppermute x9, starting transfers between devices, send(): return lax.ppermute(piece(slot), 'ctx', route)  10.5 us
    unnamed x22, local copies, waits for them, and re-layouts  5.61 us
    ppermute x9, waiting for transfers between devices, send(): return lax.ppermute(piece(slot), 'ctx', route)  5.57 us
    ppermute x9, waiting for transfers between devices, sibling(): lax.ppermute(x, 'chan', [(i, i ^ 1) for i in range(lax.axis_size('chan'))])  3.68 us
  transfers between devices with their start and end apart: 31, of which 14 were waited for; matrix products, arithmetic and copies ran while one was open for 6% of the time, Pallas kernels for 16%

profile of v5, /device:TPU:0, one launch (start us, length us, event | category | flops | bytes accessed | tf_op | source)
XLA Modules:
  0.0 120.6 jit_solution(12164937467575751651)
XLA Ops:
  0.0 1.9 %fusion = (bf16[256,512]{1,0:T(8,128)(2,1)}, bf16[256,512]{1,0:T(8,128)(2,1)}) fusion(bf16[512,512]{1,0:T(8,128)(2,1)} %refs_0_.1), kind=kLoop, calls=%fused_computation.26 | loop fusion | bytes 1048576 | tf_op jit(solution)/shard_map/slice | solution.py:583
  1.9 3.0 %collective-permute-start = (bf16[256,512]{1,0:T(8,128)(2,1)}, bf16[256,512]{1,0:T(8,128)(2,1)}, u32[]{:S(2)}, u32[]{:S(2)}) collective-permute-start(bf16[256,512]{1,0:T(8,128)(2,1)} %get-tuple-element.108), channel_id=1, source_target_pairs={{0,2},{1,3},{2,4},{3,5},{4,6},{5,7},{6,0},{7,1},{8,10},{9,11},{10,... | collective-permute-start | bytes 786440 | tf_op jit(solution)/shard_map/ppermute | solution.py:37
  4.9 2.0 %collective-permute-start.10 = (bf16[256,512]{1,0:T(8,128)(2,1)}, bf16[256,512]{1,0:T(8,128)(2,1)}, u32[]{:S(2)}, u32[]{:S(2)}) collective-permute-start(bf16[256,512]{1,0:T(8,128)(2,1)} %get-tuple-element.108), channel_id=1, source_target_pairs={{0,6},{1,7},{2,0},{3,1},{4,2},{5,3},{6,4},{7,5},{8,14},{9,15},{10,... | collective-permute-start | bytes 786440 | tf_op jit(solution)/shard_map/ppermute | solution.py:37
  6.9 1.1 slice_bitcast_fusion.3
  8.1 0.1 pad_maximum_fusion.2
  8.2 0.7 dynamic-slice_bitcast_fusion.1
  8.9 1.7 %collective-permute-start.2 = (bf16[512,128]{1,0:T(8,128)(2,1)}, bf16[512,128]{1,0:T(8,128)(2,1)S(1)}, u32[]{:S(2)}, u32[]{:S(2)}) collective-permute-start(bf16[512,128]{1,0:T(8,128)(2,1)} %get-tuple-element.101), channel_id=1, source_target_pairs={{0,8},{8,0},{16,24},{24,16},{1,9},{9,1},{17,25},{25,17},{2,10},{10... | collective-permute-start | bytes 393224 | tf_op jit(solution)/shard_map/ppermute | solution.py:478
  10.6 1.5 %collective-permute-start.3 = (bf16[512,128]{1,0:T(8,128)(2,1)}, bf16[512,128]{1,0:T(8,128)(2,1)}, u32[]{:S(2)}, u32[]{:S(2)}) collective-permute-start(bf16[512,128]{1,0:T(8,128)(2,1)} %get-tuple-element.100), channel_id=1, source_target_pairs={{0,16},{8,24},{16,0},{24,8},{1,17},{9,25},{17,1},{25,9},{2,18},{10... | collective-permute-start | bytes 393224 | tf_op jit(solution)/shard_map/ppermute | solution.py:478
  12.1 0.3 collective-permute-start.4
  12.4 0.8 dynamic_slice.55
  13.2 2.2 %dynamic-slice_bitcast_fusion.w_ref = bf16[3,1024,512]{2,1,0:T(8,128)(2,1)S(1)} fusion(bf16[4096,3,512]{2,0,1:T(8,128)(2,1)} %param.9, s32[]{:T(128)S(6)} %select_n.106), kind=kLoop, calls=%fused_computation | loop fusion | bytes 6291460 | tf_op jit(solution)/shard_map/dynamic_slice | solution.py:576
  15.4 0.9 copy-done.6
  16.3 0.2 constant_dynamic-slice_fusion.8
  16.6 2.1 %collective-permute-start.1 = (bf16[256,512]{1,0:T(8,128)(2,1)S(1)}, bf16[256,512]{1,0:T(8,128)(2,1)}, u32[]{:S(2)}, u32[]{:S(2)}) collective-permute-start(bf16[256,512]{1,0:T(8,128)(2,1)S(1)} %copy-done.8), channel_id=1, source_target_pairs={{0,6},{1,7},{2,0},{3,1},{4,2},{5,3},{6,4},{7,5},{8,14},{9,15},{10,... | collective-permute-start | bytes 786440 | tf_op jit(solution)/shard_map/ppermute | solution.py:37
  18.6 0.1 collective-permute-done.3.refs_2_
  18.8 1.7 %pad_maximum_fusion = bf16[512,2048]{1,0:T(8,128)(2,1)} fusion(bf16[512,512]{1,0:T(8,128)(2,1)S(1)} %get-tuple-element.98, bf16[512,512]{1,0:T(8,128)(2,1)S(1)} %get-tuple-element.96, bf16[512,512]{1,0:T(8,128)(2,1)S(1)} %get-tuple-element.97, bf16[512,512]{1,0:T(8,128)(2,1)S(1)} %get-tuple-element.95), kind=kLoop, calls=%fused_computation.1 | loop fusion | flops 8388608 | bytes 4194304 | tf_op jit(solution)/shard_map/concatenate | solution.py:573
  20.4 5.0 %collective-permute-done.1.refs_7_ = bf16[256,512]{1,0:T(8,128)(2,1)} collective-permute-done((bf16[256,512]{1,0:T(8,128)(2,1)S(1)}, bf16[256,512]{1,0:T(8,128)(2,1)}, u32[]{:S(2)}, u32[]{:S(2)}) %collective-permute-start.1) | collective-permute-done | bytes 262176 | tf_op jit(solution)/shard_map/ppermute | solution.py:37
  25.4 0.5 collective-permute-start.8
  25.9 4.5 %collective-permute-done.7.refs_3_ = bf16[256,512]{1,0:T(8,128)(2,1)} collective-permute-done((bf16[256,512]{1,0:T(8,128)(2,1)S(1)}, bf16[256,512]{1,0:T(8,128)(2,1)}, u32[]{:S(2)}, u32[]{:S(2)}) %collective-permute-start.7) | collective-permute-done | bytes 262176 | tf_op jit(solution)/shard_map/ppermute | solution.py:37
  30.4 0.1 stack.60.ids
  30.5 1.7 %collective-permute-start.13 = (bf16[256,512]{1,0:T(8,128)(2,1)}, bf16[256,512]{1,0:T(8,128)(2,1)}, u32[]{:S(2)}, u32[]{:S(2)}) collective-permute-start(bf16[256,512]{1,0:T(8,128)(2,1)} %collective-permute-done.1.refs_7_), channel_id=1, source_target_pairs={{0,6},{1,7},{2,0},{3,1},{4,2},{5,3},{6,4},{7,5},{8,14},{9,15},{10,... | collective-permute-start | bytes 786440 | tf_op jit(solution)/shard_map/ppermute | solution.py:37
  32.2 0.3 collective-permute-start.5
  32.6 10.8 %project.2.refs_4_ = f32[3,512,512]{2,1,0:T(8,128)} custom-call(s32[5]{0:T(128)S(1)} %stack.60.ids, bf16[3,4096,512]{2,1,0:T(8,128)(2,1)} %bitcast.28, bf16[512,512]{1,0:T(8,128)(2,1)} %refs_0_.1, bf16[512,512]{1,0:T(8,128)(2,1)} %collective-permute-done.6.refs_1_, bf16[256,512]{1,0:T(8,128)(2,1)} %collective-permute-done.refs_2_, ...), custom_call_target="tpu_custom_call" | custom-call | flops 20000000000 | bytes 20971520 | tf_op jit(solution)/shard_map/project/pallas_call | solution.py:61
  43.3 0.1 collective-permute-start.15
  43.4 1.9 %collective-permute-done.5.refs_0_ = bf16[256,512]{1,0:T(8,128)(2,1)} collective-permute-done((bf16[256,512]{1,0:T(8,128)(2,1)}, bf16[256,512]{1,0:T(8,128)(2,1)}, u32[]{:S(2)}, u32[]{:S(2)}) %collective-permute-start.5) | collective-permute-done | bytes 262176 | tf_op jit(solution)/shard_map/ppermute | solution.py:37
  45.3 0.1 pad_add_fusion.1.ids
  45.4 1.8 %collective-permute-done.14.refs_2_ = bf16[256,512]{1,0:T(8,128)(2,1)} collective-permute-done((bf16[256,512]{1,0:T(8,128)(2,1)}, bf16[256,512]{1,0:T(8,128)(2,1)}, u32[]{:S(2)}, u32[]{:S(2)}) %collective-permute-start.14) | collective-permute-done | bytes 262176 | tf_op jit(solution)/shard_map/ppermute | solution.py:41
  47.2 1.9 %copy-done.4 = f32[3,512,512]{2,1,0:T(8,128)S(1)} copy-done((f32[3,512,512]{2,1,0:T(8,128)S(1)}, f32[3,512,512]{2,1,0:T(8,128)}, u32[]{:S(2)}) %copy-start.4) | copy-done | bytes 3145752
  49.1 7.0 %project.3 = (bf16[512,512]{1,0:T(8,128)(2,1)}, bf16[16,512]{1,0:T(8,128)(2,1)}, bf16[544,128]{1,0:T(8,128)(2,1)}, bf16[544,128]{1,0:T(8,128)(2,1)}, bf16[544,128]{1,0:T(8,128)(2,1)}, /*index=5*/bf16[544,128]{1,0:T(8,128)(2,1)}) custom-call(s32[3]{0:T(128)S(1)} %pad_add_fusion.1.ids, bf16[3,1024,512]{2,1,0:T(8,128)(2,1)S(1)} %dynamic-slice_bitcast_fusion.w_ref, ...), custom_call_target="tpu_custom_call" | custom-call | flops 4000000000 | bytes 4194304 | tf_op jit(solution)/shard_map/project/pallas_call | solution.py:61
  56.0 0.2 collective-permute-start.20
  56.2 1.5 %collective-permute-start.16 = (bf16[16,512]{1,0:T(8,128)(2,1)}, bf16[16,512]{1,0:T(8,128)(2,1)S(1)}, u32[]{:S(2)}, u32[]{:S(2)}) collective-permute-start(bf16[16,512]{1,0:T(8,128)(2,1)} %get-tuple-element.54.here_ref), channel_id=1, source_target_pairs={{0,8},{8,16},{16,24},{24,0},{1,9},{9,17},{17,25},{25,1},{2,10},{10... | collective-permute-start | bytes 49160 | tf_op jit(solution)/shard_map/ppermute | solution.py:37
  57.7 1.5 %collective-permute-start.17 = (bf16[544,128]{1,0:T(8,128)(2,1)}, bf16[544,128]{1,0:T(8,128)(2,1)S(1)}, u32[]{:S(2)}, u32[]{:S(2)}) collective-permute-start(bf16[544,128]{1,0:T(8,128)(2,1)} %get-tuple-element.56), channel_id=1, source_target_pairs={{0,8},{8,0},{16,24},{24,16},{1,9},{9,1},{17,25},{25,17},{2,10},{10... | collective-permute-start | bytes 417800 | tf_op jit(solution)/shard_map/ppermute | solution.py:478
  59.2 0.5 collective-permute-start.18
  59.7 1.5 %collective-permute-start.19 = (bf16[544,128]{1,0:T(8,128)(2,1)}, bf16[544,128]{1,0:T(8,128)(2,1)S(1)}, u32[]{:S(2)}, u32[]{:S(2)}) collective-permute-start(bf16[544,128]{1,0:T(8,128)(2,1)} %get-tuple-element.58), channel_id=1, source_target_pairs={{0,24},{8,16},{16,8},{24,0},{1,25},{9,17},{17,9},{25,1},{2,26},{10... | collective-permute-start | bytes 417800 | tf_op jit(solution)/shard_map/ppermute | solution.py:478
  61.2 1.6 %copy-done.1 = bf16[1024,1024]{1,0:T(8,128)(2,1)S(1)} copy-done((bf16[1024,1024]{1,0:T(8,128)(2,1)S(1)}, bf16[1024,1024]{1,0:T(8,128)(2,1)}, u32[]{:S(2)}) %copy-start.1) | copy-done | bytes 2097176
  62.8 1.2 %copy-done.2 = bf16[512,1024]{1,0:T(8,128)(2,1)S(1)} copy-done((bf16[512,1024]{1,0:T(8,128)(2,1)S(1)}, bf16[512,1024]{1,0:T(8,128)(2,1)}, u32[]{:S(2)}) %copy-start.2) | copy-done | bytes 1048600
  64.1 2.6 %taps_spectra.1 = (bf16[1024,512]{1,0:T(8,128)(2,1)S(1)}, bf16[1024,512]{1,0:T(8,128)(2,1)S(1)}, bf16[512,1024]{1,0:T(8,128)(2,1)S(1)}) custom-call(s32[1]{0:T(128)} %bitcast.3.at, bf16[512,128]{1,0:T(8,128)(2,1)S(1)} %get-tuple-element.61.refs_0_, bf16[512,128]{1,0:T(8,128)(2,1)S(1)} %collective-permute-done.2.refs_1_, ...), custom_call_target="tpu_custom_call" | custom-call | flops 2000000000 | bytes 2097152 | tf_op jit(solution)/shard_map/taps_spectra/pallas_call | solution.py:61
  66.7 0.2 constant_dynamic-slice_fusion.3
  66.9 0.3 pad_maximum_fusion.1.w_ref
  67.2 0.6 collective-permute-done.18.refs_2_
  67.8 2.6 %long_filter.1 = (bf16[512,128]{1,0:T(8,128)(2,1)S(1)}, bf16[512,128]{1,0:T(8,128)(2,1)S(1)}, bf16[512,128]{1,0:T(8,128)(2,1)S(1)}, bf16[512,128]{1,0:T(8,128)(2,1)S(1)}) custom-call(s32[1]{0:T(128)} %bitcast.3.at, bf16[544,128]{1,0:T(8,128)(2,1)S(1)} %copy-done.5, bf16[544,128]{1,0:T(8,128)(2,1)S(1)} %collective-permute-done.17.refs_1_, ...), custom_call_target="tpu_custom_call" | custom-call | flops 3000000000 | bytes 3145728 | tf_op jit(solution)/shard_map/long_filter/pallas_call | solution.py:61
  70.5 1.3 %collective-permute-start.21 = (bf16[512,128]{1,0:T(8,128)(2,1)S(1)}, bf16[512,128]{1,0:T(8,128)(2,1)S(1)}, u32[]{:S(2)}, u32[]{:S(2)}) collective-permute-start(bf16[512,128]{1,0:T(8,128)(2,1)S(1)} %get-tuple-element.81), channel_id=1, source_target_pairs={{0,8},{8,0},{16,24},{24,16},{1,9},{9,1},{17,25},{25,17},{2,10},{10... | collective-permute-start | bytes 393224 | tf_op jit(solution)/shard_map/ppermute | solution.py:478
  71.8 0.8 collective-permute-start.22
  72.6 1.4 %collective-permute-start.23 = (bf16[512,128]{1,0:T(8,128)(2,1)S(1)}, bf16[512,128]{1,0:T(8,128)(2,1)S(1)}, u32[]{:S(2)}, u32[]{:S(2)}) collective-permute-start(bf16[512,128]{1,0:T(8,128)(2,1)S(1)} %get-tuple-element.83), channel_id=1, source_target_pairs={{0,24},{8,16},{16,8},{24,0},{1,25},{9,17},{17,9},{25,1},{2,26},{10... | collective-permute-start | bytes 393224 | tf_op jit(solution)/shard_map/ppermute | solution.py:478
  74.0 2.5 %collective-permute-done.21.refs_1_ = bf16[512,128]{1,0:T(8,128)(2,1)S(1)} collective-permute-done((bf16[512,128]{1,0:T(8,128)(2,1)S(1)}, bf16[512,128]{1,0:T(8,128)(2,1)S(1)}, u32[]{:S(2)}, u32[]{:S(2)}) %collective-permute-start.21) | collective-permute-done | bytes 131104 | tf_op jit(solution)/shard_map/ppermute | solution.py:478
  76.6 2.4 %collective-permute-done.22.refs_2_ = bf16[512,128]{1,0:T(8,128)(2,1)S(1)} collective-permute-done((bf16[512,128]{1,0:T(8,128)(2,1)S(1)}, bf16[512,128]{1,0:T(8,128)(2,1)S(1)}, u32[]{:S(2)}, u32[]{:S(2)}) %collective-permute-start.22) | collective-permute-done | bytes 131104 | tf_op jit(solution)/shard_map/ppermute | solution.py:478
  79.0 0.2 gate_blocks.1.a_ref
  79.2 0.1 collective-permute-start.24
  79.3 1.9 %collective-permute-done.24.b_ref = bf16[512,512]{1,0:T(8,128)(2,1)S(1)} collective-permute-done((bf16[512,512]{1,0:T(8,128)(2,1)S(1)}, bf16[512,512]{1,0:T(8,128)(2,1)S(1)}, u32[]{:S(2)}, u32[]{:S(2)}) %collective-permute-start.24) | collective-permute-done | bytes 524320 | tf_op jit(solution)/shard_map/ppermute | solution.py:41
  81.2 0.7 output_shares.3
  81.9 2.0 %collective-permute-start.29 = (bf16[256,512]{1,0:T(8,128)(2,1)S(1)}, bf16[256,512]{1,0:T(8,128)(2,1)S(1)}, u32[]{:S(2)}, u32[]{:S(2)}) collective-permute-start(bf16[256,512]{1,0:T(8,128)(2,1)S(1)} %get-tuple-element.89), channel_id=1, source_target_pairs={{0,6},{1,7},{2,0},{3,1},{4,2},{5,3},{6,4},{7,5},{8,14},{9,15},{10,... | collective-permute-start | bytes 786440 | tf_op jit(solution)/shard_map/ppermute | solution.py:37
  84.0 0.1 pad_add_fusion._
  84.1 3.2 %output_shares.2 = (f32[256,512]{1,0:T(8,128)S(1)}, bf16[256,512]{1,0:T(8,128)(2,1)S(1)}, bf16[256,512]{1,0:T(8,128)(2,1)S(1)}, f32[256,512]{1,0:T(8,128)S(1)}, f32[512,512]{1,0:T(8,128)S(1)}) custom-call(s32[3]{0:T(128)S(1)} %pad_add_fusion._, bf16[512,512]{1,0:T(8,128)(2,1)S(1)} %gate_blocks.1.a_ref, bf16[512,512]{1,0:T(8,128)(2,1)S(1)} %collective-permute-done.24.b_ref, ...), custom_call_target="tpu_custom_call" | custom-call | flops 1000000000 | bytes 1048576 | tf_op jit(solution)/shard_map/output_shares/pallas_call | solution.py:61
  87.2 3.8 %collective-permute-start.27 = (bf16[256,512]{1,0:T(8,128)(2,1)S(1)}, bf16[256,512]{1,0:T(8,128)(2,1)S(1)}, u32[]{:S(2)}, u32[]{:S(2)}) collective-permute-start(bf16[256,512]{1,0:T(8,128)(2,1)S(1)} %get-tuple-element.87), channel_id=1, source_target_pairs={{0,6},{1,7},{2,0},{3,1},{4,2},{5,3},{6,4},{7,5},{8,14},{9,15},{10,... | collective-permute-start | bytes 786440 | tf_op jit(solution)/shard_map/ppermute | solution.py:37
  91.1 0.1 add_convert_fusion
  91.2 3.9 %collective-permute-start.30 = (bf16[256,512]{1,0:T(8,128)(2,1)S(1)}, bf16[256,512]{1,0:T(8,128)(2,1)S(1)}, u32[]{:S(2)}, u32[]{:S(2)}) collective-permute-start(bf16[256,512]{1,0:T(8,128)(2,1)S(1)} %add_convert_fusion), channel_id=1, source_target_pairs={{0,6},{1,7},{2,0},{3,1},{4,2},{5,3},{6,4},{7,5},{8,14},{9,15},{10,... | collective-permute-start | bytes 786440 | tf_op jit(solution)/shard_map/ppermute | solution.py:37
  95.1 2.8 %collective-permute-done.25 = bf16[256,512]{1,0:T(8,128)(2,1)S(1)} collective-permute-done((bf16[256,512]{1,0:T(8,128)(2,1)S(1)}, bf16[256,512]{1,0:T(8,128)(2,1)S(1)}, u32[]{:S(2)}, u32[]{:S(2)}) %collective-permute-start.25) | collective-permute-done | bytes 262176 | tf_op jit(solution)/shard_map/ppermute | solution.py:37
  97.9 0.1 add_convert_fusion.1
  98.0 0.9 collective-permute-start.26
  98.9 3.4 %collective-permute-done.27.refs_1_ = bf16[256,512]{1,0:T(8,128)(2,1)S(1)} collective-permute-done((bf16[256,512]{1,0:T(8,128)(2,1)S(1)}, bf16[256,512]{1,0:T(8,128)(2,1)S(1)}, u32[]{:S(2)}, u32[]{:S(2)}) %collective-permute-start.27) | collective-permute-done | bytes 262176 | tf_op jit(solution)/shard_map/ppermute | solution.py:37
  102.3 6.9 %collective-permute-done.28.refs_2_ = bf16[256,512]{1,0:T(8,128)(2,1)S(1)} collective-permute-done((bf16[256,512]{1,0:T(8,128)(2,1)S(1)}, bf16[256,512]{1,0:T(8,128)(2,1)S(1)}, u32[]{:S(2)}, u32[]{:S(2)}) %collective-permute-start.28) | collective-permute-done | bytes 262176 | tf_op jit(solution)/shard_map/ppermute | solution.py:37
  109.2 4.0 %collective-permute-done.30.refs_3_ = bf16[256,512]{1,0:T(8,128)(2,1)S(1)} collective-permute-done((bf16[256,512]{1,0:T(8,128)(2,1)S(1)}, bf16[256,512]{1,0:T(8,128)(2,1)S(1)}, u32[]{:S(2)}, u32[]{:S(2)}) %collective-permute-start.30) | collective-permute-done | bytes 262176 | tf_op jit(solution)/shard_map/ppermute | solution.py:37
  113.2 6.4 %collective-permute-done.26.refs_0_ = bf16[256,512]{1,0:T(8,128)(2,1)S(1)} collective-permute-done((bf16[256,512]{1,0:T(8,128)(2,1)S(1)}, bf16[256,512]{1,0:T(8,128)(2,1)S(1)}, u32[]{:S(2)}, u32[]{:S(2)}) %collective-permute-start.26) | collective-permute-done | bytes 262176 | tf_op jit(solution)/shard_map/ppermute | solution.py:37
  119.6 0.9 add_up.1
  (49 shorter events, 0.2 us)
Async XLA Ops:
  0.0 12.4 %copy-start.9 = (bf16[3,3,512]{2,1,0:T(4,128)(2,1)S(1)}, bf16[3,3,512]{2,1,0:T(4,128)(2,1)}, u32[]{:S(2)}) copy-start(bf16[3,3,512]{2,1,0:T(4,128)(2,1)} %param.10) | copy-start | bytes 27652
  1.9 18.6 %collective-permute-start = (bf16[256,512]{1,0:T(8,128)(2,1)}, bf16[256,512]{1,0:T(8,128)(2,1)}, u32[]{:S(2)}, u32[]{:S(2)}) collective-permute-start(bf16[256,512]{1,0:T(8,128)(2,1)} %get-tuple-element.108), channel_id=1, source_target_pairs={{0,2},{1,3},{2,4},{3,5},{4,6},{5,7},{6,0},{7,1},{8,10},{9,11},{10,... | collective-permute-start | bytes 786440 | tf_op jit(solution)/shard_map/ppermute | solution.py:37
  4.9 21.0 %collective-permute-start.10 = (bf16[256,512]{1,0:T(8,128)(2,1)}, bf16[256,512]{1,0:T(8,128)(2,1)}, u32[]{:S(2)}, u32[]{:S(2)}) collective-permute-start(bf16[256,512]{1,0:T(8,128)(2,1)} %get-tuple-element.108), channel_id=1, source_target_pairs={{0,6},{1,7},{2,0},{3,1},{4,2},{5,3},{6,4},{7,5},{8,14},{9,15},{10,... | collective-permute-start | bytes 786440 | tf_op jit(solution)/shard_map/ppermute | solution.py:37
  8.9 7.7 %collective-permute-start.2 = (bf16[512,128]{1,0:T(8,128)(2,1)}, bf16[512,128]{1,0:T(8,128)(2,1)S(1)}, u32[]{:S(2)}, u32[]{:S(2)}) collective-permute-start(bf16[512,128]{1,0:T(8,128)(2,1)} %get-tuple-element.101), channel_id=1, source_target_pairs={{0,8},{8,0},{16,24},{24,16},{1,9},{9,1},{17,25},{25,17},{2,10},{10... | collective-permute-start | bytes 393224 | tf_op jit(solution)/shard_map/ppermute | solution.py:478
  10.6 8.1 %collective-permute-start.3 = (bf16[512,128]{1,0:T(8,128)(2,1)}, bf16[512,128]{1,0:T(8,128)(2,1)}, u32[]{:S(2)}, u32[]{:S(2)}) collective-permute-start(bf16[512,128]{1,0:T(8,128)(2,1)} %get-tuple-element.100), channel_id=1, source_target_pairs={{0,16},{8,24},{16,0},{24,8},{1,17},{9,25},{17,1},{25,9},{2,18},{10... | collective-permute-start | bytes 393224 | tf_op jit(solution)/shard_map/ppermute | solution.py:478
  12.1 6.6 %collective-permute-start.4 = (bf16[512,128]{1,0:T(8,128)(2,1)S(1)}, bf16[512,128]{1,0:T(8,128)(2,1)}, u32[]{:S(2)}, u32[]{:S(2)}) collective-permute-start(bf16[512,128]{1,0:T(8,128)(2,1)S(1)} %get-tuple-element.99), channel_id=1, source_target_pairs={{0,24},{8,16},{16,8},{24,0},{1,25},{9,17},{17,9},{25,1},{2,26},{10... | collective-permute-start | bytes 393224 | tf_op jit(solution)/shard_map/ppermute | solution.py:478
  13.2 3.1 %copy-start.6 = (bf16[512,4096]{1,0:T(8,128)(2,1)S(1)}, bf16[512,4096]{1,0:T(8,128)(2,1)}, u32[]{:S(2)}) copy-start(bf16[512,4096]{1,0:T(8,128)(2,1)} %param.13) | copy-start | bytes 12582916
  13.2 3.4 %copy-start.8 = (bf16[256,512]{1,0:T(8,128)(2,1)S(1)}, bf16[256,512]{1,0:T(8,128)(2,1)}, u32[]{:S(2)}) copy-start(bf16[256,512]{1,0:T(8,128)(2,1)} %get-tuple-element.107) | copy-start | bytes 786436
  16.6 8.8 %collective-permute-start.1 = (bf16[256,512]{1,0:T(8,128)(2,1)S(1)}, bf16[256,512]{1,0:T(8,128)(2,1)}, u32[]{:S(2)}, u32[]{:S(2)}) collective-permute-start(bf16[256,512]{1,0:T(8,128)(2,1)S(1)} %copy-done.8), channel_id=1, source_target_pairs={{0,6},{1,7},{2,0},{3,1},{4,2},{5,3},{6,4},{7,5},{8,14},{9,15},{10,... | collective-permute-start | bytes 786440 | tf_op jit(solution)/shard_map/ppermute | solution.py:37
  18.7 11.7 %collective-permute-start.7 = (bf16[256,512]{1,0:T(8,128)(2,1)S(1)}, bf16[256,512]{1,0:T(8,128)(2,1)}, u32[]{:S(2)}, u32[]{:S(2)}) collective-permute-start(bf16[256,512]{1,0:T(8,128)(2,1)S(1)} %copy-done.8), channel_id=1, source_target_pairs={{0,2},{1,3},{2,4},{3,5},{4,6},{5,7},{6,0},{7,1},{8,10},{9,11},{10,... | collective-permute-start | bytes 786440 | tf_op jit(solution)/shard_map/ppermute | solution.py:37
  18.7 13.8 %collective-permute-start.6 = (bf16[512,512]{1,0:T(8,128)(2,1)}, bf16[512,512]{1,0:T(8,128)(2,1)}, u32[]{:S(2)}, u32[]{:S(2)}) collective-permute-start(bf16[512,512]{1,0:T(8,128)(2,1)} %refs_0_.1), channel_id=1, source_target_pairs={{0,1},{1,0},{2,3},{3,2},{4,5},{5,4},{6,7},{7,6},{8,9},{9,8},{10,11... | collective-permute-start | bytes 1572872 | tf_op jit(solution)/shard_map/ppermute | solution.py:41
  25.4 5.1 %collective-permute-start.12 = (bf16[256,512]{1,0:T(8,128)(2,1)}, bf16[256,512]{1,0:T(8,128)(2,1)}, u32[]{:S(2)}, u32[]{:S(2)}) collective-permute-start(bf16[256,512]{1,0:T(8,128)(2,1)} %collective-permute-done.1.refs_7_), channel_id=1, source_target_pairs={{0,1},{1,0},{2,3},{3,2},{4,5},{5,4},{6,7},{7,6},{8,9},{9,8},{10,11... | collective-permute-start | bytes 786440 | tf_op jit(solution)/shard_map/ppermute | solution.py:41
  25.4 6.8 %collective-permute-start.8 = (bf16[256,512]{1,0:T(8,128)(2,1)}, bf16[256,512]{1,0:T(8,128)(2,1)}, u32[]{:S(2)}, u32[]{:S(2)}) collective-permute-start(bf16[256,512]{1,0:T(8,128)(2,1)} %collective-permute-done.refs_2_), channel_id=1, source_target_pairs={{0,1},{1,0},{2,3},{3,2},{4,5},{5,4},{6,7},{7,6},{8,9},{9,8},{10,11... | collective-permute-start | bytes 786440 | tf_op jit(solution)/shard_map/ppermute | solution.py:41
  25.9 6.6 %collective-permute-start.11 = (bf16[256,512]{1,0:T(8,128)(2,1)}, bf16[256,512]{1,0:T(8,128)(2,1)}, u32[]{:S(2)}, u32[]{:S(2)}) collective-permute-start(bf16[256,512]{1,0:T(8,128)(2,1)} %collective-permute-done.10.refs_6_), channel_id=1, source_target_pairs={{0,1},{1,0},{2,3},{3,2},{4,5},{5,4},{6,7},{7,6},{8,9},{9,8},{10,11... | collective-permute-start | bytes 786440 | tf_op jit(solution)/shard_map/ppermute | solution.py:41
  30.4 2.1 %collective-permute-start.9 = (bf16[256,512]{1,0:T(8,128)(2,1)}, bf16[256,512]{1,0:T(8,128)(2,1)}, u32[]{:S(2)}, u32[]{:S(2)}) collective-permute-start(bf16[256,512]{1,0:T(8,128)(2,1)} %collective-permute-done.7.refs_3_), channel_id=1, source_target_pairs={{0,1},{1,0},{2,3},{3,2},{4,5},{5,4},{6,7},{7,6},{8,9},{9,8},{10,11... | collective-permute-start | bytes 786440 | tf_op jit(solution)/shard_map/ppermute | solution.py:41
  30.5 12.8 %collective-permute-start.13 = (bf16[256,512]{1,0:T(8,128)(2,1)}, bf16[256,512]{1,0:T(8,128)(2,1)}, u32[]{:S(2)}, u32[]{:S(2)}) collective-permute-start(bf16[256,512]{1,0:T(8,128)(2,1)} %collective-permute-done.1.refs_7_), channel_id=1, source_target_pairs={{0,6},{1,7},{2,0},{3,1},{4,2},{5,3},{6,4},{7,5},{8,14},{9,15},{10,... | collective-permute-start | bytes 786440 | tf_op jit(solution)/shard_map/ppermute | solution.py:37
  32.2 13.1 %collective-permute-start.5 = (bf16[256,512]{1,0:T(8,128)(2,1)}, bf16[256,512]{1,0:T(8,128)(2,1)}, u32[]{:S(2)}, u32[]{:S(2)}) collective-permute-start(bf16[256,512]{1,0:T(8,128)(2,1)} %collective-permute-done.refs_2_), channel_id=1, source_target_pairs={{0,2},{1,3},{2,4},{3,5},{4,6},{5,7},{6,0},{7,1},{8,10},{9,11},{10,... | collective-permute-start | bytes 786440 | tf_op jit(solution)/shard_map/ppermute | solution.py:37
  32.6 12.7 %copy-start.10 = (bf16[3,3,512]{2,1,0:T(4,128)(2,1)S(1)}, bf16[3,3,512]{2,1,0:T(4,128)(2,1)}, u32[]{:S(2)}) copy-start(bf16[3,3,512]{2,1,0:T(4,128)(2,1)} %param.10) | copy-start | bytes 27652
  43.3 2.1 %collective-permute-start.15 = (bf16[256,512]{1,0:T(8,128)(2,1)}, bf16[256,512]{1,0:T(8,128)(2,1)}, u32[]{:S(2)}, u32[]{:S(2)}) collective-permute-start(bf16[256,512]{1,0:T(8,128)(2,1)} %collective-permute-done.13.refs_1_), channel_id=1, source_target_pairs={{0,1},{1,0},{2,3},{3,2},{4,5},{5,4},{6,7},{7,6},{8,9},{9,8},{10,11... | collective-permute-start | bytes 786440 | tf_op jit(solution)/shard_map/ppermute | solution.py:41
  45.3 1.9 %collective-permute-start.14 = (bf16[256,512]{1,0:T(8,128)(2,1)}, bf16[256,512]{1,0:T(8,128)(2,1)}, u32[]{:S(2)}, u32[]{:S(2)}) collective-permute-start(bf16[256,512]{1,0:T(8,128)(2,1)} %collective-permute-done.5.refs_0_), channel_id=1, source_target_pairs={{0,1},{1,0},{2,3},{3,2},{4,5},{5,4},{6,7},{7,6},{8,9},{9,8},{10,11... | collective-permute-start | bytes 786440 | tf_op jit(solution)/shard_map/ppermute | solution.py:41
  47.2 1.9 %copy-start.4 = (f32[3,512,512]{2,1,0:T(8,128)S(1)}, f32[3,512,512]{2,1,0:T(8,128)}, u32[]{:S(2)}) copy-start(f32[3,512,512]{2,1,0:T(8,128)} %project.2.refs_4_) | copy-start | bytes 9437188
  56.0 14.4 %collective-permute-start.20 = (bf16[512,2048]{1,0:T(8,128)(2,1)}, bf16[512,2048]{1,0:T(8,128)(2,1)S(1)}, u32[]{:S(2)}, u32[]{:S(2)}) collective-permute-start(bf16[512,2048]{1,0:T(8,128)(2,1)} %pad_maximum_fusion), channel_id=1, source_target_pairs={{0,1},{1,0},{2,3},{3,2},{4,5},{5,4},{6,7},{7,6},{8,9},{9,8},{10,11... | collective-permute-start | bytes 6291464 | tf_op jit(solution)/shard_map/ppermute | solution.py:41
  56.2 5.0 %collective-permute-start.16 = (bf16[16,512]{1,0:T(8,128)(2,1)}, bf16[16,512]{1,0:T(8,128)(2,1)S(1)}, u32[]{:S(2)}, u32[]{:S(2)}) collective-permute-start(bf16[16,512]{1,0:T(8,128)(2,1)} %get-tuple-element.54.here_ref), channel_id=1, source_target_pairs={{0,8},{8,16},{16,24},{24,0},{1,9},{9,17},{17,25},{25,1},{2,10},{10... | collective-permute-start | bytes 49160 | tf_op jit(solution)/shard_map/ppermute | solution.py:37
  57.7 9.5 %collective-permute-start.17 = (bf16[544,128]{1,0:T(8,128)(2,1)}, bf16[544,128]{1,0:T(8,128)(2,1)S(1)}, u32[]{:S(2)}, u32[]{:S(2)}) collective-permute-start(bf16[544,128]{1,0:T(8,128)(2,1)} %get-tuple-element.56), channel_id=1, source_target_pairs={{0,8},{8,0},{16,24},{24,16},{1,9},{9,1},{17,25},{25,17},{2,10},{10... | collective-permute-start | bytes 417800 | tf_op jit(solution)/shard_map/ppermute | solution.py:478
  59.2 8.6 %collective-permute-start.18 = (bf16[544,128]{1,0:T(8,128)(2,1)}, bf16[544,128]{1,0:T(8,128)(2,1)S(1)}, u32[]{:S(2)}, u32[]{:S(2)}) collective-permute-start(bf16[544,128]{1,0:T(8,128)(2,1)} %get-tuple-element.57), channel_id=1, source_target_pairs={{0,16},{8,24},{16,0},{24,8},{1,17},{9,25},{17,1},{25,9},{2,18},{10... | collective-permute-start | bytes 417800 | tf_op jit(solution)/shard_map/ppermute | solution.py:478
  59.7 8.1 %collective-permute-start.19 = (bf16[544,128]{1,0:T(8,128)(2,1)}, bf16[544,128]{1,0:T(8,128)(2,1)S(1)}, u32[]{:S(2)}, u32[]{:S(2)}) collective-permute-start(bf16[544,128]{1,0:T(8,128)(2,1)} %get-tuple-element.58), channel_id=1, source_target_pairs={{0,24},{8,16},{16,8},{24,0},{1,25},{9,17},{17,9},{25,1},{2,26},{10... | collective-permute-start | bytes 417800 | tf_op jit(solution)/shard_map/ppermute | solution.py:478
  61.2 1.6 %copy-start.1 = (bf16[1024,1024]{1,0:T(8,128)(2,1)S(1)}, bf16[1024,1024]{1,0:T(8,128)(2,1)}, u32[]{:S(2)}) copy-start(bf16[1024,1024]{1,0:T(8,128)(2,1)} %constant.107.clone.refs_4_) | copy-start | bytes 6291460
  62.8 1.2 %copy-start.2 = (bf16[512,1024]{1,0:T(8,128)(2,1)S(1)}, bf16[512,1024]{1,0:T(8,128)(2,1)}, u32[]{:S(2)}) copy-start(bf16[512,1024]{1,0:T(8,128)(2,1)} %constant.108.clone.refs_5_) | copy-start | bytes 3145732
  64.1 2.6 %copy-start.7 = (bf16[512,4096]{1,0:T(8,128)(2,1)S(1)}, bf16[512,4096]{1,0:T(8,128)(2,1)}, u32[]{:S(2)}) copy-start(bf16[512,4096]{1,0:T(8,128)(2,1)} %param.13) | copy-start | bytes 12582916
  66.7 1.1 copy-start.5
  67.8 11.2 %copy-start = (bf16[16,512]{1,0:T(8,128)(2,1)S(1)}, bf16[16,512]{1,0:T(8,128)(2,1)}, u32[]{:S(2)}) copy-start(bf16[16,512]{1,0:T(8,128)(2,1)} %get-tuple-element.54.here_ref) | copy-start | bytes 49156
  67.8 11.2 %copy-start.3 = (bf16[512,512]{1,0:T(8,128)(2,1)S(1)}, bf16[512,512]{1,0:T(8,128)(2,1)}, u32[]{:S(2)}) copy-start(bf16[512,512]{1,0:T(8,128)(2,1)} %get-tuple-element.53.gate_ref) | copy-start | bytes 1572868
  70.5 6.1 %collective-permute-start.21 = (bf16[512,128]{1,0:T(8,128)(2,1)S(1)}, bf16[512,128]{1,0:T(8,128)(2,1)S(1)}, u32[]{:S(2)}, u32[]{:S(2)}) collective-permute-start(bf16[512,128]{1,0:T(8,128)(2,1)S(1)} %get-tuple-element.81), channel_id=1, source_target_pairs={{0,8},{8,0},{16,24},{24,16},{1,9},{9,1},{17,25},{25,17},{2,10},{10... | collective-permute-start | bytes 393224 | tf_op jit(solution)/shard_map/ppermute | solution.py:478
  71.8 7.2 %collective-permute-start.22 = (bf16[512,128]{1,0:T(8,128)(2,1)S(1)}, bf16[512,128]{1,0:T(8,128)(2,1)S(1)}, u32[]{:S(2)}, u32[]{:S(2)}) collective-permute-start(bf16[512,128]{1,0:T(8,128)(2,1)S(1)} %get-tuple-element.82), channel_id=1, source_target_pairs={{0,16},{8,24},{16,0},{24,8},{1,17},{9,25},{17,1},{25,9},{2,18},{10... | collective-permute-start | bytes 393224 | tf_op jit(solution)/shard_map/ppermute | solution.py:478
  72.6 6.4 %collective-permute-start.23 = (bf16[512,128]{1,0:T(8,128)(2,1)S(1)}, bf16[512,128]{1,0:T(8,128)(2,1)S(1)}, u32[]{:S(2)}, u32[]{:S(2)}) collective-permute-start(bf16[512,128]{1,0:T(8,128)(2,1)S(1)} %get-tuple-element.83), channel_id=1, source_target_pairs={{0,24},{8,16},{16,8},{24,0},{1,25},{9,17},{17,9},{25,1},{2,26},{10... | collective-permute-start | bytes 393224 | tf_op jit(solution)/shard_map/ppermute | solution.py:478
  79.2 2.0 %collective-permute-start.24 = (bf16[512,512]{1,0:T(8,128)(2,1)S(1)}, bf16[512,512]{1,0:T(8,128)(2,1)S(1)}, u32[]{:S(2)}, u32[]{:S(2)}) collective-permute-start(bf16[512,512]{1,0:T(8,128)(2,1)S(1)} %gate_blocks.1.a_ref), channel_id=1, source_target_pairs={{0,1},{1,0},{2,3},{3,2},{4,5},{5,4},{6,7},{7,6},{8,9},{9,8},{10,11... | collective-permute-start | bytes 1572872 | tf_op jit(solution)/shard_map/ppermute | solution.py:41
  81.9 9.2 %collective-permute-start.29 = (bf16[256,512]{1,0:T(8,128)(2,1)S(1)}, bf16[256,512]{1,0:T(8,128)(2,1)S(1)}, u32[]{:S(2)}, u32[]{:S(2)}) collective-permute-start(bf16[256,512]{1,0:T(8,128)(2,1)S(1)} %get-tuple-element.89), channel_id=1, source_target_pairs={{0,6},{1,7},{2,0},{3,1},{4,2},{5,3},{6,4},{7,5},{8,14},{9,15},{10,... | collective-permute-start | bytes 786440 | tf_op jit(solution)/shard_map/ppermute | solution.py:37
  84.0 13.9 %collective-permute-start.25 = (bf16[256,512]{1,0:T(8,128)(2,1)S(1)}, bf16[256,512]{1,0:T(8,128)(2,1)S(1)}, u32[]{:S(2)}, u32[]{:S(2)}) collective-permute-start(bf16[256,512]{1,0:T(8,128)(2,1)S(1)} %get-tuple-element.85), channel_id=1, source_target_pairs={{0,2},{1,3},{2,4},{3,5},{4,6},{5,7},{6,0},{7,1},{8,10},{9,11},{10,... | collective-permute-start | bytes 786440 | tf_op jit(solution)/shard_map/ppermute | solution.py:37
  87.2 15.0 %collective-permute-start.27 = (bf16[256,512]{1,0:T(8,128)(2,1)S(1)}, bf16[256,512]{1,0:T(8,128)(2,1)S(1)}, u32[]{:S(2)}, u32[]{:S(2)}) collective-permute-start(bf16[256,512]{1,0:T(8,128)(2,1)S(1)} %get-tuple-element.87), channel_id=1, source_target_pairs={{0,6},{1,7},{2,0},{3,1},{4,2},{5,3},{6,4},{7,5},{8,14},{9,15},{10,... | collective-permute-start | bytes 786440 | tf_op jit(solution)/shard_map/ppermute | solution.py:37
  91.1 18.1 %collective-permute-start.28 = (bf16[256,512]{1,0:T(8,128)(2,1)S(1)}, bf16[256,512]{1,0:T(8,128)(2,1)S(1)}, u32[]{:S(2)}, u32[]{:S(2)}) collective-permute-start(bf16[256,512]{1,0:T(8,128)(2,1)S(1)} %get-tuple-element.88), channel_id=1, source_target_pairs={{0,2},{1,3},{2,4},{3,5},{4,6},{5,7},{6,0},{7,1},{8,10},{9,11},{10,... | collective-permute-start | bytes 786440 | tf_op jit(solution)/shard_map/ppermute | solution.py:37
  91.2 22.1 %collective-permute-start.30 = (bf16[256,512]{1,0:T(8,128)(2,1)S(1)}, bf16[256,512]{1,0:T(8,128)(2,1)S(1)}, u32[]{:S(2)}, u32[]{:S(2)}) collective-permute-start(bf16[256,512]{1,0:T(8,128)(2,1)S(1)} %add_convert_fusion), channel_id=1, source_target_pairs={{0,6},{1,7},{2,0},{3,1},{4,2},{5,3},{6,4},{7,5},{8,14},{9,15},{10,... | collective-permute-start | bytes 786440 | tf_op jit(solution)/shard_map/ppermute | solution.py:37
  98.0 21.6 %collective-permute-start.26 = (bf16[256,512]{1,0:T(8,128)(2,1)S(1)}, bf16[256,512]{1,0:T(8,128)(2,1)S(1)}, u32[]{:S(2)}, u32[]{:S(2)}) collective-permute-start(bf16[256,512]{1,0:T(8,128)(2,1)S(1)} %add_convert_fusion.1), channel_id=1, source_target_pairs={{0,2},{1,3},{2,4},{3,5},{4,6},{5,7},{6,0},{7,1},{8,10},{9,11},{10,... | collective-permute-start | bytes 786440 | tf_op jit(solution)/shard_map/ppermute | solution.py:37

commit v6 on v5

--- a/solution.py
+++ b/solution.py
@@ -85,10 +85,6 @@
     return result.astype(BF16)
 
 
-def ends(rows):
-    return jnp.concatenate([rows[:8].astype(F32), rows[-8:].astype(F32)], 0).astype(BF16)
-
-
 def first_rows(taps, before, here):
     return short_filter(taps, before[8:].astype(F32), here[:8].astype(F32))
 
@@ -97,126 +93,164 @@
     return (gate_in.astype(F32) * values.astype(F32)).astype(BF16)
 
 
-def project(pairs, chip_ids, core, me, w_in, conv_taps, groups, total=None):
+def start_copies(copies):
+    for copy in copies:
+        copy.start()
+
+
+def wait_copies(copies):
+    for copy in copies:
+        copy.wait()
+
+
+def project_most(pairs, chip_ids, core, w_in):
     count = len(pairs)
     parts = [p for pair in pairs for block in pair for p in block]
     rows = sum(p.shape[0] for p in pairs[0][0])
+    half = rows // 2
     width = parts[0].shape[1]
     streams, _, out_width = w_in.shape
     depth = 2 * width
-    share = out_width // groups
-    split = share % 128 == 0
-    finish = total is not None
+    most = (count - 1) * depth
 
     def kernel(ids, w_ref, *refs):
         part_refs, refs = refs[: len(parts)], refs[len(parts) :]
-        if finish:
-            total_ref, taps_ref, gate_ref, ends_ref, refs = *refs[:4], refs[4:]
-            in_refs, refs = refs[: len(outs) - 2], refs[len(outs) - 2 :]
-            x, kept, sums, sums_ready = refs
-        else:
-            out_ref, x, w, w_ready = refs
+        top_ref, low_ref, x, far, w, x_ready, w_ready = refs
         s = pl.program_id(0)
 
-        def w_copy(t, j):
-            first = pl.multiple_of(ids[j] * depth, depth)
-            return pltpu.make_async_copy(
-                w_ref.at[t, pl.ds(first, depth)],
-                w.at[t, pl.ds(j * depth, depth)],
-                w_ready.at[t, j],
-            )
-
-        def sum_copy(t):
-            return pltpu.make_async_copy(total_ref.at[t], sums.at[t], sums_ready.at[t])
-
-        @pl.when(s == 0)
-        def _():
-            for t in range(streams):
-                if finish:
-                    sum_copy(t).start()
-                else:
-                    for j in range(count):
-                        w_copy(t, j).start()
+        def w_copies(t):
+            for j in range(count):
+                first = pl.multiple_of(ids[j] * depth, depth)
+                yield pltpu.make_async_copy(
+                    w_ref.at[t, pl.ds(first, depth)],
+                    w.at[t, j * depth : (j + 1) * depth],
+                    w_ready.at[t, j],
+                )
+
+        def x_copies():
             at = 0
             for j in range(count):
                 for block, side in ((pairs[j][0], ids[count]), (pairs[j][1], 1 - ids[count])):
-                    place = pl.ds(pl.multiple_of(j * depth + side * width, width), width)
                     row = 0
-                    for ref in part_refs[at : at + len(block)]:
-                        x[row : row + ref.shape[0], place] = ref[...]
-                        row += ref.shape[0]
-                    at += len(block)
-
-        if not finish:
-            for j in range(count):
-                w_copy(s, j).wait()
-            out_ref[0] = dot(x[...], w[s])
-            return
-        new = dot(x[...], w_ref[0])
-        sum_copy(s).wait()
-        rounded = (new + sums[s]).astype(BF16)
-        filtered = short_filter(taps_ref, jnp.zeros((8, out_width), F32), rounded.astype(F32))
-        kept[s, :rows] = filtered
-        kept[s, rows:] = ends(rounded)
-
-        @pl.when(s == streams - 1)
+                    base = j * depth if j < count - 1 else 0
+                    place = pl.ds(pl.multiple_of(base + side * width, width), width)
+                    for part in block:
+                        target = (x if j < count - 1 else far).at[row : row + part.shape[0], place]
+                        yield pltpu.make_async_copy(part_refs[at], target, x_ready.at[at])
+                        row += part.shape[0]
+                        at += 1
+
+        @pl.when(s == 0)
         def _():
-            gate_ref[...] = kept[0, :rows]
-            ends_ref[...] = kept[0, rows:]
-            kept[0, :rows] = gated(kept[1, :rows], kept[2, :rows])
-            for slot in range(groups if split else 1):
-                q = pl.multiple_of(partner(ids[count + 1], slot, groups) * share, share)
-                columns = pl.ds(q, share) if split else slice(None)
-                in_refs[slot][:rows] = kept[0, :rows, columns]
-                for t in range(1, streams):
-                    place = rows + (t - 1) * EDGE
-                    in_refs[slot][place : place + EDGE] = kept[t, rows:, columns]
-
-    in_specs = [whole(p.shape) for p in parts]
-    operands = [w_in] + parts
-    scratch = [pltpu.VMEM((rows, count * depth), BF16)]
-
-    def by_stream(extent):
-        return pl.BlockSpec((1, extent, out_width), lambda s, ids: (s, 0, 0))
-
-    if finish:
-        taps_spec = pl.BlockSpec((KERNEL, pl.squeezed, 1, out_width), lambda s, ids: (0, s, 0, 0))
-        in_specs = [by_stream(depth)] + in_specs + [anywhere(), taps_spec]
-        operands += [total, conv_taps]
-        longer = rows + (streams - 1) * EDGE
-        outs = [pltpu.HBM((rows, out_width), BF16), pltpu.HBM((EDGE, out_width), BF16)]
-        outs += [pltpu.HBM((longer, share if split else out_width), BF16)] * (groups if split else 1)
-        out_specs = [whole(o.shape) for o in outs]
-        scratch += [
-            pltpu.VMEM((streams, rows + EDGE, out_width), BF16),
-            pltpu.VMEM((streams, rows, out_width), F32),
-            pltpu.SemaphoreType.DMA((streams,)),
-        ]
-    else:
-        in_specs = [anywhere()] + in_specs
-        outs = [pltpu.HBM((streams, rows, out_width), F32)]
-        out_specs = [by_stream(rows)]
-        scratch += [
-            pltpu.VMEM((streams, count * depth, out_width), BF16),
+            start_copies(w_copies(0))
+            start_copies(x_copies())
+            for t in range(1, streams):
+                start_copies(w_copies(t))
+            wait_copies(x_copies())
+
+        wait_copies(w_copies(s))
+        total = dot(x[...], w[s, :most])
+        top_ref[0] = (total[:half] + dot(far[...], w[s, most:])).astype(BF16)
+        low_ref[0] = total[half:]
+
+    def by_stream():
+        return pl.BlockSpec((1, half, out_width), lambda s, ids: (s, 0, 0))
+
+    shape = (streams, half, out_width)
+    return call(
+        kernel,
+        (streams,),
+        jnp.stack(list(chip_ids) + [core]).astype(jnp.int32),
+        [w_in] + parts,
+        [anywhere()] * (1 + len(parts)),
+        [jax.ShapeDtypeStruct(shape, BF16), jax.ShapeDtypeStruct(shape, F32)],
+        [by_stream(), by_stream()],
+        [
+            pltpu.VMEM((rows, most), BF16),
+            pltpu.VMEM((half, depth), BF16),
+            pltpu.VMEM((streams, most + depth, out_width), BF16),
+            pltpu.SemaphoreType.DMA((len(parts),)),
             pltpu.SemaphoreType.DMA((streams, count)),
-        ]
+        ],
+        "project_most",
+        8,
+        24,
+    )
+
+
+def project_rest(pair, core, me, w_far, top, low, conv_taps, groups):
+    streams, half, out_width = top.shape
+    rows = 2 * half
+    width = pair[0].shape[1]
+    depth = 2 * width
+    share = out_width // groups
+    split = share % 128 == 0
+    order = list(range(1, streams)) + [0]
+
+    def kernel(at, own_ref, other_ref, w_ref, top_ref, low_ref, taps_ref, gate_ref, ends_ref, *refs):
+        in_refs, refs = refs[: len(ins)], refs[len(ins) :]
+        x, w, tops, lows, kept, x_ready, ready = refs
+
+        def x_copies():
+            for k, (ref, side) in enumerate(((own_ref, at[0]), (other_ref, 1 - at[0]))):
+                place = pl.ds(pl.multiple_of(side * width, width), width)
+                yield pltpu.make_async_copy(ref, x.at[:, place], x_ready.at[k])
+
+        def copies(t):
+            for k, (ref, target) in enumerate(((w_ref, w), (low_ref, lows), (top_ref, tops))):
+                yield pltpu.make_async_copy(ref.at[t], target.at[t], ready.at[t, k])
+
+        start_copies(x_copies())
+        for t in order:
+            start_copies(copies(t))
+        wait_copies(x_copies())
+        for t in order:
+            wait_copies(copies(t))
+            bottom = (dot(x[...], w[t]) + lows[t]).astype(BF16)
+            upper = tops[t]
+            taps = [taps_ref[lag, t] for lag in range(KERNEL)]
+            first = upper.astype(F32)
+            kept[t, :half] = short_filter(taps, jnp.zeros((8, out_width), F32), first)
+            kept[t, half:rows] = short_filter(taps, first[half - 8 :], bottom.astype(F32))
+            ends = jnp.concatenate([first[:8], bottom.astype(F32)[half - 8 :]], 0)
+            kept[t, rows:] = ends.astype(BF16)
+        gate_ref[...] = kept[0, :rows]
+        ends_ref[...] = kept[0, rows:]
+        kept[0, :rows] = gated(kept[1, :rows], kept[2, :rows])
+        for slot in range(len(ins)):
+            q = pl.multiple_of(partner(at[1], slot, groups) * share, share)
+            columns = pl.ds(q, share) if split else slice(None)
+            in_refs[slot][:rows] = kept[0, :rows, columns]
+            for t in range(1, streams):
+                place = rows + (t - 1) * EDGE
+                in_refs[slot][place : place + EDGE] = kept[t, rows:, columns]
+
+    longer = rows + (streams - 1) * EDGE
+    ins = [pltpu.HBM((longer, share if split else out_width), BF16)] * (groups if split else 1)
+    outs = [pltpu.HBM((rows, out_width), BF16), pltpu.HBM((EDGE, out_width), BF16)] + ins
     found = call(
         kernel,
-        (streams,),
-        jnp.stack(list(chip_ids) + [core, me]).astype(jnp.int32),
-        operands,
-        in_specs,
+        (1,),
+        jnp.stack([core, me]).astype(jnp.int32),
+        list(pair) + [w_far, top, low, conv_taps],
+        [anywhere()] * 5 + [whole(conv_taps.shape)],
         outs,
-        out_specs,
-        scratch,
-        "project",
-        4 if finish else 20,
-        16 if finish else 51,
-    )
-    if not finish:
-        return found[0]
-    gate, gate_ends, ins = found[0], found[1], list(found[2:])
-    return gate, gate_ends, (ins if split else by_slot(ins[0], groups, me))
+        [whole(o.shape) for o in outs],
+        [
+            pltpu.VMEM((half, depth), BF16),
+            pltpu.VMEM(w_far.shape, BF16),
+            pltpu.VMEM(top.shape, BF16),
+            pltpu.VMEM(low.shape, F32),
+            pltpu.VMEM((streams, rows + EDGE, out_width), BF16),
+            pltpu.SemaphoreType.DMA((2,)),
+            pltpu.SemaphoreType.DMA((streams, 3)),
+        ],
+        "project_rest",
+        1,
+        24,
+    )
+    gate, ends, ins = found[0], found[1], list(found[2:])
+    return gate, ends, (ins if split else by_slot(ins[0], groups, me))
 
 
 def by_slot(block, groups, me):
@@ -245,7 +279,7 @@
 
     def kernel(at, *refs):
         piece_refs, refs = refs[:groups], refs[groups:]
-        forward_ref, back_ref, out_ref, forward_out, back_out, padded = refs
+        forward_ref, out_ref, padded = refs
         row_ids = lax.broadcasted_iota(jnp.int32, (span, share), 0)
         for s in range(groups):
             k = source(at[0], s, groups)
@@ -260,17 +294,11 @@
 
         padded[span : 2 * span, 0:share] = jnp.zeros((span, share), BF16)
         out_ref[...] = dot(forward_ref[...], padded[...]).astype(BF16)
-        forward_out[...] = forward_ref[:, 0:span]
-        back_out[...] = back_ref[...]
 
     shape = (2 * span, groups * share)
-    outs = [
-        jax.ShapeDtypeStruct(shape, BF16),
-        jax.ShapeDtypeStruct((2 * span, span), BF16),
-        jax.ShapeDtypeStruct(back.shape, BF16),
-    ]
-    operands = list(pieces) + [forward, back]
-    return call(
+    outs = [pltpu.HBM(shape, BF16)]
+    operands = list(pieces) + [forward]
+    (spectra,) = call(
         kernel,
         (1,),
         me[None],
@@ -280,8 +308,9 @@
         [whole(o.shape) for o in outs],
         [pltpu.VMEM(shape, BF16)],
         "taps_spectra",
-        2,
-    )
+        20,
+    )
+    return spectra, None, back
 
 
 def long_filter(pieces, taps, spectra_taps, forward_in, back, skip, me):
@@ -555,6 +584,7 @@
     out_width = w_out.shape[1] // (2 * chips)
     forward_np, back_np = half_tables(span)
     forward, back = jnp.asarray(forward_np), jnp.asarray(back_np)
+    forward_in = jnp.asarray(np.ascontiguousarray(forward_np[:, :span]))
     w_streams = jnp.transpose(w_in, (1, 0, 2))
     short_taps = conv_taps.astype(F32)[:, :, None]
 
@@ -566,7 +596,10 @@
             stack, partner(me, s, groups), 0, keepdims=False
         )
 
-    tap_blocks = exchange(pick(split_taps))
+    spectra_taps = (taps_spectra if aligned else taps_spectra_plain)(
+        exchange(pick(split_taps)), forward, back, me
+    )[0]
+    tables = (spectra_taps,)
 
     def columns(w, parity):
         starts = [(2 * z + parity) * out_width for z in range(chips)]
@@ -579,53 +612,42 @@
     skip = jnp.tile(skip, groups)[None]
     share_taps = lax.dynamic_slice_in_dim(short_taps, me * share, share, 3)
 
-    found = [(0, [inputs])]
-    up = [inputs[:half], inputs[half:]]
+    def both(blocks):
+        return blocks, [sibling(b) for b in blocks]
+
+    found = [(0, [inputs], [sibling(inputs)])]
+    upper = inputs[:half]
+    up = [upper, after(inputs, upper)[half:]]
     down = list(up)
     for d in range(1, reach):
-        up_top, down_low = shift(up[0], "chan", 2), shift(down[1], "chan", -2)
-        up_low, down_top = shift(up[1], "chan", 2), shift(down[0], "chan", -2)
-        if d == reach - 1:
-            up_top, down_low, tap_blocks, w_given, w_far, skip, share_taps = lax.optimization_barrier(
-                (up_top, down_low, tap_blocks, w_given, w_far, skip, share_taps)
-            )
-        up, down = [up_top, up_low], [down_top, down_low]
-        found += [(d, up), (-d, down)]
-    far = [shift(up[0], "chan", 2), shift(down[1], "chan", -2)]
-
-    def both(blocks):
-        return blocks, [sibling(b) for b in blocks]
-
-    def added(blocks, w, total=None):
-        return project(
-            [both(b) for _, b in blocks],
-            [(chip - d) % chips for d, _ in blocks],
-            core,
-            me,
-            w,
-            short_taps,
-            groups,
-            total,
-        )
-
-    total = added(found, w_streams)
-    far = [after(f, total) for f in far]
-    gate, gate_ends, pieces = added([(reach, far)], w_far, total)
+        up = [shift(u, "chan", 2) for u in up]
+        down = [shift(u, "chan", -2) for u in down]
+        found += [(d, *both(up)), (-d, *both(down))]
+    far_top = shift(up[0], "chan", 2)
+    far_low = shift(down[1], "chan", -2)
+    found.append((reach, *both([far_top])))
+    found[0] = (0, [after(inputs, w_given, w_far, skip, share_taps, *tables)], found[0][2])
+    top, low = project_most(
+        [(mine, theirs) for _, mine, theirs in found],
+        [(chip - d) % chips for d, _, _ in found],
+        core,
+        w_streams,
+    )
+    far_low = after(far_low, low)
+    gate, gate_ends, pieces = project_rest(
+        (far_low, sibling(far_low)), core, me, w_far, top, low, short_taps, groups
+    )
 
     pieces_in = exchange(lambda s: pieces[s])
-    before = shift(gate_ends, "ctx", 1)
+    before = shift(after(gate_ends, pieces_in[-1]), "ctx", 1)
     before = jnp.where(me > 0, before, jnp.zeros_like(before))
 
-    tap_blocks = [after(t, before) for t in tap_blocks]
-    spectra_taps, forward_in, back = (taps_spectra if aligned else taps_spectra_plain)(
-        tap_blocks, forward, back, me
-    )
-    w_own = columns(after(w_out, spectra_taps), core)
+    w_own = columns(after(w_out, gate), core)
 
     w_other = sibling(after(w_given, gate))
 
     filtered = (long_filter if aligned else long_filter_plain)(
-        pieces_in, share_taps, spectra_taps, forward_in, back, after(skip, w_own), me
+        pieces_in, share_taps, *tables, forward_in, back, after(skip, w_own), me
     )
     filtered = lax.optimization_barrier((list(filtered), w_other))[0]
     gated_out = (gate_blocks if aligned else gate_blocks_plain)(

time: 121 us -> 117 us (0.967)
  Pallas kernels: 28 us -> 22.7 us
  local copies, waits for them, and re-layouts: 13 us -> 9.96 us
  waiting for transfers between devices: 44.2 us -> 47.1 us
  starting transfers between devices: 32.8 us -> 34.4 us
    unnamed x22 -> x24, local copies, waits for them, and re-layouts: 5.61 us -> 0.05 us
    pallas_call x8, Pallas kernels: 28 us -> 22.7 us  [call(): pl.pallas_call(kernel, grid_spec=pltpu.PrefetchScalarGridSpec(num_scalar_...]
    ppermute x9, waiting for transfers between devices: 5.57 us -> 10.6 us  [send(): return lax.ppermute(piece(slot), 'ctx', route)]
    dynamic_slice x2, local copies, waits for them, and re-layouts: 0.49 us -> 3.66 us  [columns(): lax.dynamic_slice_in_dim(w, c, out_width, 1)]
    ppermute x9, starting transfers between devices: 10.5 us -> 13.1 us  [send(): return lax.ppermute(piece(slot), 'ctx', route)]
    ppermute x13, waiting for transfers between devices: 34.9 us -> 33.1 us  [shift(): lax.ppermute(x, axis, [(i, (i + distance) % size) for i in range(size)])]
    ppermute x13, starting transfers between devices: 21.4 us -> 19.9 us  [shift(): lax.ppermute(x, axis, [(i, (i + distance) % size) for i in range(size)])]
  transfers between devices with their start and end apart: 31 -> 31, of which waited for: 14 -> 13; matrix products, arithmetic and copies ran while one was open for 6% -> 10% of each run, Pallas kernels for 16% -> 14%
where the time goes in v6:
time: 117 us
  waiting for transfers between devices  47.1 us (40%)
  starting transfers between devices  34.4 us (29%)
  Pallas kernels  22.7 us (19%)
  local copies, waits for them, and re-layouts  9.96 us (9%)
  other arithmetic  2.33 us (2%)
    ppermute x13, waiting for transfers between devices, shift(): lax.ppermute(x, axis, [(i, (i + distance) % size) for i in range(size)])  33.1 us
    pallas_call x8, Pallas kernels, call(): pl.pallas_call(kernel, grid_spec=pltpu.PrefetchScalarGridSpec(num_scalar_...  22.7 us
    ppermute x13, starting transfers between devices, shift(): lax.ppermute(x, axis, [(i, (i + distance) % size) for i in range(size)])  19.9 us
    ppermute x9, starting transfers between devices, send(): return lax.ppermute(piece(slot), 'ctx', route)  13.1 us
    ppermute x9, waiting for transfers between devices, send(): return lax.ppermute(piece(slot), 'ctx', route)  10.6 us
    dynamic_slice x2, local copies, waits for them, and re-layouts, columns(): lax.dynamic_slice_in_dim(w, c, out_width, 1)  3.66 us
    ppermute x9, waiting for transfers between devices, sibling(): lax.ppermute(x, 'chan', [(i, i ^ 1) for i in range(lax.axis_size('chan'))])  3.34 us
  transfers between devices with their start and end apart: 31, of which 13 were waited for; matrix products, arithmetic and copies ran while one was open for 10% of the time, Pallas kernels for 14%

profile of v6, /device:TPU:0, one launch (start us, length us, event | category | flops | bytes accessed | tf_op | source)
XLA Modules:
  0.0 116.7 jit_solution(17384795229820034778)
XLA Ops:
  0.0 1.0 slice.18
  1.0 3.1 %collective-permute-start.6 = (bf16[256,512]{1,0:T(8,128)(2,1)S(1)}, bf16[256,512]{1,0:T(8,128)(2,1)S(1)}, u32[]{:S(2)}, u32[]{:S(2)}) collective-permute-start(bf16[256,512]{1,0:T(8,128)(2,1)S(1)} %slice.18), channel_id=1, source_target_pairs={{0,2},{1,3},{2,4},{3,5},{4,6},{5,7},{6,0},{7,1},{8,10},{9,11},{10,... | collective-permute-start | bytes 786440 | tf_op jit(solution)/shard_map/ppermute | solution.py:37
  4.0 1.0 slice.19
  5.0 2.1 %collective-permute-start = (bf16[256,512]{1,0:T(8,128)(2,1)S(1)}, bf16[256,512]{1,0:T(8,128)(2,1)S(1)}, u32[]{:S(2)}, u32[]{:S(2)}) collective-permute-start(bf16[256,512]{1,0:T(8,128)(2,1)S(1)} %slice.19), channel_id=1, source_target_pairs={{0,6},{1,7},{2,0},{3,1},{4,2},{5,3},{6,4},{7,5},{8,14},{9,15},{10,... | collective-permute-start | bytes 786440 | tf_op jit(solution)/shard_map/ppermute | solution.py:37
  7.1 0.0 collective-permute-start.7
  7.1 1.1 slice_bitcast_fusion.3
  8.3 0.1 pad_maximum_fusion.2
  8.4 1.8 %collective-permute-start.2 = (bf16[512,128]{1,0:T(8,128)(2,1)S(1)}, bf16[512,128]{1,0:T(8,128)(2,1)S(1)}, u32[]{:S(2)}, u32[]{:S(2)}) collective-permute-start(bf16[512,128]{1,0:T(8,128)(2,1)S(1)} %get-tuple-element.75), channel_id=1, source_target_pairs={{0,8},{8,0},{16,24},{24,16},{1,9},{9,1},{17,25},{25,17},{2,10},{10... | collective-permute-start | bytes 393224 | tf_op jit(solution)/shard_map/ppermute | solution.py:507
  10.2 1.5 %collective-permute-start.3 = (bf16[512,128]{1,0:T(8,128)(2,1)S(1)}, bf16[512,128]{1,0:T(8,128)(2,1)S(1)}, u32[]{:S(2)}, u32[]{:S(2)}) collective-permute-start(bf16[512,128]{1,0:T(8,128)(2,1)S(1)} %get-tuple-element.74), channel_id=1, source_target_pairs={{0,16},{8,24},{16,0},{24,8},{1,17},{9,25},{17,1},{25,9},{2,18},{10... | collective-permute-start | bytes 393224 | tf_op jit(solution)/shard_map/ppermute | solution.py:507
  11.7 1.7 %constant_dynamic-slice_fusion.8 = (bf16[512,512]{1,0:T(8,128)(2,1)S(1)}, bf16[512,512]{1,0:T(8,128)(2,1)S(1)}, bf16[512,512]{1,0:T(8,128)(2,1)S(1)}, bf16[512,512]{1,0:T(8,128)(2,1)S(1)}) fusion(bf16[512,4096]{1,0:T(8,128)(2,1)} %param.14, s32[]{:T(128)S(6)} %select_n.97, s32[]{:T(128)S(6)} %select_n.99, s32[]{:T(128)S(6)} %select_n.98, s32[]{:T(128)S(6)} %select_n.100), kind=kLoop, calls=%fused_computation.23 | loop fusion | bytes 4194320 | tf_op jit(solution)/shard_map/dynamic_slice | solution.py:606
  13.4 1.6 %pad_maximum_fusion = bf16[512,2048]{1,0:T(8,128)(2,1)} fusion(bf16[512,512]{1,0:T(8,128)(2,1)S(1)} %get-tuple-element.72, bf16[512,512]{1,0:T(8,128)(2,1)S(1)} %get-tuple-element.70, bf16[512,512]{1,0:T(8,128)(2,1)S(1)} %get-tuple-element.71, bf16[512,512]{1,0:T(8,128)(2,1)S(1)} %get-tuple-element.69), kind=kLoop, calls=%fused_computation.1 | loop fusion | flops 8388608 | bytes 4194304 | tf_op jit(solution)/shard_map/concatenate | solution.py:606
  15.0 3.9 %collective-permute-start.10 = (bf16[256,512]{1,0:T(8,128)(2,1)S(1)}, bf16[256,512]{1,0:T(8,128)(2,1)S(1)}, u32[]{:S(2)}, u32[]{:S(2)}) collective-permute-start(bf16[256,512]{1,0:T(8,128)(2,1)S(1)} %slice.18), channel_id=1, source_target_pairs={{0,6},{1,7},{2,0},{3,1},{4,2},{5,3},{6,4},{7,5},{8,14},{9,15},{10,... | collective-permute-start | bytes 786440 | tf_op jit(solution)/shard_map/ppermute | solution.py:37
  18.9 0.0 collective-permute-done.refs_7_
  18.9 0.1 collective-permute-start.12
  19.0 0.8 dynamic_slice.51
  19.8 0.1 stack.54.ids
  19.9 2.7 %collective-permute-start.4 = (bf16[512,128]{1,0:T(8,128)(2,1)S(1)}, bf16[512,128]{1,0:T(8,128)(2,1)S(1)}, u32[]{:S(2)}, u32[]{:S(2)}) collective-permute-start(bf16[512,128]{1,0:T(8,128)(2,1)S(1)} %get-tuple-element.73), channel_id=1, source_target_pairs={{0,24},{8,16},{16,8},{24,0},{1,25},{9,17},{17,9},{25,1},{2,26},{10... | collective-permute-start | bytes 393224 | tf_op jit(solution)/shard_map/ppermute | solution.py:507
  22.5 2.2 %dynamic-slice_bitcast_fusion.w_ref = bf16[3,1024,512]{2,1,0:T(8,128)(2,1)S(1)} fusion(bf16[4096,3,512]{2,0,1:T(8,128)(2,1)} %param.10, s32[]{:T(128)S(6)} %select_n.102), kind=kLoop, calls=%fused_computation | loop fusion | bytes 6291460 | tf_op jit(solution)/shard_map/dynamic_slice | solution.py:609
  24.8 1.9 %collective-permute-done.4.refs_3_ = bf16[512,128]{1,0:T(8,128)(2,1)S(1)} collective-permute-done((bf16[512,128]{1,0:T(8,128)(2,1)S(1)}, bf16[512,128]{1,0:T(8,128)(2,1)S(1)}, u32[]{:S(2)}, u32[]{:S(2)}) %collective-permute-start.4) | collective-permute-done | bytes 131104 | tf_op jit(solution)/shard_map/ppermute | solution.py:507
  26.7 0.5 collective-permute-start.8
  27.2 2.7 %collective-permute-done.10.refs_6_ = bf16[256,512]{1,0:T(8,128)(2,1)S(1)} collective-permute-done((bf16[256,512]{1,0:T(8,128)(2,1)S(1)}, bf16[256,512]{1,0:T(8,128)(2,1)S(1)}, u32[]{:S(2)}, u32[]{:S(2)}) %collective-permute-start.10) | collective-permute-done | bytes 262176 | tf_op jit(solution)/shard_map/ppermute | solution.py:37
  30.0 5.0 %collective-permute-done.13.refs_10_ = bf16[256,512]{1,0:T(8,128)(2,1)S(1)} collective-permute-done((bf16[256,512]{1,0:T(8,128)(2,1)S(1)}, bf16[256,512]{1,0:T(8,128)(2,1)S(1)}, u32[]{:S(2)}, u32[]{:S(2)}) %collective-permute-start.13) | collective-permute-done | bytes 262176 | tf_op jit(solution)/shard_map/ppermute | solution.py:37
  34.9 0.5 collective-permute-start.14
  35.5 2.4 %taps_spectra.1.refs_5_ = bf16[1024,512]{1,0:T(8,128)(2,1)} custom-call(s32[1]{0:T(128)} %bitcast.3.at, bf16[512,128]{1,0:T(8,128)(2,1)S(1)} %get-tuple-element.76.refs_0_, bf16[512,128]{1,0:T(8,128)(2,1)S(1)} %collective-permute-done.2.refs_1_, bf16[512,128]{1,0:T(8,128)(2,1)S(1)} %collective-permute-done.3.refs_2_, ...), custom_call_target="tpu_custom_call" | custom-call | flops 20000000000 | bytes 20971520 | tf_op jit(solution)/shard_map/taps_spectra/pallas_call | solution.py:61
  37.8 1.6 %collective-permute-start.1 = (bf16[256,512]{1,0:T(8,128)(2,1)S(1)}, bf16[256,512]{1,0:T(8,128)(2,1)S(1)}, u32[]{:S(2)}, u32[]{:S(2)}) collective-permute-start(bf16[256,512]{1,0:T(8,128)(2,1)S(1)} %collective-permute-done.refs_7_), channel_id=1, source_target_pairs={{0,6},{1,7},{2,0},{3,1},{4,2},{5,3},{6,4},{7,5},{8,14},{9,15},{10,... | collective-permute-start | bytes 786440 | tf_op jit(solution)/shard_map/ppermute | solution.py:37
  39.5 8.3 %project_most.1 = (bf16[3,256,512]{2,1,0:T(8,128)(2,1)S(1)}, f32[3,256,512]{2,1,0:T(8,128)S(1)}) custom-call(s32[5]{0:T(128)S(1)} %stack.54.ids, bf16[3,4096,512]{2,1,0:T(8,128)(2,1)S(1)} %bitcast.29, bf16[512,512]{1,0:T(8,128)(2,1)S(1)} %copy-done, bf16[512,512]{1,0:T(8,128)(2,1)S(1)} %collective-permute-done.5.refs_1_, ...), custom_call_target="tpu_custom_call" | custom-call | flops 8000000000 | bytes 8388608 | tf_op jit(solution)/shard_map/project_most/pallas_call | solution.py:61
  47.8 0.1 collective-permute-start.15
  47.9 0.1 pad_add_fusion.1.at
  48.0 1.4 %collective-permute-done.15.other_ref = bf16[256,512]{1,0:T(8,128)(2,1)S(1)} collective-permute-done((bf16[256,512]{1,0:T(8,128)(2,1)S(1)}, bf16[256,512]{1,0:T(8,128)(2,1)S(1)}, u32[]{:S(2)}, u32[]{:S(2)}) %collective-permute-start.15) | collective-permute-done | bytes 262176 | tf_op jit(solution)/shard_map/ppermute | solution.py:41
  49.4 4.3 %project_rest.1 = (bf16[512,512]{1,0:T(8,128)(2,1)}, bf16[16,512]{1,0:T(8,128)(2,1)}, bf16[544,128]{1,0:T(8,128)(2,1)}, bf16[544,128]{1,0:T(8,128)(2,1)}, bf16[5...) custom-call(s32[2]{0:T(128)S(1)} %pad_add_fusion.1.at, bf16[256,512]{1,0:T(8,128)(2,1)S(1)} %collective-permute-done.1.own_ref, ...), custom_call_target="tpu_custom_call" | custom-call | flops 1000000000 | bytes 1048576 | tf_op jit(solution)/shard_map/project_rest/pallas_call | solution.py:61
  53.8 0.2 collective-permute-start.20
  54.0 2.5 %collective-permute-start.16 = (bf16[544,128]{1,0:T(8,128)(2,1)}, bf16[544,128]{1,0:T(8,128)(2,1)S(1)}, u32[]{:S(2)}, u32[]{:S(2)}) collective-permute-start(bf16[544,128]{1,0:T(8,128)(2,1)} %get-tuple-element.42), channel_id=1, source_target_pairs={{0,24},{8,16},{16,8},{24,0},{1,25},{9,17},{17,9},{25,1},{2,26},{10... | collective-permute-start | bytes 417800 | tf_op jit(solution)/shard_map/ppermute | solution.py:507
  56.4 0.5 collective-permute-start.18
  57.0 0.6 collective-permute-start.19
  57.6 2.0 %constant_dynamic-slice_fusion.3 = (bf16[512,512]{1,0:T(8,128)(2,1)S(1)}, bf16[512,512]{1,0:T(8,128)(2,1)S(1)}, bf16[512,512]{1,0:T(8,128)(2,1)S(1)}, bf16[512,512]{1,0:T(8,128)(2,1)S(1)}) fusion(bf16[512,4096]{1,0:T(8,128)(2,1)} %param.14, s32[]{:T(128)S(6)} %select_n.110, s32[]{:T(128)S(6)} %select_n.113, s32[]{:T(128)S(6)} %select_n.112, s32[]{:T(128)S(6)} %select_n.111), kind=kLoop, calls=%fused_computation.18 | loop fusion | bytes 4194320 | tf_op jit(solution)/shard_map/dynamic_slice | solution.py:606
  59.5 0.3 pad_maximum_fusion.1.w_ref
  59.8 1.7 %collective-permute-done.16.refs_3_ = bf16[544,128]{1,0:T(8,128)(2,1)S(1)} collective-permute-done((bf16[544,128]{1,0:T(8,128)(2,1)}, bf16[544,128]{1,0:T(8,128)(2,1)S(1)}, u32[]{:S(2)}, u32[]{:S(2)}) %collective-permute-start.16) | collective-permute-done | bytes 139296 | tf_op jit(solution)/shard_map/ppermute | solution.py:507
  61.6 1.5 %collective-permute-start.17 = (bf16[16,512]{1,0:T(8,128)(2,1)S(1)}, bf16[16,512]{1,0:T(8,128)(2,1)S(1)}, u32[]{:S(2)}, u32[]{:S(2)}) collective-permute-start(bf16[16,512]{1,0:T(8,128)(2,1)S(1)} %copy-done.3), channel_id=1, source_target_pairs={{0,8},{8,16},{16,24},{24,0},{1,9},{9,17},{17,25},{25,1},{2,10},{10... | collective-permute-start | bytes 49160 | tf_op jit(solution)/shard_map/ppermute | solution.py:37
  63.1 1.0 collective-permute-done.18.refs_1_
  64.1 0.0 copy-start.1
  64.1 2.6 %long_filter.1 = (bf16[512,128]{1,0:T(8,128)(2,1)S(1)}, bf16[512,128]{1,0:T(8,128)(2,1)S(1)}, bf16[512,128]{1,0:T(8,128)(2,1)S(1)}, bf16[512,128]{1,0:T(8,128)(2,1)S(1)}) custom-call(s32[1]{0:T(128)} %bitcast.3.at, bf16[544,128]{1,0:T(8,128)(2,1)S(1)} %copy-done.2, bf16[544,128]{1,0:T(8,128)(2,1)S(1)} %collective-permute-done.18.refs_1_, ...), custom_call_target="tpu_custom_call" | custom-call | flops 3000000000 | bytes 3145728 | tf_op jit(solution)/shard_map/long_filter/pallas_call | solution.py:61
  66.8 1.7 %collective-permute-start.21 = (bf16[512,128]{1,0:T(8,128)(2,1)S(1)}, bf16[512,128]{1,0:T(8,128)(2,1)S(1)}, u32[]{:S(2)}, u32[]{:S(2)}) collective-permute-start(bf16[512,128]{1,0:T(8,128)(2,1)S(1)} %get-tuple-element.55), channel_id=1, source_target_pairs={{0,8},{8,0},{16,24},{24,16},{1,9},{9,1},{17,25},{25,17},{2,10},{10... | collective-permute-start | bytes 393224 | tf_op jit(solution)/shard_map/ppermute | solution.py:507
  68.5 1.2 %collective-permute-start.22 = (bf16[512,128]{1,0:T(8,128)(2,1)S(1)}, bf16[512,128]{1,0:T(8,128)(2,1)S(1)}, u32[]{:S(2)}, u32[]{:S(2)}) collective-permute-start(bf16[512,128]{1,0:T(8,128)(2,1)S(1)} %get-tuple-element.56), channel_id=1, source_target_pairs={{0,16},{8,24},{16,0},{24,8},{1,17},{9,25},{17,1},{25,9},{2,18},{10... | collective-permute-start | bytes 393224 | tf_op jit(solution)/shard_map/ppermute | solution.py:507
  69.8 0.6 collective-permute-start.23
  70.4 2.1 %collective-permute-done.21.refs_1_ = bf16[512,128]{1,0:T(8,128)(2,1)S(1)} collective-permute-done((bf16[512,128]{1,0:T(8,128)(2,1)S(1)}, bf16[512,128]{1,0:T(8,128)(2,1)S(1)}, u32[]{:S(2)}, u32[]{:S(2)}) %collective-permute-start.21) | collective-permute-done | bytes 131104 | tf_op jit(solution)/shard_map/ppermute | solution.py:507
  72.5 3.8 %collective-permute-done.22.refs_2_ = bf16[512,128]{1,0:T(8,128)(2,1)S(1)} collective-permute-done((bf16[512,128]{1,0:T(8,128)(2,1)S(1)}, bf16[512,128]{1,0:T(8,128)(2,1)S(1)}, u32[]{:S(2)}, u32[]{:S(2)}) %collective-permute-start.22) | collective-permute-done | bytes 131104 | tf_op jit(solution)/shard_map/ppermute | solution.py:507
  76.3 0.2 gate_blocks.1.a_ref
  76.6 0.1 collective-permute-start.24
  76.6 1.9 %collective-permute-done.24.b_ref = bf16[512,512]{1,0:T(8,128)(2,1)S(1)} collective-permute-done((bf16[512,512]{1,0:T(8,128)(2,1)S(1)}, bf16[512,512]{1,0:T(8,128)(2,1)S(1)}, u32[]{:S(2)}, u32[]{:S(2)}) %collective-permute-start.24) | collective-permute-done | bytes 524320 | tf_op jit(solution)/shard_map/ppermute | solution.py:41
  78.5 0.7 output_shares.3
  79.2 1.7 %collective-permute-start.29 = (bf16[256,512]{1,0:T(8,128)(2,1)S(1)}, bf16[256,512]{1,0:T(8,128)(2,1)S(1)}, u32[]{:S(2)}, u32[]{:S(2)}) collective-permute-start(bf16[256,512]{1,0:T(8,128)(2,1)S(1)} %get-tuple-element.63), channel_id=1, source_target_pairs={{0,6},{1,7},{2,0},{3,1},{4,2},{5,3},{6,4},{7,5},{8,14},{9,15},{10,... | collective-permute-start | bytes 786440 | tf_op jit(solution)/shard_map/ppermute | solution.py:37
  80.9 0.1 pad_add_fusion._
  81.0 0.4 collective-permute-start.25
  81.4 3.2 %output_shares.2 = (f32[256,512]{1,0:T(8,128)S(1)}, bf16[256,512]{1,0:T(8,128)(2,1)S(1)}, bf16[256,512]{1,0:T(8,128)(2,1)S(1)}, f32[256,512]{1,0:T(8,128)S(1)}, f32[512,512]{1,0:T(8,128)S(1)}) custom-call(s32[3]{0:T(128)S(1)} %pad_add_fusion._, bf16[512,512]{1,0:T(8,128)(2,1)S(1)} %gate_blocks.1.a_ref, bf16[512,512]{1,0:T(8,128)(2,1)S(1)} %collective-permute-done.24.b_ref, ...), custom_call_target="tpu_custom_call" | custom-call | flops 1000000000 | bytes 1048576 | tf_op jit(solution)/shard_map/output_shares/pallas_call | solution.py:61
  84.6 3.5 %collective-permute-start.27 = (bf16[256,512]{1,0:T(8,128)(2,1)S(1)}, bf16[256,512]{1,0:T(8,128)(2,1)S(1)}, u32[]{:S(2)}, u32[]{:S(2)}) collective-permute-start(bf16[256,512]{1,0:T(8,128)(2,1)S(1)} %get-tuple-element.61), channel_id=1, source_target_pairs={{0,6},{1,7},{2,0},{3,1},{4,2},{5,3},{6,4},{7,5},{8,14},{9,15},{10,... | collective-permute-start | bytes 786440 | tf_op jit(solution)/shard_map/ppermute | solution.py:37
  88.1 6.0 %collective-permute-done.29 = bf16[256,512]{1,0:T(8,128)(2,1)S(1)} collective-permute-done((bf16[256,512]{1,0:T(8,128)(2,1)S(1)}, bf16[256,512]{1,0:T(8,128)(2,1)S(1)}, u32[]{:S(2)}, u32[]{:S(2)}) %collective-permute-start.29) | collective-permute-done | bytes 262176 | tf_op jit(solution)/shard_map/ppermute | solution.py:37
  94.1 0.1 add_convert_fusion
  94.2 0.1 collective-permute-start.30
  94.2 0.1 add_convert_fusion.1
  94.3 2.1 %collective-permute-start.26 = (bf16[256,512]{1,0:T(8,128)(2,1)S(1)}, bf16[256,512]{1,0:T(8,128)(2,1)S(1)}, u32[]{:S(2)}, u32[]{:S(2)}) collective-permute-start(bf16[256,512]{1,0:T(8,128)(2,1)S(1)} %add_convert_fusion.1), channel_id=1, source_target_pairs={{0,2},{1,3},{2,4},{3,5},{4,6},{5,7},{6,0},{7,1},{8,10},{9,11},{10,... | collective-permute-start | bytes 786440 | tf_op jit(solution)/shard_map/ppermute | solution.py:37
  96.4 8.9 %collective-permute-done.27.refs_1_ = bf16[256,512]{1,0:T(8,128)(2,1)S(1)} collective-permute-done((bf16[256,512]{1,0:T(8,128)(2,1)S(1)}, bf16[256,512]{1,0:T(8,128)(2,1)S(1)}, u32[]{:S(2)}, u32[]{:S(2)}) %collective-permute-start.27) | collective-permute-done | bytes 262176 | tf_op jit(solution)/shard_map/ppermute | solution.py:37
  105.3 5.5 %collective-permute-done.30.refs_3_ = bf16[256,512]{1,0:T(8,128)(2,1)S(1)} collective-permute-done((bf16[256,512]{1,0:T(8,128)(2,1)S(1)}, bf16[256,512]{1,0:T(8,128)(2,1)S(1)}, u32[]{:S(2)}, u32[]{:S(2)}) %collective-permute-start.30) | collective-permute-done | bytes 262176 | tf_op jit(solution)/shard_map/ppermute | solution.py:37
  110.8 4.9 %collective-permute-done.26.refs_0_ = bf16[256,512]{1,0:T(8,128)(2,1)S(1)} collective-permute-done((bf16[256,512]{1,0:T(8,128)(2,1)S(1)}, bf16[256,512]{1,0:T(8,128)(2,1)S(1)}, u32[]{:S(2)}, u32[]{:S(2)}) %collective-permute-start.26) | collective-permute-done | bytes 262176 | tf_op jit(solution)/shard_map/ppermute | solution.py:37
  115.7 1.0 add_up.1
  (53 shorter events, 0.2 us)
Async XLA Ops:
  1.0 17.9 %collective-permute-start.6 = (bf16[256,512]{1,0:T(8,128)(2,1)S(1)}, bf16[256,512]{1,0:T(8,128)(2,1)S(1)}, u32[]{:S(2)}, u32[]{:S(2)}) collective-permute-start(bf16[256,512]{1,0:T(8,128)(2,1)S(1)} %slice.18), channel_id=1, source_target_pairs={{0,2},{1,3},{2,4},{3,5},{4,6},{5,7},{6,0},{7,1},{8,10},{9,11},{10,... | collective-permute-start | bytes 786440 | tf_op jit(solution)/shard_map/ppermute | solution.py:37
  5.0 13.9 %collective-permute-start = (bf16[256,512]{1,0:T(8,128)(2,1)S(1)}, bf16[256,512]{1,0:T(8,128)(2,1)S(1)}, u32[]{:S(2)}, u32[]{:S(2)}) collective-permute-start(bf16[256,512]{1,0:T(8,128)(2,1)S(1)} %slice.19), channel_id=1, source_target_pairs={{0,6},{1,7},{2,0},{3,1},{4,2},{5,3},{6,4},{7,5},{8,14},{9,15},{10,... | collective-permute-start | bytes 786440 | tf_op jit(solution)/shard_map/ppermute | solution.py:37
  7.1 19.6 %collective-permute-start.7 = (bf16[256,512]{1,0:T(8,128)(2,1)S(1)}, bf16[256,512]{1,0:T(8,128)(2,1)S(1)}, u32[]{:S(2)}, u32[]{:S(2)}) collective-permute-start(bf16[256,512]{1,0:T(8,128)(2,1)S(1)} %slice.19), channel_id=1, source_target_pairs={{0,2},{1,3},{2,4},{3,5},{4,6},{5,7},{6,0},{7,1},{8,10},{9,11},{10,... | collective-permute-start | bytes 786440 | tf_op jit(solution)/shard_map/ppermute | solution.py:37
  8.4 6.6 %collective-permute-start.2 = (bf16[512,128]{1,0:T(8,128)(2,1)S(1)}, bf16[512,128]{1,0:T(8,128)(2,1)S(1)}, u32[]{:S(2)}, u32[]{:S(2)}) collective-permute-start(bf16[512,128]{1,0:T(8,128)(2,1)S(1)} %get-tuple-element.75), channel_id=1, source_target_pairs={{0,8},{8,0},{16,24},{24,16},{1,9},{9,1},{17,25},{25,17},{2,10},{10... | collective-permute-start | bytes 393224 | tf_op jit(solution)/shard_map/ppermute | solution.py:507
  10.2 9.7 %collective-permute-start.3 = (bf16[512,128]{1,0:T(8,128)(2,1)S(1)}, bf16[512,128]{1,0:T(8,128)(2,1)S(1)}, u32[]{:S(2)}, u32[]{:S(2)}) collective-permute-start(bf16[512,128]{1,0:T(8,128)(2,1)S(1)} %get-tuple-element.74), channel_id=1, source_target_pairs={{0,16},{8,24},{16,0},{24,8},{1,17},{9,25},{17,1},{25,9},{2,18},{10... | collective-permute-start | bytes 393224 | tf_op jit(solution)/shard_map/ppermute | solution.py:507
  11.7 3.3 %copy-start.8 = (bf16[3,3,512]{2,1,0:T(4,128)(2,1)S(1)}, bf16[3,3,512]{2,1,0:T(4,128)(2,1)}, u32[]{:S(2)}) copy-start(bf16[3,3,512]{2,1,0:T(4,128)(2,1)} %param.11) | copy-start | bytes 27652
  15.0 11.7 %copy-start = (bf16[512,512]{1,0:T(8,128)(2,1)S(1)}, bf16[512,512]{1,0:T(8,128)(2,1)}, u32[]{:S(2)}) copy-start(bf16[512,512]{1,0:T(8,128)(2,1)} %refs_0_) | copy-start | bytes 1572868
  15.0 14.9 %collective-permute-start.10 = (bf16[256,512]{1,0:T(8,128)(2,1)S(1)}, bf16[256,512]{1,0:T(8,128)(2,1)S(1)}, u32[]{:S(2)}, u32[]{:S(2)}) collective-permute-start(bf16[256,512]{1,0:T(8,128)(2,1)S(1)} %slice.18), channel_id=1, source_target_pairs={{0,6},{1,7},{2,0},{3,1},{4,2},{5,3},{6,4},{7,5},{8,14},{9,15},{10,... | collective-permute-start | bytes 786440 | tf_op jit(solution)/shard_map/ppermute | solution.py:37
  18.9 16.0 %collective-permute-start.13 = (bf16[256,512]{1,0:T(8,128)(2,1)S(1)}, bf16[256,512]{1,0:T(8,128)(2,1)S(1)}, u32[]{:S(2)}, u32[]{:S(2)}) collective-permute-start(bf16[256,512]{1,0:T(8,128)(2,1)S(1)} %collective-permute-done.6.refs_2_), channel_id=1, source_target_pairs={{0,2},{1,3},{2,4},{3,5},{4,6},{5,7},{6,0},{7,1},{8,10},{9,11},{10,... | collective-permute-start | bytes 786440 | tf_op jit(solution)/shard_map/ppermute | solution.py:37
  18.9 16.0 %collective-permute-start.12 = (bf16[256,512]{1,0:T(8,128)(2,1)S(1)}, bf16[256,512]{1,0:T(8,128)(2,1)S(1)}, u32[]{:S(2)}, u32[]{:S(2)}) collective-permute-start(bf16[256,512]{1,0:T(8,128)(2,1)S(1)} %collective-permute-done.refs_7_), channel_id=1, source_target_pairs={{0,1},{1,0},{2,3},{3,2},{4,5},{5,4},{6,7},{7,6},{8,9},{9,8},{10,11... | collective-permute-start | bytes 786440 | tf_op jit(solution)/shard_map/ppermute | solution.py:41
  19.9 15.6 %copy-start.4 = (bf16[1024,1024]{1,0:T(8,128)(2,1)S(1)}, bf16[1024,1024]{1,0:T(8,128)(2,1)}, u32[]{:S(2)}) copy-start(bf16[1024,1024]{1,0:T(8,128)(2,1)} %constant.109.clone.refs_4_) | copy-start | bytes 6291460
  19.9 6.8 %collective-permute-start.4 = (bf16[512,128]{1,0:T(8,128)(2,1)S(1)}, bf16[512,128]{1,0:T(8,128)(2,1)S(1)}, u32[]{:S(2)}, u32[]{:S(2)}) collective-permute-start(bf16[512,128]{1,0:T(8,128)(2,1)S(1)} %get-tuple-element.73), channel_id=1, source_target_pairs={{0,24},{8,16},{16,8},{24,0},{1,25},{9,17},{17,9},{25,1},{2,26},{10... | collective-permute-start | bytes 393224 | tf_op jit(solution)/shard_map/ppermute | solution.py:507
  22.5 17.0 %slice-start = ((s8[12582912]{0:T(1024)(128)(4,1)}), s8[4194304]{0:T(1024)(128)(4,1)S(1)}, s32[]{:S(2)}) async-start(s8[12582912]{0:T(1024)(128)(4,1)} %bitcast.27), calls=%async_computation | async-start | bytes 8388608
  26.7 12.8 %collective-permute-start.5 = (bf16[512,512]{1,0:T(8,128)(2,1)S(1)}, bf16[512,512]{1,0:T(8,128)(2,1)S(1)}, u32[]{:S(2)}, u32[]{:S(2)}) collective-permute-start(bf16[512,512]{1,0:T(8,128)(2,1)S(1)} %copy-done), channel_id=1, source_target_pairs={{0,1},{1,0},{2,3},{3,2},{4,5},{5,4},{6,7},{7,6},{8,9},{9,8},{10,11... | collective-permute-start | bytes 1572872 | tf_op jit(solution)/shard_map/ppermute | solution.py:41
  26.7 12.8 %collective-permute-start.8 = (bf16[256,512]{1,0:T(8,128)(2,1)S(1)}, bf16[256,512]{1,0:T(8,128)(2,1)S(1)}, u32[]{:S(2)}, u32[]{:S(2)}) collective-permute-start(bf16[256,512]{1,0:T(8,128)(2,1)S(1)} %collective-permute-done.6.refs_2_), channel_id=1, source_target_pairs={{0,1},{1,0},{2,3},{3,2},{4,5},{5,4},{6,7},{7,6},{8,9},{9,8},{10,11... | collective-permute-start | bytes 786440 | tf_op jit(solution)/shard_map/ppermute | solution.py:41
  30.0 7.9 %collective-permute-start.9 = (bf16[256,512]{1,0:T(8,128)(2,1)S(1)}, bf16[256,512]{1,0:T(8,128)(2,1)S(1)}, u32[]{:S(2)}, u32[]{:S(2)}) collective-permute-start(bf16[256,512]{1,0:T(8,128)(2,1)S(1)} %collective-permute-done.7.refs_3_), channel_id=1, source_target_pairs={{0,1},{1,0},{2,3},{3,2},{4,5},{5,4},{6,7},{7,6},{8,9},{9,8},{10,11... | collective-permute-start | bytes 786440 | tf_op jit(solution)/shard_map/ppermute | solution.py:41
  34.9 4.6 %collective-permute-start.11 = (bf16[256,512]{1,0:T(8,128)(2,1)S(1)}, bf16[256,512]{1,0:T(8,128)(2,1)S(1)}, u32[]{:S(2)}, u32[]{:S(2)}) collective-permute-start(bf16[256,512]{1,0:T(8,128)(2,1)S(1)} %collective-permute-done.10.refs_6_), channel_id=1, source_target_pairs={{0,1},{1,0},{2,3},{3,2},{4,5},{5,4},{6,7},{7,6},{8,9},{9,8},{10,11... | collective-permute-start | bytes 786440 | tf_op jit(solution)/shard_map/ppermute | solution.py:41
  34.9 4.6 %collective-permute-start.14 = (bf16[256,512]{1,0:T(8,128)(2,1)S(1)}, bf16[256,512]{1,0:T(8,128)(2,1)S(1)}, u32[]{:S(2)}, u32[]{:S(2)}) collective-permute-start(bf16[256,512]{1,0:T(8,128)(2,1)S(1)} %collective-permute-done.13.refs_10_), channel_id=1, source_target_pairs={{0,1},{1,0},{2,3},{3,2},{4,5},{5,4},{6,7},{7,6},{8,9},{9,8},{10,11... | collective-permute-start | bytes 786440 | tf_op jit(solution)/shard_map/ppermute | solution.py:41
  35.5 4.1 %slice-start.1 = ((s8[12582912]{0:T(1024)(128)(4,1)}), s8[4194304]{0:T(1024)(128)(4,1)S(1)}, s32[]{:S(2)}) async-start(s8[12582912]{0:T(1024)(128)(4,1)} %bitcast.27), calls=%async_computation.1 | async-start | bytes 8388608
  35.5 4.1 %slice-start.2 = ((s8[12582912]{0:T(1024)(128)(4,1)}), s8[4194304]{0:T(1024)(128)(4,1)S(1)}, s32[]{:S(2)}) async-start(s8[12582912]{0:T(1024)(128)(4,1)} %bitcast.27), calls=%async_computation.2 | async-start | bytes 8388608
  37.8 10.0 %collective-permute-start.1 = (bf16[256,512]{1,0:T(8,128)(2,1)S(1)}, bf16[256,512]{1,0:T(8,128)(2,1)S(1)}, u32[]{:S(2)}, u32[]{:S(2)}) collective-permute-start(bf16[256,512]{1,0:T(8,128)(2,1)S(1)} %collective-permute-done.refs_7_), channel_id=1, source_target_pairs={{0,6},{1,7},{2,0},{3,1},{4,2},{5,3},{6,4},{7,5},{8,14},{9,15},{10,... | collective-permute-start | bytes 786440 | tf_op jit(solution)/shard_map/ppermute | solution.py:37
  47.8 1.6 %collective-permute-start.15 = (bf16[256,512]{1,0:T(8,128)(2,1)S(1)}, bf16[256,512]{1,0:T(8,128)(2,1)S(1)}, u32[]{:S(2)}, u32[]{:S(2)}) collective-permute-start(bf16[256,512]{1,0:T(8,128)(2,1)S(1)} %collective-permute-done.1.own_ref), channel_id=1, source_target_pairs={{0,1},{1,0},{2,3},{3,2},{4,5},{5,4},{6,7},{7,6},{8,9},{9,8},{10,11... | collective-permute-start | bytes 786440 | tf_op jit(solution)/shard_map/ppermute | solution.py:41
  53.8 13.0 %collective-permute-start.20 = (bf16[512,2048]{1,0:T(8,128)(2,1)}, bf16[512,2048]{1,0:T(8,128)(2,1)S(1)}, u32[]{:S(2)}, u32[]{:S(2)}) collective-permute-start(bf16[512,2048]{1,0:T(8,128)(2,1)} %pad_maximum_fusion), channel_id=1, source_target_pairs={{0,1},{1,0},{2,3},{3,2},{4,5},{5,4},{6,7},{7,6},{8,9},{9,8},{10,11... | collective-permute-start | bytes 6291464 | tf_op jit(solution)/shard_map/ppermute | solution.py:41
  54.0 7.6 %collective-permute-start.16 = (bf16[544,128]{1,0:T(8,128)(2,1)}, bf16[544,128]{1,0:T(8,128)(2,1)S(1)}, u32[]{:S(2)}, u32[]{:S(2)}) collective-permute-start(bf16[544,128]{1,0:T(8,128)(2,1)} %get-tuple-element.42), channel_id=1, source_target_pairs={{0,24},{8,16},{16,8},{24,0},{1,25},{9,17},{17,9},{25,1},{2,26},{10... | collective-permute-start | bytes 417800 | tf_op jit(solution)/shard_map/ppermute | solution.py:507
  56.4 7.7 %collective-permute-start.18 = (bf16[544,128]{1,0:T(8,128)(2,1)}, bf16[544,128]{1,0:T(8,128)(2,1)S(1)}, u32[]{:S(2)}, u32[]{:S(2)}) collective-permute-start(bf16[544,128]{1,0:T(8,128)(2,1)} %get-tuple-element.45), channel_id=1, source_target_pairs={{0,8},{8,0},{16,24},{24,16},{1,9},{9,1},{17,25},{25,17},{2,10},{10... | collective-permute-start | bytes 417800 | tf_op jit(solution)/shard_map/ppermute | solution.py:507
  57.0 4.6 %copy-start.3 = (bf16[16,512]{1,0:T(8,128)(2,1)S(1)}, bf16[16,512]{1,0:T(8,128)(2,1)}, u32[]{:S(2)}) copy-start(bf16[16,512]{1,0:T(8,128)(2,1)} %get-tuple-element.43.here_ref) | copy-start | bytes 49156
  57.0 7.1 %copy-start.2 = (bf16[544,128]{1,0:T(8,128)(2,1)S(1)}, bf16[544,128]{1,0:T(8,128)(2,1)}, u32[]{:S(2)}) copy-start(bf16[544,128]{1,0:T(8,128)(2,1)} %get-tuple-element.44.refs_0_) | copy-start | bytes 417796
  57.0 7.1 %copy-start.5 = (bf16[512,1024]{1,0:T(8,128)(2,1)S(1)}, bf16[512,1024]{1,0:T(8,128)(2,1)}, u32[]{:S(2)}) copy-start(bf16[512,1024]{1,0:T(8,128)(2,1)} %constant.110.clone.refs_7_) | copy-start | bytes 3145732
  57.0 7.2 %copy-start.6 = (bf16[1024,512]{1,0:T(8,128)(2,1)S(1)}, bf16[1024,512]{1,0:T(8,128)(2,1)}, u32[]{:S(2)}) copy-start(bf16[1024,512]{1,0:T(8,128)(2,1)} %constant.111.clone.refs_6_) | copy-start | bytes 3145732
  57.0 7.2 %copy-start.7 = (bf16[1024,512]{1,0:T(8,128)(2,1)S(1)}, bf16[1024,512]{1,0:T(8,128)(2,1)}, u32[]{:S(2)}) copy-start(bf16[1024,512]{1,0:T(8,128)(2,1)} %taps_spectra.1.refs_5_) | copy-start | bytes 3145732
  57.0 7.1 %collective-permute-start.19 = (bf16[544,128]{1,0:T(8,128)(2,1)}, bf16[544,128]{1,0:T(8,128)(2,1)S(1)}, u32[]{:S(2)}, u32[]{:S(2)}) collective-permute-start(bf16[544,128]{1,0:T(8,128)(2,1)} %get-tuple-element.46), channel_id=1, source_target_pairs={{0,16},{8,24},{16,0},{24,8},{1,17},{9,25},{17,1},{25,9},{2,18},{10... | collective-permute-start | bytes 417800 | tf_op jit(solution)/shard_map/ppermute | solution.py:507
  61.6 8.8 %collective-permute-start.17 = (bf16[16,512]{1,0:T(8,128)(2,1)S(1)}, bf16[16,512]{1,0:T(8,128)(2,1)S(1)}, u32[]{:S(2)}, u32[]{:S(2)}) collective-permute-start(bf16[16,512]{1,0:T(8,128)(2,1)S(1)} %copy-done.3), channel_id=1, source_target_pairs={{0,8},{8,16},{16,24},{24,0},{1,9},{9,17},{17,25},{25,1},{2,10},{10... | collective-permute-start | bytes 49160 | tf_op jit(solution)/shard_map/ppermute | solution.py:37
  64.1 12.2 %copy-start.1 = (bf16[512,512]{1,0:T(8,128)(2,1)S(1)}, bf16[512,512]{1,0:T(8,128)(2,1)}, u32[]{:S(2)}) copy-start(bf16[512,512]{1,0:T(8,128)(2,1)} %get-tuple-element.40.gate_ref) | copy-start | bytes 1572868
  66.8 5.7 %collective-permute-start.21 = (bf16[512,128]{1,0:T(8,128)(2,1)S(1)}, bf16[512,128]{1,0:T(8,128)(2,1)S(1)}, u32[]{:S(2)}, u32[]{:S(2)}) collective-permute-start(bf16[512,128]{1,0:T(8,128)(2,1)S(1)} %get-tuple-element.55), channel_id=1, source_target_pairs={{0,8},{8,0},{16,24},{24,16},{1,9},{9,1},{17,25},{25,17},{2,10},{10... | collective-permute-start | bytes 393224 | tf_op jit(solution)/shard_map/ppermute | solution.py:507
  68.5 7.8 %collective-permute-start.22 = (bf16[512,128]{1,0:T(8,128)(2,1)S(1)}, bf16[512,128]{1,0:T(8,128)(2,1)S(1)}, u32[]{:S(2)}, u32[]{:S(2)}) collective-permute-start(bf16[512,128]{1,0:T(8,128)(2,1)S(1)} %get-tuple-element.56), channel_id=1, source_target_pairs={{0,16},{8,24},{16,0},{24,8},{1,17},{9,25},{17,1},{25,9},{2,18},{10... | collective-permute-start | bytes 393224 | tf_op jit(solution)/shard_map/ppermute | solution.py:507
  69.8 6.5 %collective-permute-start.23 = (bf16[512,128]{1,0:T(8,128)(2,1)S(1)}, bf16[512,128]{1,0:T(8,128)(2,1)S(1)}, u32[]{:S(2)}, u32[]{:S(2)}) collective-permute-start(bf16[512,128]{1,0:T(8,128)(2,1)S(1)} %get-tuple-element.57), channel_id=1, source_target_pairs={{0,24},{8,16},{16,8},{24,0},{1,25},{9,17},{17,9},{25,1},{2,26},{10... | collective-permute-start | bytes 393224 | tf_op jit(solution)/shard_map/ppermute | solution.py:507
  76.6 2.0 %collective-permute-start.24 = (bf16[512,512]{1,0:T(8,128)(2,1)S(1)}, bf16[512,512]{1,0:T(8,128)(2,1)S(1)}, u32[]{:S(2)}, u32[]{:S(2)}) collective-permute-start(bf16[512,512]{1,0:T(8,128)(2,1)S(1)} %gate_blocks.1.a_ref), channel_id=1, source_target_pairs={{0,1},{1,0},{2,3},{3,2},{4,5},{5,4},{6,7},{7,6},{8,9},{9,8},{10,11... | collective-permute-start | bytes 1572872 | tf_op jit(solution)/shard_map/ppermute | solution.py:41
  79.2 14.8 %collective-permute-start.29 = (bf16[256,512]{1,0:T(8,128)(2,1)S(1)}, bf16[256,512]{1,0:T(8,128)(2,1)S(1)}, u32[]{:S(2)}, u32[]{:S(2)}) collective-permute-start(bf16[256,512]{1,0:T(8,128)(2,1)S(1)} %get-tuple-element.63), channel_id=1, source_target_pairs={{0,6},{1,7},{2,0},{3,1},{4,2},{5,3},{6,4},{7,5},{8,14},{9,15},{10,... | collective-permute-start | bytes 786440 | tf_op jit(solution)/shard_map/ppermute | solution.py:37
  81.0 13.2 %collective-permute-start.25 = (bf16[256,512]{1,0:T(8,128)(2,1)S(1)}, bf16[256,512]{1,0:T(8,128)(2,1)S(1)}, u32[]{:S(2)}, u32[]{:S(2)}) collective-permute-start(bf16[256,512]{1,0:T(8,128)(2,1)S(1)} %get-tuple-element.59), channel_id=1, source_target_pairs={{0,2},{1,3},{2,4},{3,5},{4,6},{5,7},{6,0},{7,1},{8,10},{9,11},{10,... | collective-permute-start | bytes 786440 | tf_op jit(solution)/shard_map/ppermute | solution.py:37
  84.6 20.7 %collective-permute-start.27 = (bf16[256,512]{1,0:T(8,128)(2,1)S(1)}, bf16[256,512]{1,0:T(8,128)(2,1)S(1)}, u32[]{:S(2)}, u32[]{:S(2)}) collective-permute-start(bf16[256,512]{1,0:T(8,128)(2,1)S(1)} %get-tuple-element.61), channel_id=1, source_target_pairs={{0,6},{1,7},{2,0},{3,1},{4,2},{5,3},{6,4},{7,5},{8,14},{9,15},{10,... | collective-permute-start | bytes 786440 | tf_op jit(solution)/shard_map/ppermute | solution.py:37
  88.1 17.2 %collective-permute-start.28 = (bf16[256,512]{1,0:T(8,128)(2,1)S(1)}, bf16[256,512]{1,0:T(8,128)(2,1)S(1)}, u32[]{:S(2)}, u32[]{:S(2)}) collective-permute-start(bf16[256,512]{1,0:T(8,128)(2,1)S(1)} %get-tuple-element.62), channel_id=1, source_target_pairs={{0,2},{1,3},{2,4},{3,5},{4,6},{5,7},{6,0},{7,1},{8,10},{9,11},{10,... | collective-permute-start | bytes 786440 | tf_op jit(solution)/shard_map/ppermute | solution.py:37
  94.2 16.7 %collective-permute-start.30 = (bf16[256,512]{1,0:T(8,128)(2,1)S(1)}, bf16[256,512]{1,0:T(8,128)(2,1)S(1)}, u32[]{:S(2)}, u32[]{:S(2)}) collective-permute-start(bf16[256,512]{1,0:T(8,128)(2,1)S(1)} %add_convert_fusion), channel_id=1, source_target_pairs={{0,6},{1,7},{2,0},{3,1},{4,2},{5,3},{6,4},{7,5},{8,14},{9,15},{10,... | collective-permute-start | bytes 786440 | tf_op jit(solution)/shard_map/ppermute | solution.py:37
  94.3 21.4 %collective-permute-start.26 = (bf16[256,512]{1,0:T(8,128)(2,1)S(1)}, bf16[256,512]{1,0:T(8,128)(2,1)S(1)}, u32[]{:S(2)}, u32[]{:S(2)}) collective-permute-start(bf16[256,512]{1,0:T(8,128)(2,1)S(1)} %add_convert_fusion.1), channel_id=1, source_target_pairs={{0,2},{1,3},{2,4},{3,5},{4,6},{5,7},{6,0},{7,1},{8,10},{9,11},{10,... | collective-permute-start | bytes 786440 | tf_op jit(solution)/shard_map/ppermute | solution.py:37

commit v7 on v6

--- a/solution.py
+++ b/solution.py
@@ -173,7 +173,7 @@
             pltpu.SemaphoreType.DMA((streams, count)),
         ],
         "project_most",
-        8,
+        20,
         24,
     )
 
@@ -246,7 +246,7 @@
             pltpu.SemaphoreType.DMA((streams, 3)),
         ],
         "project_rest",
-        1,
+        4,
         24,
     )
     gate, ends, ins = found[0], found[1], list(found[2:])
@@ -398,7 +398,7 @@
             pltpu.VMEM((groups, 2 * EDGE, share), BF16),
         ],
         "long_filter",
-        3,
+        6,
     )
 
 
@@ -428,6 +428,7 @@
         whole(gate.shape),
         [pltpu.VMEM(here.shape, BF16)],
         "gate_blocks",
+        3,
     )
 
 
@@ -469,6 +470,7 @@
         [whole(o.shape) for o in outs],
         [],
         "output_shares",
+        1,
     )
 
 
@@ -499,14 +501,16 @@
     )
 
 
-def exchange(piece):
+def exchange(piece, chained=False):
     groups = lax.axis_size("ctx")
-
-    def send(slot):
+    found = [piece(0)]
+    for slot in range(1, groups):
         route = [(i, partner(i, slot, groups)) for i in range(groups)]
-        return lax.ppermute(piece(slot), "ctx", route)
-
-    return [piece(0)] + [send(s) for s in range(1, groups)]
+        block = piece(slot)
+        if chained and slot > 1:
+            block = after(block, found[-1])
+        found.append(lax.ppermute(block, "ctx", route))
+    return found
 
 
 def in_order(blocks, me):
@@ -597,7 +601,7 @@
         )
 
     spectra_taps = (taps_spectra if aligned else taps_spectra_plain)(
-        exchange(pick(split_taps)), forward, back, me
+        exchange(pick(split_taps), True), forward, back, me
     )[0]
     tables = (spectra_taps,)
 
@@ -639,7 +643,7 @@
     )
 
     pieces_in = exchange(lambda s: pieces[s])
-    before = shift(after(gate_ends, pieces_in[-1]), "ctx", 1)
+    before = shift(after(gate_ends, pieces_in[1]), "ctx", 1)
     before = jnp.where(me > 0, before, jnp.zeros_like(before))
 
     w_own = columns(after(w_out, gate), core)

time: 117 us -> 116 us (level)
  transfers between devices with their start and end apart: 31 -> 31, of which waited for: 13 -> 14; matrix products, arithmetic and copies ran while one was open for 10% -> 10% of each run, Pallas kernels for 14% -> 14%
where the time goes in v7:
time: 116 us
  waiting for transfers between devices  46.1 us (40%)
  starting transfers between devices  34.8 us (30%)
  Pallas kernels  22.7 us (20%)
  local copies, waits for them, and re-layouts  9.92 us (9%)
  other arithmetic  2.34 us (2%)
    ppermute x13, waiting for transfers between devices, shift(): lax.ppermute(x, axis, [(i, (i + distance) % size) for i in range(size)])  32.6 us
    pallas_call x8, Pallas kernels, call(): pl.pallas_call(kernel, grid_spec=pltpu.PrefetchScalarGridSpec(num_scalar_...  22.7 us
    ppermute x13, starting transfers between devices, shift(): lax.ppermute(x, axis, [(i, (i + distance) % size) for i in range(size)])  20 us
    ppermute x9, starting transfers between devices, exchange(): found.append(lax.ppermute(block, 'ctx', route))  13.3 us
    ppermute x9, waiting for transfers between devices, exchange(): found.append(lax.ppermute(block, 'ctx', route))  10.2 us
    dynamic_slice x2, local copies, waits for them, and re-layouts, columns(): lax.dynamic_slice_in_dim(w, c, out_width, 1)  3.63 us
    ppermute x9, waiting for transfers between devices, sibling(): lax.ppermute(x, 'chan', [(i, i ^ 1) for i in range(lax.axis_size('chan'))])  3.34 us
  transfers between devices with their start and end apart: 31, of which 14 were waited for; matrix products, arithmetic and copies ran while one was open for 10% of the time, Pallas kernels for 14%

profile of v7, /device:TPU:0, one launch (start us, length us, event | category | flops | bytes accessed | tf_op | source)
XLA Modules:
  0.0 116.2 jit_solution(5600449116639439418)
XLA Ops:
  0.0 1.0 slice.18
  1.0 3.1 %collective-permute-start.6 = (bf16[256,512]{1,0:T(8,128)(2,1)S(1)}, bf16[256,512]{1,0:T(8,128)(2,1)S(1)}, u32[]{:S(2)}, u32[]{:S(2)}) collective-permute-start(bf16[256,512]{1,0:T(8,128)(2,1)S(1)} %slice.18), channel_id=1, source_target_pairs={{0,2},{1,3},{2,4},{3,5},{4,6},{5,7},{6,0},{7,1},{8,10},{9,11},{10,... | collective-permute-start | bytes 786440 | tf_op jit(solution)/shard_map/ppermute | solution.py:37
  4.0 1.0 slice.19
  5.0 2.1 %collective-permute-start = (bf16[256,512]{1,0:T(8,128)(2,1)S(1)}, bf16[256,512]{1,0:T(8,128)(2,1)S(1)}, u32[]{:S(2)}, u32[]{:S(2)}) collective-permute-start(bf16[256,512]{1,0:T(8,128)(2,1)S(1)} %slice.19), channel_id=1, source_target_pairs={{0,6},{1,7},{2,0},{3,1},{4,2},{5,3},{6,4},{7,5},{8,14},{9,15},{10,... | collective-permute-start | bytes 786440 | tf_op jit(solution)/shard_map/ppermute | solution.py:37
  7.1 3.8 %collective-permute-start.10 = (bf16[256,512]{1,0:T(8,128)(2,1)S(1)}, bf16[256,512]{1,0:T(8,128)(2,1)S(1)}, u32[]{:S(2)}, u32[]{:S(2)}) collective-permute-start(bf16[256,512]{1,0:T(8,128)(2,1)S(1)} %slice.18), channel_id=1, source_target_pairs={{0,6},{1,7},{2,0},{3,1},{4,2},{5,3},{6,4},{7,5},{8,14},{9,15},{10,... | collective-permute-start | bytes 786440 | tf_op jit(solution)/shard_map/ppermute | solution.py:37
  10.9 1.1 slice_bitcast_fusion.3
  12.1 0.1 pad_maximum_fusion.2
  12.2 1.8 %collective-permute-start.2 = (bf16[512,128]{1,0:T(8,128)(2,1)S(1)}, bf16[512,128]{1,0:T(8,128)(2,1)S(1)}, u32[]{:S(2)}, u32[]{:S(2)}) collective-permute-start(bf16[512,128]{1,0:T(8,128)(2,1)S(1)} %get-tuple-element.79), channel_id=1, source_target_pairs={{0,8},{8,0},{16,24},{24,16},{1,9},{9,1},{17,25},{25,17},{2,10},{10... | collective-permute-start | bytes 393224 | tf_op jit(solution)/shard_map/ppermute | solution.py:512
  14.0 1.7 %constant_dynamic-slice_fusion.8 = (bf16[512,512]{1,0:T(8,128)(2,1)S(1)}, bf16[512,512]{1,0:T(8,128)(2,1)S(1)}, bf16[512,512]{1,0:T(8,128)(2,1)S(1)}, bf16[512,512]{1,0:T(8,128)(2,1)S(1)}) fusion(bf16[512,4096]{1,0:T(8,128)(2,1)} %param.14, s32[]{:T(128)S(6)} %select_n.97, s32[]{:T(128)S(6)} %select_n.99, s32[]{:T(128)S(6)} %select_n.98, s32[]{:T(128)S(6)} %select_n.100), kind=kLoop, calls=%fused_computation.23 | loop fusion | bytes 4194320 | tf_op jit(solution)/shard_map/dynamic_slice | solution.py:610
  15.7 1.6 %collective-permute-done.2.refs_1_ = bf16[512,128]{1,0:T(8,128)(2,1)S(1)} collective-permute-done((bf16[512,128]{1,0:T(8,128)(2,1)S(1)}, bf16[512,128]{1,0:T(8,128)(2,1)S(1)}, u32[]{:S(2)}, u32[]{:S(2)}) %collective-permute-start.2) | collective-permute-done | bytes 131104 | tf_op jit(solution)/shard_map/ppermute | solution.py:512
  17.3 1.7 %collective-permute-start.3 = (bf16[512,128]{1,0:T(8,128)(2,1)S(1)}, bf16[512,128]{1,0:T(8,128)(2,1)S(1)}, u32[]{:S(2)}, u32[]{:S(2)}) collective-permute-start(bf16[512,128]{1,0:T(8,128)(2,1)S(1)} %get-tuple-element.38), channel_id=1, source_target_pairs={{0,16},{8,24},{16,0},{24,8},{1,17},{9,25},{17,1},{25,9},{2,18},{10... | collective-permute-start | bytes 393224 | tf_op jit(solution)/shard_map/ppermute | solution.py:512
  19.0 1.7 %pad_maximum_fusion = bf16[512,2048]{1,0:T(8,128)(2,1)} fusion(bf16[512,512]{1,0:T(8,128)(2,1)S(1)} %get-tuple-element.76, bf16[512,512]{1,0:T(8,128)(2,1)S(1)} %get-tuple-element.74, bf16[512,512]{1,0:T(8,128)(2,1)S(1)} %get-tuple-element.75, bf16[512,512]{1,0:T(8,128)(2,1)S(1)} %get-tuple-element.73), kind=kLoop, calls=%fused_computation.1 | loop fusion | flops 8388608 | bytes 4194304 | tf_op jit(solution)/shard_map/concatenate | solution.py:610
  20.7 0.1 collective-permute-start.13
  20.7 0.1 collective-permute-start.12
  20.9 0.8 dynamic_slice.51
  21.6 0.1 stack.54.ids
  21.7 0.5 collective-permute-done.3.refs_2_
  22.2 2.7 %collective-permute-start.4 = (bf16[512,128]{1,0:T(8,128)(2,1)S(1)}, bf16[512,128]{1,0:T(8,128)(2,1)S(1)}, u32[]{:S(2)}, u32[]{:S(2)}) collective-permute-start(bf16[512,128]{1,0:T(8,128)(2,1)S(1)} %get-tuple-element.39), channel_id=1, source_target_pairs={{0,24},{8,16},{16,8},{24,0},{1,25},{9,17},{17,9},{25,1},{2,26},{10... | collective-permute-start | bytes 393224 | tf_op jit(solution)/shard_map/ppermute | solution.py:512
  24.9 2.2 %dynamic-slice_bitcast_fusion.w_ref = bf16[3,1024,512]{2,1,0:T(8,128)(2,1)S(1)} fusion(bf16[4096,3,512]{2,0,1:T(8,128)(2,1)} %param.10, s32[]{:T(128)S(6)} %select_n.102), kind=kLoop, calls=%fused_computation | loop fusion | bytes 6291460 | tf_op jit(solution)/shard_map/dynamic_slice | solution.py:613
  27.2 0.1 collective-permute-start.5
  27.2 2.7 %collective-permute-done.10.refs_6_ = bf16[256,512]{1,0:T(8,128)(2,1)S(1)} collective-permute-done((bf16[256,512]{1,0:T(8,128)(2,1)S(1)}, bf16[256,512]{1,0:T(8,128)(2,1)S(1)}, u32[]{:S(2)}, u32[]{:S(2)}) %collective-permute-start.10) | collective-permute-done | bytes 262176 | tf_op jit(solution)/shard_map/ppermute | solution.py:37
  30.0 0.5 collective-permute-start.9
  30.5 4.4 %collective-permute-done.13.refs_10_ = bf16[256,512]{1,0:T(8,128)(2,1)S(1)} collective-permute-done((bf16[256,512]{1,0:T(8,128)(2,1)S(1)}, bf16[256,512]{1,0:T(8,128)(2,1)S(1)}, u32[]{:S(2)}, u32[]{:S(2)}) %collective-permute-start.13) | collective-permute-done | bytes 262176 | tf_op jit(solution)/shard_map/ppermute | solution.py:37
  34.9 0.5 collective-permute-start.14
  35.5 2.4 %taps_spectra.1.refs_5_ = bf16[1024,512]{1,0:T(8,128)(2,1)} custom-call(s32[1]{0:T(128)} %bitcast.3.at, bf16[512,128]{1,0:T(8,128)(2,1)S(1)} %get-tuple-element.80.refs_0_, bf16[512,128]{1,0:T(8,128)(2,1)S(1)} %collective-permute-done.2.refs_1_, bf16[512,128]{1,0:T(8,128)(2,1)S(1)} %collective-permute-done.3.refs_2_, ...), custom_call_target="tpu_custom_call" | custom-call | flops 20000000000 | bytes 20971520 | tf_op jit(solution)/shard_map/taps_spectra/pallas_call | solution.py:61
  37.8 1.6 %collective-permute-start.1 = (bf16[256,512]{1,0:T(8,128)(2,1)S(1)}, bf16[256,512]{1,0:T(8,128)(2,1)S(1)}, u32[]{:S(2)}, u32[]{:S(2)}) collective-permute-start(bf16[256,512]{1,0:T(8,128)(2,1)S(1)} %collective-permute-done.refs_7_), channel_id=1, source_target_pairs={{0,6},{1,7},{2,0},{3,1},{4,2},{5,3},{6,4},{7,5},{8,14},{9,15},{10,... | collective-permute-start | bytes 786440 | tf_op jit(solution)/shard_map/ppermute | solution.py:37
  39.5 8.3 %project_most.1 = (bf16[3,256,512]{2,1,0:T(8,128)(2,1)S(1)}, f32[3,256,512]{2,1,0:T(8,128)S(1)}) custom-call(s32[5]{0:T(128)S(1)} %stack.54.ids, bf16[3,4096,512]{2,1,0:T(8,128)(2,1)S(1)} %bitcast.29, bf16[512,512]{1,0:T(8,128)(2,1)S(1)} %copy-done, bf16[512,512]{1,0:T(8,128)(2,1)S(1)} %collective-permute-done.5.refs_1_, ...), custom_call_target="tpu_custom_call" | custom-call | flops 20000000000 | bytes 20971520 | tf_op jit(solution)/shard_map/project_most/pallas_call | solution.py:61
  47.8 0.1 collective-permute-start.15
  47.9 0.1 pad_add_fusion.1.at
  48.0 1.4 %collective-permute-done.15.other_ref = bf16[256,512]{1,0:T(8,128)(2,1)S(1)} collective-permute-done((bf16[256,512]{1,0:T(8,128)(2,1)S(1)}, bf16[256,512]{1,0:T(8,128)(2,1)S(1)}, u32[]{:S(2)}, u32[]{:S(2)}) %collective-permute-start.15) | collective-permute-done | bytes 262176 | tf_op jit(solution)/shard_map/ppermute | solution.py:41
  49.4 4.3 %project_rest.1 = (bf16[512,512]{1,0:T(8,128)(2,1)}, bf16[16,512]{1,0:T(8,128)(2,1)}, bf16[544,128]{1,0:T(8,128)(2,1)}, bf16[544,128]{1,0:T(8,128)(2,1)}, bf16[5...) custom-call(s32[2]{0:T(128)S(1)} %pad_add_fusion.1.at, bf16[256,512]{1,0:T(8,128)(2,1)S(1)} %collective-permute-done.1.own_ref, ...), custom_call_target="tpu_custom_call" | custom-call | flops 4000000000 | bytes 4194304 | tf_op jit(solution)/shard_map/project_rest/pallas_call | solution.py:61
  53.8 0.2 collective-permute-start.20
  54.0 1.5 %collective-permute-start.16 = (bf16[544,128]{1,0:T(8,128)(2,1)}, bf16[544,128]{1,0:T(8,128)(2,1)S(1)}, u32[]{:S(2)}, u32[]{:S(2)}) collective-permute-start(bf16[544,128]{1,0:T(8,128)(2,1)} %get-tuple-element.46), channel_id=1, source_target_pairs={{0,8},{8,0},{16,24},{24,16},{1,9},{9,1},{17,25},{25,17},{2,10},{10... | collective-permute-start | bytes 417800 | tf_op jit(solution)/shard_map/ppermute | solution.py:512
  55.5 1.5 %collective-permute-start.18 = (bf16[544,128]{1,0:T(8,128)(2,1)}, bf16[544,128]{1,0:T(8,128)(2,1)S(1)}, u32[]{:S(2)}, u32[]{:S(2)}) collective-permute-start(bf16[544,128]{1,0:T(8,128)(2,1)} %get-tuple-element.49), channel_id=1, source_target_pairs={{0,16},{8,24},{16,0},{24,8},{1,17},{9,25},{17,1},{25,9},{2,18},{10... | collective-permute-start | bytes 417800 | tf_op jit(solution)/shard_map/ppermute | solution.py:512
  57.0 0.5 collective-permute-start.19
  57.6 1.9 %constant_dynamic-slice_fusion.3 = (bf16[512,512]{1,0:T(8,128)(2,1)S(1)}, bf16[512,512]{1,0:T(8,128)(2,1)S(1)}, bf16[512,512]{1,0:T(8,128)(2,1)S(1)}, bf16[512,512]{1,0:T(8,128)(2,1)S(1)}) fusion(bf16[512,4096]{1,0:T(8,128)(2,1)} %param.14, s32[]{:T(128)S(6)} %select_n.110, s32[]{:T(128)S(6)} %select_n.113, s32[]{:T(128)S(6)} %select_n.112, s32[]{:T(128)S(6)} %select_n.111), kind=kLoop, calls=%fused_computation.18 | loop fusion | bytes 4194320 | tf_op jit(solution)/shard_map/dynamic_slice | solution.py:610
  59.5 0.3 pad_maximum_fusion.1.w_ref
  59.8 0.8 collective-permute-done.16.refs_1_
  60.6 1.6 %collective-permute-start.17 = (bf16[16,512]{1,0:T(8,128)(2,1)S(1)}, bf16[16,512]{1,0:T(8,128)(2,1)S(1)}, u32[]{:S(2)}, u32[]{:S(2)}) collective-permute-start(bf16[16,512]{1,0:T(8,128)(2,1)S(1)} %copy-done.1), channel_id=1, source_target_pairs={{0,8},{8,16},{16,24},{24,0},{1,9},{9,17},{17,25},{25,1},{2,10},{10... | collective-permute-start | bytes 49160 | tf_op jit(solution)/shard_map/ppermute | solution.py:37
  62.2 2.3 %collective-permute-done.18.refs_2_ = bf16[544,128]{1,0:T(8,128)(2,1)S(1)} collective-permute-done((bf16[544,128]{1,0:T(8,128)(2,1)}, bf16[544,128]{1,0:T(8,128)(2,1)S(1)}, u32[]{:S(2)}, u32[]{:S(2)}) %collective-permute-start.18) | collective-permute-done | bytes 139296 | tf_op jit(solution)/shard_map/ppermute | solution.py:512
  64.5 2.6 %long_filter.1 = (bf16[512,128]{1,0:T(8,128)(2,1)S(1)}, bf16[512,128]{1,0:T(8,128)(2,1)S(1)}, bf16[512,128]{1,0:T(8,128)(2,1)S(1)}, bf16[512,128]{1,0:T(8,128)(2,1)S(1)}) custom-call(s32[1]{0:T(128)} %bitcast.3.at, bf16[544,128]{1,0:T(8,128)(2,1)S(1)} %copy-done.7, bf16[544,128]{1,0:T(8,128)(2,1)S(1)} %collective-permute-done.16.refs_1_, ...), custom_call_target="tpu_custom_call" | custom-call | flops 6000000000 | bytes 6291456 | tf_op jit(solution)/shard_map/long_filter/pallas_call | solution.py:61
  67.2 1.3 %collective-permute-start.21 = (bf16[512,128]{1,0:T(8,128)(2,1)S(1)}, bf16[512,128]{1,0:T(8,128)(2,1)S(1)}, u32[]{:S(2)}, u32[]{:S(2)}) collective-permute-start(bf16[512,128]{1,0:T(8,128)(2,1)S(1)} %get-tuple-element.59), channel_id=1, source_target_pairs={{0,8},{8,0},{16,24},{24,16},{1,9},{9,1},{17,25},{25,17},{2,10},{10... | collective-permute-start | bytes 393224 | tf_op jit(solution)/shard_map/ppermute | solution.py:512
  68.5 0.7 collective-permute-start.22
  69.1 1.6 %collective-permute-start.23 = (bf16[512,128]{1,0:T(8,128)(2,1)S(1)}, bf16[512,128]{1,0:T(8,128)(2,1)S(1)}, u32[]{:S(2)}, u32[]{:S(2)}) collective-permute-start(bf16[512,128]{1,0:T(8,128)(2,1)S(1)} %get-tuple-element.61), channel_id=1, source_target_pairs={{0,24},{8,16},{16,8},{24,0},{1,25},{9,17},{17,9},{25,1},{2,26},{10... | collective-permute-start | bytes 393224 | tf_op jit(solution)/shard_map/ppermute | solution.py:512
  70.8 2.4 %collective-permute-done.21.refs_1_ = bf16[512,128]{1,0:T(8,128)(2,1)S(1)} collective-permute-done((bf16[512,128]{1,0:T(8,128)(2,1)S(1)}, bf16[512,128]{1,0:T(8,128)(2,1)S(1)}, u32[]{:S(2)}, u32[]{:S(2)}) %collective-permute-start.21) | collective-permute-done | bytes 131104 | tf_op jit(solution)/shard_map/ppermute | solution.py:512
  73.2 2.6 %collective-permute-done.22.refs_2_ = bf16[512,128]{1,0:T(8,128)(2,1)S(1)} collective-permute-done((bf16[512,128]{1,0:T(8,128)(2,1)S(1)}, bf16[512,128]{1,0:T(8,128)(2,1)S(1)}, u32[]{:S(2)}, u32[]{:S(2)}) %collective-permute-start.22) | collective-permute-done | bytes 131104 | tf_op jit(solution)/shard_map/ppermute | solution.py:512
  75.8 0.2 gate_blocks.1.a_ref
  76.0 0.1 collective-permute-start.24
  76.1 1.9 %collective-permute-done.24.b_ref = bf16[512,512]{1,0:T(8,128)(2,1)S(1)} collective-permute-done((bf16[512,512]{1,0:T(8,128)(2,1)S(1)}, bf16[512,512]{1,0:T(8,128)(2,1)S(1)}, u32[]{:S(2)}, u32[]{:S(2)}) %collective-permute-start.24) | collective-permute-done | bytes 524320 | tf_op jit(solution)/shard_map/ppermute | solution.py:41
  78.0 0.7 output_shares.3
  78.7 1.7 %collective-permute-start.29 = (bf16[256,512]{1,0:T(8,128)(2,1)S(1)}, bf16[256,512]{1,0:T(8,128)(2,1)S(1)}, u32[]{:S(2)}, u32[]{:S(2)}) collective-permute-start(bf16[256,512]{1,0:T(8,128)(2,1)S(1)} %get-tuple-element.67), channel_id=1, source_target_pairs={{0,6},{1,7},{2,0},{3,1},{4,2},{5,3},{6,4},{7,5},{8,14},{9,15},{10,... | collective-permute-start | bytes 786440 | tf_op jit(solution)/shard_map/ppermute | solution.py:37
  80.4 0.1 pad_add_fusion._
  80.5 0.4 collective-permute-start.25
  80.9 3.2 %output_shares.2 = (f32[256,512]{1,0:T(8,128)S(1)}, bf16[256,512]{1,0:T(8,128)(2,1)S(1)}, bf16[256,512]{1,0:T(8,128)(2,1)S(1)}, f32[256,512]{1,0:T(8,128)S(1)}, f32[512,512]{1,0:T(8,128)S(1)}) custom-call(s32[3]{0:T(128)S(1)} %pad_add_fusion._, bf16[512,512]{1,0:T(8,128)(2,1)S(1)} %gate_blocks.1.a_ref, bf16[512,512]{1,0:T(8,128)(2,1)S(1)} %collective-permute-done.24.b_ref, ...), custom_call_target="tpu_custom_call" | custom-call | flops 1000000000 | bytes 1048576 | tf_op jit(solution)/shard_map/output_shares/pallas_call | solution.py:61
  84.1 3.5 %collective-permute-start.27 = (bf16[256,512]{1,0:T(8,128)(2,1)S(1)}, bf16[256,512]{1,0:T(8,128)(2,1)S(1)}, u32[]{:S(2)}, u32[]{:S(2)}) collective-permute-start(bf16[256,512]{1,0:T(8,128)(2,1)S(1)} %get-tuple-element.65), channel_id=1, source_target_pairs={{0,6},{1,7},{2,0},{3,1},{4,2},{5,3},{6,4},{7,5},{8,14},{9,15},{10,... | collective-permute-start | bytes 786440 | tf_op jit(solution)/shard_map/ppermute | solution.py:37
  87.6 6.0 %collective-permute-done.29 = bf16[256,512]{1,0:T(8,128)(2,1)S(1)} collective-permute-done((bf16[256,512]{1,0:T(8,128)(2,1)S(1)}, bf16[256,512]{1,0:T(8,128)(2,1)S(1)}, u32[]{:S(2)}, u32[]{:S(2)}) %collective-permute-start.29) | collective-permute-done | bytes 262176 | tf_op jit(solution)/shard_map/ppermute | solution.py:37
  93.6 0.1 add_convert_fusion
  93.6 0.1 collective-permute-start.30
  93.7 0.1 add_convert_fusion.1
  93.8 2.1 %collective-permute-start.26 = (bf16[256,512]{1,0:T(8,128)(2,1)S(1)}, bf16[256,512]{1,0:T(8,128)(2,1)S(1)}, u32[]{:S(2)}, u32[]{:S(2)}) collective-permute-start(bf16[256,512]{1,0:T(8,128)(2,1)S(1)} %add_convert_fusion.1), channel_id=1, source_target_pairs={{0,2},{1,3},{2,4},{3,5},{4,6},{5,7},{6,0},{7,1},{8,10},{9,11},{10,... | collective-permute-start | bytes 786440 | tf_op jit(solution)/shard_map/ppermute | solution.py:37
  95.9 8.9 %collective-permute-done.27.refs_1_ = bf16[256,512]{1,0:T(8,128)(2,1)S(1)} collective-permute-done((bf16[256,512]{1,0:T(8,128)(2,1)S(1)}, bf16[256,512]{1,0:T(8,128)(2,1)S(1)}, u32[]{:S(2)}, u32[]{:S(2)}) %collective-permute-start.27) | collective-permute-done | bytes 262176 | tf_op jit(solution)/shard_map/ppermute | solution.py:37
  104.8 5.5 %collective-permute-done.30.refs_3_ = bf16[256,512]{1,0:T(8,128)(2,1)S(1)} collective-permute-done((bf16[256,512]{1,0:T(8,128)(2,1)S(1)}, bf16[256,512]{1,0:T(8,128)(2,1)S(1)}, u32[]{:S(2)}, u32[]{:S(2)}) %collective-permute-start.30) | collective-permute-done | bytes 262176 | tf_op jit(solution)/shard_map/ppermute | solution.py:37
  110.3 4.9 %collective-permute-done.26.refs_0_ = bf16[256,512]{1,0:T(8,128)(2,1)S(1)} collective-permute-done((bf16[256,512]{1,0:T(8,128)(2,1)S(1)}, bf16[256,512]{1,0:T(8,128)(2,1)S(1)}, u32[]{:S(2)}, u32[]{:S(2)}) %collective-permute-start.26) | collective-permute-done | bytes 262176 | tf_op jit(solution)/shard_map/ppermute | solution.py:37
  115.2 1.0 add_up.1
  (53 shorter events, 0.2 us)
Async XLA Ops:
  1.0 19.7 %collective-permute-start.6 = (bf16[256,512]{1,0:T(8,128)(2,1)S(1)}, bf16[256,512]{1,0:T(8,128)(2,1)S(1)}, u32[]{:S(2)}, u32[]{:S(2)}) collective-permute-start(bf16[256,512]{1,0:T(8,128)(2,1)S(1)} %slice.18), channel_id=1, source_target_pairs={{0,2},{1,3},{2,4},{3,5},{4,6},{5,7},{6,0},{7,1},{8,10},{9,11},{10,... | collective-permute-start | bytes 786440 | tf_op jit(solution)/shard_map/ppermute | solution.py:37
  5.0 15.7 %collective-permute-start = (bf16[256,512]{1,0:T(8,128)(2,1)S(1)}, bf16[256,512]{1,0:T(8,128)(2,1)S(1)}, u32[]{:S(2)}, u32[]{:S(2)}) collective-permute-start(bf16[256,512]{1,0:T(8,128)(2,1)S(1)} %slice.19), channel_id=1, source_target_pairs={{0,6},{1,7},{2,0},{3,1},{4,2},{5,3},{6,4},{7,5},{8,14},{9,15},{10,... | collective-permute-start | bytes 786440 | tf_op jit(solution)/shard_map/ppermute | solution.py:37
  7.1 20.0 %collective-permute-start.7 = (bf16[256,512]{1,0:T(8,128)(2,1)S(1)}, bf16[256,512]{1,0:T(8,128)(2,1)S(1)}, u32[]{:S(2)}, u32[]{:S(2)}) collective-permute-start(bf16[256,512]{1,0:T(8,128)(2,1)S(1)} %slice.19), channel_id=1, source_target_pairs={{0,2},{1,3},{2,4},{3,5},{4,6},{5,7},{6,0},{7,1},{8,10},{9,11},{10,... | collective-permute-start | bytes 786440 | tf_op jit(solution)/shard_map/ppermute | solution.py:37
  7.1 22.9 %collective-permute-start.10 = (bf16[256,512]{1,0:T(8,128)(2,1)S(1)}, bf16[256,512]{1,0:T(8,128)(2,1)S(1)}, u32[]{:S(2)}, u32[]{:S(2)}) collective-permute-start(bf16[256,512]{1,0:T(8,128)(2,1)S(1)} %slice.18), channel_id=1, source_target_pairs={{0,6},{1,7},{2,0},{3,1},{4,2},{5,3},{6,4},{7,5},{8,14},{9,15},{10,... | collective-permute-start | bytes 786440 | tf_op jit(solution)/shard_map/ppermute | solution.py:37
  12.2 5.0 %collective-permute-start.2 = (bf16[512,128]{1,0:T(8,128)(2,1)S(1)}, bf16[512,128]{1,0:T(8,128)(2,1)S(1)}, u32[]{:S(2)}, u32[]{:S(2)}) collective-permute-start(bf16[512,128]{1,0:T(8,128)(2,1)S(1)} %get-tuple-element.79), channel_id=1, source_target_pairs={{0,8},{8,0},{16,24},{24,16},{1,9},{9,1},{17,25},{25,17},{2,10},{10... | collective-permute-start | bytes 393224 | tf_op jit(solution)/shard_map/ppermute | solution.py:512
  14.0 6.7 %copy-start.8 = (bf16[3,3,512]{2,1,0:T(4,128)(2,1)S(1)}, bf16[3,3,512]{2,1,0:T(4,128)(2,1)}, u32[]{:S(2)}) copy-start(bf16[3,3,512]{2,1,0:T(4,128)(2,1)} %param.11) | copy-start | bytes 27652
  17.3 5.0 %collective-permute-start.3 = (bf16[512,128]{1,0:T(8,128)(2,1)S(1)}, bf16[512,128]{1,0:T(8,128)(2,1)S(1)}, u32[]{:S(2)}, u32[]{:S(2)}) collective-permute-start(bf16[512,128]{1,0:T(8,128)(2,1)S(1)} %get-tuple-element.38), channel_id=1, source_target_pairs={{0,16},{8,24},{16,0},{24,8},{1,17},{9,25},{17,1},{25,9},{2,18},{10... | collective-permute-start | bytes 393224 | tf_op jit(solution)/shard_map/ppermute | solution.py:512
  20.6 6.5 %copy-start = (bf16[512,512]{1,0:T(8,128)(2,1)S(1)}, bf16[512,512]{1,0:T(8,128)(2,1)}, u32[]{:S(2)}) copy-start(bf16[512,512]{1,0:T(8,128)(2,1)} %refs_0_) | copy-start | bytes 1572868
  20.7 14.3 %collective-permute-start.13 = (bf16[256,512]{1,0:T(8,128)(2,1)S(1)}, bf16[256,512]{1,0:T(8,128)(2,1)S(1)}, u32[]{:S(2)}, u32[]{:S(2)}) collective-permute-start(bf16[256,512]{1,0:T(8,128)(2,1)S(1)} %collective-permute-done.6.refs_2_), channel_id=1, source_target_pairs={{0,2},{1,3},{2,4},{3,5},{4,6},{5,7},{6,0},{7,1},{8,10},{9,11},{10,... | collective-permute-start | bytes 786440 | tf_op jit(solution)/shard_map/ppermute | solution.py:37
  20.7 14.2 %collective-permute-start.12 = (bf16[256,512]{1,0:T(8,128)(2,1)S(1)}, bf16[256,512]{1,0:T(8,128)(2,1)S(1)}, u32[]{:S(2)}, u32[]{:S(2)}) collective-permute-start(bf16[256,512]{1,0:T(8,128)(2,1)S(1)} %collective-permute-done.refs_7_), channel_id=1, source_target_pairs={{0,1},{1,0},{2,3},{3,2},{4,5},{5,4},{6,7},{7,6},{8,9},{9,8},{10,11... | collective-permute-start | bytes 786440 | tf_op jit(solution)/shard_map/ppermute | solution.py:41
  21.7 13.7 %copy-start.2 = (bf16[1024,1024]{1,0:T(8,128)(2,1)S(1)}, bf16[1024,1024]{1,0:T(8,128)(2,1)}, u32[]{:S(2)}) copy-start(bf16[1024,1024]{1,0:T(8,128)(2,1)} %constant.109.clone.refs_4_) | copy-start | bytes 6291460
  22.2 7.7 %collective-permute-start.4 = (bf16[512,128]{1,0:T(8,128)(2,1)S(1)}, bf16[512,128]{1,0:T(8,128)(2,1)S(1)}, u32[]{:S(2)}, u32[]{:S(2)}) collective-permute-start(bf16[512,128]{1,0:T(8,128)(2,1)S(1)} %get-tuple-element.39), channel_id=1, source_target_pairs={{0,24},{8,16},{16,8},{24,0},{1,25},{9,17},{17,9},{25,1},{2,26},{10... | collective-permute-start | bytes 393224 | tf_op jit(solution)/shard_map/ppermute | solution.py:512
  24.9 14.6 %slice-start = ((s8[12582912]{0:T(1024)(128)(4,1)}), s8[4194304]{0:T(1024)(128)(4,1)S(1)}, s32[]{:S(2)}) async-start(s8[12582912]{0:T(1024)(128)(4,1)} %bitcast.27), calls=%async_computation | async-start | bytes 8388608
  27.2 12.3 %collective-permute-start.5 = (bf16[512,512]{1,0:T(8,128)(2,1)S(1)}, bf16[512,512]{1,0:T(8,128)(2,1)S(1)}, u32[]{:S(2)}, u32[]{:S(2)}) collective-permute-start(bf16[512,512]{1,0:T(8,128)(2,1)S(1)} %copy-done), channel_id=1, source_target_pairs={{0,1},{1,0},{2,3},{3,2},{4,5},{5,4},{6,7},{7,6},{8,9},{9,8},{10,11... | collective-permute-start | bytes 1572872 | tf_op jit(solution)/shard_map/ppermute | solution.py:41
  30.0 9.5 %collective-permute-start.8 = (bf16[256,512]{1,0:T(8,128)(2,1)S(1)}, bf16[256,512]{1,0:T(8,128)(2,1)S(1)}, u32[]{:S(2)}, u32[]{:S(2)}) collective-permute-start(bf16[256,512]{1,0:T(8,128)(2,1)S(1)} %collective-permute-done.6.refs_2_), channel_id=1, source_target_pairs={{0,1},{1,0},{2,3},{3,2},{4,5},{5,4},{6,7},{7,6},{8,9},{9,8},{10,11... | collective-permute-start | bytes 786440 | tf_op jit(solution)/shard_map/ppermute | solution.py:41
  30.0 7.9 %collective-permute-start.9 = (bf16[256,512]{1,0:T(8,128)(2,1)S(1)}, bf16[256,512]{1,0:T(8,128)(2,1)S(1)}, u32[]{:S(2)}, u32[]{:S(2)}) collective-permute-start(bf16[256,512]{1,0:T(8,128)(2,1)S(1)} %collective-permute-done.7.refs_3_), channel_id=1, source_target_pairs={{0,1},{1,0},{2,3},{3,2},{4,5},{5,4},{6,7},{7,6},{8,9},{9,8},{10,11... | collective-permute-start | bytes 786440 | tf_op jit(solution)/shard_map/ppermute | solution.py:41
  34.9 4.6 %collective-permute-start.11 = (bf16[256,512]{1,0:T(8,128)(2,1)S(1)}, bf16[256,512]{1,0:T(8,128)(2,1)S(1)}, u32[]{:S(2)}, u32[]{:S(2)}) collective-permute-start(bf16[256,512]{1,0:T(8,128)(2,1)S(1)} %collective-permute-done.10.refs_6_), channel_id=1, source_target_pairs={{0,1},{1,0},{2,3},{3,2},{4,5},{5,4},{6,7},{7,6},{8,9},{9,8},{10,11... | collective-permute-start | bytes 786440 | tf_op jit(solution)/shard_map/ppermute | solution.py:41
  34.9 4.6 %collective-permute-start.14 = (bf16[256,512]{1,0:T(8,128)(2,1)S(1)}, bf16[256,512]{1,0:T(8,128)(2,1)S(1)}, u32[]{:S(2)}, u32[]{:S(2)}) collective-permute-start(bf16[256,512]{1,0:T(8,128)(2,1)S(1)} %collective-permute-done.13.refs_10_), channel_id=1, source_target_pairs={{0,1},{1,0},{2,3},{3,2},{4,5},{5,4},{6,7},{7,6},{8,9},{9,8},{10,11... | collective-permute-start | bytes 786440 | tf_op jit(solution)/shard_map/ppermute | solution.py:41
  35.5 4.1 %slice-start.1 = ((s8[12582912]{0:T(1024)(128)(4,1)}), s8[4194304]{0:T(1024)(128)(4,1)S(1)}, s32[]{:S(2)}) async-start(s8[12582912]{0:T(1024)(128)(4,1)} %bitcast.27), calls=%async_computation.1 | async-start | bytes 8388608
  35.5 4.1 %slice-start.2 = ((s8[12582912]{0:T(1024)(128)(4,1)}), s8[4194304]{0:T(1024)(128)(4,1)S(1)}, s32[]{:S(2)}) async-start(s8[12582912]{0:T(1024)(128)(4,1)} %bitcast.27), calls=%async_computation.2 | async-start | bytes 8388608
  37.8 10.0 %collective-permute-start.1 = (bf16[256,512]{1,0:T(8,128)(2,1)S(1)}, bf16[256,512]{1,0:T(8,128)(2,1)S(1)}, u32[]{:S(2)}, u32[]{:S(2)}) collective-permute-start(bf16[256,512]{1,0:T(8,128)(2,1)S(1)} %collective-permute-done.refs_7_), channel_id=1, source_target_pairs={{0,6},{1,7},{2,0},{3,1},{4,2},{5,3},{6,4},{7,5},{8,14},{9,15},{10,... | collective-permute-start | bytes 786440 | tf_op jit(solution)/shard_map/ppermute | solution.py:37
  47.8 1.6 %collective-permute-start.15 = (bf16[256,512]{1,0:T(8,128)(2,1)S(1)}, bf16[256,512]{1,0:T(8,128)(2,1)S(1)}, u32[]{:S(2)}, u32[]{:S(2)}) collective-permute-start(bf16[256,512]{1,0:T(8,128)(2,1)S(1)} %collective-permute-done.1.own_ref), channel_id=1, source_target_pairs={{0,1},{1,0},{2,3},{3,2},{4,5},{5,4},{6,7},{7,6},{8,9},{9,8},{10,11... | collective-permute-start | bytes 786440 | tf_op jit(solution)/shard_map/ppermute | solution.py:41
  53.8 13.4 %collective-permute-start.20 = (bf16[512,2048]{1,0:T(8,128)(2,1)}, bf16[512,2048]{1,0:T(8,128)(2,1)S(1)}, u32[]{:S(2)}, u32[]{:S(2)}) collective-permute-start(bf16[512,2048]{1,0:T(8,128)(2,1)} %pad_maximum_fusion), channel_id=1, source_target_pairs={{0,1},{1,0},{2,3},{3,2},{4,5},{5,4},{6,7},{7,6},{8,9},{9,8},{10,11... | collective-permute-start | bytes 6291464 | tf_op jit(solution)/shard_map/ppermute | solution.py:41
  54.0 6.6 %collective-permute-start.16 = (bf16[544,128]{1,0:T(8,128)(2,1)}, bf16[544,128]{1,0:T(8,128)(2,1)S(1)}, u32[]{:S(2)}, u32[]{:S(2)}) collective-permute-start(bf16[544,128]{1,0:T(8,128)(2,1)} %get-tuple-element.46), channel_id=1, source_target_pairs={{0,8},{8,0},{16,24},{24,16},{1,9},{9,1},{17,25},{25,17},{2,10},{10... | collective-permute-start | bytes 417800 | tf_op jit(solution)/shard_map/ppermute | solution.py:512
  55.5 9.0 %collective-permute-start.18 = (bf16[544,128]{1,0:T(8,128)(2,1)}, bf16[544,128]{1,0:T(8,128)(2,1)S(1)}, u32[]{:S(2)}, u32[]{:S(2)}) collective-permute-start(bf16[544,128]{1,0:T(8,128)(2,1)} %get-tuple-element.49), channel_id=1, source_target_pairs={{0,16},{8,24},{16,0},{24,8},{1,17},{9,25},{17,1},{25,9},{2,18},{10... | collective-permute-start | bytes 417800 | tf_op jit(solution)/shard_map/ppermute | solution.py:512
  57.0 3.6 %copy-start.1 = (bf16[16,512]{1,0:T(8,128)(2,1)S(1)}, bf16[16,512]{1,0:T(8,128)(2,1)}, u32[]{:S(2)}) copy-start(bf16[16,512]{1,0:T(8,128)(2,1)} %get-tuple-element.47.here_ref) | copy-start | bytes 49156
  57.0 7.5 %copy-start.3 = (bf16[512,1024]{1,0:T(8,128)(2,1)S(1)}, bf16[512,1024]{1,0:T(8,128)(2,1)}, u32[]{:S(2)}) copy-start(bf16[512,1024]{1,0:T(8,128)(2,1)} %constant.110.clone.refs_7_) | copy-start | bytes 3145732
  57.0 7.5 %copy-start.4 = (bf16[1024,512]{1,0:T(8,128)(2,1)S(1)}, bf16[1024,512]{1,0:T(8,128)(2,1)}, u32[]{:S(2)}) copy-start(bf16[1024,512]{1,0:T(8,128)(2,1)} %constant.111.clone.refs_6_) | copy-start | bytes 3145732
  57.0 7.5 %copy-start.6 = (bf16[1024,512]{1,0:T(8,128)(2,1)S(1)}, bf16[1024,512]{1,0:T(8,128)(2,1)}, u32[]{:S(2)}) copy-start(bf16[1024,512]{1,0:T(8,128)(2,1)} %taps_spectra.1.refs_5_) | copy-start | bytes 3145732
  57.0 7.5 %copy-start.7 = (bf16[544,128]{1,0:T(8,128)(2,1)S(1)}, bf16[544,128]{1,0:T(8,128)(2,1)}, u32[]{:S(2)}) copy-start(bf16[544,128]{1,0:T(8,128)(2,1)} %get-tuple-element.48.refs_0_) | copy-start | bytes 417796
  57.0 7.5 %collective-permute-start.19 = (bf16[544,128]{1,0:T(8,128)(2,1)}, bf16[544,128]{1,0:T(8,128)(2,1)S(1)}, u32[]{:S(2)}, u32[]{:S(2)}) collective-permute-start(bf16[544,128]{1,0:T(8,128)(2,1)} %get-tuple-element.50), channel_id=1, source_target_pairs={{0,24},{8,16},{16,8},{24,0},{1,25},{9,17},{17,9},{25,1},{2,26},{10... | collective-permute-start | bytes 417800 | tf_op jit(solution)/shard_map/ppermute | solution.py:512
  60.6 10.2 %collective-permute-start.17 = (bf16[16,512]{1,0:T(8,128)(2,1)S(1)}, bf16[16,512]{1,0:T(8,128)(2,1)S(1)}, u32[]{:S(2)}, u32[]{:S(2)}) collective-permute-start(bf16[16,512]{1,0:T(8,128)(2,1)S(1)} %copy-done.1), channel_id=1, source_target_pairs={{0,8},{8,16},{16,24},{24,0},{1,9},{9,17},{17,25},{25,1},{2,10},{10... | collective-permute-start | bytes 49160 | tf_op jit(solution)/shard_map/ppermute | solution.py:37
  64.5 11.3 %copy-start.5 = (bf16[512,512]{1,0:T(8,128)(2,1)S(1)}, bf16[512,512]{1,0:T(8,128)(2,1)}, u32[]{:S(2)}) copy-start(bf16[512,512]{1,0:T(8,128)(2,1)} %get-tuple-element.44.gate_ref) | copy-start | bytes 1572868
  67.2 6.0 %collective-permute-start.21 = (bf16[512,128]{1,0:T(8,128)(2,1)S(1)}, bf16[512,128]{1,0:T(8,128)(2,1)S(1)}, u32[]{:S(2)}, u32[]{:S(2)}) collective-permute-start(bf16[512,128]{1,0:T(8,128)(2,1)S(1)} %get-tuple-element.59), channel_id=1, source_target_pairs={{0,8},{8,0},{16,24},{24,16},{1,9},{9,1},{17,25},{25,17},{2,10},{10... | collective-permute-start | bytes 393224 | tf_op jit(solution)/shard_map/ppermute | solution.py:512
  68.5 7.3 %collective-permute-start.22 = (bf16[512,128]{1,0:T(8,128)(2,1)S(1)}, bf16[512,128]{1,0:T(8,128)(2,1)S(1)}, u32[]{:S(2)}, u32[]{:S(2)}) collective-permute-start(bf16[512,128]{1,0:T(8,128)(2,1)S(1)} %get-tuple-element.60), channel_id=1, source_target_pairs={{0,16},{8,24},{16,0},{24,8},{1,17},{9,25},{17,1},{25,9},{2,18},{10... | collective-permute-start | bytes 393224 | tf_op jit(solution)/shard_map/ppermute | solution.py:512
  69.1 6.7 %collective-permute-start.23 = (bf16[512,128]{1,0:T(8,128)(2,1)S(1)}, bf16[512,128]{1,0:T(8,128)(2,1)S(1)}, u32[]{:S(2)}, u32[]{:S(2)}) collective-permute-start(bf16[512,128]{1,0:T(8,128)(2,1)S(1)} %get-tuple-element.61), channel_id=1, source_target_pairs={{0,24},{8,16},{16,8},{24,0},{1,25},{9,17},{17,9},{25,1},{2,26},{10... | collective-permute-start | bytes 393224 | tf_op jit(solution)/shard_map/ppermute | solution.py:512
  76.0 2.0 %collective-permute-start.24 = (bf16[512,512]{1,0:T(8,128)(2,1)S(1)}, bf16[512,512]{1,0:T(8,128)(2,1)S(1)}, u32[]{:S(2)}, u32[]{:S(2)}) collective-permute-start(bf16[512,512]{1,0:T(8,128)(2,1)S(1)} %gate_blocks.1.a_ref), channel_id=1, source_target_pairs={{0,1},{1,0},{2,3},{3,2},{4,5},{5,4},{6,7},{7,6},{8,9},{9,8},{10,11... | collective-permute-start | bytes 1572872 | tf_op jit(solution)/shard_map/ppermute | solution.py:41
  78.7 14.8 %collective-permute-start.29 = (bf16[256,512]{1,0:T(8,128)(2,1)S(1)}, bf16[256,512]{1,0:T(8,128)(2,1)S(1)}, u32[]{:S(2)}, u32[]{:S(2)}) collective-permute-start(bf16[256,512]{1,0:T(8,128)(2,1)S(1)} %get-tuple-element.67), channel_id=1, source_target_pairs={{0,6},{1,7},{2,0},{3,1},{4,2},{5,3},{6,4},{7,5},{8,14},{9,15},{10,... | collective-permute-start | bytes 786440 | tf_op jit(solution)/shard_map/ppermute | solution.py:37
  80.5 13.2 %collective-permute-start.25 = (bf16[256,512]{1,0:T(8,128)(2,1)S(1)}, bf16[256,512]{1,0:T(8,128)(2,1)S(1)}, u32[]{:S(2)}, u32[]{:S(2)}) collective-permute-start(bf16[256,512]{1,0:T(8,128)(2,1)S(1)} %get-tuple-element.63), channel_id=1, source_target_pairs={{0,2},{1,3},{2,4},{3,5},{4,6},{5,7},{6,0},{7,1},{8,10},{9,11},{10,... | collective-permute-start | bytes 786440 | tf_op jit(solution)/shard_map/ppermute | solution.py:37
  84.1 20.7 %collective-permute-start.27 = (bf16[256,512]{1,0:T(8,128)(2,1)S(1)}, bf16[256,512]{1,0:T(8,128)(2,1)S(1)}, u32[]{:S(2)}, u32[]{:S(2)}) collective-permute-start(bf16[256,512]{1,0:T(8,128)(2,1)S(1)} %get-tuple-element.65), channel_id=1, source_target_pairs={{0,6},{1,7},{2,0},{3,1},{4,2},{5,3},{6,4},{7,5},{8,14},{9,15},{10,... | collective-permute-start | bytes 786440 | tf_op jit(solution)/shard_map/ppermute | solution.py:37
  87.5 17.2 %collective-permute-start.28 = (bf16[256,512]{1,0:T(8,128)(2,1)S(1)}, bf16[256,512]{1,0:T(8,128)(2,1)S(1)}, u32[]{:S(2)}, u32[]{:S(2)}) collective-permute-start(bf16[256,512]{1,0:T(8,128)(2,1)S(1)} %get-tuple-element.66), channel_id=1, source_target_pairs={{0,2},{1,3},{2,4},{3,5},{4,6},{5,7},{6,0},{7,1},{8,10},{9,11},{10,... | collective-permute-start | bytes 786440 | tf_op jit(solution)/shard_map/ppermute | solution.py:37
  93.6 16.7 %collective-permute-start.30 = (bf16[256,512]{1,0:T(8,128)(2,1)S(1)}, bf16[256,512]{1,0:T(8,128)(2,1)S(1)}, u32[]{:S(2)}, u32[]{:S(2)}) collective-permute-start(bf16[256,512]{1,0:T(8,128)(2,1)S(1)} %add_convert_fusion), channel_id=1, source_target_pairs={{0,6},{1,7},{2,0},{3,1},{4,2},{5,3},{6,4},{7,5},{8,14},{9,15},{10,... | collective-permute-start | bytes 786440 | tf_op jit(solution)/shard_map/ppermute | solution.py:37
  93.8 21.4 %collective-permute-start.26 = (bf16[256,512]{1,0:T(8,128)(2,1)S(1)}, bf16[256,512]{1,0:T(8,128)(2,1)S(1)}, u32[]{:S(2)}, u32[]{:S(2)}) collective-permute-start(bf16[256,512]{1,0:T(8,128)(2,1)S(1)} %add_convert_fusion.1), channel_id=1, source_target_pairs={{0,2},{1,3},{2,4},{3,5},{4,6},{5,7},{6,0},{7,1},{8,10},{9,11},{10,... | collective-permute-start | bytes 786440 | tf_op jit(solution)/shard_map/ppermute | solution.py:37

commit v8 on v7

--- a/solution.py
+++ b/solution.py
@@ -671,7 +671,8 @@
         offsets += [d, -d]
         plan.append([(0, half, F32), (half, span, BF16 if last else F32)])
         plan.append([(0, half, BF16 if last else F32), (half, span, F32)])
-    kept = list(shares(offsets + [0], plan + [[(0, span, F32)]]))
+    kept = list(shares(offsets, plan)) if offsets else []
+    kept += list(shares([0], [[(0, span, F32)]]))
     up_top, down_low = shift(up_top, "chan", 2), shift(down_low, "chan", -2)
     up_low = down_top = None
 

time: 116 us -> 116 us (level)
    pallas_call x8 -> x9, Pallas kernels: 22.7 us -> 22.5 us  [call(): pl.pallas_call(kernel, grid_spec=pltpu.PrefetchScalarGridSpec(num_scalar_...]
where the time goes in v8:
time: 116 us
  waiting for transfers between devices  46.3 us (40%)
  starting transfers between devices  34.8 us (30%)
  Pallas kernels  22.5 us (19%)
  local copies, waits for them, and re-layouts  9.92 us (9%)
  other arithmetic  2.34 us (2%)
    ppermute x13, waiting for transfers between devices, shift(): lax.ppermute(x, axis, [(i, (i + distance) % size) for i in range(size)])  32.7 us
    pallas_call x9, Pallas kernels, call(): pl.pallas_call(kernel, grid_spec=pltpu.PrefetchScalarGridSpec(num_scalar_...  22.5 us
    ppermute x13, starting transfers between devices, shift(): lax.ppermute(x, axis, [(i, (i + distance) % size) for i in range(size)])  20 us
    ppermute x9, starting transfers between devices, exchange(): found.append(lax.ppermute(block, 'ctx', route))  13.3 us
    ppermute x9, waiting for transfers between devices, exchange(): found.append(lax.ppermute(block, 'ctx', route))  10.2 us
    dynamic_slice x2, local copies, waits for them, and re-layouts, columns(): lax.dynamic_slice_in_dim(w, c, out_width, 1)  3.63 us
    ppermute x9, waiting for transfers between devices, sibling(): lax.ppermute(x, 'chan', [(i, i ^ 1) for i in range(lax.axis_size('chan'))])  3.34 us
  transfers between devices with their start and end apart: 31, of which 14 were waited for; matrix products, arithmetic and copies ran while one was open for 10% of the time, Pallas kernels for 14%

profile of v8, /device:TPU:0, one launch (start us, length us, event | category | flops | bytes accessed | tf_op | source)
XLA Modules:
  0.0 116.2 jit_solution(17222530461218373142)
XLA Ops:
  0.0 1.0 slice.18
  1.0 3.1 %collective-permute-start.6 = (bf16[256,512]{1,0:T(8,128)(2,1)S(1)}, bf16[256,512]{1,0:T(8,128)(2,1)S(1)}, u32[]{:S(2)}, u32[]{:S(2)}) collective-permute-start(bf16[256,512]{1,0:T(8,128)(2,1)S(1)} %slice.18), channel_id=1, source_target_pairs={{0,2},{1,3},{2,4},{3,5},{4,6},{5,7},{6,0},{7,1},{8,10},{9,11},{10,... | collective-permute-start | bytes 786440 | tf_op jit(solution)/shard_map/ppermute | solution.py:37
  4.0 1.0 slice.19
  5.0 2.1 %collective-permute-start = (bf16[256,512]{1,0:T(8,128)(2,1)S(1)}, bf16[256,512]{1,0:T(8,128)(2,1)S(1)}, u32[]{:S(2)}, u32[]{:S(2)}) collective-permute-start(bf16[256,512]{1,0:T(8,128)(2,1)S(1)} %slice.19), channel_id=1, source_target_pairs={{0,6},{1,7},{2,0},{3,1},{4,2},{5,3},{6,4},{7,5},{8,14},{9,15},{10,... | collective-permute-start | bytes 786440 | tf_op jit(solution)/shard_map/ppermute | solution.py:37
  7.1 3.8 %collective-permute-start.10 = (bf16[256,512]{1,0:T(8,128)(2,1)S(1)}, bf16[256,512]{1,0:T(8,128)(2,1)S(1)}, u32[]{:S(2)}, u32[]{:S(2)}) collective-permute-start(bf16[256,512]{1,0:T(8,128)(2,1)S(1)} %slice.18), channel_id=1, source_target_pairs={{0,6},{1,7},{2,0},{3,1},{4,2},{5,3},{6,4},{7,5},{8,14},{9,15},{10,... | collective-permute-start | bytes 786440 | tf_op jit(solution)/shard_map/ppermute | solution.py:37
  10.9 1.1 slice_bitcast_fusion.3
  12.1 0.1 pad_maximum_fusion.2
  12.2 1.8 %collective-permute-start.2 = (bf16[512,128]{1,0:T(8,128)(2,1)S(1)}, bf16[512,128]{1,0:T(8,128)(2,1)S(1)}, u32[]{:S(2)}, u32[]{:S(2)}) collective-permute-start(bf16[512,128]{1,0:T(8,128)(2,1)S(1)} %get-tuple-element.77), channel_id=1, source_target_pairs={{0,8},{8,0},{16,24},{24,16},{1,9},{9,1},{17,25},{25,17},{2,10},{10... | collective-permute-start | bytes 393224 | tf_op jit(solution)/shard_map/ppermute | solution.py:512
  14.0 1.7 %constant_dynamic-slice_fusion.8 = (bf16[512,512]{1,0:T(8,128)(2,1)S(1)}, bf16[512,512]{1,0:T(8,128)(2,1)S(1)}, bf16[512,512]{1,0:T(8,128)(2,1)S(1)}, bf16[512,512]{1,0:T(8,128)(2,1)S(1)}) fusion(bf16[512,4096]{1,0:T(8,128)(2,1)} %param.14, s32[]{:T(128)S(6)} %select_n.97, s32[]{:T(128)S(6)} %select_n.99, s32[]{:T(128)S(6)} %select_n.98, s32[]{:T(128)S(6)} %select_n.100), kind=kLoop, calls=%fused_computation.23 | loop fusion | bytes 4194320 | tf_op jit(solution)/shard_map/dynamic_slice | solution.py:610
  15.7 1.6 %collective-permute-done.2.refs_1_ = bf16[512,128]{1,0:T(8,128)(2,1)S(1)} collective-permute-done((bf16[512,128]{1,0:T(8,128)(2,1)S(1)}, bf16[512,128]{1,0:T(8,128)(2,1)S(1)}, u32[]{:S(2)}, u32[]{:S(2)}) %collective-permute-start.2) | collective-permute-done | bytes 131104 | tf_op jit(solution)/shard_map/ppermute | solution.py:512
  17.3 1.7 %collective-permute-start.3 = (bf16[512,128]{1,0:T(8,128)(2,1)S(1)}, bf16[512,128]{1,0:T(8,128)(2,1)S(1)}, u32[]{:S(2)}, u32[]{:S(2)}) collective-permute-start(bf16[512,128]{1,0:T(8,128)(2,1)S(1)} %get-tuple-element.37), channel_id=1, source_target_pairs={{0,16},{8,24},{16,0},{24,8},{1,17},{9,25},{17,1},{25,9},{2,18},{10... | collective-permute-start | bytes 393224 | tf_op jit(solution)/shard_map/ppermute | solution.py:512
  19.0 1.7 %pad_maximum_fusion = bf16[512,2048]{1,0:T(8,128)(2,1)} fusion(bf16[512,512]{1,0:T(8,128)(2,1)S(1)} %get-tuple-element.74, bf16[512,512]{1,0:T(8,128)(2,1)S(1)} %get-tuple-element.72, bf16[512,512]{1,0:T(8,128)(2,1)S(1)} %get-tuple-element.73, bf16[512,512]{1,0:T(8,128)(2,1)S(1)} %get-tuple-element.71), kind=kLoop, calls=%fused_computation.1 | loop fusion | flops 8388608 | bytes 4194304 | tf_op jit(solution)/shard_map/concatenate | solution.py:610
  20.7 0.1 collective-permute-start.13
  20.7 0.1 collective-permute-start.12
  20.9 0.8 dynamic_slice.51
  21.6 0.1 stack.53.ids
  21.7 0.5 collective-permute-done.3.refs_2_
  22.2 2.7 %collective-permute-start.4 = (bf16[512,128]{1,0:T(8,128)(2,1)S(1)}, bf16[512,128]{1,0:T(8,128)(2,1)S(1)}, u32[]{:S(2)}, u32[]{:S(2)}) collective-permute-start(bf16[512,128]{1,0:T(8,128)(2,1)S(1)} %get-tuple-element.38), channel_id=1, source_target_pairs={{0,24},{8,16},{16,8},{24,0},{1,25},{9,17},{17,9},{25,1},{2,26},{10... | collective-permute-start | bytes 393224 | tf_op jit(solution)/shard_map/ppermute | solution.py:512
  24.9 2.2 %dynamic-slice_bitcast_fusion.w_ref = bf16[3,1024,512]{2,1,0:T(8,128)(2,1)S(1)} fusion(bf16[4096,3,512]{2,0,1:T(8,128)(2,1)} %param.10, s32[]{:T(128)S(6)} %select_n.102), kind=kLoop, calls=%fused_computation | loop fusion | bytes 6291460 | tf_op jit(solution)/shard_map/dynamic_slice | solution.py:613
  27.2 0.1 collective-permute-start.5
  27.2 2.7 %collective-permute-done.10.refs_6_ = bf16[256,512]{1,0:T(8,128)(2,1)S(1)} collective-permute-done((bf16[256,512]{1,0:T(8,128)(2,1)S(1)}, bf16[256,512]{1,0:T(8,128)(2,1)S(1)}, u32[]{:S(2)}, u32[]{:S(2)}) %collective-permute-start.10) | collective-permute-done | bytes 262176 | tf_op jit(solution)/shard_map/ppermute | solution.py:37
  30.0 0.5 collective-permute-start.9
  30.5 4.4 %collective-permute-done.13.refs_10_ = bf16[256,512]{1,0:T(8,128)(2,1)S(1)} collective-permute-done((bf16[256,512]{1,0:T(8,128)(2,1)S(1)}, bf16[256,512]{1,0:T(8,128)(2,1)S(1)}, u32[]{:S(2)}, u32[]{:S(2)}) %collective-permute-start.13) | collective-permute-done | bytes 262176 | tf_op jit(solution)/shard_map/ppermute | solution.py:37
  34.9 0.5 collective-permute-start.14
  35.5 2.4 %taps_spectra.1.refs_5_ = bf16[1024,512]{1,0:T(8,128)(2,1)} custom-call(s32[1]{0:T(128)} %bitcast.1.at, bf16[512,128]{1,0:T(8,128)(2,1)S(1)} %get-tuple-element.78.refs_0_, bf16[512,128]{1,0:T(8,128)(2,1)S(1)} %collective-permute-done.2.refs_1_, bf16[512,128]{1,0:T(8,128)(2,1)S(1)} %collective-permute-done.3.refs_2_, ...), custom_call_target="tpu_custom_call" | custom-call | flops 20000000000 | bytes 20971520 | tf_op jit(solution)/shard_map/taps_spectra/pallas_call | solution.py:61
  37.8 1.6 %collective-permute-start.1 = (bf16[256,512]{1,0:T(8,128)(2,1)S(1)}, bf16[256,512]{1,0:T(8,128)(2,1)S(1)}, u32[]{:S(2)}, u32[]{:S(2)}) collective-permute-start(bf16[256,512]{1,0:T(8,128)(2,1)S(1)} %collective-permute-done.refs_7_), channel_id=1, source_target_pairs={{0,6},{1,7},{2,0},{3,1},{4,2},{5,3},{6,4},{7,5},{8,14},{9,15},{10,... | collective-permute-start | bytes 786440 | tf_op jit(solution)/shard_map/ppermute | solution.py:37
  39.5 8.3 %project_most.1 = (bf16[3,256,512]{2,1,0:T(8,128)(2,1)S(1)}, f32[3,256,512]{2,1,0:T(8,128)S(1)}) custom-call(s32[5]{0:T(128)S(1)} %stack.53.ids, bf16[3,4096,512]{2,1,0:T(8,128)(2,1)S(1)} %bitcast.29, bf16[512,512]{1,0:T(8,128)(2,1)S(1)} %copy-done, bf16[512,512]{1,0:T(8,128)(2,1)S(1)} %collective-permute-done.5.refs_1_, ...), custom_call_target="tpu_custom_call" | custom-call | flops 20000000000 | bytes 20971520 | tf_op jit(solution)/shard_map/project_most/pallas_call | solution.py:61
  47.8 0.1 collective-permute-start.15
  47.9 0.1 pad_add_fusion.at
  48.0 1.4 %collective-permute-done.15.other_ref = bf16[256,512]{1,0:T(8,128)(2,1)S(1)} collective-permute-done((bf16[256,512]{1,0:T(8,128)(2,1)S(1)}, bf16[256,512]{1,0:T(8,128)(2,1)S(1)}, u32[]{:S(2)}, u32[]{:S(2)}) %collective-permute-start.15) | collective-permute-done | bytes 262176 | tf_op jit(solution)/shard_map/ppermute | solution.py:41
  49.4 4.3 %project_rest.1 = (bf16[512,512]{1,0:T(8,128)(2,1)}, bf16[16,512]{1,0:T(8,128)(2,1)}, bf16[544,128]{1,0:T(8,128)(2,1)}, bf16[544,128]{1,0:T(8,128)(2,1)}, bf16[5...) custom-call(s32[2]{0:T(128)S(1)} %pad_add_fusion.at, bf16[256,512]{1,0:T(8,128)(2,1)S(1)} %collective-permute-done.1.own_ref, ...), custom_call_target="tpu_custom_call" | custom-call | flops 4000000000 | bytes 4194304 | tf_op jit(solution)/shard_map/project_rest/pallas_call | solution.py:61
  53.8 0.2 collective-permute-start.20
  54.0 1.5 %collective-permute-start.16 = (bf16[544,128]{1,0:T(8,128)(2,1)}, bf16[544,128]{1,0:T(8,128)(2,1)S(1)}, u32[]{:S(2)}, u32[]{:S(2)}) collective-permute-start(bf16[544,128]{1,0:T(8,128)(2,1)} %get-tuple-element.45), channel_id=1, source_target_pairs={{0,8},{8,0},{16,24},{24,16},{1,9},{9,1},{17,25},{25,17},{2,10},{10... | collective-permute-start | bytes 417800 | tf_op jit(solution)/shard_map/ppermute | solution.py:512
  55.5 1.5 %collective-permute-start.18 = (bf16[544,128]{1,0:T(8,128)(2,1)}, bf16[544,128]{1,0:T(8,128)(2,1)S(1)}, u32[]{:S(2)}, u32[]{:S(2)}) collective-permute-start(bf16[544,128]{1,0:T(8,128)(2,1)} %get-tuple-element.48), channel_id=1, source_target_pairs={{0,16},{8,24},{16,0},{24,8},{1,17},{9,25},{17,1},{25,9},{2,18},{10... | collective-permute-start | bytes 417800 | tf_op jit(solution)/shard_map/ppermute | solution.py:512
  57.0 0.5 collective-permute-start.19
  57.6 1.9 %constant_dynamic-slice_fusion.3 = (bf16[512,512]{1,0:T(8,128)(2,1)S(1)}, bf16[512,512]{1,0:T(8,128)(2,1)S(1)}, bf16[512,512]{1,0:T(8,128)(2,1)S(1)}, bf16[512,512]{1,0:T(8,128)(2,1)S(1)}) fusion(bf16[512,4096]{1,0:T(8,128)(2,1)} %param.14, s32[]{:T(128)S(6)} %select_n.110, s32[]{:T(128)S(6)} %select_n.113, s32[]{:T(128)S(6)} %select_n.112, s32[]{:T(128)S(6)} %select_n.111), kind=kLoop, calls=%fused_computation.18 | loop fusion | bytes 4194320 | tf_op jit(solution)/shard_map/dynamic_slice | solution.py:610
  59.5 0.3 pad_maximum_fusion.1.w_ref
  59.8 0.8 collective-permute-done.16.refs_1_
  60.6 1.6 %collective-permute-start.17 = (bf16[16,512]{1,0:T(8,128)(2,1)S(1)}, bf16[16,512]{1,0:T(8,128)(2,1)S(1)}, u32[]{:S(2)}, u32[]{:S(2)}) collective-permute-start(bf16[16,512]{1,0:T(8,128)(2,1)S(1)} %copy-done.1), channel_id=1, source_target_pairs={{0,8},{8,16},{16,24},{24,0},{1,9},{9,17},{17,25},{25,1},{2,10},{10... | collective-permute-start | bytes 49160 | tf_op jit(solution)/shard_map/ppermute | solution.py:37
  62.2 2.3 %collective-permute-done.18.refs_2_ = bf16[544,128]{1,0:T(8,128)(2,1)S(1)} collective-permute-done((bf16[544,128]{1,0:T(8,128)(2,1)}, bf16[544,128]{1,0:T(8,128)(2,1)S(1)}, u32[]{:S(2)}, u32[]{:S(2)}) %collective-permute-start.18) | collective-permute-done | bytes 139296 | tf_op jit(solution)/shard_map/ppermute | solution.py:512
  64.5 2.6 %long_filter.1 = (bf16[512,128]{1,0:T(8,128)(2,1)S(1)}, bf16[512,128]{1,0:T(8,128)(2,1)S(1)}, bf16[512,128]{1,0:T(8,128)(2,1)S(1)}, bf16[512,128]{1,0:T(8,128)(2,1)S(1)}) custom-call(s32[1]{0:T(128)} %bitcast.1.at, bf16[544,128]{1,0:T(8,128)(2,1)S(1)} %copy-done.7, bf16[544,128]{1,0:T(8,128)(2,1)S(1)} %collective-permute-done.16.refs_1_, ...), custom_call_target="tpu_custom_call" | custom-call | flops 6000000000 | bytes 6291456 | tf_op jit(solution)/shard_map/long_filter/pallas_call | solution.py:61
  67.2 1.3 %collective-permute-start.21 = (bf16[512,128]{1,0:T(8,128)(2,1)S(1)}, bf16[512,128]{1,0:T(8,128)(2,1)S(1)}, u32[]{:S(2)}, u32[]{:S(2)}) collective-permute-start(bf16[512,128]{1,0:T(8,128)(2,1)S(1)} %get-tuple-element.58), channel_id=1, source_target_pairs={{0,8},{8,0},{16,24},{24,16},{1,9},{9,1},{17,25},{25,17},{2,10},{10... | collective-permute-start | bytes 393224 | tf_op jit(solution)/shard_map/ppermute | solution.py:512
  68.5 0.7 collective-permute-start.22
  69.1 1.6 %collective-permute-start.23 = (bf16[512,128]{1,0:T(8,128)(2,1)S(1)}, bf16[512,128]{1,0:T(8,128)(2,1)S(1)}, u32[]{:S(2)}, u32[]{:S(2)}) collective-permute-start(bf16[512,128]{1,0:T(8,128)(2,1)S(1)} %get-tuple-element.60), channel_id=1, source_target_pairs={{0,24},{8,16},{16,8},{24,0},{1,25},{9,17},{17,9},{25,1},{2,26},{10... | collective-permute-start | bytes 393224 | tf_op jit(solution)/shard_map/ppermute | solution.py:512
  70.8 2.4 %collective-permute-done.21.refs_1_ = bf16[512,128]{1,0:T(8,128)(2,1)S(1)} collective-permute-done((bf16[512,128]{1,0:T(8,128)(2,1)S(1)}, bf16[512,128]{1,0:T(8,128)(2,1)S(1)}, u32[]{:S(2)}, u32[]{:S(2)}) %collective-permute-start.21) | collective-permute-done | bytes 131104 | tf_op jit(solution)/shard_map/ppermute | solution.py:512
  73.2 2.6 %collective-permute-done.22.refs_2_ = bf16[512,128]{1,0:T(8,128)(2,1)S(1)} collective-permute-done((bf16[512,128]{1,0:T(8,128)(2,1)S(1)}, bf16[512,128]{1,0:T(8,128)(2,1)S(1)}, u32[]{:S(2)}, u32[]{:S(2)}) %collective-permute-start.22) | collective-permute-done | bytes 131104 | tf_op jit(solution)/shard_map/ppermute | solution.py:512
  75.8 0.2 gate_blocks.1.a_ref
  76.0 0.1 collective-permute-start.24
  76.1 1.9 %collective-permute-done.24.b_ref = bf16[512,512]{1,0:T(8,128)(2,1)S(1)} collective-permute-done((bf16[512,512]{1,0:T(8,128)(2,1)S(1)}, bf16[512,512]{1,0:T(8,128)(2,1)S(1)}, u32[]{:S(2)}, u32[]{:S(2)}) %collective-permute-start.24) | collective-permute-done | bytes 524320 | tf_op jit(solution)/shard_map/ppermute | solution.py:41
  78.0 0.7 output_shares.4
  78.7 1.7 %collective-permute-start.29 = (bf16[256,512]{1,0:T(8,128)(2,1)S(1)}, bf16[256,512]{1,0:T(8,128)(2,1)S(1)}, u32[]{:S(2)}, u32[]{:S(2)}) collective-permute-start(bf16[256,512]{1,0:T(8,128)(2,1)S(1)} %get-tuple-element.65), channel_id=1, source_target_pairs={{0,6},{1,7},{2,0},{3,1},{4,2},{5,3},{6,4},{7,5},{8,14},{9,15},{10,... | collective-permute-start | bytes 786440 | tf_op jit(solution)/shard_map/ppermute | solution.py:37
  80.4 0.1 pad_add_fusion.1._
  80.5 0.4 collective-permute-start.25
  80.9 2.3 %output_shares.5 = (f32[256,512]{1,0:T(8,128)S(1)}, bf16[256,512]{1,0:T(8,128)(2,1)S(1)}, bf16[256,512]{1,0:T(8,128)(2,1)S(1)}, f32[256,512]{1,0:T(8,128)S(1)}) custom-call(s32[2]{0:T(128)S(1)} %pad_add_fusion.1._, bf16[512,512]{1,0:T(8,128)(2,1)S(1)} %gate_blocks.1.a_ref, bf16[512,512]{1,0:T(8,128)(2,1)S(1)} %collective-permute-done.24.b_ref, ...), custom_call_target="tpu_custom_call" | custom-call | flops 1000000000 | bytes 1048576 | tf_op jit(solution)/shard_map/output_shares/pallas_call | solution.py:61
  83.2 3.5 %collective-permute-start.27 = (bf16[256,512]{1,0:T(8,128)(2,1)S(1)}, bf16[256,512]{1,0:T(8,128)(2,1)S(1)}, u32[]{:S(2)}, u32[]{:S(2)}) collective-permute-start(bf16[256,512]{1,0:T(8,128)(2,1)S(1)} %get-tuple-element.63), channel_id=1, source_target_pairs={{0,6},{1,7},{2,0},{3,1},{4,2},{5,3},{6,4},{7,5},{8,14},{9,15},{10,... | collective-permute-start | bytes 786440 | tf_op jit(solution)/shard_map/ppermute | solution.py:37
  86.7 6.9 %collective-permute-done.29 = bf16[256,512]{1,0:T(8,128)(2,1)S(1)} collective-permute-done((bf16[256,512]{1,0:T(8,128)(2,1)S(1)}, bf16[256,512]{1,0:T(8,128)(2,1)S(1)}, u32[]{:S(2)}, u32[]{:S(2)}) %collective-permute-start.29) | collective-permute-done | bytes 262176 | tf_op jit(solution)/shard_map/ppermute | solution.py:37
  93.6 0.1 add_convert_fusion
  93.7 0.1 add_convert_fusion.1
  93.8 2.1 %collective-permute-start.26 = (bf16[256,512]{1,0:T(8,128)(2,1)S(1)}, bf16[256,512]{1,0:T(8,128)(2,1)S(1)}, u32[]{:S(2)}, u32[]{:S(2)}) collective-permute-start(bf16[256,512]{1,0:T(8,128)(2,1)S(1)} %add_convert_fusion.1), channel_id=1, source_target_pairs={{0,2},{1,3},{2,4},{3,5},{4,6},{5,7},{6,0},{7,1},{8,10},{9,11},{10,... | collective-permute-start | bytes 786440 | tf_op jit(solution)/shard_map/ppermute | solution.py:37
  95.9 0.7 output_shares.3.own_ref
  96.6 8.2 %collective-permute-done.27.refs_1_ = bf16[256,512]{1,0:T(8,128)(2,1)S(1)} collective-permute-done((bf16[256,512]{1,0:T(8,128)(2,1)S(1)}, bf16[256,512]{1,0:T(8,128)(2,1)S(1)}, u32[]{:S(2)}, u32[]{:S(2)}) %collective-permute-start.27) | collective-permute-done | bytes 262176 | tf_op jit(solution)/shard_map/ppermute | solution.py:37
  104.8 5.5 %collective-permute-done.30.refs_3_ = bf16[256,512]{1,0:T(8,128)(2,1)S(1)} collective-permute-done((bf16[256,512]{1,0:T(8,128)(2,1)S(1)}, bf16[256,512]{1,0:T(8,128)(2,1)S(1)}, u32[]{:S(2)}, u32[]{:S(2)}) %collective-permute-start.30) | collective-permute-done | bytes 262176 | tf_op jit(solution)/shard_map/ppermute | solution.py:37
  110.3 4.9 %collective-permute-done.26.refs_0_ = bf16[256,512]{1,0:T(8,128)(2,1)S(1)} collective-permute-done((bf16[256,512]{1,0:T(8,128)(2,1)S(1)}, bf16[256,512]{1,0:T(8,128)(2,1)S(1)}, u32[]{:S(2)}, u32[]{:S(2)}) %collective-permute-start.26) | collective-permute-done | bytes 262176 | tf_op jit(solution)/shard_map/ppermute | solution.py:37
  115.2 1.0 add_up.1
  (54 shorter events, 0.3 us)
Async XLA Ops:
  1.0 19.7 %collective-permute-start.6 = (bf16[256,512]{1,0:T(8,128)(2,1)S(1)}, bf16[256,512]{1,0:T(8,128)(2,1)S(1)}, u32[]{:S(2)}, u32[]{:S(2)}) collective-permute-start(bf16[256,512]{1,0:T(8,128)(2,1)S(1)} %slice.18), channel_id=1, source_target_pairs={{0,2},{1,3},{2,4},{3,5},{4,6},{5,7},{6,0},{7,1},{8,10},{9,11},{10,... | collective-permute-start | bytes 786440 | tf_op jit(solution)/shard_map/ppermute | solution.py:37
  5.0 15.7 %collective-permute-start = (bf16[256,512]{1,0:T(8,128)(2,1)S(1)}, bf16[256,512]{1,0:T(8,128)(2,1)S(1)}, u32[]{:S(2)}, u32[]{:S(2)}) collective-permute-start(bf16[256,512]{1,0:T(8,128)(2,1)S(1)} %slice.19), channel_id=1, source_target_pairs={{0,6},{1,7},{2,0},{3,1},{4,2},{5,3},{6,4},{7,5},{8,14},{9,15},{10,... | collective-permute-start | bytes 786440 | tf_op jit(solution)/shard_map/ppermute | solution.py:37
  7.1 20.0 %collective-permute-start.7 = (bf16[256,512]{1,0:T(8,128)(2,1)S(1)}, bf16[256,512]{1,0:T(8,128)(2,1)S(1)}, u32[]{:S(2)}, u32[]{:S(2)}) collective-permute-start(bf16[256,512]{1,0:T(8,128)(2,1)S(1)} %slice.19), channel_id=1, source_target_pairs={{0,2},{1,3},{2,4},{3,5},{4,6},{5,7},{6,0},{7,1},{8,10},{9,11},{10,... | collective-permute-start | bytes 786440 | tf_op jit(solution)/shard_map/ppermute | solution.py:37
  7.1 22.9 %collective-permute-start.10 = (bf16[256,512]{1,0:T(8,128)(2,1)S(1)}, bf16[256,512]{1,0:T(8,128)(2,1)S(1)}, u32[]{:S(2)}, u32[]{:S(2)}) collective-permute-start(bf16[256,512]{1,0:T(8,128)(2,1)S(1)} %slice.18), channel_id=1, source_target_pairs={{0,6},{1,7},{2,0},{3,1},{4,2},{5,3},{6,4},{7,5},{8,14},{9,15},{10,... | collective-permute-start | bytes 786440 | tf_op jit(solution)/shard_map/ppermute | solution.py:37
  12.2 5.0 %collective-permute-start.2 = (bf16[512,128]{1,0:T(8,128)(2,1)S(1)}, bf16[512,128]{1,0:T(8,128)(2,1)S(1)}, u32[]{:S(2)}, u32[]{:S(2)}) collective-permute-start(bf16[512,128]{1,0:T(8,128)(2,1)S(1)} %get-tuple-element.77), channel_id=1, source_target_pairs={{0,8},{8,0},{16,24},{24,16},{1,9},{9,1},{17,25},{25,17},{2,10},{10... | collective-permute-start | bytes 393224 | tf_op jit(solution)/shard_map/ppermute | solution.py:512
  14.0 6.7 %copy-start.8 = (bf16[3,3,512]{2,1,0:T(4,128)(2,1)S(1)}, bf16[3,3,512]{2,1,0:T(4,128)(2,1)}, u32[]{:S(2)}) copy-start(bf16[3,3,512]{2,1,0:T(4,128)(2,1)} %param.11) | copy-start | bytes 27652
  17.3 5.0 %collective-permute-start.3 = (bf16[512,128]{1,0:T(8,128)(2,1)S(1)}, bf16[512,128]{1,0:T(8,128)(2,1)S(1)}, u32[]{:S(2)}, u32[]{:S(2)}) collective-permute-start(bf16[512,128]{1,0:T(8,128)(2,1)S(1)} %get-tuple-element.37), channel_id=1, source_target_pairs={{0,16},{8,24},{16,0},{24,8},{1,17},{9,25},{17,1},{25,9},{2,18},{10... | collective-permute-start | bytes 393224 | tf_op jit(solution)/shard_map/ppermute | solution.py:512
  20.6 6.5 %copy-start = (bf16[512,512]{1,0:T(8,128)(2,1)S(1)}, bf16[512,512]{1,0:T(8,128)(2,1)}, u32[]{:S(2)}) copy-start(bf16[512,512]{1,0:T(8,128)(2,1)} %refs_0_) | copy-start | bytes 1572868
  20.7 14.3 %collective-permute-start.13 = (bf16[256,512]{1,0:T(8,128)(2,1)S(1)}, bf16[256,512]{1,0:T(8,128)(2,1)S(1)}, u32[]{:S(2)}, u32[]{:S(2)}) collective-permute-start(bf16[256,512]{1,0:T(8,128)(2,1)S(1)} %collective-permute-done.6.refs_2_), channel_id=1, source_target_pairs={{0,2},{1,3},{2,4},{3,5},{4,6},{5,7},{6,0},{7,1},{8,10},{9,11},{10,... | collective-permute-start | bytes 786440 | tf_op jit(solution)/shard_map/ppermute | solution.py:37
  20.7 14.2 %collective-permute-start.12 = (bf16[256,512]{1,0:T(8,128)(2,1)S(1)}, bf16[256,512]{1,0:T(8,128)(2,1)S(1)}, u32[]{:S(2)}, u32[]{:S(2)}) collective-permute-start(bf16[256,512]{1,0:T(8,128)(2,1)S(1)} %collective-permute-done.refs_7_), channel_id=1, source_target_pairs={{0,1},{1,0},{2,3},{3,2},{4,5},{5,4},{6,7},{7,6},{8,9},{9,8},{10,11... | collective-permute-start | bytes 786440 | tf_op jit(solution)/shard_map/ppermute | solution.py:41
  21.7 13.7 %copy-start.2 = (bf16[1024,1024]{1,0:T(8,128)(2,1)S(1)}, bf16[1024,1024]{1,0:T(8,128)(2,1)}, u32[]{:S(2)}) copy-start(bf16[1024,1024]{1,0:T(8,128)(2,1)} %constant.109.clone.refs_4_) | copy-start | bytes 6291460
  22.2 7.7 %collective-permute-start.4 = (bf16[512,128]{1,0:T(8,128)(2,1)S(1)}, bf16[512,128]{1,0:T(8,128)(2,1)S(1)}, u32[]{:S(2)}, u32[]{:S(2)}) collective-permute-start(bf16[512,128]{1,0:T(8,128)(2,1)S(1)} %get-tuple-element.38), channel_id=1, source_target_pairs={{0,24},{8,16},{16,8},{24,0},{1,25},{9,17},{17,9},{25,1},{2,26},{10... | collective-permute-start | bytes 393224 | tf_op jit(solution)/shard_map/ppermute | solution.py:512
  24.9 14.6 %slice-start = ((s8[12582912]{0:T(1024)(128)(4,1)}), s8[4194304]{0:T(1024)(128)(4,1)S(1)}, s32[]{:S(2)}) async-start(s8[12582912]{0:T(1024)(128)(4,1)} %bitcast.27), calls=%async_computation | async-start | bytes 8388608
  27.2 12.3 %collective-permute-start.5 = (bf16[512,512]{1,0:T(8,128)(2,1)S(1)}, bf16[512,512]{1,0:T(8,128)(2,1)S(1)}, u32[]{:S(2)}, u32[]{:S(2)}) collective-permute-start(bf16[512,512]{1,0:T(8,128)(2,1)S(1)} %copy-done), channel_id=1, source_target_pairs={{0,1},{1,0},{2,3},{3,2},{4,5},{5,4},{6,7},{7,6},{8,9},{9,8},{10,11... | collective-permute-start | bytes 1572872 | tf_op jit(solution)/shard_map/ppermute | solution.py:41
  30.0 9.5 %collective-permute-start.8 = (bf16[256,512]{1,0:T(8,128)(2,1)S(1)}, bf16[256,512]{1,0:T(8,128)(2,1)S(1)}, u32[]{:S(2)}, u32[]{:S(2)}) collective-permute-start(bf16[256,512]{1,0:T(8,128)(2,1)S(1)} %collective-permute-done.6.refs_2_), channel_id=1, source_target_pairs={{0,1},{1,0},{2,3},{3,2},{4,5},{5,4},{6,7},{7,6},{8,9},{9,8},{10,11... | collective-permute-start | bytes 786440 | tf_op jit(solution)/shard_map/ppermute | solution.py:41
  30.0 7.9 %collective-permute-start.9 = (bf16[256,512]{1,0:T(8,128)(2,1)S(1)}, bf16[256,512]{1,0:T(8,128)(2,1)S(1)}, u32[]{:S(2)}, u32[]{:S(2)}) collective-permute-start(bf16[256,512]{1,0:T(8,128)(2,1)S(1)} %collective-permute-done.7.refs_3_), channel_id=1, source_target_pairs={{0,1},{1,0},{2,3},{3,2},{4,5},{5,4},{6,7},{7,6},{8,9},{9,8},{10,11... | collective-permute-start | bytes 786440 | tf_op jit(solution)/shard_map/ppermute | solution.py:41
  34.9 4.6 %collective-permute-start.11 = (bf16[256,512]{1,0:T(8,128)(2,1)S(1)}, bf16[256,512]{1,0:T(8,128)(2,1)S(1)}, u32[]{:S(2)}, u32[]{:S(2)}) collective-permute-start(bf16[256,512]{1,0:T(8,128)(2,1)S(1)} %collective-permute-done.10.refs_6_), channel_id=1, source_target_pairs={{0,1},{1,0},{2,3},{3,2},{4,5},{5,4},{6,7},{7,6},{8,9},{9,8},{10,11... | collective-permute-start | bytes 786440 | tf_op jit(solution)/shard_map/ppermute | solution.py:41
  34.9 4.6 %collective-permute-start.14 = (bf16[256,512]{1,0:T(8,128)(2,1)S(1)}, bf16[256,512]{1,0:T(8,128)(2,1)S(1)}, u32[]{:S(2)}, u32[]{:S(2)}) collective-permute-start(bf16[256,512]{1,0:T(8,128)(2,1)S(1)} %collective-permute-done.13.refs_10_), channel_id=1, source_target_pairs={{0,1},{1,0},{2,3},{3,2},{4,5},{5,4},{6,7},{7,6},{8,9},{9,8},{10,11... | collective-permute-start | bytes 786440 | tf_op jit(solution)/shard_map/ppermute | solution.py:41
  35.5 4.1 %slice-start.1 = ((s8[12582912]{0:T(1024)(128)(4,1)}), s8[4194304]{0:T(1024)(128)(4,1)S(1)}, s32[]{:S(2)}) async-start(s8[12582912]{0:T(1024)(128)(4,1)} %bitcast.27), calls=%async_computation.1 | async-start | bytes 8388608
  35.5 4.1 %slice-start.2 = ((s8[12582912]{0:T(1024)(128)(4,1)}), s8[4194304]{0:T(1024)(128)(4,1)S(1)}, s32[]{:S(2)}) async-start(s8[12582912]{0:T(1024)(128)(4,1)} %bitcast.27), calls=%async_computation.2 | async-start | bytes 8388608
  37.8 10.0 %collective-permute-start.1 = (bf16[256,512]{1,0:T(8,128)(2,1)S(1)}, bf16[256,512]{1,0:T(8,128)(2,1)S(1)}, u32[]{:S(2)}, u32[]{:S(2)}) collective-permute-start(bf16[256,512]{1,0:T(8,128)(2,1)S(1)} %collective-permute-done.refs_7_), channel_id=1, source_target_pairs={{0,6},{1,7},{2,0},{3,1},{4,2},{5,3},{6,4},{7,5},{8,14},{9,15},{10,... | collective-permute-start | bytes 786440 | tf_op jit(solution)/shard_map/ppermute | solution.py:37
  47.8 1.6 %collective-permute-start.15 = (bf16[256,512]{1,0:T(8,128)(2,1)S(1)}, bf16[256,512]{1,0:T(8,128)(2,1)S(1)}, u32[]{:S(2)}, u32[]{:S(2)}) collective-permute-start(bf16[256,512]{1,0:T(8,128)(2,1)S(1)} %collective-permute-done.1.own_ref), channel_id=1, source_target_pairs={{0,1},{1,0},{2,3},{3,2},{4,5},{5,4},{6,7},{7,6},{8,9},{9,8},{10,11... | collective-permute-start | bytes 786440 | tf_op jit(solution)/shard_map/ppermute | solution.py:41
  53.8 13.4 %collective-permute-start.20 = (bf16[512,2048]{1,0:T(8,128)(2,1)}, bf16[512,2048]{1,0:T(8,128)(2,1)S(1)}, u32[]{:S(2)}, u32[]{:S(2)}) collective-permute-start(bf16[512,2048]{1,0:T(8,128)(2,1)} %pad_maximum_fusion), channel_id=1, source_target_pairs={{0,1},{1,0},{2,3},{3,2},{4,5},{5,4},{6,7},{7,6},{8,9},{9,8},{10,11... | collective-permute-start | bytes 6291464 | tf_op jit(solution)/shard_map/ppermute | solution.py:41
  54.0 6.6 %collective-permute-start.16 = (bf16[544,128]{1,0:T(8,128)(2,1)}, bf16[544,128]{1,0:T(8,128)(2,1)S(1)}, u32[]{:S(2)}, u32[]{:S(2)}) collective-permute-start(bf16[544,128]{1,0:T(8,128)(2,1)} %get-tuple-element.45), channel_id=1, source_target_pairs={{0,8},{8,0},{16,24},{24,16},{1,9},{9,1},{17,25},{25,17},{2,10},{10... | collective-permute-start | bytes 417800 | tf_op jit(solution)/shard_map/ppermute | solution.py:512
  55.5 9.0 %collective-permute-start.18 = (bf16[544,128]{1,0:T(8,128)(2,1)}, bf16[544,128]{1,0:T(8,128)(2,1)S(1)}, u32[]{:S(2)}, u32[]{:S(2)}) collective-permute-start(bf16[544,128]{1,0:T(8,128)(2,1)} %get-tuple-element.48), channel_id=1, source_target_pairs={{0,16},{8,24},{16,0},{24,8},{1,17},{9,25},{17,1},{25,9},{2,18},{10... | collective-permute-start | bytes 417800 | tf_op jit(solution)/shard_map/ppermute | solution.py:512
  57.0 3.6 %copy-start.1 = (bf16[16,512]{1,0:T(8,128)(2,1)S(1)}, bf16[16,512]{1,0:T(8,128)(2,1)}, u32[]{:S(2)}) copy-start(bf16[16,512]{1,0:T(8,128)(2,1)} %get-tuple-element.46.here_ref) | copy-start | bytes 49156
  57.0 7.5 %copy-start.3 = (bf16[512,1024]{1,0:T(8,128)(2,1)S(1)}, bf16[512,1024]{1,0:T(8,128)(2,1)}, u32[]{:S(2)}) copy-start(bf16[512,1024]{1,0:T(8,128)(2,1)} %constant.110.clone.refs_7_) | copy-start | bytes 3145732
  57.0 7.5 %copy-start.4 = (bf16[1024,512]{1,0:T(8,128)(2,1)S(1)}, bf16[1024,512]{1,0:T(8,128)(2,1)}, u32[]{:S(2)}) copy-start(bf16[1024,512]{1,0:T(8,128)(2,1)} %constant.111.clone.refs_6_) | copy-start | bytes 3145732
  57.0 7.5 %copy-start.6 = (bf16[1024,512]{1,0:T(8,128)(2,1)S(1)}, bf16[1024,512]{1,0:T(8,128)(2,1)}, u32[]{:S(2)}) copy-start(bf16[1024,512]{1,0:T(8,128)(2,1)} %taps_spectra.1.refs_5_) | copy-start | bytes 3145732
  57.0 7.5 %copy-start.7 = (bf16[544,128]{1,0:T(8,128)(2,1)S(1)}, bf16[544,128]{1,0:T(8,128)(2,1)}, u32[]{:S(2)}) copy-start(bf16[544,128]{1,0:T(8,128)(2,1)} %get-tuple-element.47.refs_0_) | copy-start | bytes 417796
  57.0 7.5 %collective-permute-start.19 = (bf16[544,128]{1,0:T(8,128)(2,1)}, bf16[544,128]{1,0:T(8,128)(2,1)S(1)}, u32[]{:S(2)}, u32[]{:S(2)}) collective-permute-start(bf16[544,128]{1,0:T(8,128)(2,1)} %get-tuple-element.49), channel_id=1, source_target_pairs={{0,24},{8,16},{16,8},{24,0},{1,25},{9,17},{17,9},{25,1},{2,26},{10... | collective-permute-start | bytes 417800 | tf_op jit(solution)/shard_map/ppermute | solution.py:512
  60.6 10.2 %collective-permute-start.17 = (bf16[16,512]{1,0:T(8,128)(2,1)S(1)}, bf16[16,512]{1,0:T(8,128)(2,1)S(1)}, u32[]{:S(2)}, u32[]{:S(2)}) collective-permute-start(bf16[16,512]{1,0:T(8,128)(2,1)S(1)} %copy-done.1), channel_id=1, source_target_pairs={{0,8},{8,16},{16,24},{24,0},{1,9},{9,17},{17,25},{25,1},{2,10},{10... | collective-permute-start | bytes 49160 | tf_op jit(solution)/shard_map/ppermute | solution.py:37
  64.5 11.3 %copy-start.5 = (bf16[512,512]{1,0:T(8,128)(2,1)S(1)}, bf16[512,512]{1,0:T(8,128)(2,1)}, u32[]{:S(2)}) copy-start(bf16[512,512]{1,0:T(8,128)(2,1)} %get-tuple-element.43.gate_ref) | copy-start | bytes 1572868
  67.2 6.0 %collective-permute-start.21 = (bf16[512,128]{1,0:T(8,128)(2,1)S(1)}, bf16[512,128]{1,0:T(8,128)(2,1)S(1)}, u32[]{:S(2)}, u32[]{:S(2)}) collective-permute-start(bf16[512,128]{1,0:T(8,128)(2,1)S(1)} %get-tuple-element.58), channel_id=1, source_target_pairs={{0,8},{8,0},{16,24},{24,16},{1,9},{9,1},{17,25},{25,17},{2,10},{10... | collective-permute-start | bytes 393224 | tf_op jit(solution)/shard_map/ppermute | solution.py:512
  68.5 7.3 %collective-permute-start.22 = (bf16[512,128]{1,0:T(8,128)(2,1)S(1)}, bf16[512,128]{1,0:T(8,128)(2,1)S(1)}, u32[]{:S(2)}, u32[]{:S(2)}) collective-permute-start(bf16[512,128]{1,0:T(8,128)(2,1)S(1)} %get-tuple-element.59), channel_id=1, source_target_pairs={{0,16},{8,24},{16,0},{24,8},{1,17},{9,25},{17,1},{25,9},{2,18},{10... | collective-permute-start | bytes 393224 | tf_op jit(solution)/shard_map/ppermute | solution.py:512
  69.1 6.7 %collective-permute-start.23 = (bf16[512,128]{1,0:T(8,128)(2,1)S(1)}, bf16[512,128]{1,0:T(8,128)(2,1)S(1)}, u32[]{:S(2)}, u32[]{:S(2)}) collective-permute-start(bf16[512,128]{1,0:T(8,128)(2,1)S(1)} %get-tuple-element.60), channel_id=1, source_target_pairs={{0,24},{8,16},{16,8},{24,0},{1,25},{9,17},{17,9},{25,1},{2,26},{10... | collective-permute-start | bytes 393224 | tf_op jit(solution)/shard_map/ppermute | solution.py:512
  76.0 2.0 %collective-permute-start.24 = (bf16[512,512]{1,0:T(8,128)(2,1)S(1)}, bf16[512,512]{1,0:T(8,128)(2,1)S(1)}, u32[]{:S(2)}, u32[]{:S(2)}) collective-permute-start(bf16[512,512]{1,0:T(8,128)(2,1)S(1)} %gate_blocks.1.a_ref), channel_id=1, source_target_pairs={{0,1},{1,0},{2,3},{3,2},{4,5},{5,4},{6,7},{7,6},{8,9},{9,8},{10,11... | collective-permute-start | bytes 1572872 | tf_op jit(solution)/shard_map/ppermute | solution.py:41
  78.7 14.8 %collective-permute-start.29 = (bf16[256,512]{1,0:T(8,128)(2,1)S(1)}, bf16[256,512]{1,0:T(8,128)(2,1)S(1)}, u32[]{:S(2)}, u32[]{:S(2)}) collective-permute-start(bf16[256,512]{1,0:T(8,128)(2,1)S(1)} %get-tuple-element.65), channel_id=1, source_target_pairs={{0,6},{1,7},{2,0},{3,1},{4,2},{5,3},{6,4},{7,5},{8,14},{9,15},{10,... | collective-permute-start | bytes 786440 | tf_op jit(solution)/shard_map/ppermute | solution.py:37
  80.5 13.2 %collective-permute-start.25 = (bf16[256,512]{1,0:T(8,128)(2,1)S(1)}, bf16[256,512]{1,0:T(8,128)(2,1)S(1)}, u32[]{:S(2)}, u32[]{:S(2)}) collective-permute-start(bf16[256,512]{1,0:T(8,128)(2,1)S(1)} %get-tuple-element.61), channel_id=1, source_target_pairs={{0,2},{1,3},{2,4},{3,5},{4,6},{5,7},{6,0},{7,1},{8,10},{9,11},{10,... | collective-permute-start | bytes 786440 | tf_op jit(solution)/shard_map/ppermute | solution.py:37
  83.2 21.6 %collective-permute-start.27 = (bf16[256,512]{1,0:T(8,128)(2,1)S(1)}, bf16[256,512]{1,0:T(8,128)(2,1)S(1)}, u32[]{:S(2)}, u32[]{:S(2)}) collective-permute-start(bf16[256,512]{1,0:T(8,128)(2,1)S(1)} %get-tuple-element.63), channel_id=1, source_target_pairs={{0,6},{1,7},{2,0},{3,1},{4,2},{5,3},{6,4},{7,5},{8,14},{9,15},{10,... | collective-permute-start | bytes 786440 | tf_op jit(solution)/shard_map/ppermute | solution.py:37
  86.7 18.1 %collective-permute-start.28 = (bf16[256,512]{1,0:T(8,128)(2,1)S(1)}, bf16[256,512]{1,0:T(8,128)(2,1)S(1)}, u32[]{:S(2)}, u32[]{:S(2)}) collective-permute-start(bf16[256,512]{1,0:T(8,128)(2,1)S(1)} %get-tuple-element.64), channel_id=1, source_target_pairs={{0,2},{1,3},{2,4},{3,5},{4,6},{5,7},{6,0},{7,1},{8,10},{9,11},{10,... | collective-permute-start | bytes 786440 | tf_op jit(solution)/shard_map/ppermute | solution.py:37
  93.6 16.7 %collective-permute-start.30 = (bf16[256,512]{1,0:T(8,128)(2,1)S(1)}, bf16[256,512]{1,0:T(8,128)(2,1)S(1)}, u32[]{:S(2)}, u32[]{:S(2)}) collective-permute-start(bf16[256,512]{1,0:T(8,128)(2,1)S(1)} %add_convert_fusion), channel_id=1, source_target_pairs={{0,6},{1,7},{2,0},{3,1},{4,2},{5,3},{6,4},{7,5},{8,14},{9,15},{10,... | collective-permute-start | bytes 786440 | tf_op jit(solution)/shard_map/ppermute | solution.py:37
  93.8 21.4 %collective-permute-start.26 = (bf16[256,512]{1,0:T(8,128)(2,1)S(1)}, bf16[256,512]{1,0:T(8,128)(2,1)S(1)}, u32[]{:S(2)}, u32[]{:S(2)}) collective-permute-start(bf16[256,512]{1,0:T(8,128)(2,1)S(1)} %add_convert_fusion.1), channel_id=1, source_target_pairs={{0,2},{1,3},{2,4},{3,5},{4,6},{5,7},{6,0},{7,1},{8,10},{9,11},{10,... | collective-permute-start | bytes 786440 | tf_op jit(solution)/shard_map/ppermute | solution.py:37
